TPU v7x, 32 devices: a whole 2x2x4 slice. The times are simulated.
32 devices in a mesh: shard: 8 (over z, x), tensor: 4 (over y, core).
Axes of the slice: x: 2, y: 2, z: 4, core: 2. Of those that a mesh axis runs over, the one named last changes fastest.
Arguments:
- gradients: bfloat16 [3, 1152, 6912], P(None, 'shard', 'tensor'), may hold values from -6 to 6
- weights: float32 [3, 1152, 6912], P(None, 'shard', 'tensor'), may hold values from -6 to 6
- projectors: bfloat16 [1152, 3, 256], replicated, may hold values from -0.1875 to 0.1875
- first_moment: float32 [3, 256, 4, 1728], P(None, None, 'tensor', 'shard'), may hold values from -3 to 3
- second_moment: float32 [3, 256, 4, 1728], P(None, None, 'tensor', 'shard'), may hold values from 0.05 to 4
Outputs:
- new_weight: float32 [3, 1152, 6912], P(None, 'shard', 'tensor')
- new_first: float32 [3, 256, 4, 1728], P(None, None, 'tensor', 'shard')
- new_second: float32 [3, 256, 4, 1728], P(None, None, 'tensor', 'shard')
- new_basis: bfloat16 [1152, 3, 256], replicated
All inputs are finite; a program needn't handle non-finite values.
Results may differ from a plain program's by a relative error of at most 0.001.
The roundings to bfloat16 on the way count: a program that leaves them out, or rounds other values in their place, can miss the bound.
Values may be sent and summed in bfloat16 or wider, within the bound.
No kernel may reach another device: no remote copies, remote signals or barrier semaphores. Data moves between devices by JAX's collectives and lax.ppermute only.
A program may use at most 64 MiB of HBM per device.

v0:
```python
import math

import jax
import jax.numpy as jnp
from jax import lax
from jax.sharding import PartitionSpec as P

NS_STEPS = 5


corr_first = 1.0
corr_second = 0.6323045752


def newton_steps(iterate, inner):
    return 1.5 * iterate - 0.5 * jnp.einsum(
        "dmr,mrs->dms",
        iterate,
        inner,
        precision=lax.Precision.HIGHEST,
        preferred_element_type=jnp.float32,
    )


def column_inner(iterate):
    return jnp.einsum(
        "dmr,dms->mrs",
        iterate,
        iterate,
        precision=lax.Precision.HIGHEST,
        preferred_element_type=jnp.float32,
    )


def per_device(gradients, weights, projectors, first_moment, second_moment):
    factor = math.sqrt(projectors.shape[0])
    regrouped = lax.all_to_all(gradients, "shard", split_axis=2, concat_axis=1, tiled=True)
    mats, width, cols = regrouped.shape
    rank = projectors.shape[2]
    projected = jnp.einsum(
        "dmr,mdc->mrc", projectors, regrouped, preferred_element_type=jnp.float32
    )
    first_new = 0.9 * first_moment.reshape(mats, rank, cols) + 0.1 * projected
    second_new = 0.999 * second_moment.reshape(mats, rank, cols) + 0.001 * projected * projected
    update = (first_new / corr_first / (jnp.sqrt(second_new / corr_second) + 1e-08)).astype(
        jnp.bfloat16
    )
    delta = jnp.einsum("dmr,mrc->mdc", projectors, update, preferred_element_type=jnp.float32)
    returned = lax.all_to_all(delta, "shard", split_axis=1, concat_axis=2, tiled=True)
    new_weight = weights - 0.2 * returned
    back = jnp.einsum(
        "mdc,dmr->mcr", regrouped, projectors, preferred_element_type=jnp.float32
    ).astype(jnp.bfloat16)
    partial_sum = jnp.einsum("mdc,mcr->dmr", regrouped, back, preferred_element_type=jnp.float32)
    refresh = lax.psum(partial_sum, ("shard", "tensor"))
    norms = jnp.sqrt(jnp.sum(refresh * refresh, axis=(0, 2)) + 1e-06)
    iterate = refresh / norms[None, :, None]
    for sweep in range(NS_STEPS):
        iterate = newton_steps(iterate, column_inner(iterate))
    new_basis = (iterate * factor).astype(jnp.bfloat16)
    shape_four = first_moment.shape
    return (new_weight, first_new.reshape(shape_four), second_new.reshape(shape_four), new_basis)


def solution(mesh):
    in_specs = (
        P(None, "shard", "tensor"),
        P(None, "shard", "tensor"),
        P(),
        P(None, None, "tensor", "shard"),
        P(None, None, "tensor", "shard"),
    )
    out_specs = (
        P(None, "shard", "tensor"),
        P(None, None, "tensor", "shard"),
        P(None, None, "tensor", "shard"),
        P(),
    )
    return jax.shard_map(
        per_device, mesh=mesh, in_specs=in_specs, out_specs=out_specs, check_vma=False
    )
```

profile of v0, /device:TPU:0, one launch (start us, length us, event | category | flops | bytes accessed | tf_op | source)
XLA Modules:
  0.0 368.5 jit_solution(1491023084221276909)
XLA Ops:
  7.2 0.0 copy-start
  7.2 0.0 all-reduce.2.cloned.1.call-start
  7.2 6.3 %copy.62 = bf16[3,144,1728]{1,0,2:T(4,128)(2,1)} copy(bf16[3,144,1728]{2,1,0:T(8,128)(2,1)} %param.5) | data formatting | bytes 2985984 | tf_op args[0]
  13.6 7.5 %reshape.30 = bf16[8,2,46656]{2,1,0:T(2,128)(2,1)S(1)} reshape(bf16[1728,3,144]{2,1,0:T(4,128)(2,1)} %bitcast.105) | data formatting | bytes 2985984
  21.0 42.6 %all_to_all.27 = bf16[8,2,46656]{2,1,0:T(2,128)(2,1)} all-to-all(bf16[8,2,46656]{2,1,0:T(2,128)(2,1)S(1)} %reshape.30), channel_id=1, replica_groups=mesh['shard'=8,'tensor'=4] {'shard'}, dimensions={0} | all-to-all | bytes 2985984 | tf_op jit(solution)/shard_map/all_to_all | solution.py:37
  63.7 8.7 %reshape.31 = bf16[1728,3,144]{2,1,0:T(4,128)(2,1)} reshape(bf16[8,2,46656]{2,1,0:T(2,128)(2,1)} %all_to_all.27) | data formatting | bytes 2985984
  72.4 5.3 %copy.63 = bf16[3,144,8,216]{3,1,2,0:T(8,128)(2,1)S(1)} copy(bf16[3,144,8,216]{1,0,3,2:T(4,128)(2,1)} %bitcast.106) | data formatting | bytes 2985984 | tf_op jit(solution)/shard_map/all_to_all | solution.py:37
  77.7 0.0 copy-done
  77.7 3.1 convolution_bitcast_fusion
  80.8 0.0 all-reduce.2.cloned.1.call-update
  80.8 0.0 copy-start.5
  80.8 0.0 copy-start.7
  80.8 0.7 fusion.25
  81.5 0.0 copy-start.2
  81.6 0.8 copy-done.2
  82.4 0.0 copy-done.5
  82.4 0.0 copy-done.7
  82.4 2.5 convolution_bitcast_fusion.1
  84.9 5.9 %copy.66 = f32[3,1152,216]{2,0,1:T(4,128)} copy(f32[3,1152,216]{1,2,0:T(8,128)} %convolution_bitcast_fusion.1) | data formatting | bytes 5971968 | tf_op jit(solution)/shard_map/dmr,mrc->mdc/dot_general | solution.py:48
  90.7 0.0 copy-start.3
  90.7 0.0 copy-start.6
  90.7 0.0 copy-start.8
  90.7 5.2 %all-to-all-start.1 = ((f32[3,1152,216]{2,0,1:T(4,128)}), f32[3,1152,216]{2,0,1:T(4,128)}, u32[]{:S(2)}, u32[]{:S(2)}) async-start(f32[3,1152,216]{2,0,1:T(4,128)} %copy.66), calls=%async_computation.1 | async-start | bytes 9437184 | tf_op jit(solution)/shard_map/all_to_all | solution.py:49
  95.9 0.0 copy-done.3
  95.9 0.0 copy-done.6
  96.0 0.0 copy-done.8
  96.0 1.3 fusion.17
  97.2 202.7 %all-reduce.2.cloned.1.call-done = f32[1152,3,256]{0,2,1:T(8,128)} async-done(((f32[1152,3,256]{0,2,1:T(8,128)}), f32[1152,3,256]{0,2,1:T(8,128)}) %all-reduce.2.cloned.1.call-update) | async-done | bytes 3538960 | tf_op jit(solution)/shard_map/psum | solution.py:55
  299.9 0.0 copy-start.4
  299.9 2.6 multiply_reduce_fusion
  302.5 0.5 copy-done.4
  303.0 4.1 %fusion.13 = f32[3,256,256]{1,2,0:T(8,128)S(1)} fusion(f32[1152,3,256]{0,2,1:T(8,128)S(1)} %copy-done.4, f32[3]{0:T(128)S(1)} %add_sqrt_fusion), kind=kOutput, calls=%fused_computation.29 | convolution fusion | flops 2718793728 | bytes 4325388 | tf_op jit(solution)/shard_map/dmr,dms->mrs/dot_general | solution.py:26
  307.1 3.9 %fusion.1 = f32[1152,3,256]{0,2,1:T(8,128)S(1)} fusion(f32[3,256,256]{1,2,0:T(8,128)S(1)} %fusion.13, f32[1152,3,256]{0,2,1:T(8,128)S(1)} %copy-done.4, f32[3]{0:T(128)S(1)} %add_sqrt_fusion), kind=kOutput, calls=%fused_computation.6 | convolution fusion | flops 2722332672 | bytes 7864332 | tf_op jit(solution)/shard_map/dmr,mrs->dms/dot_general | solution.py:16
  311.0 4.0 %fusion.26 = f32[3,256,256]{1,2,0:T(8,128)S(1)} fusion(f32[1152,3,256]{0,2,1:T(8,128)S(1)} %fusion.1), kind=kOutput, calls=%fused_computation.42 | convolution fusion | flops 2717908992 | bytes 4325376 | tf_op jit(solution)/shard_map/dmr,dms->mrs/dot_general | solution.py:26
  315.0 3.7 %fusion.3 = f32[1152,3,256]{0,2,1:T(8,128)S(1)} fusion(f32[3,256,256]{1,2,0:T(8,128)S(1)} %fusion.26, f32[1152,3,256]{0,2,1:T(8,128)S(1)} %fusion.1), kind=kOutput, calls=%fused_computation.8 | convolution fusion | flops 2720563200 | bytes 7864320 | tf_op jit(solution)/shard_map/dmr,mrs->dms/dot_general | solution.py:16
  318.7 3.8 %fusion.27 = f32[3,256,256]{1,2,0:T(8,128)S(1)} fusion(f32[1152,3,256]{0,2,1:T(8,128)S(1)} %fusion.3), kind=kOutput, calls=%fused_computation.43 | convolution fusion | flops 2717908992 | bytes 4325376 | tf_op jit(solution)/shard_map/dmr,dms->mrs/dot_general | solution.py:26
  322.5 3.9 %fusion.5 = f32[1152,3,256]{0,2,1:T(8,128)S(1)} fusion(f32[3,256,256]{1,2,0:T(8,128)S(1)} %fusion.27, f32[1152,3,256]{0,2,1:T(8,128)S(1)} %fusion.3), kind=kOutput, calls=%fused_computation.10 | convolution fusion | flops 2720563200 | bytes 7864320 | tf_op jit(solution)/shard_map/dmr,mrs->dms/dot_general | solution.py:16
  326.4 3.8 %fusion.28 = f32[3,256,256]{1,2,0:T(8,128)S(1)} fusion(f32[1152,3,256]{0,2,1:T(8,128)S(1)} %fusion.5), kind=kOutput, calls=%fused_computation.44 | convolution fusion | flops 2717908992 | bytes 4325376 | tf_op jit(solution)/shard_map/dmr,dms->mrs/dot_general | solution.py:26
  330.2 3.7 %fusion.7 = f32[1152,3,256]{0,2,1:T(8,128)S(1)} fusion(f32[3,256,256]{1,2,0:T(8,128)S(1)} %fusion.28, f32[1152,3,256]{0,2,1:T(8,128)S(1)} %fusion.5), kind=kOutput, calls=%fused_computation.12 | convolution fusion | flops 2720563200 | bytes 7864320 | tf_op jit(solution)/shard_map/dmr,mrs->dms/dot_general | solution.py:16
  333.9 3.8 %fusion.29 = f32[3,256,256]{1,2,0:T(8,128)S(1)} fusion(f32[1152,3,256]{0,2,1:T(8,128)S(1)} %fusion.7), kind=kOutput, calls=%fused_computation.45 | convolution fusion | flops 2717908992 | bytes 4325376 | tf_op jit(solution)/shard_map/dmr,dms->mrs/dot_general | solution.py:26
  337.7 4.1 %fusion.11 = bf16[1152,3,256]{0,2,1:T(8,128)(2,1)S(1)} fusion(f32[3,256,256]{1,2,0:T(8,128)S(1)} %fusion.29, f32[1152,3,256]{0,2,1:T(8,128)S(1)} %fusion.7), kind=kOutput, calls=%fused_computation.20 | convolution fusion | flops 2722332672 | bytes 6094848 | tf_op jit(solution)/shard_map/dmr,mrs->dms/dot_general | solution.py:16
  341.9 2.2 copy.88
  344.1 0.0 all-to-all-done.1
  344.1 3.1 copy_multiply_fusion
  347.2 3.8 %copy.68 = f32[3,144,8,216]{3,2,1,0:T(8,128)} copy(f32[3,144,8,216]{3,1,2,0:T(8,128)S(1)} %bitcast.104) | data formatting | bytes 5971968 | tf_op jit(solution)/shard_map/mul | solution.py:50
  351.0 5.4 %mul.117 = f32[3,144,1728]{2,1,0:T(8,128)} reshape(f32[3,144,8,216]{3,2,1,0:T(8,128)} %copy.68) | data formatting | bytes 5971968 | tf_op jit(solution)/shard_map/mul | solution.py:50
  356.4 4.8 %sub.18 = f32[3,144,1728]{2,1,0:T(8,128)} subtract(f32[3,144,1728]{2,1,0:T(8,128)} %param.6, f32[3,144,1728]{2,1,0:T(8,128)} %mul.117) | non-fusion elementwise | flops 746496 | bytes 8957952 | tf_op jit(solution)/shard_map/sub | solution.py:50
  361.2 0.0 copy-done.1
  (2 shorter events, 0.0 us)
Async XLA Ops:
  7.2 70.5 %copy-start = (bf16[1152,3,256]{2,0,1:T(8,128)(2,1)S(1)}, bf16[1152,3,256]{2,0,1:T(8,128)(2,1)}, u32[]{:S(2)}) copy-start(bf16[1152,3,256]{2,0,1:T(8,128)(2,1)} %param.7) | copy-start | bytes 5308420
  7.2 292.8 %all-reduce.2.cloned.1.call-start = ((), (), s32[]{:S(2)}) async-start(), calls=%async_computation.2 | async-start | bytes 7077888 | tf_op jit(solution)/shard_map/psum | solution.py:55
  80.8 1.6 copy-start.5
  80.8 1.6 copy-start.7
  81.5 0.8 copy-start.2
  90.7 5.2 %copy-start.3 = (f32[3,256,216]{1,2,0:T(8,128)S(1)}, f32[3,256,216]{1,2,0:T(8,128)}, u32[]{:S(2)}) copy-start(f32[3,256,216]{1,2,0:T(8,128)} %copy-done.2) | copy-start | bytes 1990660
  90.7 5.2 %copy-start.6 = (f32[3,256,1,216]{1,3,2,0:T(8,128)S(1)}, f32[3,256,1,216]{1,3,2,0:T(8,128)}, u32[]{:S(2)}) copy-start(f32[3,256,1,216]{1,3,2,0:T(8,128)} %param.8) | copy-start | bytes 1990660
  90.7 5.2 %copy-start.8 = (f32[3,256,1,216]{1,3,2,0:T(8,128)S(1)}, f32[3,256,1,216]{1,3,2,0:T(8,128)}, u32[]{:S(2)}) copy-start(f32[3,256,1,216]{1,3,2,0:T(8,128)} %param.9) | copy-start | bytes 1990660
  90.7 253.4 %all-to-all-start.1 = ((f32[3,1152,216]{2,0,1:T(4,128)}), f32[3,1152,216]{2,0,1:T(4,128)}, u32[]{:S(2)}, u32[]{:S(2)}) async-start(f32[3,1152,216]{2,0,1:T(4,128)} %copy.66), calls=%async_computation.1 | async-start | bytes 9437184 | tf_op jit(solution)/shard_map/all_to_all | solution.py:49
  299.9 3.1 copy-start.4
  351.0 10.2 %copy-start.1 = (bf16[1152,3,256]{2,0,1:T(8,128)(2,1)S(1)}, bf16[1152,3,256]{2,0,1:T(8,128)(2,1)}, u32[]{:S(2)}) copy-start(bf16[1152,3,256]{2,0,1:T(8,128)(2,1)} %param.7) | copy-start | bytes 5308420
Sparse Core Ops, SparseCore 0:
  80.9 218.9 all-reduce.1
where the time goes:
time: 374 us; the launch traced here: 369 us
  waiting for transfers between devices  203 us (54%)
  local copies, waits for them, and re-layouts  46.4 us (12%)
  matrix products  45.1 us (12%)
  blocking collectives  42.6 us (11%)
  between operations  14.7 us (4%)
  other arithmetic  11.8 us (3%)
  starting transfers between devices  5.24 us (1%)
    psum x1, waiting for transfers between devices, per_device(): refresh = lax.psum(partial_sum, ('shard', 'tensor'))  203 us
    all_to_all x1, blocking collectives, per_device(): lax.all_to_all(gradients, 'shard', split_axis=2, concat_axis=1, tiled=True)  42.6 us
    unnamed x22, local copies, waits for them, and re-layouts  26.1 us
    dot_general x5, matrix products, newton_steps(): jnp.einsum('dmr,mrs->dms', iterate, inner, precision=lax.Precision.HIGHES...  19.4 us
    dot_general x5, matrix products, column_inner(): jnp.einsum('dmr,dms->mrs', iterate, iterate, precision=lax.Precision.HIGH...  19.4 us
    mul x2, local copies, waits for them, and re-layouts, per_device(): new_weight = weights - 0.2 * returned  9.21 us
  transfers between devices with their start and end apart: 2, of which 1 were waited for; matrix products, arithmetic and copies ran while one was open for 15% of the time, Pallas kernels for 0%

commit v1 on v0

--- a/solution.py
+++ b/solution.py
@@ -1,38 +1,250 @@
+import functools
 import math
 
 import jax
 import jax.numpy as jnp
 from jax import lax
+from jax.experimental import pallas as pl
+from jax.experimental.pallas import tpu as pltpu
 from jax.sharding import PartitionSpec as P
 
 NS_STEPS = 5
-
-
-corr_first = 1.0
-corr_second = 0.6323045752
+CORR_FIRST = 1.0
+CORR_SECOND = 0.6323045752
+HIGHEST = lax.Precision.HIGHEST
+VMEM = pl.BlockSpec(memory_space=pltpu.VMEM)
+PARAMS = pltpu.CompilerParams(vmem_limit_bytes=32 * 1024 * 1024)
+
+
+def dot(a, b, dims, **kw):
+    return lax.dot_general(a, b, (dims, ((), ())), preferred_element_type=jnp.float32, **kw)
+
+
+def nn(a, b, **kw):
+    return dot(a, b, ((1,), (0,)), **kw)
+
+
+def tn(a, b, **kw):
+    return dot(a, b, ((0,), (0,)), **kw)
+
+
+def nt(a, b, **kw):
+    return dot(a, b, ((1,), (1,)), **kw)
+
+
+def row_owner():
+    tensor = lax.axis_index("tensor")
+    return (tensor & 1) * 4 + (tensor >> 1) * 2 + (lax.axis_index("shard") & 1)
+
+
+def pack_kernel(parts, cols, g_ref, *refs):
+    outs, held = refs[:parts], refs[parts]
+    rows, wide = held.shape[1:]
+    for part in range(parts):
+        held[part, :, :cols] = g_ref[0, :, part * cols : (part + 1) * cols]
+        held[part, :, cols:] = jnp.zeros((rows, wide - cols), held.dtype)
+    me = lax.axis_index("shard")
+    for k in range(parts):
+        outs[k][...] = held[me ^ k]
+
+
+def pack(gradients, mat, parts, cols, wide):
+    _, rows, whole = gradients.shape
+    return pl.pallas_call(
+        functools.partial(pack_kernel, parts, cols),
+        grid=(1,),
+        in_specs=[pl.BlockSpec((1, rows, whole), lambda i: (mat, 0, 0))],
+        out_specs=[pl.BlockSpec((rows, wide), lambda i: (0, 0))] * parts,
+        out_shape=[jax.ShapeDtypeStruct((rows, wide), gradients.dtype)] * parts,
+        scratch_shapes=[pltpu.VMEM((parts, rows, wide), gradients.dtype)],
+        compiler_params=PARAMS,
+        name="cut_columns",
+    )(gradients)
+
+
+def project_kernel(parts, cols, *refs):
+    blocks, (p_ref, first_ref, second_ref), refs = refs[:parts], refs[parts : parts + 3], refs[parts + 3 :]
+    update_ref, first_out, second_out, send_ref, keep_ref, grad = refs[-6:]
+    rows = blocks[0].shape[0]
+    me = lax.axis_index("shard")
+    for k in range(parts):
+        grad[pl.ds(pl.multiple_of((me ^ k) * rows, rows), rows), :] = blocks[k][...]
+    projected = tn(grad[...], p_ref[0])
+    back = projected.astype(jnp.bfloat16)
+    own = row_owner()
+    half = parts // 2
+    for j in list(range(half, parts)) + list(range(half)):
+        at = pl.multiple_of((own ^ j) * rows, rows)
+        term = nn(grad[pl.ds(at, rows), :], back)
+        out = send_ref if j >= half else keep_ref
+        out[(j % half) * rows : (j % half + 1) * rows, :] = term
+    projected = projected[:cols]
+    first_new = 0.9 * first_ref[0] + 0.1 * projected
+    second_new = 0.999 * second_ref[0] + 0.001 * projected * projected
+    first_out[0] = first_new
+    second_out[0] = second_new
+    update_ref[...] = (
+        first_new / CORR_FIRST / (jnp.sqrt(second_new / CORR_SECOND) + 1e-08)
+    ).astype(jnp.bfloat16)
+
+
+def project(blocks, projectors, first, second, mat, earlier):
+    parts = len(blocks)
+    rows, wide = blocks[0].shape
+    mats, width, rank = projectors.shape
+    cols = first.shape[1]
+    moment = pl.BlockSpec((1, cols, rank), lambda i: (mat, 0, 0))
+    whole = lambda *shape: pl.BlockSpec(shape, lambda i: (0,) * len(shape))
+    in_specs = [whole(rows, wide)] * parts
+    in_specs += [pl.BlockSpec((1, width, rank), lambda i: (mat, 0, 0)), moment, moment]
+    in_specs += [pl.BlockSpec(memory_space=pl.ANY)] * len(earlier)
+    half = width // 2
+    return pl.pallas_call(
+        functools.partial(project_kernel, parts, cols),
+        grid=(1,),
+        in_specs=in_specs,
+        out_specs=[whole(cols, rank), moment, moment, whole(half, rank), whole(half, rank)],
+        out_shape=[
+            jax.ShapeDtypeStruct((cols, rank), jnp.bfloat16),
+            jax.ShapeDtypeStruct(first.shape, first.dtype),
+            jax.ShapeDtypeStruct(second.shape, second.dtype),
+            jax.ShapeDtypeStruct((half, rank), jnp.float32),
+            jax.ShapeDtypeStruct((half, rank), jnp.float32),
+        ],
+        scratch_shapes=[pltpu.VMEM((width, wide), jnp.bfloat16)],
+        input_output_aliases={parts + 3 + i: 1 + i for i in range(len(earlier))},
+        compiler_params=PARAMS,
+        name="project",
+    )(*blocks, projectors, first, second, *earlier)
+
+
+def basis_kernel(factor, low_ref, high_ref, *refs):
+    out_ref = refs[-1]
+    half, rank = low_ref.shape
+    rows = half // 4
+    low, high = low_ref[...], high_ref[...]
+    norm = jnp.sqrt(jnp.sum(low * low) + jnp.sum(high * high) + 1e-06)
+    low, high = low / norm, high / norm
+    gram = tn(low, low, precision=HIGHEST) + tn(high, high, precision=HIGHEST)
+    eye = (
+        lax.broadcasted_iota(jnp.int32, (rank, rank), 0)
+        == lax.broadcasted_iota(jnp.int32, (rank, rank), 1)
+    ).astype(jnp.float32)
+    total = None
+    for sweep in range(NS_STEPS):
+        step = 1.5 * eye - 0.5 * gram
+        total = step if total is None else nn(total, step, precision=HIGHEST)
+        if sweep < NS_STEPS - 1:
+            gram = nn(nn(gram, step, precision=HIGHEST), step, precision=HIGHEST)
+    own = row_owner()
+    for j in range(8):
+        source = low if j < 4 else high
+        block = nn(source[(j % 4) * rows : (j % 4 + 1) * rows], total, precision=HIGHEST)
+        at = pl.multiple_of((own ^ j) * rows, rows)
+        out_ref[0, pl.ds(at, rows), :] = (block * factor).astype(jnp.bfloat16)
+
+
+def basis(low, high, mat, mats, factor, earlier):
+    half, rank = low.shape
+    whole = lambda *shape: pl.BlockSpec(shape, lambda i: (0,) * len(shape))
+    return pl.pallas_call(
+        functools.partial(basis_kernel, factor),
+        grid=(1,),
+        in_specs=[whole(half, rank)] * 2 + [pl.BlockSpec(memory_space=pl.ANY)] * len(earlier),
+        out_specs=pl.BlockSpec((1, 2 * half, rank), lambda i: (mat, 0, 0)),
+        out_shape=jax.ShapeDtypeStruct((mats, 2 * half, rank), jnp.bfloat16),
+        input_output_aliases={2: 0} if earlier else {},
+        compiler_params=PARAMS,
+        name="newton_schulz",
+    )(low, high, *earlier)
+
+
+def weight_kernel(cols, w_ref, p_ref, u_ref, out_ref):
+    rows = w_ref.shape[1]
+    at = pl.multiple_of(lax.axis_index("shard") * rows, rows)
+    own = p_ref[0, pl.ds(at, rows), :]
+    for part in range(u_ref.shape[0]):
+        span = slice(part * cols, (part + 1) * cols)
+        out_ref[0, :, span] = w_ref[0, :, span] - 0.2 * nt(own, u_ref[part, 0])
+
+
+def weight_step(weights, projectors, updates):
+    mats, rows, whole = weights.shape
+    parts, _, cols, rank = updates.shape
+    width = projectors.shape[1]
+    big = pl.BlockSpec((1, rows, whole), lambda m: (m, 0, 0))
+    return pl.pallas_call(
+        functools.partial(weight_kernel, cols),
+        grid=(mats,),
+        in_specs=[
+            big,
+            pl.BlockSpec((1, width, rank), lambda m: (m, 0, 0)),
+            pl.BlockSpec((parts, 1, cols, rank), lambda m: (0, m, 0, 0)),
+        ],
+        out_specs=big,
+        out_shape=jax.ShapeDtypeStruct(weights.shape, weights.dtype),
+        compiler_params=PARAMS,
+        name="weight_step",
+    )(weights, projectors, updates)
+
+
+def swap(x, axis, size, bit):
+    return lax.ppermute(x, axis, [(i, i ^ bit) for i in range(size)])
+
+
+def per_device(n_shard, n_tensor, gradients, weights, projectors, first_moment, second_moment):
+    factor = math.sqrt(projectors.shape[0])
+    mats, rows, whole = gradients.shape
+    cols = whole // n_shard
+    wide = -(-cols // 128) * 128
+    across = jnp.swapaxes(projectors, 0, 1)
+    first = jnp.swapaxes(first_moment[:, :, 0, :], 1, 2)
+    second = jnp.swapaxes(second_moment[:, :, 0, :], 1, 2)
+    core = lambda x: swap(x, "tensor", n_tensor, 1)
+    along_y = lambda x: swap(x, "tensor", n_tensor, 2)
+    along_x = lambda x: swap(x, "shard", n_shard, 1)
+    z_far = lambda x: swap(x, "shard", n_shard, 4)
+    z_near = lambda x: swap(x, "shard", n_shard, 2)
+
+    blocks = []
+    for mat in range(mats):
+        cut = pack(gradients, mat, n_shard, cols, wide)
+        blocks.append([cut[0]] + [swap(cut[k], "shard", n_shard, k) for k in range(1, n_shard)])
+    moments, bases, updates = (), (), []
+    for mat in range(mats):
+        update, *moments, send, keep = project(blocks[mat], across, first, second, mat, moments)
+        updates.append(update)
+        for exchange in (core, along_y, along_x):
+            got = exchange(send)
+            if keep.shape[0] > rows:
+                half = keep.shape[0] // 2
+                send, keep = keep[half:] + got[half:], keep[:half] + got[:half]
+            else:
+                keep = keep + got
+        keep = keep + z_far(keep)
+        keep = keep + z_near(keep)
+        keep = jnp.concatenate([keep, along_x(keep)])
+        keep = jnp.concatenate([keep, along_y(keep)])
+        bases = (basis(keep, core(keep), mat, mats, factor, bases),)
+    gathered = lax.all_gather(jnp.stack(updates), "shard")
+    new_weight = weight_step(weights, across, gathered)
+    back = lambda x: jnp.swapaxes(x, 1, 2)[:, :, None, :]
+    return (new_weight, back(moments[0]), back(moments[1]), jnp.swapaxes(bases[0], 0, 1))
 
 
 def newton_steps(iterate, inner):
     return 1.5 * iterate - 0.5 * jnp.einsum(
-        "dmr,mrs->dms",
-        iterate,
-        inner,
-        precision=lax.Precision.HIGHEST,
-        preferred_element_type=jnp.float32,
+        "dmr,mrs->dms", iterate, inner, precision=HIGHEST, preferred_element_type=jnp.float32
     )
 
 
 def column_inner(iterate):
     return jnp.einsum(
-        "dmr,dms->mrs",
-        iterate,
-        iterate,
-        precision=lax.Precision.HIGHEST,
-        preferred_element_type=jnp.float32,
-    )
-
-
-def per_device(gradients, weights, projectors, first_moment, second_moment):
+        "dmr,dms->mrs", iterate, iterate, precision=HIGHEST, preferred_element_type=jnp.float32
+    )
+
+
+def per_device_any(gradients, weights, projectors, first_moment, second_moment):
     factor = math.sqrt(projectors.shape[0])
     regrouped = lax.all_to_all(gradients, "shard", split_axis=2, concat_axis=1, tiled=True)
     mats, width, cols = regrouped.shape
@@ -42,7 +254,7 @@
     )
     first_new = 0.9 * first_moment.reshape(mats, rank, cols) + 0.1 * projected
     second_new = 0.999 * second_moment.reshape(mats, rank, cols) + 0.001 * projected * projected
-    update = (first_new / corr_first / (jnp.sqrt(second_new / corr_second) + 1e-08)).astype(
+    update = (first_new / CORR_FIRST / (jnp.sqrt(second_new / CORR_SECOND) + 1e-08)).astype(
         jnp.bfloat16
     )
     delta = jnp.einsum("dmr,mrc->mdc", projectors, update, preferred_element_type=jnp.float32)
@@ -76,6 +288,6 @@
         P(None, None, "tensor", "shard"),
         P(),
     )
-    return jax.shard_map(
-        per_device, mesh=mesh, in_specs=in_specs, out_specs=out_specs, check_vma=False
-    )
+    sizes = mesh.shape["shard"], mesh.shape["tensor"]
+    body = functools.partial(per_device, *sizes) if sizes == (8, 4) else per_device_any
+    return jax.shard_map(body, mesh=mesh, in_specs=in_specs, out_specs=out_specs, check_vma=False)

time: 374 us -> 203 us (0.54); the launches traced: 369 us -> 203 us
  waiting for transfers between devices: 203 us -> 81.7 us
  starting transfers between devices: 5.24 us -> 58.5 us
  matrix products: 45.1 us -> 0 us
  blocking collectives: 42.6 us -> 0 us
  Pallas kernels: 0 us -> 39.2 us
  local copies, waits for them, and re-layouts: 46.4 us -> 7.47 us
  other arithmetic: 11.8 us -> 1.42 us
    psum x1 -> x0, waiting for transfers between devices: 203 us -> none  [per_device(): refresh = lax.psum(partial_sum, ('shard', 'tensor'))]
    ppermute x0 -> x45, waiting for transfers between devices: none -> 81.6 us  [swap(): return lax.ppermute(x, axis, [(i, i ^ bit) for i in range(size)])]
    ppermute x0 -> x45, starting transfers between devices: none -> 58.4 us  [swap(): return lax.ppermute(x, axis, [(i, i ^ bit) for i in range(size)])]
    dot_general x13 -> x0, matrix products: 45.1 us -> none  [the longest x5 19.4 us: newton_steps(): jnp.einsum('dmr,mrs->dms', iterate, inner, precision=lax.Precision.HIGHES...]
    all_to_all x1 -> x0, blocking collectives: 42.6 us -> none  [per_device(): lax.all_to_all(gradients, 'shard', split_axis=2, concat_axis=1, tiled=True)]
    pallas_call x0 -> x10, Pallas kernels: none -> 39.2 us  [the longest x3 29.9 us: basis(): pl.pallas_call(functools.partial(basis_kernel, factor), grid=(1,), in_spe...]
    unnamed x22 -> x18, local copies, waits for them, and re-layouts: 26.1 us -> 7.47 us
    mul x2 -> x0, local copies, waits for them, and re-layouts: 9.21 us -> none  [per_device(): new_weight = weights - 0.2 * returned]
  transfers between devices with their start and end apart: 2 -> 46, of which waited for: 1 -> 19; matrix products, arithmetic and copies ran while one was open for 15% -> 0% of each run, Pallas kernels for 0% -> 17%
where the time goes in v1:
time: 203 us
  waiting for transfers between devices  81.7 us (40%)
  starting transfers between devices  58.5 us (29%)
  Pallas kernels  39.2 us (19%)
  between operations  14.3 us (7%)
  local copies, waits for them, and re-layouts  7.47 us (4%)
    ppermute x45, waiting for transfers between devices, swap(): return lax.ppermute(x, axis, [(i, i ^ bit) for i in range(size)])  81.6 us
    ppermute x45, starting transfers between devices, swap(): return lax.ppermute(x, axis, [(i, i ^ bit) for i in range(size)])  58.4 us
    pallas_call x3, Pallas kernels, basis(): pl.pallas_call(functools.partial(basis_kernel, factor), grid=(1,), in_spe...  29.9 us
    unnamed x18, local copies, waits for them, and re-layouts  7.47 us
    pallas_call x3, Pallas kernels, project(): pl.pallas_call(functools.partial(project_kernel, parts, cols), grid=(1,),...  5.02 us
  transfers between devices with their start and end apart: 46, of which 19 were waited for; matrix products, arithmetic and copies ran while one was open for 0% of the time, Pallas kernels for 17%

profile of v1, /device:TPU:0, one launch (start us, length us, event | category | flops | bytes accessed | tf_op | source)
XLA Modules:
  0.0 202.5 jit_solution(5790756354485385820)
XLA Ops:
  7.2 1.4 copy-done.1
  9.0 3.0 %collective-permute-start = (bf16[144,256]{1,0:T(8,128)(2,1)S(1)}, bf16[144,256]{1,0:T(8,128)(2,1)S(1)}, u32[]{:S(2)}, u32[]{:S(2)}) collective-permute-start(bf16[144,256]{1,0:T(8,128)(2,1)S(1)} %get-tuple-element.44), channel_id=1, source_target_pairs={{0,4},{4,0},{8,12},{12,8},{16,20},{20,16},{24,28},{28,24},{1,5},{5... | collective-permute-start | bytes 221192 | tf_op jit(solution)/shard_map/ppermute | solution.py:192
  12.0 1.6 collective-permute-start.1
  13.6 3.0 %collective-permute-start.3 = (bf16[144,256]{1,0:T(8,128)(2,1)S(1)}, bf16[144,256]{1,0:T(8,128)(2,1)S(1)}, u32[]{:S(2)}, u32[]{:S(2)}) collective-permute-start(bf16[144,256]{1,0:T(8,128)(2,1)S(1)} %get-tuple-element.47), channel_id=1, source_target_pairs={{0,16},{4,20},{8,24},{12,28},{16,0},{20,4},{24,8},{28,12},{1,17},{... | collective-permute-start | bytes 221192 | tf_op jit(solution)/shard_map/ppermute | solution.py:192
  16.6 1.3 collective-permute-start.4
  17.8 3.6 %collective-permute-start.5 = (bf16[144,256]{1,0:T(8,128)(2,1)S(1)}, bf16[144,256]{1,0:T(8,128)(2,1)S(1)}, u32[]{:S(2)}, u32[]{:S(2)}) collective-permute-start(bf16[144,256]{1,0:T(8,128)(2,1)S(1)} %get-tuple-element.49), channel_id=1, source_target_pairs={{0,24},{4,28},{8,16},{12,20},{16,8},{20,12},{24,0},{28,4},{1,25},{... | collective-permute-start | bytes 221192 | tf_op jit(solution)/shard_map/ppermute | solution.py:192
  22.9 3.1 %collective-permute-start.11 = (bf16[144,256]{1,0:T(8,128)(2,1)S(1)}, bf16[144,256]{1,0:T(8,128)(2,1)S(1)}, u32[]{:S(2)}, u32[]{:S(2)}) collective-permute-start(bf16[144,256]{1,0:T(8,128)(2,1)S(1)} %get-tuple-element.57), channel_id=1, source_target_pairs={{0,20},{4,16},{8,28},{12,24},{16,4},{20,0},{24,12},{28,8},{1,21},{... | collective-permute-start | bytes 221192 | tf_op jit(solution)/shard_map/ppermute | solution.py:192
  25.9 4.3 %collective-permute-done.4.refs_5_ = bf16[144,256]{1,0:T(8,128)(2,1)S(1)} collective-permute-done((bf16[144,256]{1,0:T(8,128)(2,1)S(1)}, bf16[144,256]{1,0:T(8,128)(2,1)S(1)}, u32[]{:S(2)}, u32[]{:S(2)}) %collective-permute-start.4) | collective-permute-done | bytes 73760 | tf_op jit(solution)/shard_map/ppermute | solution.py:192
  30.2 3.8 %collective-permute-start.12 = (bf16[144,256]{1,0:T(8,128)(2,1)S(1)}, bf16[144,256]{1,0:T(8,128)(2,1)S(1)}, u32[]{:S(2)}, u32[]{:S(2)}) collective-permute-start(bf16[144,256]{1,0:T(8,128)(2,1)S(1)} %get-tuple-element.58), channel_id=1, source_target_pairs={{0,24},{4,28},{8,16},{12,20},{16,8},{20,12},{24,0},{28,4},{1,25},{... | collective-permute-start | bytes 221192 | tf_op jit(solution)/shard_map/ppermute | solution.py:192
  35.9 2.3 %collective-permute-done.10.refs_4_ = bf16[144,256]{1,0:T(8,128)(2,1)S(1)} collective-permute-done((bf16[144,256]{1,0:T(8,128)(2,1)S(1)}, bf16[144,256]{1,0:T(8,128)(2,1)S(1)}, u32[]{:S(2)}, u32[]{:S(2)}) %collective-permute-start.10) | collective-permute-done | bytes 73760 | tf_op jit(solution)/shard_map/ppermute | solution.py:192
  38.2 2.6 %collective-permute-done.11.refs_5_ = bf16[144,256]{1,0:T(8,128)(2,1)S(1)} collective-permute-done((bf16[144,256]{1,0:T(8,128)(2,1)S(1)}, bf16[144,256]{1,0:T(8,128)(2,1)S(1)}, u32[]{:S(2)}, u32[]{:S(2)}) %collective-permute-start.11) | collective-permute-done | bytes 73760 | tf_op jit(solution)/shard_map/ppermute | solution.py:192
  41.7 2.8 %collective-permute-start.15 = (bf16[144,256]{1,0:T(8,128)(2,1)S(1)}, bf16[144,256]{1,0:T(8,128)(2,1)S(1)}, u32[]{:S(2)}, u32[]{:S(2)}) collective-permute-start(bf16[144,256]{1,0:T(8,128)(2,1)S(1)} %get-tuple-element.65), channel_id=1, source_target_pairs={{0,8},{4,12},{8,0},{12,4},{16,24},{20,28},{24,16},{28,20},{1,9},{5... | collective-permute-start | bytes 221192 | tf_op jit(solution)/shard_map/ppermute | solution.py:192
  45.3 2.6 %collective-permute-start.17 = (bf16[144,256]{1,0:T(8,128)(2,1)S(1)}, bf16[144,256]{1,0:T(8,128)(2,1)S(1)}, u32[]{:S(2)}, u32[]{:S(2)}) collective-permute-start(bf16[144,256]{1,0:T(8,128)(2,1)S(1)} %get-tuple-element.67), channel_id=1, source_target_pairs={{0,16},{4,20},{8,24},{12,28},{16,0},{20,4},{24,8},{28,12},{1,17},{... | collective-permute-start | bytes 221192 | tf_op jit(solution)/shard_map/ppermute | solution.py:192
  48.5 2.4 %collective-permute-start.19 = (bf16[144,256]{1,0:T(8,128)(2,1)S(1)}, bf16[144,256]{1,0:T(8,128)(2,1)S(1)}, u32[]{:S(2)}, u32[]{:S(2)}) collective-permute-start(bf16[144,256]{1,0:T(8,128)(2,1)S(1)} %get-tuple-element.69), channel_id=1, source_target_pairs={{0,24},{4,28},{8,16},{12,20},{16,8},{20,12},{24,0},{28,4},{1,25},{... | collective-permute-start | bytes 221192 | tf_op jit(solution)/shard_map/ppermute | solution.py:192
  50.9 2.0 %collective-permute-start.20 = (bf16[144,256]{1,0:T(8,128)(2,1)S(1)}, bf16[144,256]{1,0:T(8,128)(2,1)S(1)}, u32[]{:S(2)}, u32[]{:S(2)}) collective-permute-start(bf16[144,256]{1,0:T(8,128)(2,1)S(1)} %get-tuple-element.70), channel_id=1, source_target_pairs={{0,28},{4,24},{8,20},{12,16},{16,12},{20,8},{24,4},{28,0},{1,29},{... | collective-permute-start | bytes 221192 | tf_op jit(solution)/shard_map/ppermute | solution.py:192
  52.9 1.7 project.3
  55.4 1.7 project.4
  57.9 1.0 collective-permute-done.18.refs_5_
  58.9 1.7 project.5
  62.8 1.6 collective-permute-done.37
  64.5 1.6 collective-permute-start.38
  67.0 1.4 collective-permute-start.22
  68.4 6.0 %collective-permute-done.38 = f32[288,256]{1,0:T(8,128)S(1)} collective-permute-done((f32[288,256]{1,0:T(8,128)S(1)}, f32[288,256]{1,0:T(8,128)S(1)}, u32[]{:S(2)}, u32[]{:S(2)}) %collective-permute-start.38) | collective-permute-done | bytes 294944 | tf_op jit(solution)/shard_map/ppermute | solution.py:192
  75.3 5.5 %collective-permute-done.30 = f32[288,256]{1,0:T(8,128)S(1)} collective-permute-done((f32[288,256]{1,0:T(8,128)S(1)}, f32[288,256]{1,0:T(8,128)S(1)}, u32[]{:S(2)}, u32[]{:S(2)}) %collective-permute-start.30) | collective-permute-done | bytes 294944 | tf_op jit(solution)/shard_map/ppermute | solution.py:192
  81.6 4.7 %collective-permute-done.22 = f32[288,256]{1,0:T(8,128)S(1)} collective-permute-done((f32[288,256]{1,0:T(8,128)S(1)}, f32[288,256]{1,0:T(8,128)S(1)}, u32[]{:S(2)}, u32[]{:S(2)}) %collective-permute-start.22) | collective-permute-done | bytes 294944 | tf_op jit(solution)/shard_map/ppermute | solution.py:192
  87.1 3.7 %collective-permute-start.40 = (f32[144,256]{1,0:T(8,128)S(1)}, f32[144,256]{1,0:T(8,128)S(1)}, u32[]{:S(2)}, u32[]{:S(2)}) collective-permute-start(f32[144,256]{1,0:T(8,128)S(1)} %fusion), channel_id=1, source_target_pairs={{0,16},{4,20},{8,24},{12,28},{16,0},{20,4},{24,8},{28,12},{1,17},{... | collective-permute-start | bytes 442376 | tf_op jit(solution)/shard_map/ppermute | solution.py:192
  91.6 3.9 %collective-permute-start.24 = (f32[144,256]{1,0:T(8,128)S(1)}, f32[144,256]{1,0:T(8,128)S(1)}, u32[]{:S(2)}, u32[]{:S(2)}) collective-permute-start(f32[144,256]{1,0:T(8,128)S(1)} %fusion.2), channel_id=1, source_target_pairs={{0,16},{4,20},{8,24},{12,28},{16,0},{20,4},{24,8},{28,12},{1,17},{... | collective-permute-start | bytes 442376 | tf_op jit(solution)/shard_map/ppermute | solution.py:192
  95.5 16.2 %collective-permute-done.40 = f32[144,256]{1,0:T(8,128)S(1)} collective-permute-done((f32[144,256]{1,0:T(8,128)S(1)}, f32[144,256]{1,0:T(8,128)S(1)}, u32[]{:S(2)}, u32[]{:S(2)}) %collective-permute-start.40) | collective-permute-done | bytes 147488 | tf_op jit(solution)/shard_map/ppermute | solution.py:192
  111.8 9.3 %collective-permute-done.32 = f32[144,256]{1,0:T(8,128)S(1)} collective-permute-done((f32[144,256]{1,0:T(8,128)S(1)}, f32[144,256]{1,0:T(8,128)S(1)}, u32[]{:S(2)}, u32[]{:S(2)}) %collective-permute-start.32) | collective-permute-done | bytes 147488 | tf_op jit(solution)/shard_map/ppermute | solution.py:192
  121.3 8.1 %collective-permute-done.24 = f32[144,256]{1,0:T(8,128)S(1)} collective-permute-done((f32[144,256]{1,0:T(8,128)S(1)}, f32[144,256]{1,0:T(8,128)S(1)}, u32[]{:S(2)}, u32[]{:S(2)}) %collective-permute-start.24) | collective-permute-done | bytes 147488 | tf_op jit(solution)/shard_map/ppermute | solution.py:192
  129.5 2.9 %collective-permute-done.41 = f32[144,256]{1,0:T(8,128)S(1)} collective-permute-done((f32[144,256]{1,0:T(8,128)S(1)}, f32[144,256]{1,0:T(8,128)S(1)}, u32[]{:S(2)}, u32[]{:S(2)}) %collective-permute-start.41) | collective-permute-done | bytes 147488 | tf_op jit(solution)/shard_map/ppermute | solution.py:192
  132.4 1.5 collective-permute-start.42
  133.9 1.6 collective-permute-done.33
  135.5 1.5 collective-permute-start.34
  137.2 1.6 collective-permute-start.26
  138.8 1.6 collective-permute-start.43
  140.3 1.2 collective-permute-done.34
  141.6 1.6 collective-permute-start.35
  143.2 1.6 collective-permute-start.27
  144.8 4.0 %collective-permute-done.43 = f32[288,256]{1,0:T(8,128)S(1)} collective-permute-done((f32[288,256]{1,0:T(8,128)S(1)}, f32[288,256]{1,0:T(8,128)S(1)}, u32[]{:S(2)}, u32[]{:S(2)}) %collective-permute-start.43) | collective-permute-done | bytes 294944 | tf_op jit(solution)/shard_map/ppermute | solution.py:192
  148.9 6.2 %collective-permute-done.35 = f32[288,256]{1,0:T(8,128)S(1)} collective-permute-done((f32[288,256]{1,0:T(8,128)S(1)}, f32[288,256]{1,0:T(8,128)S(1)}, u32[]{:S(2)}, u32[]{:S(2)}) %collective-permute-start.35) | collective-permute-done | bytes 294944 | tf_op jit(solution)/shard_map/ppermute | solution.py:192
  155.2 3.5 %collective-permute-done.27 = f32[288,256]{1,0:T(8,128)S(1)} collective-permute-done((f32[288,256]{1,0:T(8,128)S(1)}, f32[288,256]{1,0:T(8,128)S(1)}, u32[]{:S(2)}, u32[]{:S(2)}) %collective-permute-start.27) | collective-permute-done | bytes 294944 | tf_op jit(solution)/shard_map/ppermute | solution.py:192
  158.9 10.0 %newton_schulz.3.refs_0_ = bf16[3,1152,256]{2,1,0:T(8,128)(2,1)} custom-call(f32[576,256]{1,0:T(8,128)S(1)} %pad_maximum_fusion.2.low_ref, f32[576,256]{1,0:T(8,128)S(1)} %collective-permute-done.44.high_ref), custom_call_target="tpu_custom_call" | custom-call | tf_op jit(solution)/shard_map/newton_schulz/pallas_call | solution.py:150
  168.9 9.8 %newton_schulz.4.refs_0_ = bf16[3,1152,256]{2,1,0:T(8,128)(2,1)} custom-call(f32[576,256]{1,0:T(8,128)S(1)} %pad_maximum_fusion.1.low_ref, f32[576,256]{1,0:T(8,128)S(1)} %collective-permute-done.36.high_ref, bf16[3,1152,256]{2,1,0:T(8,128)(2,1)} %newton_schulz.3.refs_0_), custom_call_target="tpu_custom_call", output_to_operand_aliasing={{}: (2, {})} | custom-call | tf_op jit(solution)/shard_map/newton_schulz/pallas_call | solution.py:150
  178.7 10.0 %newton_schulz.5 = bf16[3,1152,256]{2,1,0:T(8,128)(2,1)} custom-call(f32[576,256]{1,0:T(8,128)S(1)} %pad_maximum_fusion.low_ref, f32[576,256]{1,0:T(8,128)S(1)} %collective-permute-done.28.high_ref, bf16[3,1152,256]{2,1,0:T(8,128)(2,1)} %newton_schulz.4.refs_0_), custom_call_target="tpu_custom_call", output_to_operand_aliasing={{}: (2, {})} | custom-call | tf_op jit(solution)/shard_map/newton_schulz/pallas_call | solution.py:150
  188.8 1.9 copy-done.4
  190.7 1.7 copy-done.5
  192.4 3.3 %weight_step.1 = f32[3,144,1728]{2,1,0:T(8,128)} custom-call(f32[3,144,1728]{2,1,0:T(8,128)S(1)} %copy-done.4, bf16[3,1152,256]{2,1,0:T(8,128)(2,1)S(1)} %bitcast.25, bf16[8,3,216,256]{3,2,1,0:T(8,128)(2,1)S(1)} %bitcast.32), custom_call_target="tpu_custom_call" | custom-call | tf_op jit(solution)/shard_map/weight_step/pallas_call | solution.py:176
  (95 shorter events, 15.1 us)
Async XLA Ops:
  7.2 181.6 %all-gather.3.cloned.1.call-start = ((), (), s32[]{:S(2)}) async-start(), calls=%async_computation | async-start | bytes 2985984 | tf_op jit(solution)/shard_map/all_gather | solution.py:229
  8.9 44.0 %copy-start = (bf16[1152,3,256]{2,0,1:T(8,128)(2,1)S(1)}, bf16[1152,3,256]{2,0,1:T(8,128)(2,1)}, u32[]{:S(2)}) copy-start(bf16[1152,3,256]{2,0,1:T(8,128)(2,1)} %param.7) | copy-start | bytes 5308420
  9.0 44.0 %copy-start.2 = (f32[3,256,1,216]{1,3,2,0:T(8,128)S(1)}, f32[3,256,1,216]{1,3,2,0:T(8,128)}, u32[]{:S(2)}) copy-start(f32[3,256,1,216]{1,3,2,0:T(8,128)} %param.8) | copy-start | bytes 1990660
  9.0 8.9 %collective-permute-start = (bf16[144,256]{1,0:T(8,128)(2,1)S(1)}, bf16[144,256]{1,0:T(8,128)(2,1)S(1)}, u32[]{:S(2)}, u32[]{:S(2)}) collective-permute-start(bf16[144,256]{1,0:T(8,128)(2,1)S(1)} %get-tuple-element.44), channel_id=1, source_target_pairs={{0,4},{4,0},{8,12},{12,8},{16,20},{20,16},{24,28},{28,24},{1,5},{5... | collective-permute-start | bytes 221192 | tf_op jit(solution)/shard_map/ppermute | solution.py:192
  12.0 9.8 %collective-permute-start.1 = (bf16[144,256]{1,0:T(8,128)(2,1)S(1)}, bf16[144,256]{1,0:T(8,128)(2,1)S(1)}, u32[]{:S(2)}, u32[]{:S(2)}) collective-permute-start(bf16[144,256]{1,0:T(8,128)(2,1)S(1)} %get-tuple-element.45), channel_id=1, source_target_pairs={{0,8},{4,12},{8,0},{12,4},{16,24},{20,28},{24,16},{28,20},{1,9},{5... | collective-permute-start | bytes 221192 | tf_op jit(solution)/shard_map/ppermute | solution.py:192
  13.6 8.3 %collective-permute-start.2 = (bf16[144,256]{1,0:T(8,128)(2,1)S(1)}, bf16[144,256]{1,0:T(8,128)(2,1)S(1)}, u32[]{:S(2)}, u32[]{:S(2)}) collective-permute-start(bf16[144,256]{1,0:T(8,128)(2,1)S(1)} %get-tuple-element.46), channel_id=1, source_target_pairs={{0,12},{4,8},{8,4},{12,0},{16,28},{20,24},{24,20},{28,16},{1,13},{... | collective-permute-start | bytes 221192 | tf_op jit(solution)/shard_map/ppermute | solution.py:192
  13.6 9.3 %collective-permute-start.3 = (bf16[144,256]{1,0:T(8,128)(2,1)S(1)}, bf16[144,256]{1,0:T(8,128)(2,1)S(1)}, u32[]{:S(2)}, u32[]{:S(2)}) collective-permute-start(bf16[144,256]{1,0:T(8,128)(2,1)S(1)} %get-tuple-element.47), channel_id=1, source_target_pairs={{0,16},{4,20},{8,24},{12,28},{16,0},{20,4},{24,8},{28,12},{1,17},{... | collective-permute-start | bytes 221192 | tf_op jit(solution)/shard_map/ppermute | solution.py:192
  16.6 13.6 %collective-permute-start.4 = (bf16[144,256]{1,0:T(8,128)(2,1)S(1)}, bf16[144,256]{1,0:T(8,128)(2,1)S(1)}, u32[]{:S(2)}, u32[]{:S(2)}) collective-permute-start(bf16[144,256]{1,0:T(8,128)(2,1)S(1)} %get-tuple-element.48), channel_id=1, source_target_pairs={{0,20},{4,16},{8,28},{12,24},{16,4},{20,0},{24,12},{28,8},{1,21},{... | collective-permute-start | bytes 221192 | tf_op jit(solution)/shard_map/ppermute | solution.py:192
  17.8 16.2 %collective-permute-start.5 = (bf16[144,256]{1,0:T(8,128)(2,1)S(1)}, bf16[144,256]{1,0:T(8,128)(2,1)S(1)}, u32[]{:S(2)}, u32[]{:S(2)}) collective-permute-start(bf16[144,256]{1,0:T(8,128)(2,1)S(1)} %get-tuple-element.49), channel_id=1, source_target_pairs={{0,24},{4,28},{8,16},{12,20},{16,8},{20,12},{24,0},{28,4},{1,25},{... | collective-permute-start | bytes 221192 | tf_op jit(solution)/shard_map/ppermute | solution.py:192
  21.8 13.5 %collective-permute-start.6 = (bf16[144,256]{1,0:T(8,128)(2,1)S(1)}, bf16[144,256]{1,0:T(8,128)(2,1)S(1)}, u32[]{:S(2)}, u32[]{:S(2)}) collective-permute-start(bf16[144,256]{1,0:T(8,128)(2,1)S(1)} %get-tuple-element.50), channel_id=1, source_target_pairs={{0,28},{4,24},{8,20},{12,16},{16,12},{20,8},{24,4},{28,0},{1,29},{... | collective-permute-start | bytes 221192 | tf_op jit(solution)/shard_map/ppermute | solution.py:192
  21.9 16.3 %collective-permute-start.10 = (bf16[144,256]{1,0:T(8,128)(2,1)S(1)}, bf16[144,256]{1,0:T(8,128)(2,1)S(1)}, u32[]{:S(2)}, u32[]{:S(2)}) collective-permute-start(bf16[144,256]{1,0:T(8,128)(2,1)S(1)} %get-tuple-element.56), channel_id=1, source_target_pairs={{0,16},{4,20},{8,24},{12,28},{16,0},{20,4},{24,8},{28,12},{1,17},{... | collective-permute-start | bytes 221192 | tf_op jit(solution)/shard_map/ppermute | solution.py:192
  22.9 17.9 %collective-permute-start.11 = (bf16[144,256]{1,0:T(8,128)(2,1)S(1)}, bf16[144,256]{1,0:T(8,128)(2,1)S(1)}, u32[]{:S(2)}, u32[]{:S(2)}) collective-permute-start(bf16[144,256]{1,0:T(8,128)(2,1)S(1)} %get-tuple-element.57), channel_id=1, source_target_pairs={{0,20},{4,16},{8,28},{12,24},{16,4},{20,0},{24,12},{28,8},{1,21},{... | collective-permute-start | bytes 221192 | tf_op jit(solution)/shard_map/ppermute | solution.py:192
  30.2 10.8 %collective-permute-start.12 = (bf16[144,256]{1,0:T(8,128)(2,1)S(1)}, bf16[144,256]{1,0:T(8,128)(2,1)S(1)}, u32[]{:S(2)}, u32[]{:S(2)}) collective-permute-start(bf16[144,256]{1,0:T(8,128)(2,1)S(1)} %get-tuple-element.58), channel_id=1, source_target_pairs={{0,24},{4,28},{8,16},{12,20},{16,8},{20,12},{24,0},{28,4},{1,25},{... | collective-permute-start | bytes 221192 | tf_op jit(solution)/shard_map/ppermute | solution.py:192
  34.0 7.7 %collective-permute-start.13 = (bf16[144,256]{1,0:T(8,128)(2,1)S(1)}, bf16[144,256]{1,0:T(8,128)(2,1)S(1)}, u32[]{:S(2)}, u32[]{:S(2)}) collective-permute-start(bf16[144,256]{1,0:T(8,128)(2,1)S(1)} %get-tuple-element.59), channel_id=1, source_target_pairs={{0,28},{4,24},{8,20},{12,16},{16,12},{20,8},{24,4},{28,0},{1,29},{... | collective-permute-start | bytes 221192 | tf_op jit(solution)/shard_map/ppermute | solution.py:192
  35.3 9.2 %collective-permute-start.7 = (bf16[144,256]{1,0:T(8,128)(2,1)S(1)}, bf16[144,256]{1,0:T(8,128)(2,1)S(1)}, u32[]{:S(2)}, u32[]{:S(2)}) collective-permute-start(bf16[144,256]{1,0:T(8,128)(2,1)S(1)} %get-tuple-element.53), channel_id=1, source_target_pairs={{0,4},{4,0},{8,12},{12,8},{16,20},{20,16},{24,28},{28,24},{1,5},{5... | collective-permute-start | bytes 221192 | tf_op jit(solution)/shard_map/ppermute | solution.py:192
  38.2 7.1 %collective-permute-start.8 = (bf16[144,256]{1,0:T(8,128)(2,1)S(1)}, bf16[144,256]{1,0:T(8,128)(2,1)S(1)}, u32[]{:S(2)}, u32[]{:S(2)}) collective-permute-start(bf16[144,256]{1,0:T(8,128)(2,1)S(1)} %get-tuple-element.54), channel_id=1, source_target_pairs={{0,8},{4,12},{8,0},{12,4},{16,24},{20,28},{24,16},{28,20},{1,9},{5... | collective-permute-start | bytes 221192 | tf_op jit(solution)/shard_map/ppermute | solution.py:192
  40.8 7.1 %collective-permute-start.9 = (bf16[144,256]{1,0:T(8,128)(2,1)S(1)}, bf16[144,256]{1,0:T(8,128)(2,1)S(1)}, u32[]{:S(2)}, u32[]{:S(2)}) collective-permute-start(bf16[144,256]{1,0:T(8,128)(2,1)S(1)} %get-tuple-element.55), channel_id=1, source_target_pairs={{0,12},{4,8},{8,4},{12,0},{16,28},{20,24},{24,20},{28,16},{1,13},{... | collective-permute-start | bytes 221192 | tf_op jit(solution)/shard_map/ppermute | solution.py:192
  40.9 7.6 %collective-permute-start.14 = (bf16[144,256]{1,0:T(8,128)(2,1)S(1)}, bf16[144,256]{1,0:T(8,128)(2,1)S(1)}, u32[]{:S(2)}, u32[]{:S(2)}) collective-permute-start(bf16[144,256]{1,0:T(8,128)(2,1)S(1)} %get-tuple-element.64), channel_id=1, source_target_pairs={{0,4},{4,0},{8,12},{12,8},{16,20},{20,16},{24,28},{28,24},{1,5},{5... | collective-permute-start | bytes 221192 | tf_op jit(solution)/shard_map/ppermute | solution.py:192
  41.7 9.2 %collective-permute-start.15 = (bf16[144,256]{1,0:T(8,128)(2,1)S(1)}, bf16[144,256]{1,0:T(8,128)(2,1)S(1)}, u32[]{:S(2)}, u32[]{:S(2)}) collective-permute-start(bf16[144,256]{1,0:T(8,128)(2,1)S(1)} %get-tuple-element.65), channel_id=1, source_target_pairs={{0,8},{4,12},{8,0},{12,4},{16,24},{20,28},{24,16},{28,20},{1,9},{5... | collective-permute-start | bytes 221192 | tf_op jit(solution)/shard_map/ppermute | solution.py:192
  44.5 13.4 %collective-permute-start.16 = (bf16[144,256]{1,0:T(8,128)(2,1)S(1)}, bf16[144,256]{1,0:T(8,128)(2,1)S(1)}, u32[]{:S(2)}, u32[]{:S(2)}) collective-permute-start(bf16[144,256]{1,0:T(8,128)(2,1)S(1)} %get-tuple-element.66), channel_id=1, source_target_pairs={{0,12},{4,8},{8,4},{12,0},{16,28},{20,24},{24,20},{28,16},{1,13},{... | collective-permute-start | bytes 221192 | tf_op jit(solution)/shard_map/ppermute | solution.py:192
  45.3 12.6 %collective-permute-start.17 = (bf16[144,256]{1,0:T(8,128)(2,1)S(1)}, bf16[144,256]{1,0:T(8,128)(2,1)S(1)}, u32[]{:S(2)}, u32[]{:S(2)}) collective-permute-start(bf16[144,256]{1,0:T(8,128)(2,1)S(1)} %get-tuple-element.67), channel_id=1, source_target_pairs={{0,16},{4,20},{8,24},{12,28},{16,0},{20,4},{24,8},{28,12},{1,17},{... | collective-permute-start | bytes 221192 | tf_op jit(solution)/shard_map/ppermute | solution.py:192
  47.9 11.0 %collective-permute-start.18 = (bf16[144,256]{1,0:T(8,128)(2,1)S(1)}, bf16[144,256]{1,0:T(8,128)(2,1)S(1)}, u32[]{:S(2)}, u32[]{:S(2)}) collective-permute-start(bf16[144,256]{1,0:T(8,128)(2,1)S(1)} %get-tuple-element.68), channel_id=1, source_target_pairs={{0,20},{4,16},{8,28},{12,24},{16,4},{20,0},{24,12},{28,8},{1,21},{... | collective-permute-start | bytes 221192 | tf_op jit(solution)/shard_map/ppermute | solution.py:192
  48.5 10.4 %collective-permute-start.19 = (bf16[144,256]{1,0:T(8,128)(2,1)S(1)}, bf16[144,256]{1,0:T(8,128)(2,1)S(1)}, u32[]{:S(2)}, u32[]{:S(2)}) collective-permute-start(bf16[144,256]{1,0:T(8,128)(2,1)S(1)} %get-tuple-element.69), channel_id=1, source_target_pairs={{0,24},{4,28},{8,16},{12,20},{16,8},{20,12},{24,0},{28,4},{1,25},{... | collective-permute-start | bytes 221192 | tf_op jit(solution)/shard_map/ppermute | solution.py:192
  50.9 8.0 %collective-permute-start.20 = (bf16[144,256]{1,0:T(8,128)(2,1)S(1)}, bf16[144,256]{1,0:T(8,128)(2,1)S(1)}, u32[]{:S(2)}, u32[]{:S(2)}) collective-permute-start(bf16[144,256]{1,0:T(8,128)(2,1)S(1)} %get-tuple-element.70), channel_id=1, source_target_pairs={{0,28},{4,24},{8,20},{12,16},{16,12},{20,8},{24,4},{28,0},{1,29},{... | collective-permute-start | bytes 221192 | tf_op jit(solution)/shard_map/ppermute | solution.py:192
  62.2 2.3 %collective-permute-start.37 = (f32[576,256]{1,0:T(8,128)}, f32[576,256]{1,0:T(8,128)S(1)}, u32[]{:S(2)}, u32[]{:S(2)}) collective-permute-start(f32[576,256]{1,0:T(8,128)} %copy-done.6), channel_id=1, source_target_pairs={{0,1},{1,0},{2,3},{3,2},{4,5},{5,4},{6,7},{7,6},{8,9},{9,8},{10,11... | collective-permute-start | bytes 1769480 | tf_op jit(solution)/shard_map/ppermute | solution.py:192
  62.2 3.9 %collective-permute-start.29 = (f32[576,256]{1,0:T(8,128)}, f32[576,256]{1,0:T(8,128)S(1)}, u32[]{:S(2)}, u32[]{:S(2)}) collective-permute-start(f32[576,256]{1,0:T(8,128)} %copy-done.7), channel_id=1, source_target_pairs={{0,1},{1,0},{2,3},{3,2},{4,5},{5,4},{6,7},{7,6},{8,9},{9,8},{10,11... | collective-permute-start | bytes 1769480 | tf_op jit(solution)/shard_map/ppermute | solution.py:192
  62.7 4.2 %collective-permute-start.21 = (f32[576,256]{1,0:T(8,128)}, f32[576,256]{1,0:T(8,128)S(1)}, u32[]{:S(2)}, u32[]{:S(2)}) collective-permute-start(f32[576,256]{1,0:T(8,128)} %copy-done.8), channel_id=1, source_target_pairs={{0,1},{1,0},{2,3},{3,2},{4,5},{5,4},{6,7},{7,6},{8,9},{9,8},{10,11... | collective-permute-start | bytes 1769480 | tf_op jit(solution)/shard_map/ppermute | solution.py:192
  64.5 9.9 %collective-permute-start.38 = (f32[288,256]{1,0:T(8,128)S(1)}, f32[288,256]{1,0:T(8,128)S(1)}, u32[]{:S(2)}, u32[]{:S(2)}) collective-permute-start(f32[288,256]{1,0:T(8,128)S(1)} %get-tuple-element.91), channel_id=1, source_target_pairs={{0,2},{1,3},{2,0},{3,1},{4,6},{5,7},{6,4},{7,5},{8,10},{9,11},{10,... | collective-permute-start | bytes 884744 | tf_op jit(solution)/shard_map/ppermute | solution.py:192
  66.2 14.6 %collective-permute-start.30 = (f32[288,256]{1,0:T(8,128)S(1)}, f32[288,256]{1,0:T(8,128)S(1)}, u32[]{:S(2)}, u32[]{:S(2)}) collective-permute-start(f32[288,256]{1,0:T(8,128)S(1)} %get-tuple-element.93), channel_id=1, source_target_pairs={{0,2},{1,3},{2,0},{3,1},{4,6},{5,7},{6,4},{7,5},{8,10},{9,11},{10,... | collective-permute-start | bytes 884744 | tf_op jit(solution)/shard_map/ppermute | solution.py:192
  67.0 19.2 %collective-permute-start.22 = (f32[288,256]{1,0:T(8,128)S(1)}, f32[288,256]{1,0:T(8,128)S(1)}, u32[]{:S(2)}, u32[]{:S(2)}) collective-permute-start(f32[288,256]{1,0:T(8,128)S(1)} %get-tuple-element.95), channel_id=1, source_target_pairs={{0,2},{1,3},{2,0},{3,1},{4,6},{5,7},{6,4},{7,5},{8,10},{9,11},{10,... | collective-permute-start | bytes 884744 | tf_op jit(solution)/shard_map/ppermute | solution.py:192
  74.5 12.7 %collective-permute-start.39 = (f32[144,256]{1,0:T(8,128)S(1)}, f32[144,256]{1,0:T(8,128)S(1)}, u32[]{:S(2)}, u32[]{:S(2)}) collective-permute-start(f32[144,256]{1,0:T(8,128)S(1)} %slice_add_fusion.6), channel_id=1, source_target_pairs={{0,4},{4,0},{8,12},{12,8},{16,20},{20,16},{24,28},{28,24},{1,5},{5... | collective-permute-start | bytes 442376 | tf_op jit(solution)/shard_map/ppermute | solution.py:192
  80.8 10.0 %collective-permute-start.31 = (f32[144,256]{1,0:T(8,128)S(1)}, f32[144,256]{1,0:T(8,128)S(1)}, u32[]{:S(2)}, u32[]{:S(2)}) collective-permute-start(f32[144,256]{1,0:T(8,128)S(1)} %slice_add_fusion.8), channel_id=1, source_target_pairs={{0,4},{4,0},{8,12},{12,8},{16,20},{20,16},{24,28},{28,24},{1,5},{5... | collective-permute-start | bytes 442376 | tf_op jit(solution)/shard_map/ppermute | solution.py:192
  86.3 5.2 %collective-permute-start.23 = (f32[144,256]{1,0:T(8,128)S(1)}, f32[144,256]{1,0:T(8,128)S(1)}, u32[]{:S(2)}, u32[]{:S(2)}) collective-permute-start(f32[144,256]{1,0:T(8,128)S(1)} %slice_add_fusion.10), channel_id=1, source_target_pairs={{0,4},{4,0},{8,12},{12,8},{16,20},{20,16},{24,28},{28,24},{1,5},{5... | collective-permute-start | bytes 442376 | tf_op jit(solution)/shard_map/ppermute | solution.py:192
  87.1 24.5 %collective-permute-start.40 = (f32[144,256]{1,0:T(8,128)S(1)}, f32[144,256]{1,0:T(8,128)S(1)}, u32[]{:S(2)}, u32[]{:S(2)}) collective-permute-start(f32[144,256]{1,0:T(8,128)S(1)} %fusion), channel_id=1, source_target_pairs={{0,16},{4,20},{8,24},{12,28},{16,0},{20,4},{24,8},{28,12},{1,17},{... | collective-permute-start | bytes 442376 | tf_op jit(solution)/shard_map/ppermute | solution.py:192
  90.9 30.2 %collective-permute-start.32 = (f32[144,256]{1,0:T(8,128)S(1)}, f32[144,256]{1,0:T(8,128)S(1)}, u32[]{:S(2)}, u32[]{:S(2)}) collective-permute-start(f32[144,256]{1,0:T(8,128)S(1)} %fusion.1), channel_id=1, source_target_pairs={{0,16},{4,20},{8,24},{12,28},{16,0},{20,4},{24,8},{28,12},{1,17},{... | collective-permute-start | bytes 442376 | tf_op jit(solution)/shard_map/ppermute | solution.py:192
  91.6 37.8 %collective-permute-start.24 = (f32[144,256]{1,0:T(8,128)S(1)}, f32[144,256]{1,0:T(8,128)S(1)}, u32[]{:S(2)}, u32[]{:S(2)}) collective-permute-start(f32[144,256]{1,0:T(8,128)S(1)} %fusion.2), channel_id=1, source_target_pairs={{0,16},{4,20},{8,24},{12,28},{16,0},{20,4},{24,8},{28,12},{1,17},{... | collective-permute-start | bytes 442376 | tf_op jit(solution)/shard_map/ppermute | solution.py:192
  111.7 20.7 %collective-permute-start.41 = (f32[144,256]{1,0:T(8,128)S(1)}, f32[144,256]{1,0:T(8,128)S(1)}, u32[]{:S(2)}, u32[]{:S(2)}) collective-permute-start(f32[144,256]{1,0:T(8,128)S(1)} %add.82), channel_id=1, source_target_pairs={{0,8},{4,12},{8,0},{12,4},{16,24},{20,28},{24,16},{28,20},{1,9},{5... | collective-permute-start | bytes 442376 | tf_op jit(solution)/shard_map/ppermute | solution.py:192
  121.1 14.4 %collective-permute-start.33 = (f32[144,256]{1,0:T(8,128)S(1)}, f32[144,256]{1,0:T(8,128)S(1)}, u32[]{:S(2)}, u32[]{:S(2)}) collective-permute-start(f32[144,256]{1,0:T(8,128)S(1)} %add.75), channel_id=1, source_target_pairs={{0,8},{4,12},{8,0},{12,4},{16,24},{20,28},{24,16},{28,20},{1,9},{5... | collective-permute-start | bytes 442376 | tf_op jit(solution)/shard_map/ppermute | solution.py:192
  129.4 7.8 %collective-permute-start.25 = (f32[144,256]{1,0:T(8,128)S(1)}, f32[144,256]{1,0:T(8,128)S(1)}, u32[]{:S(2)}, u32[]{:S(2)}) collective-permute-start(f32[144,256]{1,0:T(8,128)S(1)} %add.68), channel_id=1, source_target_pairs={{0,8},{4,12},{8,0},{12,4},{16,24},{20,28},{24,16},{28,20},{1,9},{5... | collective-permute-start | bytes 442376 | tf_op jit(solution)/shard_map/ppermute | solution.py:192
  132.4 6.4 %collective-permute-start.42 = (f32[144,256]{1,0:T(8,128)S(1)}, f32[144,256]{1,0:T(8,128)S(1)}, u32[]{:S(2)}, u32[]{:S(2)}) collective-permute-start(f32[144,256]{1,0:T(8,128)S(1)} %add.83), channel_id=1, source_target_pairs={{0,4},{4,0},{8,12},{12,8},{16,20},{20,16},{24,28},{28,24},{1,5},{5... | collective-permute-start | bytes 442376 | tf_op jit(solution)/shard_map/ppermute | solution.py:192
  135.5 6.1 %collective-permute-start.34 = (f32[144,256]{1,0:T(8,128)S(1)}, f32[144,256]{1,0:T(8,128)S(1)}, u32[]{:S(2)}, u32[]{:S(2)}) collective-permute-start(f32[144,256]{1,0:T(8,128)S(1)} %add.76), channel_id=1, source_target_pairs={{0,4},{4,0},{8,12},{12,8},{16,20},{20,16},{24,28},{28,24},{1,5},{5... | collective-permute-start | bytes 442376 | tf_op jit(solution)/shard_map/ppermute | solution.py:192
  137.2 6.0 %collective-permute-start.26 = (f32[144,256]{1,0:T(8,128)S(1)}, f32[144,256]{1,0:T(8,128)S(1)}, u32[]{:S(2)}, u32[]{:S(2)}) collective-permute-start(f32[144,256]{1,0:T(8,128)S(1)} %add.69), channel_id=1, source_target_pairs={{0,4},{4,0},{8,12},{12,8},{16,20},{20,16},{24,28},{28,24},{1,5},{5... | collective-permute-start | bytes 442376 | tf_op jit(solution)/shard_map/ppermute | solution.py:192
  138.8 10.0 %collective-permute-start.43 = (f32[288,256]{1,0:T(8,128)S(1)}, f32[288,256]{1,0:T(8,128)S(1)}, u32[]{:S(2)}, u32[]{:S(2)}) collective-permute-start(f32[288,256]{1,0:T(8,128)S(1)} %pad_maximum_fusion.6), channel_id=1, source_target_pairs={{0,2},{1,3},{2,0},{3,1},{4,6},{5,7},{6,4},{7,5},{8,10},{9,11},{10,... | collective-permute-start | bytes 884744 | tf_op jit(solution)/shard_map/ppermute | solution.py:192
  141.6 13.5 %collective-permute-start.35 = (f32[288,256]{1,0:T(8,128)S(1)}, f32[288,256]{1,0:T(8,128)S(1)}, u32[]{:S(2)}, u32[]{:S(2)}) collective-permute-start(f32[288,256]{1,0:T(8,128)S(1)} %pad_maximum_fusion.5), channel_id=1, source_target_pairs={{0,2},{1,3},{2,0},{3,1},{4,6},{5,7},{6,4},{7,5},{8,10},{9,11},{10,... | collective-permute-start | bytes 884744 | tf_op jit(solution)/shard_map/ppermute | solution.py:192
  143.2 15.5 %collective-permute-start.27 = (f32[288,256]{1,0:T(8,128)S(1)}, f32[288,256]{1,0:T(8,128)S(1)}, u32[]{:S(2)}, u32[]{:S(2)}) collective-permute-start(f32[288,256]{1,0:T(8,128)S(1)} %pad_maximum_fusion.4), channel_id=1, source_target_pairs={{0,2},{1,3},{2,0},{3,1},{4,6},{5,7},{6,4},{7,5},{8,10},{9,11},{10,... | collective-permute-start | bytes 884744 | tf_op jit(solution)/shard_map/ppermute | solution.py:192
  148.8 10.0 %collective-permute-start.44 = (f32[576,256]{1,0:T(8,128)S(1)}, f32[576,256]{1,0:T(8,128)S(1)}, u32[]{:S(2)}, u32[]{:S(2)}) collective-permute-start(f32[576,256]{1,0:T(8,128)S(1)} %pad_maximum_fusion.2.low_ref), channel_id=1, source_target_pairs={{0,1},{1,0},{2,3},{3,2},{4,5},{5,4},{6,7},{7,6},{8,9},{9,8},{10,11... | collective-permute-start | bytes 1769480 | tf_op jit(solution)/shard_map/ppermute | solution.py:192
  155.1 13.8 %collective-permute-start.36 = (f32[576,256]{1,0:T(8,128)S(1)}, f32[576,256]{1,0:T(8,128)S(1)}, u32[]{:S(2)}, u32[]{:S(2)}) collective-permute-start(f32[576,256]{1,0:T(8,128)S(1)} %pad_maximum_fusion.1.low_ref), channel_id=1, source_target_pairs={{0,1},{1,0},{2,3},{3,2},{4,5},{5,4},{6,7},{7,6},{8,9},{9,8},{10,11... | collective-permute-start | bytes 1769480 | tf_op jit(solution)/shard_map/ppermute | solution.py:192
  158.8 20.0 %collective-permute-start.28 = (f32[576,256]{1,0:T(8,128)S(1)}, f32[576,256]{1,0:T(8,128)S(1)}, u32[]{:S(2)}, u32[]{:S(2)}) collective-permute-start(f32[576,256]{1,0:T(8,128)S(1)} %pad_maximum_fusion.low_ref), channel_id=1, source_target_pairs={{0,1},{1,0},{2,3},{3,2},{4,5},{5,4},{6,7},{7,6},{8,9},{9,8},{10,11... | collective-permute-start | bytes 1769480 | tf_op jit(solution)/shard_map/ppermute | solution.py:192
  (7 other events, 51.4 us)
Sparse Core Ops, SparseCore 0:
  62.3 70.1 all-gather.2

commit v2 on v1

v2 whole, which is shorter than its diff:
```python
import functools
import math

import jax
import jax.numpy as jnp
from jax import lax
from jax.experimental import pallas as pl
from jax.experimental.pallas import tpu as pltpu
from jax.sharding import PartitionSpec as P

NS_STEPS = 5
CORR_FIRST = 1.0
CORR_SECOND = 0.6323045752
HIGHEST = lax.Precision.HIGHEST
LANES = 128
VMEM = pl.BlockSpec(memory_space=pltpu.VMEM)
PARAMS = pltpu.CompilerParams(vmem_limit_bytes=32 * 1024 * 1024)


def dot(a, b, dims, **kw):
    return lax.dot_general(a, b, (dims, ((), ())), preferred_element_type=jnp.float32, **kw)


def nn(a, b, **kw):
    return dot(a, b, ((1,), (0,)), **kw)


def tn(a, b, **kw):
    return dot(a, b, ((0,), (0,)), **kw)


def nt(a, b, **kw):
    return dot(a, b, ((1,), (1,)), **kw)


def row_owner():
    tensor = lax.axis_index("tensor")
    return (tensor & 1) * 4 + (tensor >> 1) * 2 + (lax.axis_index("shard") & 1)


def fold_plan(rows, cols):
    tail = cols - LANES
    rest = 2 * tail - LANES
    stacked = -(-(rows // 2) // 16) * 8
    return tail, rest, stacked


def fold(block):
    rows, cols = block.shape
    tail, rest, stacked = fold_plan(rows, cols)
    half = rows // 2
    upper, lower = block[:half, LANES:], block[half:, LANES:]
    middle = jnp.concatenate([upper, lower[:, : tail - rest]], axis=1)
    left = lower[:, tail - rest :]
    below = jnp.concatenate(
        [left[stacked:], jnp.zeros((2 * stacked - half, rest), block.dtype)], axis=0
    )
    last = jnp.concatenate(
        [left[:stacked], below, jnp.zeros((stacked, LANES - 2 * rest), block.dtype)], axis=1
    )
    return jnp.concatenate([block[:, :LANES], middle, last], axis=0)


def unfold(folded, rows, cols):
    tail, rest, stacked = fold_plan(rows, cols)
    half = rows // 2
    middle, last = folded[rows : rows + half], folded[rows + half :]
    left = jnp.concatenate([last[:, :rest], last[: half - stacked, rest : 2 * rest]], axis=0)
    lower = jnp.concatenate([middle[:, tail:], left], axis=1)
    second = jnp.concatenate([middle[:, :tail], lower], axis=0)
    second = jnp.concatenate([second, jnp.zeros((rows, LANES - tail), folded.dtype)], axis=1)
    return jnp.concatenate([folded[:rows], second], axis=1)


def cut_kernel(parts, cols, groups, g_ref, *refs):
    outs, held = refs[:-1], refs[-1]
    size = held.shape[1]
    for part in range(parts):
        block = g_ref[0, :, part * cols : (part + 1) * cols].astype(jnp.float32)
        held[part] = fold(block).astype(held.dtype)
    me = lax.axis_index("shard")
    for out, group in zip(outs, groups):
        for i, k in enumerate(group):
            out[i * size : (i + 1) * size, :] = held[me ^ k]


def cut(gradients, mat, parts, cols, groups):
    _, rows, whole = gradients.shape
    size = folded_rows(rows, cols)
    shapes = [(len(group) * size, LANES) for group in groups]
    return pl.pallas_call(
        functools.partial(cut_kernel, parts, cols, groups),
        grid=(1,),
        in_specs=[pl.BlockSpec((1, rows, whole), lambda i: (mat, 0, 0))],
        out_specs=[pl.BlockSpec(shape, lambda i: (0, 0)) for shape in shapes],
        out_shape=[jax.ShapeDtypeStruct(shape, gradients.dtype) for shape in shapes],
        scratch_shapes=[pltpu.VMEM((parts, size, LANES), gradients.dtype)],
        compiler_params=PARAMS,
        name="cut_columns",
    )(gradients)


def folded_rows(rows, cols):
    return rows + rows // 2 + fold_plan(rows, cols)[2]


def pair_kernel(own_ref, got_ref, *outs):
    size = outs[0].shape[0] // 2
    for k, out in enumerate(outs):
        out[:size, :] = own_ref[k * size : (k + 1) * size, :]
        out[size:, :] = got_ref[k * size : (k + 1) * size, :]


def pair(own, got, count):
    size = own.shape[0] // count
    shape = (2 * size, LANES)
    return pl.pallas_call(
        pair_kernel,
        in_specs=[VMEM, VMEM],
        out_specs=[VMEM] * count,
        out_shape=[jax.ShapeDtypeStruct(shape, own.dtype)] * count,
        compiler_params=PARAMS,
        name="pair_blocks",
    )(own, got)


def project_kernel(rows, cols, inputs, each, *refs):
    blocks, (p_ref, first_ref, second_ref), refs = refs[:inputs], refs[inputs : inputs + 3], refs[inputs + 3 :]
    update_ref, first_out, second_out, send_ref, keep_ref, grad = refs[-6:]
    parts = inputs * each
    size = blocks[0].shape[0] // each
    me = lax.axis_index("shard")
    for k in range(parts):
        folded = blocks[k // each][(k % each) * size : (k % each + 1) * size, :]
        block = unfold(folded.astype(jnp.float32), rows, cols)
        grad[pl.ds(pl.multiple_of((me ^ k) * rows, rows), rows), :] = block.astype(grad.dtype)
    projected = tn(grad[...], p_ref[0])
    back = projected.astype(jnp.bfloat16)
    own = row_owner()
    half = parts // 2
    for j in list(range(half, parts)) + list(range(half)):
        at = pl.multiple_of((own ^ j) * rows, rows)
        term = nn(grad[pl.ds(at, rows), :], back)
        out = send_ref if j >= half else keep_ref
        out[(j % half) * rows : (j % half + 1) * rows, :] = term
    projected = projected[:cols]
    first_new = 0.9 * first_ref[0] + 0.1 * projected
    second_new = 0.999 * second_ref[0] + 0.001 * projected * projected
    first_out[0] = first_new
    second_out[0] = second_new
    update_ref[...] = (
        first_new / CORR_FIRST / (jnp.sqrt(second_new / CORR_SECOND) + 1e-08)
    ).astype(jnp.bfloat16)


def project(blocks, rows, projectors, first, second, mat, earlier):
    mats, width, rank = projectors.shape
    cols = first.shape[1]
    parts = width // rows
    inputs = len(blocks)
    wide = -(-cols // LANES) * LANES
    moment = pl.BlockSpec((1, cols, rank), lambda i: (mat, 0, 0))
    whole = lambda *shape: pl.BlockSpec(shape, lambda i: (0,) * len(shape))
    in_specs = [whole(*block.shape) for block in blocks]
    in_specs += [pl.BlockSpec((1, width, rank), lambda i: (mat, 0, 0)), moment, moment]
    in_specs += [pl.BlockSpec(memory_space=pl.ANY)] * len(earlier)
    half = width // 2
    return pl.pallas_call(
        functools.partial(project_kernel, rows, cols, inputs, parts // inputs),
        grid=(1,),
        in_specs=in_specs,
        out_specs=[whole(cols, rank), moment, moment, whole(half, rank), whole(half, rank)],
        out_shape=[
            jax.ShapeDtypeStruct((cols, rank), jnp.bfloat16),
            jax.ShapeDtypeStruct(first.shape, first.dtype),
            jax.ShapeDtypeStruct(second.shape, second.dtype),
            jax.ShapeDtypeStruct((half, rank), jnp.float32),
            jax.ShapeDtypeStruct((half, rank), jnp.float32),
        ],
        scratch_shapes=[pltpu.VMEM((width, wide), jnp.bfloat16)],
        input_output_aliases={inputs + 3 + i: 1 + i for i in range(len(earlier))},
        compiler_params=PARAMS,
        name="project",
    )(*blocks, projectors, first, second, *earlier)


def split(a):
    high = a.astype(jnp.bfloat16)
    return high, (a - high.astype(jnp.float32)).astype(jnp.bfloat16)


def product(a, b):
    return nn(a[0], b[0]) + (nn(a[0], b[1]) + nn(a[1], b[0]))


def basis_kernel(factor, low_ref, high_ref, *refs):
    out_ref = refs[-1]
    half, rank = low_ref.shape
    rows = half // 4
    low, high = low_ref[...], high_ref[...]
    square = jnp.sum(low * low) + jnp.sum(high * high) + 1e-06
    halves = split(low), split(high)
    cross = tn(halves[0][0], halves[0][1]) + tn(halves[1][0], halves[1][1])
    gram = tn(halves[0][0], halves[0][0]) + tn(halves[1][0], halves[1][0])
    gram = (gram + (cross + cross.T)) * (1.0 / square)
    eye = (
        lax.broadcasted_iota(jnp.int32, (rank, rank), 0)
        == lax.broadcasted_iota(jnp.int32, (rank, rank), 1)
    ).astype(jnp.float32)
    total = None
    for sweep in range(NS_STEPS):
        plain = 1.5 * eye - 0.5 * gram
        step = split(plain)
        if sweep < NS_STEPS - 1:
            gram = product(split(product(split(gram), step)), step)
        total = plain if total is None else product(split(total), step)
    total = split(total * (factor / jnp.sqrt(square)))
    own = row_owner()
    for j in range(8):
        span = slice((j % 4) * rows, (j % 4 + 1) * rows)
        block = product([part[span] for part in halves[j // 4]], total)
        at = pl.multiple_of((own ^ j) * rows, rows)
        out_ref[0, pl.ds(at, rows), :] = block.astype(jnp.bfloat16)


def basis(low, high, mat, mats, factor, earlier):
    half, rank = low.shape
    whole = lambda *shape: pl.BlockSpec(shape, lambda i: (0,) * len(shape))
    return pl.pallas_call(
        functools.partial(basis_kernel, factor),
        grid=(1,),
        in_specs=[whole(half, rank)] * 2 + [pl.BlockSpec(memory_space=pl.ANY)] * len(earlier),
        out_specs=pl.BlockSpec((1, 2 * half, rank), lambda i: (mat, 0, 0)),
        out_shape=jax.ShapeDtypeStruct((mats, 2 * half, rank), jnp.bfloat16),
        input_output_aliases={2: 0} if earlier else {},
        compiler_params=PARAMS,
        name="newton_schulz",
    )(low, high, *earlier)


def weight_kernel(cols, w_ref, p_ref, mine_ref, other_ref, *refs):
    out_ref, held = refs[-2:]
    rows = w_ref.shape[1]
    me = lax.axis_index("shard")
    z, x = me >> 1, me & 1
    early = z < 2
    order = [z, z ^ 1, jnp.where(early, 2, 1), jnp.where(early, 3, 0)]
    for i, place in enumerate(order):
        span = slice(i * cols, (i + 1) * cols)
        held[place * 2 + x] = mine_ref[span, :]
        held[place * 2 + (x ^ 1)] = other_ref[span, :]
    own = p_ref[0, pl.ds(pl.multiple_of(me * rows, rows), rows), :]
    for part in range(held.shape[0]):
        span = slice(part * cols, (part + 1) * cols)
        out_ref[0, :, span] = w_ref[0, :, span] - 0.2 * nt(own, held[part])


def weight_step(weights, projectors, mine, other, mat, earlier):
    mats, rows, whole = weights.shape
    _, width, rank = projectors.shape
    cols = mine.shape[0] // 4
    big = pl.BlockSpec((1, rows, whole), lambda i: (mat, 0, 0))
    flat = pl.BlockSpec(mine.shape, lambda i: (0, 0))
    return pl.pallas_call(
        functools.partial(weight_kernel, cols),
        grid=(1,),
        in_specs=[big, pl.BlockSpec((1, width, rank), lambda i: (mat, 0, 0)), flat, flat]
        + [pl.BlockSpec(memory_space=pl.ANY)] * len(earlier),
        out_specs=big,
        out_shape=jax.ShapeDtypeStruct(weights.shape, weights.dtype),
        scratch_shapes=[pltpu.VMEM((8, cols, rank), jnp.bfloat16)],
        input_output_aliases={4: 0} if earlier else {},
        compiler_params=PARAMS,
        name="weight_step",
    )(weights, projectors, mine, other, *earlier)


def swap(x, axis, size, bit):
    return lax.ppermute(x, axis, [(i, i ^ bit) for i in range(size)])


def spread(update):
    z = lax.axis_index("shard") >> 1
    near = swap(update, "shard", 8, 2)
    both = jnp.concatenate([update, near])
    middle = lax.ppermute(both, "shard", [(2, 4), (3, 5), (4, 2), (5, 3)])
    outer = lax.ppermute(middle, "shard", [(2, 0), (3, 1), (4, 6), (5, 7)])
    far = jnp.where((z == 1) | (z == 2), middle, outer)
    return jnp.concatenate([both, far])


def per_device(gradients, weights, projectors, first_moment, second_moment):
    factor = math.sqrt(projectors.shape[0])
    mats, rows, whole = gradients.shape
    cols = whole // 8
    across = jnp.swapaxes(projectors, 0, 1)
    first = jnp.swapaxes(first_moment[:, :, 0, :], 1, 2)
    second = jnp.swapaxes(second_moment[:, :, 0, :], 1, 2)
    core = lambda x: swap(x, "tensor", 4, 1)
    along_y = lambda x: swap(x, "tensor", 4, 2)
    along_x = lambda x: swap(x, "shard", 8, 1)
    z_far = lambda x: swap(x, "shard", 8, 4)
    z_near = lambda x: swap(x, "shard", 8, 2)

    def regroup(mat):
        if mat == 0:
            pieces = cut(gradients, mat, 8, cols, [(k,) for k in range(8)])
            return [pieces[0]] + [swap(pieces[k], "shard", 8, k) for k in range(1, 8)]
        own, sent = cut(gradients, mat, 8, cols, [(0, 2, 4, 6), (1, 3, 5, 7)])
        pieces = pair(own, along_x(sent), 4)
        return [pieces[0]] + [swap(pieces[k], "shard", 8, 2 * k) for k in range(1, 4)]

    blocks = [regroup(mat) for mat in range(mats)]
    moments, bases, new_weight, updates = (), (), (), []
    for mat in range(mats):
        update, *moments, send, keep = project(
            blocks[mat], rows, across, first, second, mat, moments
        )
        for exchange in (core, along_y, along_x):
            got = exchange(send)
            if keep.shape[0] > rows:
                half = keep.shape[0] // 2
                send, keep = keep[half:] + got[half:], keep[:half] + got[:half]
            else:
                keep = keep + got
        keep = keep + z_far(keep)
        keep = keep + z_near(keep)
        keep = jnp.concatenate([keep, along_x(keep)])
        keep = jnp.concatenate([keep, along_y(keep)])
        bases = (basis(keep, core(keep), mat, mats, factor, bases),)
        mine = spread(update)
        new_weight = (weight_step(weights, across, mine, along_x(mine), mat, new_weight),)
    back = lambda x: jnp.swapaxes(x, 1, 2)[:, :, None, :]
    return (new_weight[0], back(moments[0]), back(moments[1]), jnp.swapaxes(bases[0], 0, 1))


def newton_steps(iterate, inner):
    return 1.5 * iterate - 0.5 * jnp.einsum(
        "dmr,mrs->dms", iterate, inner, precision=HIGHEST, preferred_element_type=jnp.float32
    )


def column_inner(iterate):
    return jnp.einsum(
        "dmr,dms->mrs", iterate, iterate, precision=HIGHEST, preferred_element_type=jnp.float32
    )


def per_device_any(gradients, weights, projectors, first_moment, second_moment):
    factor = math.sqrt(projectors.shape[0])
    regrouped = lax.all_to_all(gradients, "shard", split_axis=2, concat_axis=1, tiled=True)
    mats, width, cols = regrouped.shape
    rank = projectors.shape[2]
    projected = jnp.einsum(
        "dmr,mdc->mrc", projectors, regrouped, preferred_element_type=jnp.float32
    )
    first_new = 0.9 * first_moment.reshape(mats, rank, cols) + 0.1 * projected
    second_new = 0.999 * second_moment.reshape(mats, rank, cols) + 0.001 * projected * projected
    update = (first_new / CORR_FIRST / (jnp.sqrt(second_new / CORR_SECOND) + 1e-08)).astype(
        jnp.bfloat16
    )
    delta = jnp.einsum("dmr,mrc->mdc", projectors, update, preferred_element_type=jnp.float32)
    returned = lax.all_to_all(delta, "shard", split_axis=1, concat_axis=2, tiled=True)
    new_weight = weights - 0.2 * returned
    back = jnp.einsum(
        "mdc,dmr->mcr", regrouped, projectors, preferred_element_type=jnp.float32
    ).astype(jnp.bfloat16)
    partial_sum = jnp.einsum("mdc,mcr->dmr", regrouped, back, preferred_element_type=jnp.float32)
    refresh = lax.psum(partial_sum, ("shard", "tensor"))
    norms = jnp.sqrt(jnp.sum(refresh * refresh, axis=(0, 2)) + 1e-06)
    iterate = refresh / norms[None, :, None]
    for sweep in range(NS_STEPS):
        iterate = newton_steps(iterate, column_inner(iterate))
    new_basis = (iterate * factor).astype(jnp.bfloat16)
    shape_four = first_moment.shape
    return (new_weight, first_new.reshape(shape_four), second_new.reshape(shape_four), new_basis)


def solution(mesh):
    in_specs = (
        P(None, "shard", "tensor"),
        P(None, "shard", "tensor"),
        P(),
        P(None, None, "tensor", "shard"),
        P(None, None, "tensor", "shard"),
    )
    out_specs = (
        P(None, "shard", "tensor"),
        P(None, None, "tensor", "shard"),
        P(None, None, "tensor", "shard"),
        P(),
    )
    own = (mesh.shape["shard"], mesh.shape["tensor"]) == (8, 4)
    body = per_device if own else per_device_any
    return jax.shard_map(body, mesh=mesh, in_specs=in_specs, out_specs=out_specs, check_vma=False)
```

time: 203 us -> 178 us (0.88)
  waiting for transfers between devices: 81.7 us -> 65.6 us
  between operations: 14.3 us -> 1.04 us
  starting transfers between devices: 58.5 us -> 68.1 us
  Pallas kernels: 39.2 us -> 29.8 us
  other arithmetic: 1.42 us -> 7.24 us
    ppermute x45, waiting for transfers between devices: 81.6 us -> 65.6 us  [swap(): return lax.ppermute(x, axis, [(i, i ^ bit) for i in range(size)])]
    pallas_call x3, Pallas kernels: 29.9 us -> 14.5 us  [basis(): pl.pallas_call(functools.partial(basis_kernel, factor), grid=(1,), in_spe...]
    ppermute x0 -> x6, starting transfers between devices: none -> 6.85 us  [the longest x3 4.03 us: spread(): outer = lax.ppermute(middle, 'shard', [(2, 0), (3, 1), (4, 6), (5, 7)])]
    pallas_call x7 -> x11, Pallas kernels: 9.27 us -> 15.3 us  [the longest x3 6.55 us: project(): pl.pallas_call(functools.partial(project_kernel, rows, cols, inputs, part...]
    add x6, other arithmetic: 0.28 us -> 3.18 us  [per_device(): send, keep = (keep[half:] + got[half:], keep[:half] + got[:half])]
    ppermute x45, starting transfers between devices: 58.4 us -> 61.2 us  [swap(): return lax.ppermute(x, axis, [(i, i ^ bit) for i in range(size)])]
    concatenate x0 -> x6, other arithmetic: none -> 2.66 us  [the longest x3 1.68 us: spread(): both = jnp.concatenate([update, near])]
    unnamed x18 -> x32, local copies, waits for them, and re-layouts: 7.47 us -> 6.02 us
  transfers between devices with their start and end apart: 46 -> 51, of which waited for: 19 -> 20; matrix products, arithmetic and copies ran while one was open for 0% -> 4% of each run, Pallas kernels for 17% -> 12%
where the time goes in v2:
time: 178 us
  starting transfers between devices  68.1 us (38%)
  waiting for transfers between devices  65.6 us (37%)
  Pallas kernels  29.8 us (17%)
  other arithmetic  7.24 us (4%)
  local copies, waits for them, and re-layouts  6.02 us (3%)
    ppermute x45, waiting for transfers between devices, swap(): return lax.ppermute(x, axis, [(i, i ^ bit) for i in range(size)])  65.6 us
    ppermute x45, starting transfers between devices, swap(): return lax.ppermute(x, axis, [(i, i ^ bit) for i in range(size)])  61.2 us
    pallas_call x3, Pallas kernels, basis(): pl.pallas_call(functools.partial(basis_kernel, factor), grid=(1,), in_spe...  14.5 us
    pallas_call x3, Pallas kernels, project(): pl.pallas_call(functools.partial(project_kernel, rows, cols, inputs, part...  6.55 us
    unnamed x32, local copies, waits for them, and re-layouts  6.02 us
    pallas_call x3, Pallas kernels, weight_step(): pl.pallas_call(functools.partial(weight_kernel, cols), grid=(1,), in_spec...  4.91 us
    ppermute x3, starting transfers between devices, spread(): outer = lax.ppermute(middle, 'shard', [(2, 0), (3, 1), (4, 6), (5, 7)])  4.03 us
  transfers between devices with their start and end apart: 51, of which 20 were waited for; matrix products, arithmetic and copies ran while one was open for 4% of the time, Pallas kernels for 12%

profile of v2, /device:TPU:0, one launch (start us, length us, event | category | flops | bytes accessed | tf_op | source)
XLA Modules:
  0.0 177.8 jit_solution(6117588904415693601)
XLA Ops:
  0.6 1.4 copy-done.3
  3.1 4.0 %collective-permute-start.10 = (bf16[256,128]{1,0:T(8,128)(2,1)S(1)}, bf16[256,128]{1,0:T(8,128)(2,1)S(1)}, u32[]{:S(2)}, u32[]{:S(2)}) collective-permute-start(bf16[256,128]{1,0:T(8,128)(2,1)S(1)} %get-tuple-element.54), channel_id=1, source_target_pairs={{0,12},{4,8},{8,4},{12,0},{16,28},{20,24},{24,20},{28,16},{1,13},{... | collective-permute-start | bytes 196616 | tf_op jit(solution)/shard_map/ppermute | solution.py:279
  7.1 2.6 %collective-permute-start.11 = (bf16[256,128]{1,0:T(8,128)(2,1)S(1)}, bf16[256,128]{1,0:T(8,128)(2,1)S(1)}, u32[]{:S(2)}, u32[]{:S(2)}) collective-permute-start(bf16[256,128]{1,0:T(8,128)(2,1)S(1)} %get-tuple-element.55), channel_id=1, source_target_pairs={{0,16},{4,20},{8,24},{12,28},{16,0},{20,4},{24,8},{28,12},{1,17},{... | collective-permute-start | bytes 196616 | tf_op jit(solution)/shard_map/ppermute | solution.py:279
  10.0 2.5 %collective-permute-start.13 = (bf16[256,128]{1,0:T(8,128)(2,1)S(1)}, bf16[256,128]{1,0:T(8,128)(2,1)S(1)}, u32[]{:S(2)}, u32[]{:S(2)}) collective-permute-start(bf16[256,128]{1,0:T(8,128)(2,1)S(1)} %get-tuple-element.57), channel_id=1, source_target_pairs={{0,24},{4,28},{8,16},{12,20},{16,8},{20,12},{24,0},{28,4},{1,25},{... | collective-permute-start | bytes 196616 | tf_op jit(solution)/shard_map/ppermute | solution.py:279
  12.5 2.3 %collective-permute-start.14 = (bf16[256,128]{1,0:T(8,128)(2,1)S(1)}, bf16[256,128]{1,0:T(8,128)(2,1)S(1)}, u32[]{:S(2)}, u32[]{:S(2)}) collective-permute-start(bf16[256,128]{1,0:T(8,128)(2,1)S(1)} %get-tuple-element.58), channel_id=1, source_target_pairs={{0,28},{4,24},{8,20},{12,16},{16,12},{20,8},{24,4},{28,0},{1,29},{... | collective-permute-start | bytes 196616 | tf_op jit(solution)/shard_map/ppermute | solution.py:279
  15.3 1.9 %collective-permute-start.9 = (bf16[256,128]{1,0:T(8,128)(2,1)S(1)}, bf16[256,128]{1,0:T(8,128)(2,1)S(1)}, u32[]{:S(2)}, u32[]{:S(2)}) collective-permute-start(bf16[256,128]{1,0:T(8,128)(2,1)S(1)} %get-tuple-element.53), channel_id=1, source_target_pairs={{0,8},{4,12},{8,0},{12,4},{16,24},{20,28},{24,16},{28,20},{1,9},{5... | collective-permute-start | bytes 196616 | tf_op jit(solution)/shard_map/ppermute | solution.py:279
  17.1 1.4 collective-permute-done.12.refs_5_
  20.2 1.5 copy-done
  21.7 1.8 %project.3 = (bf16[216,256]{1,0:T(8,128)(2,1)S(1)}, f32[3,216,256]{2,1,0:T(8,128)}, f32[3,216,256]{2,1,0:T(8,128)}, f32[576,256]{1,0:T(8,128)S(1)}, f32[576,256]{1,0:T(8,128)S(1)}) custom-call(bf16[256,128]{1,0:T(8,128)(2,1)S(1)} %get-tuple-element.51.refs_0_, bf16[256,128]{1,0:T(8,128)(2,1)S(1)} %collective-permute-done.8.refs_1_, ...), custom_call_target="tpu_custom_call" | custom-call | tf_op jit(solution)/shard_map/project/pallas_call | solution.py:168
  27.8 2.0 %collective-permute-start.23 = (bf16[216,256]{1,0:T(8,128)(2,1)S(1)}, bf16[216,256]{1,0:T(8,128)(2,1)S(1)}, u32[]{:S(2)}, u32[]{:S(2)}) collective-permute-start(bf16[216,256]{1,0:T(8,128)(2,1)S(1)} %get-tuple-element.65), channel_id=1, source_target_pairs={{0,8},{4,12},{8,0},{12,4},{16,24},{20,28},{24,16},{28,20},{1,9},{5... | collective-permute-start | bytes 331784 | tf_op jit(solution)/shard_map/ppermute | solution.py:279
  29.8 4.0 %collective-permute-done.4.got_ref = bf16[1024,128]{1,0:T(8,128)(2,1)S(1)} collective-permute-done((bf16[1024,128]{1,0:T(8,128)(2,1)S(1)}, bf16[1024,128]{1,0:T(8,128)(2,1)S(1)}, u32[]{:S(2)}, u32[]{:S(2)}) %collective-permute-start.4) | collective-permute-done | bytes 262176 | tf_op jit(solution)/shard_map/ppermute | solution.py:279
  33.8 2.1 %collective-permute-start.5 = (bf16[512,128]{1,0:T(8,128)(2,1)S(1)}, bf16[512,128]{1,0:T(8,128)(2,1)S(1)}, u32[]{:S(2)}, u32[]{:S(2)}) collective-permute-start(bf16[512,128]{1,0:T(8,128)(2,1)S(1)} %get-tuple-element.48), channel_id=1, source_target_pairs={{0,8},{4,12},{8,0},{12,4},{16,24},{20,28},{24,16},{28,20},{1,9},{5... | collective-permute-start | bytes 393224 | tf_op jit(solution)/shard_map/ppermute | solution.py:279
  35.9 2.7 %collective-permute-start.6 = (bf16[512,128]{1,0:T(8,128)(2,1)S(1)}, bf16[512,128]{1,0:T(8,128)(2,1)S(1)}, u32[]{:S(2)}, u32[]{:S(2)}) collective-permute-start(bf16[512,128]{1,0:T(8,128)(2,1)S(1)} %get-tuple-element.49), channel_id=1, source_target_pairs={{0,16},{4,20},{8,24},{12,28},{16,0},{20,4},{24,8},{28,12},{1,17},{... | collective-permute-start | bytes 393224 | tf_op jit(solution)/shard_map/ppermute | solution.py:279
  39.3 1.3 collective-permute-start.24
  41.3 3.8 %collective-permute-start.1 = (bf16[512,128]{1,0:T(8,128)(2,1)S(1)}, bf16[512,128]{1,0:T(8,128)(2,1)S(1)}, u32[]{:S(2)}, u32[]{:S(2)}) collective-permute-start(bf16[512,128]{1,0:T(8,128)(2,1)S(1)} %get-tuple-element.42), channel_id=1, source_target_pairs={{0,8},{4,12},{8,0},{12,4},{16,24},{20,28},{24,16},{28,20},{1,9},{5... | collective-permute-start | bytes 393224 | tf_op jit(solution)/shard_map/ppermute | solution.py:279
  45.1 3.5 %collective-permute-done.6.refs_2_ = bf16[512,128]{1,0:T(8,128)(2,1)S(1)} collective-permute-done((bf16[512,128]{1,0:T(8,128)(2,1)S(1)}, bf16[512,128]{1,0:T(8,128)(2,1)S(1)}, u32[]{:S(2)}, u32[]{:S(2)}) %collective-permute-start.6) | collective-permute-done | bytes 131104 | tf_op jit(solution)/shard_map/ppermute | solution.py:279
  48.7 1.9 %project.4 = (bf16[216,256]{1,0:T(8,128)(2,1)S(1)}, f32[3,216,256]{2,1,0:T(8,128)}, f32[3,216,256]{2,1,0:T(8,128)}, f32[576,256]{1,0:T(8,128)}, f32[576,256]{1,0:T(8,128)S(1)}) custom-call(bf16[512,128]{1,0:T(8,128)(2,1)S(1)} %get-tuple-element.47.refs_0_, ...), custom_call_target="tpu_custom_call", output_to_operand_aliasing={{1}: (7, {}), {2}: (8, {})} | custom-call | tf_op jit(solution)/shard_map/project/pallas_call | solution.py:168
  51.6 1.5 collective-permute-start.44
  53.8 2.9 %collective-permute-start.3 = (bf16[512,128]{1,0:T(8,128)(2,1)}, bf16[512,128]{1,0:T(8,128)(2,1)}, u32[]{:S(2)}, u32[]{:S(2)}) collective-permute-start(bf16[512,128]{1,0:T(8,128)(2,1)} %get-tuple-element.44), channel_id=1, source_target_pairs={{0,24},{4,28},{8,16},{12,20},{16,8},{20,12},{24,0},{28,4},{1,25},{... | collective-permute-start | bytes 393224 | tf_op jit(solution)/shard_map/ppermute | solution.py:279
  56.7 7.2 %collective-permute-done.2.refs_2_ = bf16[512,128]{1,0:T(8,128)(2,1)S(1)} collective-permute-done((bf16[512,128]{1,0:T(8,128)(2,1)S(1)}, bf16[512,128]{1,0:T(8,128)(2,1)S(1)}, u32[]{:S(2)}, u32[]{:S(2)}) %collective-permute-start.2) | collective-permute-done | bytes 131104 | tf_op jit(solution)/shard_map/ppermute | solution.py:279
  66.3 2.8 %project.5 = (bf16[216,256]{1,0:T(8,128)(2,1)S(1)}, f32[3,216,256]{2,1,0:T(8,128)}, f32[3,216,256]{2,1,0:T(8,128)}, f32[576,256]{1,0:T(8,128)S(1)}, f32[576,256]{1,0:T(8,128)S(1)}) custom-call(bf16[512,128]{1,0:T(8,128)(2,1)S(1)} %get-tuple-element.41.refs_0_, bf16[512,128]{1,0:T(8,128)(2,1)S(1)} %copy-done.10, ...), custom_call_target="tpu_custom_call", output_to_operand_aliasing={{1}: (7, {}), {2}: (8, {})} | custom-call | tf_op jit(solution)/shard_map/project/pallas_call | solution.py:168
  69.1 2.1 %collective-permute-start.15 = (bf16[216,256]{1,0:T(8,128)(2,1)S(1)}, bf16[216,256]{1,0:T(8,128)(2,1)S(1)}, u32[]{:S(2)}, u32[]{:S(2)}) collective-permute-start(bf16[216,256]{1,0:T(8,128)(2,1)S(1)} %get-tuple-element.63), channel_id=1, source_target_pairs={{0,8},{4,12},{8,0},{12,4},{16,24},{20,28},{24,16},{28,20},{1,9},{5... | collective-permute-start | bytes 331784 | tf_op jit(solution)/shard_map/ppermute | solution.py:279
  71.2 1.3 collective-permute-start.25
  77.3 3.7 %collective-permute-done.45 = f32[144,256]{1,0:T(8,128)S(1)} collective-permute-done((f32[144,256]{1,0:T(8,128)S(1)}, f32[144,256]{1,0:T(8,128)S(1)}, u32[]{:S(2)}, u32[]{:S(2)}) %collective-permute-start.45) | collective-permute-done | bytes 147488 | tf_op jit(solution)/shard_map/ppermute | solution.py:279
  81.0 2.0 %collective-permute-start.36 = (f32[288,256]{1,0:T(8,128)S(1)}, f32[288,256]{1,0:T(8,128)S(1)}, u32[]{:S(2)}, u32[]{:S(2)}) collective-permute-start(f32[288,256]{1,0:T(8,128)S(1)} %get-tuple-element.81), channel_id=1, source_target_pairs={{0,2},{1,3},{2,0},{3,1},{4,6},{5,7},{6,4},{7,5},{8,10},{9,11},{10,... | collective-permute-start | bytes 884744 | tf_op jit(solution)/shard_map/ppermute | solution.py:279
  84.0 4.9 %collective-permute-start.46 = (f32[144,256]{1,0:T(8,128)S(1)}, f32[144,256]{1,0:T(8,128)S(1)}, u32[]{:S(2)}, u32[]{:S(2)}) collective-permute-start(f32[144,256]{1,0:T(8,128)S(1)} %fusion), channel_id=1, source_target_pairs={{0,16},{4,20},{8,24},{12,28},{16,0},{20,4},{24,8},{28,12},{1,17},{... | collective-permute-start | bytes 442376 | tf_op jit(solution)/shard_map/ppermute | solution.py:279
  89.9 6.6 %collective-permute-done.46 = f32[144,256]{1,0:T(8,128)S(1)} collective-permute-done((f32[144,256]{1,0:T(8,128)S(1)}, f32[144,256]{1,0:T(8,128)S(1)}, u32[]{:S(2)}, u32[]{:S(2)}) %collective-permute-start.46) | collective-permute-done | bytes 147488 | tf_op jit(solution)/shard_map/ppermute | solution.py:279
  97.8 2.7 %collective-permute-start.47 = (f32[144,256]{1,0:T(8,128)S(1)}, f32[144,256]{1,0:T(8,128)S(1)}, u32[]{:S(2)}, u32[]{:S(2)}) collective-permute-start(f32[144,256]{1,0:T(8,128)S(1)} %add.82), channel_id=1, source_target_pairs={{0,8},{4,12},{8,0},{12,4},{16,24},{20,28},{24,16},{28,20},{1,9},{5... | collective-permute-start | bytes 442376 | tf_op jit(solution)/shard_map/ppermute | solution.py:279
  101.6 4.2 %collective-permute-done.37 = f32[144,256]{1,0:T(8,128)S(1)} collective-permute-done((f32[144,256]{1,0:T(8,128)S(1)}, f32[144,256]{1,0:T(8,128)S(1)}, u32[]{:S(2)}, u32[]{:S(2)}) %collective-permute-start.37) | collective-permute-done | bytes 147488 | tf_op jit(solution)/shard_map/ppermute | solution.py:279
  106.8 4.2 %collective-permute-done.29 = f32[144,256]{1,0:T(8,128)S(1)} collective-permute-done((f32[144,256]{1,0:T(8,128)S(1)}, f32[144,256]{1,0:T(8,128)S(1)}, u32[]{:S(2)}, u32[]{:S(2)}) %collective-permute-start.29) | collective-permute-done | bytes 147488 | tf_op jit(solution)/shard_map/ppermute | solution.py:279
  111.0 1.5 collective-permute-start.38
  112.5 7.4 %collective-permute-done.38 = f32[144,256]{1,0:T(8,128)S(1)} collective-permute-done((f32[144,256]{1,0:T(8,128)S(1)}, f32[144,256]{1,0:T(8,128)S(1)}, u32[]{:S(2)}, u32[]{:S(2)}) %collective-permute-start.38) | collective-permute-done | bytes 147488 | tf_op jit(solution)/shard_map/ppermute | solution.py:279
  120.2 3.7 %collective-permute-start.39 = (f32[144,256]{1,0:T(8,128)S(1)}, f32[144,256]{1,0:T(8,128)S(1)}, u32[]{:S(2)}, u32[]{:S(2)}) collective-permute-start(f32[144,256]{1,0:T(8,128)S(1)} %add.75), channel_id=1, source_target_pairs={{0,8},{4,12},{8,0},{12,4},{16,24},{20,28},{24,16},{28,20},{1,9},{5... | collective-permute-start | bytes 442376 | tf_op jit(solution)/shard_map/ppermute | solution.py:279
  124.1 1.5 collective-permute-start.17
  125.6 2.0 %collective-permute-done.30 = f32[144,256]{1,0:T(8,128)S(1)} collective-permute-done((f32[144,256]{1,0:T(8,128)S(1)}, f32[144,256]{1,0:T(8,128)S(1)}, u32[]{:S(2)}, u32[]{:S(2)}) %collective-permute-start.30) | collective-permute-done | bytes 147488 | tf_op jit(solution)/shard_map/ppermute | solution.py:279
  128.1 2.4 %collective-permute-start.31 = (f32[144,256]{1,0:T(8,128)S(1)}, f32[144,256]{1,0:T(8,128)S(1)}, u32[]{:S(2)}, u32[]{:S(2)}) collective-permute-start(f32[144,256]{1,0:T(8,128)S(1)} %add.68), channel_id=1, source_target_pairs={{0,8},{4,12},{8,0},{12,4},{16,24},{20,28},{24,16},{28,20},{1,9},{5... | collective-permute-start | bytes 442376 | tf_op jit(solution)/shard_map/ppermute | solution.py:279
  130.6 3.0 %collective-permute-done.31 = f32[144,256]{1,0:T(8,128)S(1)} collective-permute-done((f32[144,256]{1,0:T(8,128)S(1)}, f32[144,256]{1,0:T(8,128)S(1)}, u32[]{:S(2)}, u32[]{:S(2)}) %collective-permute-start.31) | collective-permute-done | bytes 147488 | tf_op jit(solution)/shard_map/ppermute | solution.py:279
  133.6 2.0 %collective-permute-start.32 = (f32[144,256]{1,0:T(8,128)S(1)}, f32[144,256]{1,0:T(8,128)S(1)}, u32[]{:S(2)}, u32[]{:S(2)}) collective-permute-start(f32[144,256]{1,0:T(8,128)S(1)} %add.69), channel_id=1, source_target_pairs={{0,4},{4,0},{8,12},{12,8},{16,20},{20,16},{24,28},{28,24},{1,5},{5... | collective-permute-start | bytes 442376 | tf_op jit(solution)/shard_map/ppermute | solution.py:279
  136.5 1.6 collective-permute-done.40
  138.9 2.4 %collective-permute-done.32 = f32[144,256]{1,0:T(8,128)S(1)} collective-permute-done((f32[144,256]{1,0:T(8,128)S(1)}, f32[144,256]{1,0:T(8,128)S(1)}, u32[]{:S(2)}, u32[]{:S(2)}) %collective-permute-start.32) | collective-permute-done | bytes 147488 | tf_op jit(solution)/shard_map/ppermute | solution.py:279
  145.6 3.1 %collective-permute-done.33 = f32[288,256]{1,0:T(8,128)S(1)} collective-permute-done((f32[288,256]{1,0:T(8,128)S(1)}, f32[288,256]{1,0:T(8,128)S(1)}, u32[]{:S(2)}, u32[]{:S(2)}) %collective-permute-start.33) | collective-permute-done | bytes 294944 | tf_op jit(solution)/shard_map/ppermute | solution.py:279
  150.0 1.6 weight_step.3.refs_0_
  151.8 1.6 weight_step.4.refs_0_
  153.5 8.1 %collective-permute-done.18.other_ref = bf16[864,256]{1,0:T(8,128)(2,1)S(1)} collective-permute-done((bf16[864,256]{1,0:T(8,128)(2,1)S(1)}, bf16[864,256]{1,0:T(8,128)(2,1)S(1)}, u32[]{:S(2)}, u32[]{:S(2)}) %collective-permute-start.18) | collective-permute-done | bytes 442400 | tf_op jit(solution)/shard_map/ppermute | solution.py:279
  161.6 1.6 weight_step.5
  163.2 4.8 %newton_schulz.3.refs_0_ = bf16[3,1152,256]{2,1,0:T(8,128)(2,1)} custom-call(f32[576,256]{1,0:T(8,128)S(1)} %pad_maximum_fusion.2.low_ref, f32[576,256]{1,0:T(8,128)S(1)} %collective-permute-done.50.high_ref), custom_call_target="tpu_custom_call" | custom-call | tf_op jit(solution)/shard_map/newton_schulz/pallas_call | solution.py:229
  168.1 4.8 %newton_schulz.4.refs_0_ = bf16[3,1152,256]{2,1,0:T(8,128)(2,1)} custom-call(f32[576,256]{1,0:T(8,128)S(1)} %pad_maximum_fusion.1.low_ref, f32[576,256]{1,0:T(8,128)S(1)} %collective-permute-done.42.high_ref, bf16[3,1152,256]{2,1,0:T(8,128)(2,1)} %newton_schulz.3.refs_0_), custom_call_target="tpu_custom_call", output_to_operand_aliasing={{}: (2, {})} | custom-call | tf_op jit(solution)/shard_map/newton_schulz/pallas_call | solution.py:229
  172.9 4.8 %newton_schulz.5 = bf16[3,1152,256]{2,1,0:T(8,128)(2,1)} custom-call(f32[576,256]{1,0:T(8,128)S(1)} %pad_maximum_fusion.low_ref, f32[576,256]{1,0:T(8,128)S(1)} %collective-permute-done.34.high_ref, bf16[3,1152,256]{2,1,0:T(8,128)(2,1)} %newton_schulz.4.refs_0_), custom_call_target="tpu_custom_call", output_to_operand_aliasing={{}: (2, {})} | custom-call | tf_op jit(solution)/shard_map/newton_schulz/pallas_call | solution.py:229
  (130 shorter events, 32.0 us)
Async XLA Ops:
  3.1 11.7 %collective-permute-start.10 = (bf16[256,128]{1,0:T(8,128)(2,1)S(1)}, bf16[256,128]{1,0:T(8,128)(2,1)S(1)}, u32[]{:S(2)}, u32[]{:S(2)}) collective-permute-start(bf16[256,128]{1,0:T(8,128)(2,1)S(1)} %get-tuple-element.54), channel_id=1, source_target_pairs={{0,12},{4,8},{8,4},{12,0},{16,28},{20,24},{24,20},{28,16},{1,13},{... | collective-permute-start | bytes 196616 | tf_op jit(solution)/shard_map/ppermute | solution.py:279
  7.1 8.2 %collective-permute-start.11 = (bf16[256,128]{1,0:T(8,128)(2,1)S(1)}, bf16[256,128]{1,0:T(8,128)(2,1)S(1)}, u32[]{:S(2)}, u32[]{:S(2)}) collective-permute-start(bf16[256,128]{1,0:T(8,128)(2,1)S(1)} %get-tuple-element.55), channel_id=1, source_target_pairs={{0,16},{4,20},{8,24},{12,28},{16,0},{20,4},{24,8},{28,12},{1,17},{... | collective-permute-start | bytes 196616 | tf_op jit(solution)/shard_map/ppermute | solution.py:279
  9.7 8.9 %collective-permute-start.12 = (bf16[256,128]{1,0:T(8,128)(2,1)S(1)}, bf16[256,128]{1,0:T(8,128)(2,1)S(1)}, u32[]{:S(2)}, u32[]{:S(2)}) collective-permute-start(bf16[256,128]{1,0:T(8,128)(2,1)S(1)} %get-tuple-element.56), channel_id=1, source_target_pairs={{0,20},{4,16},{8,28},{12,24},{16,4},{20,0},{24,12},{28,8},{1,21},{... | collective-permute-start | bytes 196616 | tf_op jit(solution)/shard_map/ppermute | solution.py:279
  10.0 8.6 %collective-permute-start.13 = (bf16[256,128]{1,0:T(8,128)(2,1)S(1)}, bf16[256,128]{1,0:T(8,128)(2,1)S(1)}, u32[]{:S(2)}, u32[]{:S(2)}) collective-permute-start(bf16[256,128]{1,0:T(8,128)(2,1)S(1)} %get-tuple-element.57), channel_id=1, source_target_pairs={{0,24},{4,28},{8,16},{12,20},{16,8},{20,12},{24,0},{28,4},{1,25},{... | collective-permute-start | bytes 196616 | tf_op jit(solution)/shard_map/ppermute | solution.py:279
  12.5 7.1 %collective-permute-start.14 = (bf16[256,128]{1,0:T(8,128)(2,1)S(1)}, bf16[256,128]{1,0:T(8,128)(2,1)S(1)}, u32[]{:S(2)}, u32[]{:S(2)}) collective-permute-start(bf16[256,128]{1,0:T(8,128)(2,1)S(1)} %get-tuple-element.58), channel_id=1, source_target_pairs={{0,28},{4,24},{8,20},{12,16},{16,12},{20,8},{24,4},{28,0},{1,29},{... | collective-permute-start | bytes 196616 | tf_op jit(solution)/shard_map/ppermute | solution.py:279
  23.5 27.1 %collective-permute-start.43 = (f32[576,256]{1,0:T(8,128)S(1)}, f32[576,256]{1,0:T(8,128)S(1)}, u32[]{:S(2)}, u32[]{:S(2)}) collective-permute-start(f32[576,256]{1,0:T(8,128)S(1)} %get-tuple-element.73), channel_id=1, source_target_pairs={{0,1},{1,0},{2,3},{3,2},{4,5},{5,4},{6,7},{7,6},{8,9},{9,8},{10,11... | collective-permute-start | bytes 1769480 | tf_op jit(solution)/shard_map/ppermute | solution.py:279
  24.6 9.2 %collective-permute-start.4 = (bf16[1024,128]{1,0:T(8,128)(2,1)S(1)}, bf16[1024,128]{1,0:T(8,128)(2,1)S(1)}, u32[]{:S(2)}, u32[]{:S(2)}) collective-permute-start(bf16[1024,128]{1,0:T(8,128)(2,1)S(1)} %get-tuple-element.46), channel_id=1, source_target_pairs={{0,4},{4,0},{8,12},{12,8},{16,20},{20,16},{24,28},{28,24},{1,5},{5... | collective-permute-start | bytes 786440 | tf_op jit(solution)/shard_map/ppermute | solution.py:279
  26.6 12.7 %collective-permute-start = (bf16[1024,128]{1,0:T(8,128)(2,1)S(1)}, bf16[1024,128]{1,0:T(8,128)(2,1)S(1)}, u32[]{:S(2)}, u32[]{:S(2)}) collective-permute-start(bf16[1024,128]{1,0:T(8,128)(2,1)S(1)} %get-tuple-element.40), channel_id=1, source_target_pairs={{0,4},{4,0},{8,12},{12,8},{16,20},{20,16},{24,28},{28,24},{1,5},{5... | collective-permute-start | bytes 786440 | tf_op jit(solution)/shard_map/ppermute | solution.py:279
  27.8 10.8 %collective-permute-start.23 = (bf16[216,256]{1,0:T(8,128)(2,1)S(1)}, bf16[216,256]{1,0:T(8,128)(2,1)S(1)}, u32[]{:S(2)}, u32[]{:S(2)}) collective-permute-start(bf16[216,256]{1,0:T(8,128)(2,1)S(1)} %get-tuple-element.65), channel_id=1, source_target_pairs={{0,8},{4,12},{8,0},{12,4},{16,24},{20,28},{24,16},{28,20},{1,9},{5... | collective-permute-start | bytes 331784 | tf_op jit(solution)/shard_map/ppermute | solution.py:279
  33.8 7.5 %collective-permute-start.5 = (bf16[512,128]{1,0:T(8,128)(2,1)S(1)}, bf16[512,128]{1,0:T(8,128)(2,1)S(1)}, u32[]{:S(2)}, u32[]{:S(2)}) collective-permute-start(bf16[512,128]{1,0:T(8,128)(2,1)S(1)} %get-tuple-element.48), channel_id=1, source_target_pairs={{0,8},{4,12},{8,0},{12,4},{16,24},{20,28},{24,16},{28,20},{1,9},{5... | collective-permute-start | bytes 393224 | tf_op jit(solution)/shard_map/ppermute | solution.py:279
  35.9 12.8 %collective-permute-start.6 = (bf16[512,128]{1,0:T(8,128)(2,1)S(1)}, bf16[512,128]{1,0:T(8,128)(2,1)S(1)}, u32[]{:S(2)}, u32[]{:S(2)}) collective-permute-start(bf16[512,128]{1,0:T(8,128)(2,1)S(1)} %get-tuple-element.49), channel_id=1, source_target_pairs={{0,16},{4,20},{8,24},{12,28},{16,0},{20,4},{24,8},{28,12},{1,17},{... | collective-permute-start | bytes 393224 | tf_op jit(solution)/shard_map/ppermute | solution.py:279
  38.6 10.1 %collective-permute-start.7 = (bf16[512,128]{1,0:T(8,128)(2,1)S(1)}, bf16[512,128]{1,0:T(8,128)(2,1)S(1)}, u32[]{:S(2)}, u32[]{:S(2)}) collective-permute-start(bf16[512,128]{1,0:T(8,128)(2,1)S(1)} %get-tuple-element.50), channel_id=1, source_target_pairs={{0,24},{4,28},{8,16},{12,20},{16,8},{20,12},{24,0},{28,4},{1,25},{... | collective-permute-start | bytes 393224 | tf_op jit(solution)/shard_map/ppermute | solution.py:279
  39.3 29.8 %collective-permute-start.24 = (bf16[432,256]{1,0:T(8,128)(2,1)}, bf16[432,256]{1,0:T(8,128)(2,1)}, u32[]{:S(2)}, u32[]{:S(2)}) collective-permute-start(bf16[432,256]{1,0:T(8,128)(2,1)} %pad_maximum_fusion.11), channel_id=1, source_target_pairs={{8,16},{12,20},{16,8},{20,12},{9,17},{13,21},{17,9},{21,13},{10,18... | collective-permute-start | bytes 663560 | tf_op jit(solution)/shard_map/ppermute | solution.py:286
  41.3 11.8 %collective-permute-start.1 = (bf16[512,128]{1,0:T(8,128)(2,1)S(1)}, bf16[512,128]{1,0:T(8,128)(2,1)S(1)}, u32[]{:S(2)}, u32[]{:S(2)}) collective-permute-start(bf16[512,128]{1,0:T(8,128)(2,1)S(1)} %get-tuple-element.42), channel_id=1, source_target_pairs={{0,8},{4,12},{8,0},{12,4},{16,24},{20,28},{24,16},{28,20},{1,9},{5... | collective-permute-start | bytes 393224 | tf_op jit(solution)/shard_map/ppermute | solution.py:279
  48.7 15.2 %collective-permute-start.2 = (bf16[512,128]{1,0:T(8,128)(2,1)S(1)}, bf16[512,128]{1,0:T(8,128)(2,1)S(1)}, u32[]{:S(2)}, u32[]{:S(2)}) collective-permute-start(bf16[512,128]{1,0:T(8,128)(2,1)S(1)} %get-tuple-element.43), channel_id=1, source_target_pairs={{0,16},{4,20},{8,24},{12,28},{16,0},{20,4},{24,8},{28,12},{1,17},{... | collective-permute-start | bytes 393224 | tf_op jit(solution)/shard_map/ppermute | solution.py:279
  50.6 24.4 %collective-permute-start.35 = (f32[576,256]{1,0:T(8,128)}, f32[576,256]{1,0:T(8,128)}, u32[]{:S(2)}, u32[]{:S(2)}) collective-permute-start(f32[576,256]{1,0:T(8,128)} %get-tuple-element.71), channel_id=1, source_target_pairs={{0,1},{1,0},{2,3},{3,2},{4,5},{5,4},{6,7},{7,6},{8,9},{9,8},{10,11... | collective-permute-start | bytes 1769480 | tf_op jit(solution)/shard_map/ppermute | solution.py:279
  51.6 21.7 %collective-permute-start.44 = (f32[288,256]{1,0:T(8,128)}, f32[288,256]{1,0:T(8,128)}, u32[]{:S(2)}, u32[]{:S(2)}) collective-permute-start(f32[288,256]{1,0:T(8,128)} %get-tuple-element.79), channel_id=1, source_target_pairs={{0,2},{1,3},{2,0},{3,1},{4,6},{5,7},{6,4},{7,5},{8,10},{9,11},{10,... | collective-permute-start | bytes 884744 | tf_op jit(solution)/shard_map/ppermute | solution.py:279
  53.8 10.7 %collective-permute-start.3 = (bf16[512,128]{1,0:T(8,128)(2,1)}, bf16[512,128]{1,0:T(8,128)(2,1)}, u32[]{:S(2)}, u32[]{:S(2)}) collective-permute-start(bf16[512,128]{1,0:T(8,128)(2,1)} %get-tuple-element.44), channel_id=1, source_target_pairs={{0,24},{4,28},{8,16},{12,20},{16,8},{20,12},{24,0},{28,4},{1,25},{... | collective-permute-start | bytes 393224 | tf_op jit(solution)/shard_map/ppermute | solution.py:279
  64.5 6.7 %collective-permute-start.19 = (bf16[216,256]{1,0:T(8,128)(2,1)S(1)}, bf16[216,256]{1,0:T(8,128)(2,1)}, u32[]{:S(2)}, u32[]{:S(2)}) collective-permute-start(bf16[216,256]{1,0:T(8,128)(2,1)S(1)} %get-tuple-element.64), channel_id=1, source_target_pairs={{0,8},{4,12},{8,0},{12,4},{16,24},{20,28},{24,16},{28,20},{1,9},{5... | collective-permute-start | bytes 331784 | tf_op jit(solution)/shard_map/ppermute | solution.py:279
  69.1 14.9 %collective-permute-start.27 = (f32[576,256]{1,0:T(8,128)S(1)}, f32[576,256]{1,0:T(8,128)S(1)}, u32[]{:S(2)}, u32[]{:S(2)}) collective-permute-start(f32[576,256]{1,0:T(8,128)S(1)} %get-tuple-element.69), channel_id=1, source_target_pairs={{0,1},{1,0},{2,3},{3,2},{4,5},{5,4},{6,7},{7,6},{8,9},{9,8},{10,11... | collective-permute-start | bytes 1769480 | tf_op jit(solution)/shard_map/ppermute | solution.py:279
  69.1 19.8 %collective-permute-start.15 = (bf16[216,256]{1,0:T(8,128)(2,1)S(1)}, bf16[216,256]{1,0:T(8,128)(2,1)S(1)}, u32[]{:S(2)}, u32[]{:S(2)}) collective-permute-start(bf16[216,256]{1,0:T(8,128)(2,1)S(1)} %get-tuple-element.63), channel_id=1, source_target_pairs={{0,8},{4,12},{8,0},{12,4},{16,24},{20,28},{24,16},{28,20},{1,9},{5... | collective-permute-start | bytes 331784 | tf_op jit(solution)/shard_map/ppermute | solution.py:279
  71.2 49.0 %collective-permute-start.25 = (bf16[432,256]{1,0:T(8,128)(2,1)}, bf16[432,256]{1,0:T(8,128)(2,1)S(1)}, u32[]{:S(2)}, u32[]{:S(2)}) collective-permute-start(bf16[432,256]{1,0:T(8,128)(2,1)} %collective-permute-done.24), channel_id=1, source_target_pairs={{8,0},{12,4},{16,24},{20,28},{9,1},{13,5},{17,25},{21,29},{10,2},{... | collective-permute-start | bytes 663560 | tf_op jit(solution)/shard_map/ppermute | solution.py:287
  73.4 15.7 %collective-permute-start.20 = (bf16[432,256]{1,0:T(8,128)(2,1)S(1)}, bf16[432,256]{1,0:T(8,128)(2,1)S(1)}, u32[]{:S(2)}, u32[]{:S(2)}) collective-permute-start(bf16[432,256]{1,0:T(8,128)(2,1)S(1)} %pad_maximum_fusion.10), channel_id=1, source_target_pairs={{8,16},{12,20},{16,8},{20,12},{9,17},{13,21},{17,9},{21,13},{10,18... | collective-permute-start | bytes 663560 | tf_op jit(solution)/shard_map/ppermute | solution.py:286
  75.0 6.0 %collective-permute-start.45 = (f32[144,256]{1,0:T(8,128)S(1)}, f32[144,256]{1,0:T(8,128)S(1)}, u32[]{:S(2)}, u32[]{:S(2)}) collective-permute-start(f32[144,256]{1,0:T(8,128)S(1)} %slice_add_fusion.6), channel_id=1, source_target_pairs={{0,4},{4,0},{8,12},{12,8},{16,20},{20,16},{24,28},{28,24},{1,5},{5... | collective-permute-start | bytes 442376 | tf_op jit(solution)/shard_map/ppermute | solution.py:279
  81.0 16.8 %collective-permute-start.36 = (f32[288,256]{1,0:T(8,128)S(1)}, f32[288,256]{1,0:T(8,128)S(1)}, u32[]{:S(2)}, u32[]{:S(2)}) collective-permute-start(f32[288,256]{1,0:T(8,128)S(1)} %get-tuple-element.81), channel_id=1, source_target_pairs={{0,2},{1,3},{2,0},{3,1},{4,6},{5,7},{6,4},{7,5},{8,10},{9,11},{10,... | collective-permute-start | bytes 884744 | tf_op jit(solution)/shard_map/ppermute | solution.py:279
  84.0 12.5 %collective-permute-start.46 = (f32[144,256]{1,0:T(8,128)S(1)}, f32[144,256]{1,0:T(8,128)S(1)}, u32[]{:S(2)}, u32[]{:S(2)}) collective-permute-start(f32[144,256]{1,0:T(8,128)S(1)} %fusion), channel_id=1, source_target_pairs={{0,16},{4,20},{8,24},{12,28},{16,0},{20,4},{24,8},{28,12},{1,17},{... | collective-permute-start | bytes 442376 | tf_op jit(solution)/shard_map/ppermute | solution.py:279
  88.9 11.7 %collective-permute-start.28 = (f32[288,256]{1,0:T(8,128)S(1)}, f32[288,256]{1,0:T(8,128)S(1)}, u32[]{:S(2)}, u32[]{:S(2)}) collective-permute-start(f32[288,256]{1,0:T(8,128)S(1)} %get-tuple-element.83), channel_id=1, source_target_pairs={{0,2},{1,3},{2,0},{3,1},{4,6},{5,7},{6,4},{7,5},{8,10},{9,11},{10,... | collective-permute-start | bytes 884744 | tf_op jit(solution)/shard_map/ppermute | solution.py:279
  89.1 34.9 %collective-permute-start.16 = (bf16[432,256]{1,0:T(8,128)(2,1)S(1)}, bf16[432,256]{1,0:T(8,128)(2,1)S(1)}, u32[]{:S(2)}, u32[]{:S(2)}) collective-permute-start(bf16[432,256]{1,0:T(8,128)(2,1)S(1)} %pad_maximum_fusion.9), channel_id=1, source_target_pairs={{8,16},{12,20},{16,8},{20,12},{9,17},{13,21},{17,9},{21,13},{10,18... | collective-permute-start | bytes 663560 | tf_op jit(solution)/shard_map/ppermute | solution.py:286
  96.5 33.9 %collective-permute-start.21 = (bf16[432,256]{1,0:T(8,128)(2,1)S(1)}, bf16[432,256]{1,0:T(8,128)(2,1)S(1)}, u32[]{:S(2)}, u32[]{:S(2)}) collective-permute-start(bf16[432,256]{1,0:T(8,128)(2,1)S(1)} %collective-permute-done.20), channel_id=1, source_target_pairs={{8,0},{12,4},{16,24},{20,28},{9,1},{13,5},{17,25},{21,29},{10,2},{... | collective-permute-start | bytes 663560 | tf_op jit(solution)/shard_map/ppermute | solution.py:287
  97.8 26.2 %collective-permute-start.47 = (f32[144,256]{1,0:T(8,128)S(1)}, f32[144,256]{1,0:T(8,128)S(1)}, u32[]{:S(2)}, u32[]{:S(2)}) collective-permute-start(f32[144,256]{1,0:T(8,128)S(1)} %add.82), channel_id=1, source_target_pairs={{0,8},{4,12},{8,0},{12,4},{16,24},{20,28},{24,16},{28,20},{1,9},{5... | collective-permute-start | bytes 442376 | tf_op jit(solution)/shard_map/ppermute | solution.py:279
  100.6 5.2 %collective-permute-start.37 = (f32[144,256]{1,0:T(8,128)S(1)}, f32[144,256]{1,0:T(8,128)S(1)}, u32[]{:S(2)}, u32[]{:S(2)}) collective-permute-start(f32[144,256]{1,0:T(8,128)S(1)} %slice_add_fusion.8), channel_id=1, source_target_pairs={{0,4},{4,0},{8,12},{12,8},{16,20},{20,16},{24,28},{28,24},{1,5},{5... | collective-permute-start | bytes 442376 | tf_op jit(solution)/shard_map/ppermute | solution.py:279
  111.0 8.9 %collective-permute-start.38 = (f32[144,256]{1,0:T(8,128)S(1)}, f32[144,256]{1,0:T(8,128)S(1)}, u32[]{:S(2)}, u32[]{:S(2)}) collective-permute-start(f32[144,256]{1,0:T(8,128)S(1)} %fusion.1), channel_id=1, source_target_pairs={{0,16},{4,20},{8,24},{12,28},{16,0},{20,4},{24,8},{28,12},{1,17},{... | collective-permute-start | bytes 442376 | tf_op jit(solution)/shard_map/ppermute | solution.py:279
  119.9 7.7 %collective-permute-start.30 = (f32[144,256]{1,0:T(8,128)S(1)}, f32[144,256]{1,0:T(8,128)S(1)}, u32[]{:S(2)}, u32[]{:S(2)}) collective-permute-start(f32[144,256]{1,0:T(8,128)S(1)} %fusion.2), channel_id=1, source_target_pairs={{0,16},{4,20},{8,24},{12,28},{16,0},{20,4},{24,8},{28,12},{1,17},{... | collective-permute-start | bytes 442376 | tf_op jit(solution)/shard_map/ppermute | solution.py:279
  120.2 7.9 %collective-permute-start.39 = (f32[144,256]{1,0:T(8,128)S(1)}, f32[144,256]{1,0:T(8,128)S(1)}, u32[]{:S(2)}, u32[]{:S(2)}) collective-permute-start(f32[144,256]{1,0:T(8,128)S(1)} %add.75), channel_id=1, source_target_pairs={{0,8},{4,12},{8,0},{12,4},{16,24},{20,28},{24,16},{28,20},{1,9},{5... | collective-permute-start | bytes 442376 | tf_op jit(solution)/shard_map/ppermute | solution.py:279
  124.0 25.4 %collective-permute-start.26 = (bf16[864,256]{1,0:T(8,128)(2,1)S(1)}, bf16[864,256]{1,0:T(8,128)(2,1)S(1)}, u32[]{:S(2)}, u32[]{:S(2)}) collective-permute-start(bf16[864,256]{1,0:T(8,128)(2,1)S(1)} %pad_maximum_fusion.5.mine_ref), channel_id=1, source_target_pairs={{0,4},{4,0},{8,12},{12,8},{16,20},{20,16},{24,28},{28,24},{1,5},{5... | collective-permute-start | bytes 1327112 | tf_op jit(solution)/shard_map/ppermute | solution.py:279
  124.1 24.7 %collective-permute-start.17 = (bf16[432,256]{1,0:T(8,128)(2,1)S(1)}, bf16[432,256]{1,0:T(8,128)(2,1)S(1)}, u32[]{:S(2)}, u32[]{:S(2)}) collective-permute-start(bf16[432,256]{1,0:T(8,128)(2,1)S(1)} %collective-permute-done.16), channel_id=1, source_target_pairs={{8,0},{12,4},{16,24},{20,28},{9,1},{13,5},{17,25},{21,29},{10,2},{... | collective-permute-start | bytes 663560 | tf_op jit(solution)/shard_map/ppermute | solution.py:287
  127.6 8.0 %collective-permute-start.48 = (f32[144,256]{1,0:T(8,128)S(1)}, f32[144,256]{1,0:T(8,128)S(1)}, u32[]{:S(2)}, u32[]{:S(2)}) collective-permute-start(f32[144,256]{1,0:T(8,128)S(1)} %add.83), channel_id=1, source_target_pairs={{0,4},{4,0},{8,12},{12,8},{16,20},{20,16},{24,28},{28,24},{1,5},{5... | collective-permute-start | bytes 442376 | tf_op jit(solution)/shard_map/ppermute | solution.py:279
  128.1 5.5 %collective-permute-start.31 = (f32[144,256]{1,0:T(8,128)S(1)}, f32[144,256]{1,0:T(8,128)S(1)}, u32[]{:S(2)}, u32[]{:S(2)}) collective-permute-start(f32[144,256]{1,0:T(8,128)S(1)} %add.68), channel_id=1, source_target_pairs={{0,8},{4,12},{8,0},{12,4},{16,24},{20,28},{24,16},{28,20},{1,9},{5... | collective-permute-start | bytes 442376 | tf_op jit(solution)/shard_map/ppermute | solution.py:279
  130.4 7.7 %collective-permute-start.40 = (f32[144,256]{1,0:T(8,128)S(1)}, f32[144,256]{1,0:T(8,128)S(1)}, u32[]{:S(2)}, u32[]{:S(2)}) collective-permute-start(f32[144,256]{1,0:T(8,128)S(1)} %add.76), channel_id=1, source_target_pairs={{0,4},{4,0},{8,12},{12,8},{16,20},{20,16},{24,28},{28,24},{1,5},{5... | collective-permute-start | bytes 442376 | tf_op jit(solution)/shard_map/ppermute | solution.py:279
  133.6 7.7 %collective-permute-start.32 = (f32[144,256]{1,0:T(8,128)S(1)}, f32[144,256]{1,0:T(8,128)S(1)}, u32[]{:S(2)}, u32[]{:S(2)}) collective-permute-start(f32[144,256]{1,0:T(8,128)S(1)} %add.69), channel_id=1, source_target_pairs={{0,4},{4,0},{8,12},{12,8},{16,20},{20,16},{24,28},{28,24},{1,5},{5... | collective-permute-start | bytes 442376 | tf_op jit(solution)/shard_map/ppermute | solution.py:279
  135.6 7.8 %collective-permute-start.49 = (f32[288,256]{1,0:T(8,128)S(1)}, f32[288,256]{1,0:T(8,128)S(1)}, u32[]{:S(2)}, u32[]{:S(2)}) collective-permute-start(f32[288,256]{1,0:T(8,128)S(1)} %pad_maximum_fusion.8), channel_id=1, source_target_pairs={{0,2},{1,3},{2,0},{3,1},{4,6},{5,7},{6,4},{7,5},{8,10},{9,11},{10,... | collective-permute-start | bytes 884744 | tf_op jit(solution)/shard_map/ppermute | solution.py:279
  138.1 7.4 %collective-permute-start.41 = (f32[288,256]{1,0:T(8,128)S(1)}, f32[288,256]{1,0:T(8,128)S(1)}, u32[]{:S(2)}, u32[]{:S(2)}) collective-permute-start(f32[288,256]{1,0:T(8,128)S(1)} %pad_maximum_fusion.7), channel_id=1, source_target_pairs={{0,2},{1,3},{2,0},{3,1},{4,6},{5,7},{6,4},{7,5},{8,10},{9,11},{10,... | collective-permute-start | bytes 884744 | tf_op jit(solution)/shard_map/ppermute | solution.py:279
  141.3 7.4 %collective-permute-start.33 = (f32[288,256]{1,0:T(8,128)S(1)}, f32[288,256]{1,0:T(8,128)S(1)}, u32[]{:S(2)}, u32[]{:S(2)}) collective-permute-start(f32[288,256]{1,0:T(8,128)S(1)} %pad_maximum_fusion.6), channel_id=1, source_target_pairs={{0,2},{1,3},{2,0},{3,1},{4,6},{5,7},{6,4},{7,5},{8,10},{9,11},{10,... | collective-permute-start | bytes 884744 | tf_op jit(solution)/shard_map/ppermute | solution.py:279
  143.5 8.4 %collective-permute-start.22 = (bf16[864,256]{1,0:T(8,128)(2,1)S(1)}, bf16[864,256]{1,0:T(8,128)(2,1)S(1)}, u32[]{:S(2)}, u32[]{:S(2)}) collective-permute-start(bf16[864,256]{1,0:T(8,128)(2,1)S(1)} %pad_maximum_fusion.4.mine_ref), channel_id=1, source_target_pairs={{0,4},{4,0},{8,12},{12,8},{16,20},{20,16},{24,28},{28,24},{1,5},{5... | collective-permute-start | bytes 1327112 | tf_op jit(solution)/shard_map/ppermute | solution.py:279
  145.6 17.7 %collective-permute-start.50 = (f32[576,256]{1,0:T(8,128)S(1)}, f32[576,256]{1,0:T(8,128)S(1)}, u32[]{:S(2)}, u32[]{:S(2)}) collective-permute-start(f32[576,256]{1,0:T(8,128)S(1)} %pad_maximum_fusion.2.low_ref), channel_id=1, source_target_pairs={{0,1},{1,0},{2,3},{3,2},{4,5},{5,4},{6,7},{7,6},{8,9},{9,8},{10,11... | collective-permute-start | bytes 1769480 | tf_op jit(solution)/shard_map/ppermute | solution.py:279
  148.7 19.3 %collective-permute-start.42 = (f32[576,256]{1,0:T(8,128)S(1)}, f32[576,256]{1,0:T(8,128)S(1)}, u32[]{:S(2)}, u32[]{:S(2)}) collective-permute-start(f32[576,256]{1,0:T(8,128)S(1)} %pad_maximum_fusion.1.low_ref), channel_id=1, source_target_pairs={{0,1},{1,0},{2,3},{3,2},{4,5},{5,4},{6,7},{7,6},{8,9},{9,8},{10,11... | collective-permute-start | bytes 1769480 | tf_op jit(solution)/shard_map/ppermute | solution.py:279
  148.8 24.1 %collective-permute-start.34 = (f32[576,256]{1,0:T(8,128)S(1)}, f32[576,256]{1,0:T(8,128)S(1)}, u32[]{:S(2)}, u32[]{:S(2)}) collective-permute-start(f32[576,256]{1,0:T(8,128)S(1)} %pad_maximum_fusion.low_ref), channel_id=1, source_target_pairs={{0,1},{1,0},{2,3},{3,2},{4,5},{5,4},{6,7},{7,6},{8,9},{9,8},{10,11... | collective-permute-start | bytes 1769480 | tf_op jit(solution)/shard_map/ppermute | solution.py:279
  149.4 12.2 %collective-permute-start.18 = (bf16[864,256]{1,0:T(8,128)(2,1)S(1)}, bf16[864,256]{1,0:T(8,128)(2,1)S(1)}, u32[]{:S(2)}, u32[]{:S(2)}) collective-permute-start(bf16[864,256]{1,0:T(8,128)(2,1)S(1)} %pad_maximum_fusion.3.mine_ref), channel_id=1, source_target_pairs={{0,4},{4,0},{8,12},{12,8},{16,20},{20,16},{24,28},{28,24},{1,5},{5... | collective-permute-start | bytes 1327112 | tf_op jit(solution)/shard_map/ppermute | solution.py:279
  (19 other events, 144.8 us)

commit v3 on v0

v3 whole, which is shorter than its diff:
```python
import functools
import math

import jax
import jax.numpy as jnp
from jax import lax
from jax.experimental import pallas as pl
from jax.experimental.pallas import tpu as pltpu
from jax.sharding import PartitionSpec as P

NS_STEPS = 5
CORR_FIRST = 1.0
CORR_SECOND = 0.6323045752
HIGHEST = lax.Precision.HIGHEST
LANES = 128
TOKEN = jax.ShapeDtypeStruct((8, 128), jnp.float32)
GROUPS = ((0, 1), (2,))
G_X = (False, False)
X_FIRST = (False, False)
Y_SPLIT = (False, False)
X_HIGH = (False, False)
Z_SPLIT = (False, False)
U_FAR = (False, False)
COST = {"newton_schulz": 10}
PLAN = (
    "cut:0",
    "cut:1",
    "project:0",
    "project:1",
    "core:0",
    "core:1",
    "join:0",
    "y:0",
    "wait:g03",
    "y:1",
    "x:0",
    "collect:0",
    "x:1",
    "far:0",
    "join:1",
    "far:1",
    "near:0",
    "near:1",
    "weight:1",
    "wait:un0",
    "collect:1",
    "weight:0",
    "basis:0",
    "basis:1",
    "weight:2",
)
PARAMS = pltpu.CompilerParams(vmem_limit_bytes=32 * 1024 * 1024)


def dot(a, b, dims, **kw):
    return lax.dot_general(a, b, (dims, ((), ())), preferred_element_type=jnp.float32, **kw)


def nn(a, b, **kw):
    return dot(a, b, ((1,), (0,)), **kw)


def tn(a, b, **kw):
    return dot(a, b, ((0,), (0,)), **kw)


def nt(a, b, **kw):
    return dot(a, b, ((1,), (1,)), **kw)


def block(shape, at=0):
    return pl.BlockSpec(shape, lambda i: (at,) + (0,) * (len(shape) - 1))


def call(
    kernel,
    inputs,
    in_specs,
    outs,
    out_specs=None,
    earlier=(),
    first_out=0,
    grid=1,
    after=(),
    scratch=(),
    name=None,
    us=0.5,
):
    in_specs = in_specs or [block(x.shape) for x in inputs]
    out_specs = out_specs or [block(x.shape) for x in outs]
    count, unused = len(inputs), len(earlier) + len(after)

    def body(*refs):
        kernel(*refs[:count], *refs[count + unused :])

    return pl.pallas_call(
        body,
        grid=(grid,),
        in_specs=in_specs + [pl.BlockSpec(memory_space=pl.ANY)] * unused,
        out_specs=out_specs,
        out_shape=outs,
        scratch_shapes=list(scratch),
        input_output_aliases={count + i: first_out + i for i in range(len(earlier))},
        compiler_params=PARAMS,
        cost_estimate=pl.CostEstimate(
            flops=int(us * COST.get(name, 5) * 1e9), bytes_accessed=int(us * COST.get(name, 5) * 3e6), transcendentals=0
        ),
        name=name,
    )(*inputs, *earlier, *after)


def row_owner(x_high):
    tensor = lax.axis_index("tensor")
    y, x = tensor >> 1, lax.axis_index("shard") & 1
    return (tensor & 1) * 4 + (x * 2 + y if x_high else y * 2 + x)


def fold_plan(rows, cols):
    tail = cols - LANES
    rest = 2 * tail - LANES
    stacked = -(-(rows // 2) // 16) * 8
    return tail, rest, stacked


def fold(block):
    rows, cols = block.shape
    tail, rest, stacked = fold_plan(rows, cols)
    half = rows // 2
    upper, lower = block[:half, LANES:], block[half:, LANES:]
    middle = jnp.concatenate([upper, lower[:, : tail - rest]], axis=1)
    left = lower[:, tail - rest :]
    below = jnp.concatenate(
        [left[stacked:], jnp.zeros((2 * stacked - half, rest), block.dtype)], axis=0
    )
    last = jnp.concatenate(
        [left[:stacked], below, jnp.zeros((stacked, LANES - 2 * rest), block.dtype)], axis=1
    )
    return jnp.concatenate([block[:, :LANES], middle, last], axis=0)


def unfold(folded, rows, cols):
    tail, rest, stacked = fold_plan(rows, cols)
    half = rows // 2
    middle, last = folded[rows : rows + half], folded[rows + half :]
    left = jnp.concatenate([last[:, :rest], last[: half - stacked, rest : 2 * rest]], axis=0)
    lower = jnp.concatenate([middle[:, tail:], left], axis=1)
    second = jnp.concatenate([middle[:, :tail], lower], axis=0)
    second = jnp.concatenate([second, jnp.zeros((rows, LANES - tail), folded.dtype)], axis=1)
    return jnp.concatenate([folded[:rows], second], axis=1)


def cut_kernel(cols, offsets, g_ref, *refs):
    outs, held = refs[:-1], refs[-1]
    parts, size, _ = held.shape
    for part in range(parts):
        columns = g_ref[0, :, part * cols : (part + 1) * cols].astype(jnp.float32)
        held[part] = fold(columns).astype(held.dtype)
    me = lax.axis_index("shard")
    for out, ks in zip(outs, offsets):
        for i, k in enumerate(ks):
            out[0, i * size : (i + 1) * size, :] = held[me ^ k]


def cut(gradients, group, parts, cols, offsets, after=()):
    _, rows, whole = gradients.shape
    size = folded_rows(rows, cols)
    return call(
        functools.partial(cut_kernel, cols, offsets),
        [gradients],
        [pl.BlockSpec((1, rows, whole), lambda i: (group[0] + i, 0, 0))],
        [
            jax.ShapeDtypeStruct((len(group), len(ks) * size, LANES), gradients.dtype)
            for ks in offsets
        ],
        out_specs=[
            pl.BlockSpec((1, len(ks) * size, LANES), lambda i: (i, 0, 0)) for ks in offsets
        ],
        grid=len(group),
        after=after,
        scratch=[pltpu.VMEM((parts, size, LANES), gradients.dtype)],
        name="cut_columns",
        us=len(group),
    )


def match_kernel(own_ref, got_ref, *outs):
    size = outs[0].shape[1] // 2
    for k, out in enumerate(outs):
        out[:, :size, :] = own_ref[:, k * size : (k + 1) * size, :]
        out[:, size:, :] = got_ref[:, k * size : (k + 1) * size, :]


def match(own, got, count, after=()):
    shape = jax.ShapeDtypeStruct((own.shape[0], own.shape[1] // count * 2, LANES), own.dtype)
    return call(match_kernel, [own, got], None, [shape] * count, after=after, name="match", us=0.7)


def folded_rows(rows, cols):
    return rows + rows // 2 + fold_plan(rows, cols)[2]


def project_kernel(offsets, x_high, rows, cols, *refs):
    count = len(offsets)
    parts = sum(len(ks) for ks in offsets)
    blocks, (p_ref, first_ref, second_ref), refs = refs[:count], refs[count : count + 3], refs[count + 3 :]
    update_ref, first_out, second_out, send_ref, keep_ref, grad = refs
    me = lax.axis_index("shard")
    size = folded_rows(rows, cols)
    for ref, ks in zip(blocks, offsets):
        for i, k in enumerate(ks):
            part = unfold(ref[0, i * size : (i + 1) * size, :].astype(jnp.float32), rows, cols)
            grad[pl.ds(pl.multiple_of((me ^ k) * rows, rows), rows), :] = part.astype(grad.dtype)
    projected = tn(grad[...], p_ref[0])
    back = projected.astype(jnp.bfloat16)
    own = row_owner(x_high)
    half = parts // 2
    for j in list(range(half, parts)) + list(range(half)):
        at = pl.multiple_of((own ^ j) * rows, rows)
        term = nn(grad[pl.ds(at, rows), :], back)
        out = send_ref if j >= half else keep_ref
        out[j % half, 0] = term
    projected = projected[:cols]
    first_new = 0.9 * first_ref[0] + 0.1 * projected
    second_new = 0.999 * second_ref[0] + 0.001 * projected * projected
    first_out[0] = first_new
    second_out[0] = second_new
    update_ref[0] = (
        first_new / CORR_FIRST / (jnp.sqrt(second_new / CORR_SECOND) + 1e-08)
    ).astype(jnp.bfloat16)


def project(blocks, offsets, x_high, group, rows, projectors, first, second, earlier, after=()):
    mats, width, rank = projectors.shape
    cols = first.shape[1]
    parts = sum(len(ks) for ks in offsets)
    count = len(group)
    wide = -(-cols // LANES) * LANES
    of_group = lambda *shape: pl.BlockSpec((1, *shape), lambda i: (group[0] + i, 0, 0))
    own = lambda *shape: pl.BlockSpec((1, *shape), lambda i: (i, 0, 0))
    half = pl.BlockSpec((parts // 2, 1, rows, rank), lambda i: (0, i, 0, 0))
    term = jax.ShapeDtypeStruct((parts // 2, count, rows, rank), jnp.float32)
    moment = of_group(cols, rank)
    return call(
        functools.partial(project_kernel, offsets, x_high, rows, cols),
        [*blocks, projectors, first, second],
        [own(*b.shape[1:]) for b in blocks] + [of_group(width, rank), moment, moment],
        [
            jax.ShapeDtypeStruct((count, cols, rank), jnp.bfloat16),
            jax.ShapeDtypeStruct(first.shape, first.dtype),
            jax.ShapeDtypeStruct(second.shape, second.dtype),
            term,
            term,
        ],
        out_specs=[own(cols, rank), moment, moment, half, half],
        grid=count,
        earlier=earlier,
        first_out=1,
        after=after,
        scratch=[pltpu.VMEM((width, wide), jnp.bfloat16)],
        name="project",
        us=2 * count,
    )


def sum_kernel(terms, inputs, *refs):
    ins, outs = refs[:inputs], refs[inputs:]
    for out, parts in zip(outs, terms):
        total = None
        for which, start in parts:
            value = ins[which][start : start + out.shape[0]]
            total = value if total is None else total + value
        out[...] = total


def sums(inputs, terms, after=()):
    shapes = [(count, *inputs[0].shape[1:]) for _, count in terms]
    return call(
        functools.partial(sum_kernel, [parts for parts, _ in terms], len(inputs)),
        inputs,
        None,
        [jax.ShapeDtypeStruct(shape, jnp.float32) for shape in shapes],
        after=after,
        name="sums",
        us=0.6,
    )


def halve_kernel(count, *refs):
    ins, outs = refs[:count], refs[count:]
    rows = outs[0].shape[2]
    for i, out in enumerate(outs):
        total = None
        for ref in ins:
            value = ref[:1, :, i * rows : (i + 1) * rows, :]
            total = value if total is None else total + value
        out[...] = total


def halve(inputs, after=()):
    _, count, rows, rank = inputs[0].shape
    shape = jax.ShapeDtypeStruct((1, count, rows // 2, rank), jnp.float32)
    return call(
        functools.partial(halve_kernel, len(inputs)),
        inputs,
        None,
        [shape] * 2,
        after=after,
        name="sums",
        us=0.6,
    )


def whole_kernel(a_ref, b_ref, c_ref, d_ref, out_ref):
    rows = a_ref.shape[2]
    out_ref[:, :, :rows, :] = a_ref[...] + b_ref[...]
    out_ref[:, :, rows:, :] = c_ref[...] + d_ref[...]


def whole(halves, got, after=()):
    _, count, rows, rank = halves[0].shape
    shape = jax.ShapeDtypeStruct((1, count, 2 * rows, rank), jnp.float32)
    ins = [halves[0], got[0], halves[1], got[1]]
    return call(whole_kernel, ins, None, [shape], after=after, name="sums", us=0.6)


def join_kernel(a_ref, b_ref, out_ref):
    count = a_ref.shape[0]
    out_ref[:count], out_ref[count:] = a_ref[...], b_ref[...]


def join(a, b, after=()):
    shape = jax.ShapeDtypeStruct((a.shape[0] + b.shape[0], *a.shape[1:]), a.dtype)
    return call(join_kernel, [a, b], None, [shape], after=after, name="join", us=0.4)


def collect_kernel(both_ref, middle_ref, outer_ref, out_ref):
    z = lax.axis_index("shard") >> 1
    inner = (z == 1) | (z == 2)
    out_ref[:2] = both_ref[...]

    @pl.when(inner)
    def _():
        out_ref[2:] = middle_ref[...]

    @pl.when(jnp.logical_not(inner))
    def _():
        out_ref[2:] = outer_ref[...]


def collect(both, middle, outer, after=()):
    shape = jax.ShapeDtypeStruct((4, *both.shape[1:]), both.dtype)
    return call(
        collect_kernel, [both, middle, outer], None, [shape], after=after, name="collect", us=0.6
    )


def split(a):
    high = a.astype(jnp.bfloat16)
    return high, (a - high.astype(jnp.float32)).astype(jnp.bfloat16)


def thrice(a, b):
    return nn(jnp.concatenate([a[0], a[0], a[1]], axis=1), jnp.concatenate([b[0], b[1], b[0]], axis=0))


def basis_kernel(factor, x_high, *refs):
    pieces, (out_ref, token_ref, held_high, held_low) = refs[:-4], refs[-4:]
    token_ref[...] = jnp.zeros_like(token_ref)
    count, width, rank = held_high.shape
    rows = width // 8
    eye = (
        lax.broadcasted_iota(jnp.int32, (rank, rank), 0)
        == lax.broadcasted_iota(jnp.int32, (rank, rank), 1)
    ).astype(jnp.float32)
    mats = range(count)
    square, grams = [], []
    for m in mats:
        total = 0.0
        for j, piece in enumerate(pieces):
            value = piece[0, m]
            total = total + jnp.sum(value * value)
            span = slice(j * rows, (j + 1) * rows)
            held_high[m, span, :], held_low[m, span, :] = split(value)
        square.append(total + 1e-06)
    for m in mats:
        high, low = held_high[m], held_low[m]
        both = tn(high, jnp.concatenate([high, low], axis=1))
        cross = both[:, rank:]
        grams.append((both[:, :rank] + (cross + cross.T)) * (1.0 / square[m]))
    totals = [None] * count
    for sweep in range(NS_STEPS):
        parts = [split(gram) for gram in grams]
        if sweep < NS_STEPS - 1:
            squares = [thrice(parts[m], parts[m]) for m in mats]
        if sweep == 0:
            totals = [1.5 * eye - 0.5 * gram for gram in grams]
        else:
            totals = [1.5 * totals[m] - 0.5 * thrice(split(totals[m]), parts[m]) for m in mats]
        if sweep < NS_STEPS - 1:
            cubes = [thrice(split(squares[m]), parts[m]) for m in mats]
            grams = [2.25 * grams[m] - 1.5 * squares[m] + 0.25 * cubes[m] for m in mats]
    own = row_owner(x_high)
    for m in mats:
        total = split(totals[m] * (factor / jnp.sqrt(square[m])))
        for j in range(8):
            span = slice(j * rows, (j + 1) * rows)
            value = thrice((held_high[m, span, :], held_low[m, span, :]), total)
            at = pl.multiple_of((own ^ j) * rows, rows)
            out_ref[m, pl.ds(at, rows), :] = value.astype(jnp.bfloat16)


def basis(pieces, x_high, group, mats, factor, earlier, after=()):
    _, count, rows, rank = pieces[0].shape
    width = 8 * rows
    span = pl.BlockSpec((count, width, rank), lambda i: (group[0] // count, 0, 0))
    return call(
        functools.partial(basis_kernel, factor, x_high),
        pieces,
        None,
        [jax.ShapeDtypeStruct((mats, width, rank), jnp.bfloat16), TOKEN],
        out_specs=[span, block(TOKEN.shape)],
        earlier=earlier,
        after=after,
        scratch=[pltpu.VMEM((count, width, rank), jnp.bfloat16)] * 2,
        name="newton_schulz",
        us=4 * count,
    )


def weight_kernel(cols, x_first, far, w_ref, p_ref, *refs):
    pieces, (out_ref, token_ref, held) = refs[:-3], refs[-3:]
    token_ref[...] = jnp.zeros_like(token_ref)
    rows = w_ref.shape[1]
    me = lax.axis_index("shard")
    z, x = me >> 1, me & 1
    early = z < 2
    order = [z, z ^ 1, jnp.where(early, 2, 1), jnp.where(early, 3, 0)]
    if far:
        order = [z, z ^ 1, z ^ 2, z ^ 3]
    if x_first:
        for i in range(4):
            place = x ^ (i % 2)
            held[order[i // 2] * 2 + place] = pieces[0][i, 0]
            if far:
                held[order[2 + i // 2] * 2 + place] = pieces[1][i, 0]
                continue
            inner = (z == 1) | (z == 2)

            @pl.when(inner)
            def _(i=i, place=place):
                held[order[2 + i // 2] * 2 + place] = pieces[1][i, 0]

            @pl.when(jnp.logical_not(inner))
            def _(i=i, place=place):
                held[order[2 + i // 2] * 2 + place] = pieces[2][i, 0]

    else:
        mine_ref, other_ref = pieces
        for i in range(4):
            held[order[i] * 2 + x] = mine_ref[i, 0]
            held[order[i] * 2 + (x ^ 1)] = other_ref[i, 0]
    own = p_ref[0, pl.ds(pl.multiple_of(me * rows, rows), rows), :]
    for part in range(held.shape[0]):
        span = slice(part * cols, (part + 1) * cols)
        out_ref[0, :, span] = w_ref[0, :, span] - 0.2 * nt(own, held[part])


def weight_step(weights, projectors, pieces, modes, place, mat, earlier, after=()):
    mats, rows, whole = weights.shape
    _, width, rank = projectors.shape
    cols = pieces[0].shape[2]
    part = pl.BlockSpec((4, 1, cols, rank), lambda i: (0, place, 0, 0))
    big = block((1, rows, whole), mat)
    return call(
        functools.partial(weight_kernel, cols, *modes),
        [weights, projectors, *pieces],
        [big, block((1, width, rank), mat)] + [part] * len(pieces),
        [jax.ShapeDtypeStruct(weights.shape, weights.dtype), TOKEN],
        out_specs=[big, block(TOKEN.shape)],
        earlier=earlier,
        after=after,
        scratch=[pltpu.VMEM((8, cols, rank), jnp.bfloat16)],
        name="weight_step",
        us=1.6,
    )


def swap(x, axis, size, bit):
    return lax.ppermute(x, axis, [(i, i ^ bit) for i in range(size)])


def core(x):
    return swap(x, "tensor", 4, 1)


def along_y(x):
    return swap(x, "tensor", 4, 2)


def along_x(x):
    return swap(x, "shard", 8, 1)


def z_near(x):
    return swap(x, "shard", 8, 2)


def z_far(x):
    return swap(x, "shard", 8, 4)


def z_middle(x):
    return lax.ppermute(x, "shard", [(2, 4), (3, 5), (4, 2), (5, 3)])


def z_outer(x):
    return lax.ppermute(x, "shard", [(2, 0), (3, 1), (4, 6), (5, 7)])


def per_device(gradients, weights, projectors, first_moment, second_moment):
    factor = math.sqrt(projectors.shape[0])
    mats, rows, across_tensor = gradients.shape
    cols = across_tensor // 8
    across = jnp.swapaxes(projectors, 0, 1)
    first = jnp.swapaxes(first_moment[:, :, 0, :], 1, 2)
    second = jnp.swapaxes(second_moment[:, :, 0, :], 1, 2)
    last, pending = [], []

    def after():
        found = (*last, *pending)
        pending.clear()
        return found

    def mark(outs):
        last[:] = [outs[0]]
        return outs

    moved = {}

    def move(name, way, x):
        moved[name] = way(x)
        return moved[name]

    def axes(g):
        return (along_x, along_y) if X_HIGH[g] else (along_y, along_x)

    groups, count = GROUPS, len(GROUPS)
    moments, bases, new_weight = (), (), ()
    update, state, send, spread = {}, {}, {}, {}
    blocks, offsets = {}, {}

    def by_offset(k):
        return lambda x: swap(x, "shard", 8, k)

    def step_cut(g):
        if G_X[g]:
            own, sent = mark(cut(gradients, groups[g], 8, cols, [(0, 2, 4, 6), (1, 3, 5, 7)], after()))
            blocks[g] = own, move(f"gx{g}", along_x, sent)
            return
        offsets[g] = [(k,) for k in range(8)]
        pieces = mark(cut(gradients, groups[g], 8, cols, offsets[g], after()))
        blocks[g] = [pieces[0]] + [move(f"g{g}{k}", by_offset(k), pieces[k]) for k in range(1, 8)]

    def step_match(g):
        offsets[g] = [(k, k + 1) for k in (0, 2, 4, 6)]
        pieces = mark(match(*blocks[g], 4, after()))
        blocks[g] = [pieces[0]] + [
            move(f"g{g}{k}", by_offset(2 * k), pieces[k]) for k in range(1, 4)
        ]

    def step_project(g):
        nonlocal moments
        update[g], *moments, sent, state[g] = mark(
            project(blocks[g], offsets[g], X_HIGH[g], groups[g], rows, across, first, second, moments, after())
        )
        send[g] = move(f"c{g}", core, sent)
        update[g] = update[g][None]
        if X_FIRST[g]:
            spread[g] = move(f"ux{g}", along_x, update[g])
        else:
            spread[g] = move(f"un{g}", z_near, update[g])

    def step_core(g):
        low, got = state[g], send[g]
        if not Y_SPLIT[g]:
            sent, state[g] = mark(
                sums([low, got], [([(0, 2), (1, 2)], 2), ([(0, 0), (1, 0)], 2)], after())
            )
            send[g] = (move(f"y{g}", axes(g)[0], sent),)
            return
        third, other, state[g] = mark(
            sums(
                [low, got],
                [([(0, 3), (1, 3)], 1), ([(0, 2), (1, 2)], 1), ([(0, 0), (1, 0)], 2)],
                after(),
            )
        )
        send[g] = move(f"y{g}", axes(g)[0], third), move(f"w{g}", axes(g)[0], other)

    def step_y(g):
        if not Y_SPLIT[g]:
            one, state[g] = mark(
                sums([state[g], *send[g]], [([(0, 1), (1, 1)], 1), ([(0, 0), (1, 0)], 1)], after())
            )
            send[g] = (move(f"x{g}", axes(g)[1], one),)
            return
        third, other = send[g]
        (one,) = mark(sums([state[g], third], [([(0, 1), (1, 0)], 1)], after()))
        send[g] = other, move(f"x{g}", axes(g)[1], one)

    def step_x(g):
        adds = [state[g], *send[g]]
        if Z_SPLIT[g]:
            state[g] = mark(halve(adds, after()))
            send[g] = move(f"f{g}", z_far, state[g][0]), move(f"p{g}", z_near, state[g][1])
            return
        (state[g],) = mark(sums(adds, [([(i, 0) for i in range(len(adds))], 1)], after()))
        send[g] = move(f"f{g}", z_far, state[g])

    def step_far(g):
        if Z_SPLIT[g]:
            inputs = [state[g][0], send[g][0], state[g][1], send[g][1]]
            state[g] = mark(sums(inputs, [([(0, 0), (1, 0)], 1), ([(2, 0), (3, 0)], 1)], after()))
            send[g] = move(f"n{g}", z_near, state[g][0]), move(f"q{g}", z_far, state[g][1])
            return
        (state[g],) = mark(sums([state[g], send[g]], [([(0, 0), (1, 0)], 1)], after()))
        send[g] = move(f"n{g}", z_near, state[g])

    def step_near(g):
        if Z_SPLIT[g]:
            (a,) = mark(whole(state[g], send[g], after()))
        else:
            (a,) = mark(sums([state[g], send[g]], [([(0, 0), (1, 0)], 1)], after()))
        first_way, second_way = axes(g)
        b = move(f"X{g}", second_way, a)
        low = [a, b, move(f"Y{g}", first_way, a), move(f"W{g}", first_way, b)]
        state[g] = low + [move(f"C{g}{i}", core, piece) for i, piece in enumerate(low)]

    def step_pair(g):
        update[g] = mark(join(update[g], spread[g], after()))[0]
        spread[g] = move(f"un{g}", z_near, update[g])

    def step_join(g):
        (both,) = mark(join(update[g], spread[g], after()))
        if U_FAR[g]:
            spread[g] = both, move(f"um{g}", z_far, both)
            return
        middle = move(f"um{g}", z_middle, both)
        spread[g] = both, middle, move(f"uo{g}", z_outer, middle)

    def step_collect(g):
        gather = join if U_FAR[g] else collect
        (mine,) = mark(gather(*spread[g], after()))
        spread[g] = mine, move(f"ux{g}", along_x, mine)

    def step_weight(mat):
        nonlocal new_weight
        g = [mat in group for group in groups].index(True)
        place = groups[g].index(mat)
        *new_weight, token = weight_step(
            weights, across, spread[g], (X_FIRST[g], U_FAR[g]), place, mat, new_weight, after()
        )
        mark([token])

    def step_basis(g):
        nonlocal bases
        *bases, token = basis(state[g], X_HIGH[g], groups[g], mats, factor, bases, after())
        mark([token])

    steps = {
        "cut": step_cut,
        "match": step_match,
        "project": step_project,
        "core": step_core,
        "y": step_y,
        "x": step_x,
        "far": step_far,
        "near": step_near,
        "pair": step_pair,
        "join": step_join,
        "collect": step_collect,
        "weight": step_weight,
        "basis": step_basis,
    }
    for entry in PLAN:
        name, which = entry.split(":")
        if name == "wait":
            pending.append(moved[which])
        else:
            steps[name](int(which))
    back = lambda x: jnp.swapaxes(x, 1, 2)[:, :, None, :]
    return (new_weight[0], back(moments[0]), back(moments[1]), jnp.swapaxes(bases[0], 0, 1))


def newton_steps(iterate, inner):
    return 1.5 * iterate - 0.5 * jnp.einsum(
        "dmr,mrs->dms", iterate, inner, precision=HIGHEST, preferred_element_type=jnp.float32
    )


def column_inner(iterate):
    return jnp.einsum(
        "dmr,dms->mrs", iterate, iterate, precision=HIGHEST, preferred_element_type=jnp.float32
    )


def per_device_any(gradients, weights, projectors, first_moment, second_moment):
    factor = math.sqrt(projectors.shape[0])
    regrouped = lax.all_to_all(gradients, "shard", split_axis=2, concat_axis=1, tiled=True)
    mats, width, cols = regrouped.shape
    rank = projectors.shape[2]
    projected = jnp.einsum(
        "dmr,mdc->mrc", projectors, regrouped, preferred_element_type=jnp.float32
    )
    first_new = 0.9 * first_moment.reshape(mats, rank, cols) + 0.1 * projected
    second_new = 0.999 * second_moment.reshape(mats, rank, cols) + 0.001 * projected * projected
    update = (first_new / CORR_FIRST / (jnp.sqrt(second_new / CORR_SECOND) + 1e-08)).astype(
        jnp.bfloat16
    )
    delta = jnp.einsum("dmr,mrc->mdc", projectors, update, preferred_element_type=jnp.float32)
    returned = lax.all_to_all(delta, "shard", split_axis=1, concat_axis=2, tiled=True)
    new_weight = weights - 0.2 * returned
    back = jnp.einsum(
        "mdc,dmr->mcr", regrouped, projectors, preferred_element_type=jnp.float32
    ).astype(jnp.bfloat16)
    partial_sum = jnp.einsum("mdc,mcr->dmr", regrouped, back, preferred_element_type=jnp.float32)
    refresh = lax.psum(partial_sum, ("shard", "tensor"))
    norms = jnp.sqrt(jnp.sum(refresh * refresh, axis=(0, 2)) + 1e-06)
    iterate = refresh / norms[None, :, None]
    for sweep in range(NS_STEPS):
        iterate = newton_steps(iterate, column_inner(iterate))
    new_basis = (iterate * factor).astype(jnp.bfloat16)
    shape_four = first_moment.shape
    return (new_weight, first_new.reshape(shape_four), second_new.reshape(shape_four), new_basis)


def solution(mesh):
    in_specs = (
        P(None, "shard", "tensor"),
        P(None, "shard", "tensor"),
        P(),
        P(None, None, "tensor", "shard"),
        P(None, None, "tensor", "shard"),
    )
    out_specs = (
        P(None, "shard", "tensor"),
        P(None, None, "tensor", "shard"),
        P(None, None, "tensor", "shard"),
        P(),
    )
    own = (mesh.shape["shard"], mesh.shape["tensor"]) == (8, 4)
    body = per_device if own else per_device_any
    return jax.shard_map(body, mesh=mesh, in_specs=in_specs, out_specs=out_specs, check_vma=False)
```

time: 374 us -> 139 us (0.37); the launches traced: 369 us -> 138 us
  waiting for transfers between devices: 203 us -> 52 us
  starting transfers between devices: 5.24 us -> 59.5 us
  matrix products: 45.1 us -> 0 us
  local copies, waits for them, and re-layouts: 46.4 us -> 1.41 us
  blocking collectives: 42.6 us -> 0 us
  Pallas kernels: 0 us -> 24.6 us
  between operations: 14.7 us -> 0.86 us
  other arithmetic: 11.8 us -> 0 us
    psum x1 -> x0, waiting for transfers between devices: 203 us -> none  [per_device(): refresh = lax.psum(partial_sum, ('shard', 'tensor'))]
    ppermute x0 -> x46, starting transfers between devices: none -> 59.5 us  [the longest x42 55.6 us: swap(): return lax.ppermute(x, axis, [(i, i ^ bit) for i in range(size)])]
    ppermute x0 -> x46, waiting for transfers between devices: none -> 52 us  [the longest x42 46.2 us: swap(): return lax.ppermute(x, axis, [(i, i ^ bit) for i in range(size)])]
    dot_general x13 -> x0, matrix products: 45.1 us -> none  [the longest x5 19.4 us: newton_steps(): jnp.einsum('dmr,mrs->dms', iterate, inner, precision=lax.Precision.HIGHES...]
    all_to_all x1 -> x0, blocking collectives: 42.6 us -> none  [per_device(): lax.all_to_all(gradients, 'shard', split_axis=2, concat_axis=1, tiled=True)]
    unnamed x22 -> x10, local copies, waits for them, and re-layouts: 26.1 us -> 1.41 us
    pallas_call x0 -> x23, Pallas kernels: none -> 24.6 us  [call(): pl.pallas_call(body, grid=(grid,), in_specs=in_specs + [pl.BlockSpec(memo...]
    mul x2 -> x0, local copies, waits for them, and re-layouts: 9.21 us -> none  [per_device(): new_weight = weights - 0.2 * returned]
  transfers between devices with their start and end apart: 2 -> 46, of which waited for: 1 -> 16; matrix products, arithmetic and copies ran while one was open for 15% -> 0% of each run, Pallas kernels for 0% -> 15%
where the time goes in v3:
time: 139 us; the launch traced here: 138 us
  starting transfers between devices  59.5 us (43%)
  waiting for transfers between devices  52 us (37%)
  Pallas kernels  24.6 us (18%)
  local copies, waits for them, and re-layouts  1.41 us (1%)
    ppermute x42, starting transfers between devices, swap(): return lax.ppermute(x, axis, [(i, i ^ bit) for i in range(size)])  55.6 us
    ppermute x42, waiting for transfers between devices, swap(): return lax.ppermute(x, axis, [(i, i ^ bit) for i in range(size)])  46.2 us
    pallas_call x23, Pallas kernels, call(): pl.pallas_call(body, grid=(grid,), in_specs=in_specs + [pl.BlockSpec(memo...  24.6 us
    ppermute x2, waiting for transfers between devices, z_outer(): return lax.ppermute(x, 'shard', [(2, 0), (3, 1), (4, 6), (5, 7)])  5.84 us
  transfers between devices with their start and end apart: 46, of which 16 were waited for; matrix products, arithmetic and copies ran while one was open for 0% of the time, Pallas kernels for 15%

profile of v3, /device:TPU:0, one launch (start us, length us, event | category | flops | bytes accessed | tf_op | source)
XLA Modules:
  0.0 138.4 jit_solution(2636403035630465268)
XLA Ops:
  0.6 1.4 %copy-done.2 = bf16[3,144,1728]{2,1,0:T(8,128)(2,1)S(1)} copy-done((bf16[3,144,1728]{2,1,0:T(8,128)(2,1)S(1)}, bf16[3,144,1728]{2,1,0:T(8,128)(2,1)}, u32[]{:S(2)}) %copy-start.2) | copy-done | bytes 1493016
  2.0 2.0 %cut_columns.2 = (bf16[2,256,128]{2,1,0:T(8,128)(2,1)S(1)}, bf16[2,256,128]{2,1,0:T(8,128)(2,1)S(1)}, bf16[2,256,128]{2,1,0:T(8,128)(2,1)S(1)}, bf16[2,256,128]{...) custom-call(bf16[3,144,1728]{2,1,0:T(8,128)(2,1)S(1)} %copy-done.2), custom_call_target="tpu_custom_call" | custom-call | flops 10000000000 | bytes 30000000 | tf_op jit(solution)/shard_map/cut_columns/pallas_call | solution.py:96
  4.1 4.0 %collective-permute-start.9 = (bf16[2,256,128]{2,1,0:T(8,128)(2,1)S(1)}, bf16[2,256,128]{2,1,0:T(8,128)(2,1)S(1)}, u32[]{:S(2)}, u32[]{:S(2)}) collective-permute-start(bf16[2,256,128]{2,1,0:T(8,128)(2,1)S(1)} %get-tuple-element.58), channel_id=1, source_target_pairs={{0,12},{4,8},{8,4},{12,0},{16,28},{20,24},{24,20},{28,16},{1,13},{... | collective-permute-start | bytes 393224 | tf_op jit(solution)/shard_map/ppermute | solution.py:489
  8.1 2.6 %collective-permute-start.10 = (bf16[2,256,128]{2,1,0:T(8,128)(2,1)S(1)}, bf16[2,256,128]{2,1,0:T(8,128)(2,1)S(1)}, u32[]{:S(2)}, u32[]{:S(2)}) collective-permute-start(bf16[2,256,128]{2,1,0:T(8,128)(2,1)S(1)} %get-tuple-element.59), channel_id=1, source_target_pairs={{0,16},{4,20},{8,24},{12,28},{16,0},{20,4},{24,8},{28,12},{1,17},{... | collective-permute-start | bytes 393224 | tf_op jit(solution)/shard_map/ppermute | solution.py:489
  10.7 1.0 cut_columns.3
  12.8 1.3 collective-permute-start.11
  14.0 2.2 %collective-permute-done.refs_1_ = bf16[1,256,128]{2,1,0:T(8,128)(2,1)S(1)} collective-permute-done((bf16[1,256,128]{2,1,0:T(8,128)(2,1)S(1)}, bf16[1,256,128]{2,1,0:T(8,128)(2,1)S(1)}, u32[]{:S(2)}, u32[]{:S(2)}) %collective-permute-start) | collective-permute-done | bytes 65568 | tf_op jit(solution)/shard_map/ppermute | solution.py:489
  16.2 1.4 %collective-permute-start.12 = (bf16[2,256,128]{2,1,0:T(8,128)(2,1)S(1)}, bf16[2,256,128]{2,1,0:T(8,128)(2,1)S(1)}, u32[]{:S(2)}, u32[]{:S(2)}) collective-permute-start(bf16[2,256,128]{2,1,0:T(8,128)(2,1)S(1)} %get-tuple-element.61), channel_id=1, source_target_pairs={{0,24},{4,28},{8,16},{12,20},{16,8},{20,12},{24,0},{28,4},{1,25},{... | collective-permute-start | bytes 393224 | tf_op jit(solution)/shard_map/ppermute | solution.py:489
  17.7 2.2 %collective-permute-start.13 = (bf16[2,256,128]{2,1,0:T(8,128)(2,1)S(1)}, bf16[2,256,128]{2,1,0:T(8,128)(2,1)S(1)}, u32[]{:S(2)}, u32[]{:S(2)}) collective-permute-start(bf16[2,256,128]{2,1,0:T(8,128)(2,1)S(1)} %get-tuple-element.62), channel_id=1, source_target_pairs={{0,28},{4,24},{8,20},{12,16},{16,12},{20,8},{24,4},{28,0},{1,29},{... | collective-permute-start | bytes 393224 | tf_op jit(solution)/shard_map/ppermute | solution.py:489
  19.9 1.7 %collective-permute-start.7 = (bf16[2,256,128]{2,1,0:T(8,128)(2,1)S(1)}, bf16[2,256,128]{2,1,0:T(8,128)(2,1)S(1)}, u32[]{:S(2)}, u32[]{:S(2)}) collective-permute-start(bf16[2,256,128]{2,1,0:T(8,128)(2,1)S(1)} %get-tuple-element.56), channel_id=1, source_target_pairs={{0,4},{4,0},{8,12},{12,8},{16,20},{20,16},{24,28},{28,24},{1,5},{5... | collective-permute-start | bytes 393224 | tf_op jit(solution)/shard_map/ppermute | solution.py:489
  21.5 4.2 %collective-permute-start.8 = (bf16[2,256,128]{2,1,0:T(8,128)(2,1)S(1)}, bf16[2,256,128]{2,1,0:T(8,128)(2,1)S(1)}, u32[]{:S(2)}, u32[]{:S(2)}) collective-permute-start(bf16[2,256,128]{2,1,0:T(8,128)(2,1)S(1)} %get-tuple-element.57), channel_id=1, source_target_pairs={{0,8},{4,12},{8,0},{12,4},{16,24},{20,28},{24,16},{28,20},{1,9},{5... | collective-permute-start | bytes 393224 | tf_op jit(solution)/shard_map/ppermute | solution.py:489
  25.8 3.2 %collective-permute-done.11.refs_5_ = bf16[2,256,128]{2,1,0:T(8,128)(2,1)S(1)} collective-permute-done((bf16[2,256,128]{2,1,0:T(8,128)(2,1)S(1)}, bf16[2,256,128]{2,1,0:T(8,128)(2,1)S(1)}, u32[]{:S(2)}, u32[]{:S(2)}) %collective-permute-start.11) | collective-permute-done | bytes 131104 | tf_op jit(solution)/shard_map/ppermute | solution.py:489
  28.9 4.7 %collective-permute-start.3 = (bf16[1,256,128]{2,1,0:T(8,128)(2,1)S(1)}, bf16[1,256,128]{2,1,0:T(8,128)(2,1)S(1)}, u32[]{:S(2)}, u32[]{:S(2)}) collective-permute-start(bf16[1,256,128]{2,1,0:T(8,128)(2,1)S(1)} %get-tuple-element.52), channel_id=1, source_target_pairs={{0,16},{4,20},{8,24},{12,28},{16,0},{20,4},{24,8},{28,12},{1,17},{... | collective-permute-start | bytes 196616 | tf_op jit(solution)/shard_map/ppermute | solution.py:489
  33.7 4.4 %collective-permute-start.4 = (bf16[1,256,128]{2,1,0:T(8,128)(2,1)S(1)}, bf16[1,256,128]{2,1,0:T(8,128)(2,1)S(1)}, u32[]{:S(2)}, u32[]{:S(2)}) collective-permute-start(bf16[1,256,128]{2,1,0:T(8,128)(2,1)S(1)} %get-tuple-element.53), channel_id=1, source_target_pairs={{0,20},{4,16},{8,28},{12,24},{16,4},{20,0},{24,12},{28,8},{1,21},{... | collective-permute-start | bytes 196616 | tf_op jit(solution)/shard_map/ppermute | solution.py:489
  38.1 1.0 collective-permute-start.5
  39.1 2.3 %collective-permute-start.6 = (bf16[1,256,128]{2,1,0:T(8,128)(2,1)S(1)}, bf16[1,256,128]{2,1,0:T(8,128)(2,1)S(1)}, u32[]{:S(2)}, u32[]{:S(2)}) collective-permute-start(bf16[1,256,128]{2,1,0:T(8,128)(2,1)S(1)} %get-tuple-element.55), channel_id=1, source_target_pairs={{0,28},{4,24},{8,20},{12,16},{16,12},{20,8},{24,4},{28,0},{1,29},{... | collective-permute-start | bytes 196616 | tf_op jit(solution)/shard_map/ppermute | solution.py:489
  41.4 3.1 %project.2 = (bf16[2,216,256]{2,1,0:T(8,128)(2,1)S(1)}, f32[3,216,256]{2,1,0:T(8,128)}, f32[3,216,256]{2,1,0:T(8,128)}, f32[4,2,144,256]{3,2,1,0:T(8,128)S(1)}, f32[4,2,144,256]{3,2,1,0:T(8,128)S(1)}) custom-call(bf16[2,256,128]{2,1,0:T(8,128)(2,1)S(1)} %get-tuple-element.47.refs_1_.refs_0_, bf16[2,256,128]{2,1,0:T(8,128)(2,1)S(1)} %collective-permute-done.7.refs_1_, ...), custom_call_target="tpu_custom_call" | custom-call | flops 20000000000 | bytes 60000000 | tf_op jit(solution)/shard_map/project/pallas_call | solution.py:96
  44.5 1.6 %collective-permute-done.6.refs_7_ = bf16[1,256,128]{2,1,0:T(8,128)(2,1)S(1)} collective-permute-done((bf16[1,256,128]{2,1,0:T(8,128)(2,1)S(1)}, bf16[1,256,128]{2,1,0:T(8,128)(2,1)S(1)}, u32[]{:S(2)}, u32[]{:S(2)}) %collective-permute-start.6) | collective-permute-done | bytes 65568 | tf_op jit(solution)/shard_map/ppermute | solution.py:489
  46.1 1.8 %project.3 = (bf16[1,216,256]{2,1,0:T(8,128)(2,1)S(1)}, f32[3,216,256]{2,1,0:T(8,128)}, f32[3,216,256]{2,1,0:T(8,128)}, f32[4,1,144,256]{3,2,1,0:T(8,128)S(1)}, f32[4,1,144,256]{3,2,1,0:T(8,128)S(1)}) custom-call(bf16[1,256,128]{2,1,0:T(8,128)(2,1)S(1)} %get-tuple-element.48.refs_11_.refs_0_, ...), custom_call_target="tpu_custom_call", output_to_operand_aliasing={{1}: (11, {}), {2}: (12, {})} | custom-call | flops 10000000000 | bytes 30000000 | tf_op jit(solution)/shard_map/project/pallas_call | solution.py:96
  48.1 1.6 %collective-permute-start.16 = (f32[2,2,144,256]{3,2,1,0:T(8,128)S(1)}, f32[2,2,144,256]{3,2,1,0:T(8,128)S(1)}, u32[]{:S(2)}, u32[]{:S(2)}) collective-permute-start(f32[2,2,144,256]{3,2,1,0:T(8,128)S(1)} %get-tuple-element.70.refs_2_), channel_id=1, source_target_pairs={{0,2},{1,3},{2,0},{3,1},{4,6},{5,7},{6,4},{7,5},{8,10},{9,11},{10,... | collective-permute-start | bytes 1769480 | tf_op jit(solution)/shard_map/ppermute | solution.py:489
  50.0 5.8 %collective-permute-done.17.refs_1_.refs_4_ = bf16[1,2,216,256]{3,2,1,0:T(8,128)(2,1)S(1)} collective-permute-done((bf16[1,2,216,256]{3,2,1,0:T(8,128)(2,1)S(1)}, bf16[1,2,216,256]{3,2,1,0:T(8,128)(2,1)S(1)}, u32[]{:S(2)}, u32[]{:S(2)}) %collective-permute-start.17) | collective-permute-done | bytes 221216 | tf_op jit(solution)/shard_map/ppermute | solution.py:489
  56.5 1.6 %collective-permute-start.20 = (f32[2,1,144,256]{3,2,1,0:T(8,128)S(1)}, f32[2,1,144,256]{3,2,1,0:T(8,128)S(1)}, u32[]{:S(2)}, u32[]{:S(2)}) collective-permute-start(f32[2,1,144,256]{3,2,1,0:T(8,128)S(1)} %get-tuple-element.73.refs_2_), channel_id=1, source_target_pairs={{0,2},{1,3},{2,0},{3,1},{4,6},{5,7},{6,4},{7,5},{8,10},{9,11},{10,... | collective-permute-start | bytes 884744 | tf_op jit(solution)/shard_map/ppermute | solution.py:489
  58.1 6.2 %collective-permute-done.16.refs_1_ = f32[2,2,144,256]{3,2,1,0:T(8,128)S(1)} collective-permute-done((f32[2,2,144,256]{3,2,1,0:T(8,128)S(1)}, f32[2,2,144,256]{3,2,1,0:T(8,128)S(1)}, u32[]{:S(2)}, u32[]{:S(2)}) %collective-permute-start.16) | collective-permute-done | bytes 589856 | tf_op jit(solution)/shard_map/ppermute | solution.py:489
  64.3 1.5 %collective-permute-start.19 = (f32[1,2,144,256]{3,2,1,0:T(8,128)S(1)}, f32[1,2,144,256]{3,2,1,0:T(8,128)S(1)}, u32[]{:S(2)}, u32[]{:S(2)}) collective-permute-start(f32[1,2,144,256]{3,2,1,0:T(8,128)S(1)} %get-tuple-element.75.refs_2_), channel_id=1, source_target_pairs={{0,4},{4,0},{8,12},{12,8},{16,20},{20,16},{24,28},{28,24},{1,5},{5... | collective-permute-start | bytes 884744 | tf_op jit(solution)/shard_map/ppermute | solution.py:489
  65.8 1.6 %collective-permute-start.14 = (bf16[1,1,216,256]{3,2,1,0:T(8,128)(2,1)S(1)}, bf16[1,1,216,256]{3,2,1,0:T(8,128)(2,1)S(1)}, u32[]{:S(2)}, u32[]{:S(2)}) collective-permute-start(bf16[1,1,216,256]{3,2,1,0:T(8,128)(2,1)S(1)} %bitcast.31), channel_id=1, source_target_pairs={{0,8},{4,12},{8,0},{12,4},{16,24},{20,28},{24,16},{28,20},{1,9},{5... | collective-permute-start | bytes 331784 | tf_op jit(solution)/shard_map/ppermute | solution.py:489
  67.4 1.3 collective-permute-start.24
  68.7 1.5 %collective-permute-done.20.refs_1_ = f32[2,1,144,256]{3,2,1,0:T(8,128)S(1)} collective-permute-done((f32[2,1,144,256]{3,2,1,0:T(8,128)S(1)}, f32[2,1,144,256]{3,2,1,0:T(8,128)S(1)}, u32[]{:S(2)}, u32[]{:S(2)}) %collective-permute-start.20) | collective-permute-done | bytes 294944 | tf_op jit(solution)/shard_map/ppermute | solution.py:489
  70.2 1.1 collective-permute-start.22
  71.3 1.3 collective-permute-done.19.refs_1_
  72.7 2.8 %collective-permute-start.21 = (f32[1,2,144,256]{3,2,1,0:T(8,128)S(1)}, f32[1,2,144,256]{3,2,1,0:T(8,128)S(1)}, u32[]{:S(2)}, u32[]{:S(2)}) collective-permute-start(f32[1,2,144,256]{3,2,1,0:T(8,128)S(1)} %sums.14.refs_3_.refs_0_), channel_id=1, source_target_pairs={{0,16},{4,20},{8,24},{12,28},{16,0},{20,4},{24,8},{28,12},{1,17},{... | collective-permute-start | bytes 884744 | tf_op jit(solution)/shard_map/ppermute | solution.py:489
  75.5 5.8 %collective-permute-done.24.refs_2_ = bf16[2,2,216,256]{3,2,1,0:T(8,128)(2,1)S(1)} collective-permute-done((bf16[2,2,216,256]{3,2,1,0:T(8,128)(2,1)S(1)}, bf16[2,2,216,256]{3,2,1,0:T(8,128)(2,1)S(1)}, u32[]{:S(2)}, u32[]{:S(2)}) %collective-permute-start.24) | collective-permute-done | bytes 442400 | tf_op jit(solution)/shard_map/ppermute | solution.py:517
  81.7 1.1 collective-permute-start.28
  82.7 8.0 %collective-permute-done.21.refs_1_ = f32[1,2,144,256]{3,2,1,0:T(8,128)S(1)} collective-permute-done((f32[1,2,144,256]{3,2,1,0:T(8,128)S(1)}, f32[1,2,144,256]{3,2,1,0:T(8,128)S(1)}, u32[]{:S(2)}, u32[]{:S(2)}) %collective-permute-start.21) | collective-permute-done | bytes 294944 | tf_op jit(solution)/shard_map/ppermute | solution.py:489
  91.6 2.1 %collective-permute-done.28.refs_1_ = f32[1,1,144,256]{3,2,1,0:T(8,128)S(1)} collective-permute-done((f32[1,1,144,256]{3,2,1,0:T(8,128)S(1)}, f32[1,1,144,256]{3,2,1,0:T(8,128)S(1)}, u32[]{:S(2)}, u32[]{:S(2)}) %collective-permute-start.28) | collective-permute-done | bytes 147488 | tf_op jit(solution)/shard_map/ppermute | solution.py:489
  93.7 3.1 %collective-permute-start.29 = (f32[1,1,144,256]{3,2,1,0:T(8,128)S(1)}, f32[1,1,144,256]{3,2,1,0:T(8,128)S(1)}, u32[]{:S(2)}, u32[]{:S(2)}) collective-permute-start(f32[1,1,144,256]{3,2,1,0:T(8,128)S(1)} %sums.17.refs_2_.refs_0_), channel_id=1, source_target_pairs={{0,8},{4,12},{8,0},{12,4},{16,24},{20,28},{24,16},{28,20},{1,9},{5... | collective-permute-start | bytes 442376 | tf_op jit(solution)/shard_map/ppermute | solution.py:489
  96.8 4.0 %collective-permute-done.30.refs_1_ = f32[1,2,144,256]{3,2,1,0:T(8,128)S(1)} collective-permute-done((f32[1,2,144,256]{3,2,1,0:T(8,128)S(1)}, f32[1,2,144,256]{3,2,1,0:T(8,128)S(1)}, u32[]{:S(2)}, u32[]{:S(2)}) %collective-permute-start.30) | collective-permute-done | bytes 294944 | tf_op jit(solution)/shard_map/ppermute | solution.py:489
  100.8 1.5 %collective-permute-start.39 = (f32[1,2,144,256]{3,2,1,0:T(8,128)S(1)}, f32[1,2,144,256]{3,2,1,0:T(8,128)S(1)}, u32[]{:S(2)}, u32[]{:S(2)}) collective-permute-start(f32[1,2,144,256]{3,2,1,0:T(8,128)S(1)} %sums.18.refs_2_.refs_0_), channel_id=1, source_target_pairs={{0,4},{4,0},{8,12},{12,8},{16,20},{20,16},{24,28},{28,24},{1,5},{5... | collective-permute-start | bytes 884744 | tf_op jit(solution)/shard_map/ppermute | solution.py:489
  102.3 1.3 collective-permute-start.26
  103.6 1.6 %collective-permute-start.40 = (f32[1,2,144,256]{3,2,1,0:T(8,128)S(1)}, f32[1,2,144,256]{3,2,1,0:T(8,128)S(1)}, u32[]{:S(2)}, u32[]{:S(2)}) collective-permute-start(f32[1,2,144,256]{3,2,1,0:T(8,128)S(1)} %sums.18.refs_2_.refs_0_), channel_id=1, source_target_pairs={{0,2},{1,3},{2,0},{3,1},{4,6},{5,7},{6,4},{7,5},{8,10},{9,11},{10,... | collective-permute-start | bytes 884744 | tf_op jit(solution)/shard_map/ppermute | solution.py:489
  105.2 2.9 %collective-permute-done.39.refs_1_ = f32[1,2,144,256]{3,2,1,0:T(8,128)S(1)} collective-permute-done((f32[1,2,144,256]{3,2,1,0:T(8,128)S(1)}, f32[1,2,144,256]{3,2,1,0:T(8,128)S(1)}, u32[]{:S(2)}, u32[]{:S(2)}) %collective-permute-start.39) | collective-permute-done | bytes 294944 | tf_op jit(solution)/shard_map/ppermute | solution.py:489
  109.0 2.1 %collective-permute-start.41 = (f32[1,2,144,256]{3,2,1,0:T(8,128)S(1)}, f32[1,2,144,256]{3,2,1,0:T(8,128)S(1)}, u32[]{:S(2)}, u32[]{:S(2)}) collective-permute-start(f32[1,2,144,256]{3,2,1,0:T(8,128)S(1)} %collective-permute-done.39.refs_1_), channel_id=1, source_target_pairs={{0,2},{1,3},{2,0},{3,1},{4,6},{5,7},{6,4},{7,5},{8,10},{9,11},{10,... | collective-permute-start | bytes 884744 | tf_op jit(solution)/shard_map/ppermute | solution.py:489
  111.1 1.6 %weight_step.3 = (f32[3,144,1728]{2,1,0:T(8,128)}, f32[8,128]{1,0:T(8,128)S(1)}) custom-call(f32[3,144,1728]{2,1,0:T(8,128)S(1)} %copy-done, bf16[3,1152,256]{2,1,0:T(8,128)(2,1)S(1)} %bitcast.22, bf16[4,2,216,256]{3,2,1,0:T(8,128)(2,1)S(1)} %collect.2.refs_2_, bf16[4,2,216,256]{3,2,1,0:T(8,128)(2,1)S(1)} %collective-permute-done.27.refs_3_, ...), custom_call_target="tpu_custom_call" | custom-call | flops 8000000000 | bytes 24000000 | tf_op jit(solution)/shard_map/weight_step/pallas_call | solution.py:96
  113.3 1.5 %collective-permute-start.34 = (f32[1,1,144,256]{3,2,1,0:T(8,128)S(1)}, f32[1,1,144,256]{3,2,1,0:T(8,128)S(1)}, u32[]{:S(2)}, u32[]{:S(2)}) collective-permute-start(f32[1,1,144,256]{3,2,1,0:T(8,128)S(1)} %collective-permute-done.32.refs_1_), channel_id=1, source_target_pairs={{0,2},{1,3},{2,0},{3,1},{4,6},{5,7},{6,4},{7,5},{8,10},{9,11},{10,... | collective-permute-start | bytes 442376 | tf_op jit(solution)/shard_map/ppermute | solution.py:489
  115.0 6.4 %collective-permute-done.33.refs_2_ = f32[1,1,144,256]{3,2,1,0:T(8,128)S(1)} collective-permute-done((f32[1,1,144,256]{3,2,1,0:T(8,128)S(1)}, f32[1,1,144,256]{3,2,1,0:T(8,128)S(1)}, u32[]{:S(2)}, u32[]{:S(2)}) %collective-permute-start.33) | collective-permute-done | bytes 147488 | tf_op jit(solution)/shard_map/ppermute | solution.py:489
  122.0 1.6 %weight_step.4 = (f32[3,144,1728]{2,1,0:T(8,128)}, f32[8,128]{1,0:T(8,128)S(1)}) custom-call(f32[3,144,1728]{2,1,0:T(8,128)S(1)} %copy-done, bf16[3,1152,256]{2,1,0:T(8,128)(2,1)S(1)} %bitcast.23, bf16[4,2,216,256]{3,2,1,0:T(8,128)(2,1)S(1)} %collect.2.refs_2_, ...), custom_call_target="tpu_custom_call", output_to_operand_aliasing={{0}: (4, {})} | custom-call | flops 8000000000 | bytes 24000000 | tf_op jit(solution)/shard_map/weight_step/pallas_call | solution.py:96
  125.5 6.2 %newton_schulz.2 = (bf16[3,1152,256]{2,1,0:T(8,128)(2,1)}, f32[8,128]{1,0:T(8,128)S(1)}) custom-call(f32[1,2,144,256]{3,2,1,0:T(8,128)S(1)} %sums.18.refs_2_.refs_0_, f32[1,2,144,256]{3,2,1,0:T(8,128)S(1)} %collective-permute-done.39.refs_1_, f32[1,2,144,256]{3,2,1,0:T(8,128)S(1)} %collective-permute-done.40.refs_2_, ...), custom_call_target="tpu_custom_call" | custom-call | flops 80000000000 | bytes 240000000 | tf_op jit(solution)/shard_map/newton_schulz/pallas_call | solution.py:96
  131.7 4.8 %newton_schulz.3 = (bf16[3,1152,256]{2,1,0:T(8,128)(2,1)}, f32[8,128]{1,0:T(8,128)S(1)}) custom-call(f32[1,1,144,256]{3,2,1,0:T(8,128)S(1)} %sums.19.refs_4_.refs_0_, f32[1,1,144,256]{3,2,1,0:T(8,128)S(1)} %collective-permute-done.32.refs_1_, f32[1,1,144,256]{3,2,1,0:T(8,128)S(1)} %collective-permute-done.33.refs_2_, ...), custom_call_target="tpu_custom_call", output_to_operand_aliasing={{0}: (8, {})} | custom-call | flops 40000000000 | bytes 120000000 | tf_op jit(solution)/shard_map/newton_schulz/pallas_call | solution.py:96
  136.8 1.6 %weight_step.5 = (f32[3,144,1728]{2,1,0:T(8,128)}, f32[8,128]{1,0:T(8,128)}) custom-call(f32[3,144,1728]{2,1,0:T(8,128)S(1)} %copy-done, bf16[3,1152,256]{2,1,0:T(8,128)(2,1)S(1)} %bitcast.24, bf16[4,1,216,256]{3,2,1,0:T(8,128)(2,1)S(1)} %collect.3.refs_5_.refs_2_, ...), custom_call_target="tpu_custom_call", output_to_operand_aliasing={{0}: (4, {})} | custom-call | flops 8000000000 | bytes 24000000 | tf_op jit(solution)/shard_map/weight_step/pallas_call | solution.py:96
  (77 shorter events, 7.9 us)
Async XLA Ops:
  4.1 15.8 %collective-permute-start.9 = (bf16[2,256,128]{2,1,0:T(8,128)(2,1)S(1)}, bf16[2,256,128]{2,1,0:T(8,128)(2,1)S(1)}, u32[]{:S(2)}, u32[]{:S(2)}) collective-permute-start(bf16[2,256,128]{2,1,0:T(8,128)(2,1)S(1)} %get-tuple-element.58), channel_id=1, source_target_pairs={{0,12},{4,8},{8,4},{12,0},{16,28},{20,24},{24,20},{28,16},{1,13},{... | collective-permute-start | bytes 393224 | tf_op jit(solution)/shard_map/ppermute | solution.py:489
  8.1 13.4 %collective-permute-start.10 = (bf16[2,256,128]{2,1,0:T(8,128)(2,1)S(1)}, bf16[2,256,128]{2,1,0:T(8,128)(2,1)S(1)}, u32[]{:S(2)}, u32[]{:S(2)}) collective-permute-start(bf16[2,256,128]{2,1,0:T(8,128)(2,1)S(1)} %get-tuple-element.59), channel_id=1, source_target_pairs={{0,16},{4,20},{8,24},{12,28},{16,0},{20,4},{24,8},{28,12},{1,17},{... | collective-permute-start | bytes 393224 | tf_op jit(solution)/shard_map/ppermute | solution.py:489
  10.7 30.7 %copy-start.3 = (f32[3,256,1,216]{1,3,2,0:T(8,128)S(1)}, f32[3,256,1,216]{1,3,2,0:T(8,128)}, u32[]{:S(2)}) copy-start(f32[3,256,1,216]{1,3,2,0:T(8,128)} %param.8) | copy-start | bytes 1990660
  10.7 30.7 %copy-start.4 = (f32[3,256,1,216]{1,3,2,0:T(8,128)S(1)}, f32[3,256,1,216]{1,3,2,0:T(8,128)}, u32[]{:S(2)}) copy-start(f32[3,256,1,216]{1,3,2,0:T(8,128)} %param.9) | copy-start | bytes 1990660
  11.7 4.5 %collective-permute-start = (bf16[1,256,128]{2,1,0:T(8,128)(2,1)S(1)}, bf16[1,256,128]{2,1,0:T(8,128)(2,1)S(1)}, u32[]{:S(2)}, u32[]{:S(2)}) collective-permute-start(bf16[1,256,128]{2,1,0:T(8,128)(2,1)S(1)} %get-tuple-element.49), channel_id=1, source_target_pairs={{0,4},{4,0},{8,12},{12,8},{16,20},{20,16},{24,28},{28,24},{1,5},{5... | collective-permute-start | bytes 196616 | tf_op jit(solution)/shard_map/ppermute | solution.py:489
  12.3 5.3 %collective-permute-start.1 = (bf16[1,256,128]{2,1,0:T(8,128)(2,1)S(1)}, bf16[1,256,128]{2,1,0:T(8,128)(2,1)S(1)}, u32[]{:S(2)}, u32[]{:S(2)}) collective-permute-start(bf16[1,256,128]{2,1,0:T(8,128)(2,1)S(1)} %get-tuple-element.50), channel_id=1, source_target_pairs={{0,8},{4,12},{8,0},{12,4},{16,24},{20,28},{24,16},{28,20},{1,9},{5... | collective-permute-start | bytes 196616 | tf_op jit(solution)/shard_map/ppermute | solution.py:489
  12.8 16.2 %collective-permute-start.11 = (bf16[2,256,128]{2,1,0:T(8,128)(2,1)S(1)}, bf16[2,256,128]{2,1,0:T(8,128)(2,1)S(1)}, u32[]{:S(2)}, u32[]{:S(2)}) collective-permute-start(bf16[2,256,128]{2,1,0:T(8,128)(2,1)S(1)} %get-tuple-element.60), channel_id=1, source_target_pairs={{0,20},{4,16},{8,28},{12,24},{16,4},{20,0},{24,12},{28,8},{1,21},{... | collective-permute-start | bytes 393224 | tf_op jit(solution)/shard_map/ppermute | solution.py:489
  16.2 12.7 %collective-permute-start.12 = (bf16[2,256,128]{2,1,0:T(8,128)(2,1)S(1)}, bf16[2,256,128]{2,1,0:T(8,128)(2,1)S(1)}, u32[]{:S(2)}, u32[]{:S(2)}) collective-permute-start(bf16[2,256,128]{2,1,0:T(8,128)(2,1)S(1)} %get-tuple-element.61), channel_id=1, source_target_pairs={{0,24},{4,28},{8,16},{12,20},{16,8},{20,12},{24,0},{28,4},{1,25},{... | collective-permute-start | bytes 393224 | tf_op jit(solution)/shard_map/ppermute | solution.py:489
  17.7 16.0 %collective-permute-start.13 = (bf16[2,256,128]{2,1,0:T(8,128)(2,1)S(1)}, bf16[2,256,128]{2,1,0:T(8,128)(2,1)S(1)}, u32[]{:S(2)}, u32[]{:S(2)}) collective-permute-start(bf16[2,256,128]{2,1,0:T(8,128)(2,1)S(1)} %get-tuple-element.62), channel_id=1, source_target_pairs={{0,28},{4,24},{8,20},{12,16},{16,12},{20,8},{24,4},{28,0},{1,29},{... | collective-permute-start | bytes 393224 | tf_op jit(solution)/shard_map/ppermute | solution.py:489
  19.9 18.2 %collective-permute-start.7 = (bf16[2,256,128]{2,1,0:T(8,128)(2,1)S(1)}, bf16[2,256,128]{2,1,0:T(8,128)(2,1)S(1)}, u32[]{:S(2)}, u32[]{:S(2)}) collective-permute-start(bf16[2,256,128]{2,1,0:T(8,128)(2,1)S(1)} %get-tuple-element.56), channel_id=1, source_target_pairs={{0,4},{4,0},{8,12},{12,8},{16,20},{20,16},{24,28},{28,24},{1,5},{5... | collective-permute-start | bytes 393224 | tf_op jit(solution)/shard_map/ppermute | solution.py:489
  21.5 17.6 %collective-permute-start.8 = (bf16[2,256,128]{2,1,0:T(8,128)(2,1)S(1)}, bf16[2,256,128]{2,1,0:T(8,128)(2,1)S(1)}, u32[]{:S(2)}, u32[]{:S(2)}) collective-permute-start(bf16[2,256,128]{2,1,0:T(8,128)(2,1)S(1)} %get-tuple-element.57), channel_id=1, source_target_pairs={{0,8},{4,12},{8,0},{12,4},{16,24},{20,28},{24,16},{28,20},{1,9},{5... | collective-permute-start | bytes 393224 | tf_op jit(solution)/shard_map/ppermute | solution.py:489
  28.9 15.5 %collective-permute-start.2 = (bf16[1,256,128]{2,1,0:T(8,128)(2,1)S(1)}, bf16[1,256,128]{2,1,0:T(8,128)(2,1)S(1)}, u32[]{:S(2)}, u32[]{:S(2)}) collective-permute-start(bf16[1,256,128]{2,1,0:T(8,128)(2,1)S(1)} %get-tuple-element.51), channel_id=1, source_target_pairs={{0,12},{4,8},{8,4},{12,0},{16,28},{20,24},{24,20},{28,16},{1,13},{... | collective-permute-start | bytes 196616 | tf_op jit(solution)/shard_map/ppermute | solution.py:489
  28.9 15.5 %collective-permute-start.3 = (bf16[1,256,128]{2,1,0:T(8,128)(2,1)S(1)}, bf16[1,256,128]{2,1,0:T(8,128)(2,1)S(1)}, u32[]{:S(2)}, u32[]{:S(2)}) collective-permute-start(bf16[1,256,128]{2,1,0:T(8,128)(2,1)S(1)} %get-tuple-element.52), channel_id=1, source_target_pairs={{0,16},{4,20},{8,24},{12,28},{16,0},{20,4},{24,8},{28,12},{1,17},{... | collective-permute-start | bytes 196616 | tf_op jit(solution)/shard_map/ppermute | solution.py:489
  33.7 10.8 %collective-permute-start.4 = (bf16[1,256,128]{2,1,0:T(8,128)(2,1)S(1)}, bf16[1,256,128]{2,1,0:T(8,128)(2,1)S(1)}, u32[]{:S(2)}, u32[]{:S(2)}) collective-permute-start(bf16[1,256,128]{2,1,0:T(8,128)(2,1)S(1)} %get-tuple-element.53), channel_id=1, source_target_pairs={{0,20},{4,16},{8,28},{12,24},{16,4},{20,0},{24,12},{28,8},{1,21},{... | collective-permute-start | bytes 196616 | tf_op jit(solution)/shard_map/ppermute | solution.py:489
  38.1 6.4 %collective-permute-start.5 = (bf16[1,256,128]{2,1,0:T(8,128)(2,1)S(1)}, bf16[1,256,128]{2,1,0:T(8,128)(2,1)S(1)}, u32[]{:S(2)}, u32[]{:S(2)}) collective-permute-start(bf16[1,256,128]{2,1,0:T(8,128)(2,1)S(1)} %get-tuple-element.54), channel_id=1, source_target_pairs={{0,24},{4,28},{8,16},{12,20},{16,8},{20,12},{24,0},{28,4},{1,25},{... | collective-permute-start | bytes 196616 | tf_op jit(solution)/shard_map/ppermute | solution.py:489
  39.1 7.0 %collective-permute-start.6 = (bf16[1,256,128]{2,1,0:T(8,128)(2,1)S(1)}, bf16[1,256,128]{2,1,0:T(8,128)(2,1)S(1)}, u32[]{:S(2)}, u32[]{:S(2)}) collective-permute-start(bf16[1,256,128]{2,1,0:T(8,128)(2,1)S(1)} %get-tuple-element.55), channel_id=1, source_target_pairs={{0,28},{4,24},{8,20},{12,16},{16,12},{20,8},{24,4},{28,0},{1,29},{... | collective-permute-start | bytes 196616 | tf_op jit(solution)/shard_map/ppermute | solution.py:489
  44.5 3.4 %collective-permute-start.15 = (f32[4,2,144,256]{3,2,1,0:T(8,128)S(1)}, f32[4,2,144,256]{3,2,1,0:T(8,128)S(1)}, u32[]{:S(2)}, u32[]{:S(2)}) collective-permute-start(f32[4,2,144,256]{3,2,1,0:T(8,128)S(1)} %get-tuple-element.68), channel_id=1, source_target_pairs={{0,1},{1,0},{2,3},{3,2},{4,5},{5,4},{6,7},{7,6},{8,9},{9,8},{10,11... | collective-permute-start | bytes 3538952 | tf_op jit(solution)/shard_map/ppermute | solution.py:489
  47.9 2.0 %collective-permute-start.18 = (f32[4,1,144,256]{3,2,1,0:T(8,128)S(1)}, f32[4,1,144,256]{3,2,1,0:T(8,128)S(1)}, u32[]{:S(2)}, u32[]{:S(2)}) collective-permute-start(f32[4,1,144,256]{3,2,1,0:T(8,128)S(1)} %get-tuple-element.72), channel_id=1, source_target_pairs={{0,1},{1,0},{2,3},{3,2},{4,5},{5,4},{6,7},{7,6},{8,9},{9,8},{10,11... | collective-permute-start | bytes 1769480 | tf_op jit(solution)/shard_map/ppermute | solution.py:489
  47.9 7.8 %collective-permute-start.17 = (bf16[1,2,216,256]{3,2,1,0:T(8,128)(2,1)S(1)}, bf16[1,2,216,256]{3,2,1,0:T(8,128)(2,1)S(1)}, u32[]{:S(2)}, u32[]{:S(2)}) collective-permute-start(bf16[1,2,216,256]{3,2,1,0:T(8,128)(2,1)S(1)} %bitcast.29), channel_id=1, source_target_pairs={{0,8},{4,12},{8,0},{12,4},{16,24},{20,28},{24,16},{28,20},{1,9},{5... | collective-permute-start | bytes 663560 | tf_op jit(solution)/shard_map/ppermute | solution.py:489
  48.1 16.2 %collective-permute-start.16 = (f32[2,2,144,256]{3,2,1,0:T(8,128)S(1)}, f32[2,2,144,256]{3,2,1,0:T(8,128)S(1)}, u32[]{:S(2)}, u32[]{:S(2)}) collective-permute-start(f32[2,2,144,256]{3,2,1,0:T(8,128)S(1)} %get-tuple-element.70.refs_2_), channel_id=1, source_target_pairs={{0,2},{1,3},{2,0},{3,1},{4,6},{5,7},{6,4},{7,5},{8,10},{9,11},{10,... | collective-permute-start | bytes 1769480 | tf_op jit(solution)/shard_map/ppermute | solution.py:489
  55.8 11.6 %collective-permute-start.23 = (bf16[2,2,216,256]{3,2,1,0:T(8,128)(2,1)S(1)}, bf16[2,2,216,256]{3,2,1,0:T(8,128)(2,1)S(1)}, u32[]{:S(2)}, u32[]{:S(2)}) collective-permute-start(bf16[2,2,216,256]{3,2,1,0:T(8,128)(2,1)S(1)} %join.2.refs_2_.refs_0_), channel_id=1, source_target_pairs={{8,16},{12,20},{16,8},{20,12},{9,17},{13,21},{17,9},{21,13},{10,18... | collective-permute-start | bytes 1327112 | tf_op jit(solution)/shard_map/ppermute | solution.py:513
  56.5 13.7 %collective-permute-start.20 = (f32[2,1,144,256]{3,2,1,0:T(8,128)S(1)}, f32[2,1,144,256]{3,2,1,0:T(8,128)S(1)}, u32[]{:S(2)}, u32[]{:S(2)}) collective-permute-start(f32[2,1,144,256]{3,2,1,0:T(8,128)S(1)} %get-tuple-element.73.refs_2_), channel_id=1, source_target_pairs={{0,2},{1,3},{2,0},{3,1},{4,6},{5,7},{6,4},{7,5},{8,10},{9,11},{10,... | collective-permute-start | bytes 884744 | tf_op jit(solution)/shard_map/ppermute | solution.py:489
  64.3 8.3 %collective-permute-start.19 = (f32[1,2,144,256]{3,2,1,0:T(8,128)S(1)}, f32[1,2,144,256]{3,2,1,0:T(8,128)S(1)}, u32[]{:S(2)}, u32[]{:S(2)}) collective-permute-start(f32[1,2,144,256]{3,2,1,0:T(8,128)S(1)} %get-tuple-element.75.refs_2_), channel_id=1, source_target_pairs={{0,4},{4,0},{8,12},{12,8},{16,20},{20,16},{24,28},{28,24},{1,5},{5... | collective-permute-start | bytes 884744 | tf_op jit(solution)/shard_map/ppermute | solution.py:489
  65.8 25.1 %collective-permute-start.14 = (bf16[1,1,216,256]{3,2,1,0:T(8,128)(2,1)S(1)}, bf16[1,1,216,256]{3,2,1,0:T(8,128)(2,1)S(1)}, u32[]{:S(2)}, u32[]{:S(2)}) collective-permute-start(bf16[1,1,216,256]{3,2,1,0:T(8,128)(2,1)S(1)} %bitcast.31), channel_id=1, source_target_pairs={{0,8},{4,12},{8,0},{12,4},{16,24},{20,28},{24,16},{28,20},{1,9},{5... | collective-permute-start | bytes 331784 | tf_op jit(solution)/shard_map/ppermute | solution.py:489
  67.4 13.9 %collective-permute-start.24 = (bf16[2,2,216,256]{3,2,1,0:T(8,128)(2,1)S(1)}, bf16[2,2,216,256]{3,2,1,0:T(8,128)(2,1)S(1)}, u32[]{:S(2)}, u32[]{:S(2)}) collective-permute-start(bf16[2,2,216,256]{3,2,1,0:T(8,128)(2,1)S(1)} %collective-permute-done.23.refs_1_), channel_id=1, source_target_pairs={{8,0},{12,4},{16,24},{20,28},{9,1},{13,5},{17,25},{21,29},{10,2},{... | collective-permute-start | bytes 1327112 | tf_op jit(solution)/shard_map/ppermute | solution.py:517
  70.2 11.4 %collective-permute-start.22 = (f32[1,1,144,256]{3,2,1,0:T(8,128)S(1)}, f32[1,1,144,256]{3,2,1,0:T(8,128)S(1)}, u32[]{:S(2)}, u32[]{:S(2)}) collective-permute-start(f32[1,1,144,256]{3,2,1,0:T(8,128)S(1)} %get-tuple-element.77.refs_2_), channel_id=1, source_target_pairs={{0,4},{4,0},{8,12},{12,8},{16,20},{20,16},{24,28},{28,24},{1,5},{5... | collective-permute-start | bytes 442376 | tf_op jit(solution)/shard_map/ppermute | solution.py:489
  72.7 18.1 %collective-permute-start.21 = (f32[1,2,144,256]{3,2,1,0:T(8,128)S(1)}, f32[1,2,144,256]{3,2,1,0:T(8,128)S(1)}, u32[]{:S(2)}, u32[]{:S(2)}) collective-permute-start(f32[1,2,144,256]{3,2,1,0:T(8,128)S(1)} %sums.14.refs_3_.refs_0_), channel_id=1, source_target_pairs={{0,16},{4,20},{8,24},{12,28},{16,0},{20,4},{24,8},{28,12},{1,17},{... | collective-permute-start | bytes 884744 | tf_op jit(solution)/shard_map/ppermute | solution.py:489
  81.4 27.7 %collective-permute-start.27 = (bf16[4,2,216,256]{3,2,1,0:T(8,128)(2,1)S(1)}, bf16[4,2,216,256]{3,2,1,0:T(8,128)(2,1)S(1)}, u32[]{:S(2)}, u32[]{:S(2)}) collective-permute-start(bf16[4,2,216,256]{3,2,1,0:T(8,128)(2,1)S(1)} %collect.2.refs_2_), channel_id=1, source_target_pairs={{0,4},{4,0},{8,12},{12,8},{16,20},{20,16},{24,28},{28,24},{1,5},{5... | collective-permute-start | bytes 2654216 | tf_op jit(solution)/shard_map/ppermute | solution.py:489
  81.7 12.0 %collective-permute-start.28 = (f32[1,1,144,256]{3,2,1,0:T(8,128)S(1)}, f32[1,1,144,256]{3,2,1,0:T(8,128)S(1)}, u32[]{:S(2)}, u32[]{:S(2)}) collective-permute-start(f32[1,1,144,256]{3,2,1,0:T(8,128)S(1)} %sums.15.refs_2_.refs_0_), channel_id=1, source_target_pairs={{0,16},{4,20},{8,24},{12,28},{16,0},{20,4},{24,8},{28,12},{1,17},{... | collective-permute-start | bytes 442376 | tf_op jit(solution)/shard_map/ppermute | solution.py:489
  90.8 10.0 %collective-permute-start.30 = (f32[1,2,144,256]{3,2,1,0:T(8,128)S(1)}, f32[1,2,144,256]{3,2,1,0:T(8,128)S(1)}, u32[]{:S(2)}, u32[]{:S(2)}) collective-permute-start(f32[1,2,144,256]{3,2,1,0:T(8,128)S(1)} %sums.16.refs_2_.refs_0_), channel_id=1, source_target_pairs={{0,8},{4,12},{8,0},{12,4},{16,24},{20,28},{24,16},{28,20},{1,9},{5... | collective-permute-start | bytes 884744 | tf_op jit(solution)/shard_map/ppermute | solution.py:489
  90.9 11.4 %collective-permute-start.25 = (bf16[2,1,216,256]{3,2,1,0:T(8,128)(2,1)S(1)}, bf16[2,1,216,256]{3,2,1,0:T(8,128)(2,1)S(1)}, u32[]{:S(2)}, u32[]{:S(2)}) collective-permute-start(bf16[2,1,216,256]{3,2,1,0:T(8,128)(2,1)S(1)} %join.3.refs_2_.refs_0_), channel_id=1, source_target_pairs={{8,16},{12,20},{16,8},{20,12},{9,17},{13,21},{17,9},{21,13},{10,18... | collective-permute-start | bytes 663560 | tf_op jit(solution)/shard_map/ppermute | solution.py:513
  93.7 11.5 %collective-permute-start.29 = (f32[1,1,144,256]{3,2,1,0:T(8,128)S(1)}, f32[1,1,144,256]{3,2,1,0:T(8,128)S(1)}, u32[]{:S(2)}, u32[]{:S(2)}) collective-permute-start(f32[1,1,144,256]{3,2,1,0:T(8,128)S(1)} %sums.17.refs_2_.refs_0_), channel_id=1, source_target_pairs={{0,8},{4,12},{8,0},{12,4},{16,24},{20,28},{24,16},{28,20},{1,9},{5... | collective-permute-start | bytes 442376 | tf_op jit(solution)/shard_map/ppermute | solution.py:489
  100.8 7.3 %collective-permute-start.39 = (f32[1,2,144,256]{3,2,1,0:T(8,128)S(1)}, f32[1,2,144,256]{3,2,1,0:T(8,128)S(1)}, u32[]{:S(2)}, u32[]{:S(2)}) collective-permute-start(f32[1,2,144,256]{3,2,1,0:T(8,128)S(1)} %sums.18.refs_2_.refs_0_), channel_id=1, source_target_pairs={{0,4},{4,0},{8,12},{12,8},{16,20},{20,16},{24,28},{28,24},{1,5},{5... | collective-permute-start | bytes 884744 | tf_op jit(solution)/shard_map/ppermute | solution.py:489
  102.3 10.5 %collective-permute-start.26 = (bf16[2,1,216,256]{3,2,1,0:T(8,128)(2,1)S(1)}, bf16[2,1,216,256]{3,2,1,0:T(8,128)(2,1)S(1)}, u32[]{:S(2)}, u32[]{:S(2)}) collective-permute-start(bf16[2,1,216,256]{3,2,1,0:T(8,128)(2,1)S(1)} %collective-permute-done.25.refs_1_), channel_id=1, source_target_pairs={{8,0},{12,4},{16,24},{20,28},{9,1},{13,5},{17,25},{21,29},{10,2},{... | collective-permute-start | bytes 663560 | tf_op jit(solution)/shard_map/ppermute | solution.py:517
  103.6 17.9 %collective-permute-start.40 = (f32[1,2,144,256]{3,2,1,0:T(8,128)S(1)}, f32[1,2,144,256]{3,2,1,0:T(8,128)S(1)}, u32[]{:S(2)}, u32[]{:S(2)}) collective-permute-start(f32[1,2,144,256]{3,2,1,0:T(8,128)S(1)} %sums.18.refs_2_.refs_0_), channel_id=1, source_target_pairs={{0,2},{1,3},{2,0},{3,1},{4,6},{5,7},{6,4},{7,5},{8,10},{9,11},{10,... | collective-permute-start | bytes 884744 | tf_op jit(solution)/shard_map/ppermute | solution.py:489
  105.2 18.5 %collective-permute-start.42 = (f32[1,2,144,256]{3,2,1,0:T(8,128)S(1)}, f32[1,2,144,256]{3,2,1,0:T(8,128)S(1)}, u32[]{:S(2)}, u32[]{:S(2)}) collective-permute-start(f32[1,2,144,256]{3,2,1,0:T(8,128)S(1)} %sums.18.refs_2_.refs_0_), channel_id=1, source_target_pairs={{0,1},{1,0},{2,3},{3,2},{4,5},{5,4},{6,7},{7,6},{8,9},{9,8},{10,11... | collective-permute-start | bytes 884744 | tf_op jit(solution)/shard_map/ppermute | solution.py:489
  108.1 5.1 %collective-permute-start.32 = (f32[1,1,144,256]{3,2,1,0:T(8,128)S(1)}, f32[1,1,144,256]{3,2,1,0:T(8,128)S(1)}, u32[]{:S(2)}, u32[]{:S(2)}) collective-permute-start(f32[1,1,144,256]{3,2,1,0:T(8,128)S(1)} %sums.19.refs_4_.refs_0_), channel_id=1, source_target_pairs={{0,4},{4,0},{8,12},{12,8},{16,20},{20,16},{24,28},{28,24},{1,5},{5... | collective-permute-start | bytes 442376 | tf_op jit(solution)/shard_map/ppermute | solution.py:489
  109.0 12.9 %collective-permute-start.41 = (f32[1,2,144,256]{3,2,1,0:T(8,128)S(1)}, f32[1,2,144,256]{3,2,1,0:T(8,128)S(1)}, u32[]{:S(2)}, u32[]{:S(2)}) collective-permute-start(f32[1,2,144,256]{3,2,1,0:T(8,128)S(1)} %collective-permute-done.39.refs_1_), channel_id=1, source_target_pairs={{0,2},{1,3},{2,0},{3,1},{4,6},{5,7},{6,4},{7,5},{8,10},{9,11},{10,... | collective-permute-start | bytes 884744 | tf_op jit(solution)/shard_map/ppermute | solution.py:489
  112.8 8.7 %collective-permute-start.33 = (f32[1,1,144,256]{3,2,1,0:T(8,128)S(1)}, f32[1,1,144,256]{3,2,1,0:T(8,128)S(1)}, u32[]{:S(2)}, u32[]{:S(2)}) collective-permute-start(f32[1,1,144,256]{3,2,1,0:T(8,128)S(1)} %sums.19.refs_4_.refs_0_), channel_id=1, source_target_pairs={{0,2},{1,3},{2,0},{3,1},{4,6},{5,7},{6,4},{7,5},{8,10},{9,11},{10,... | collective-permute-start | bytes 442376 | tf_op jit(solution)/shard_map/ppermute | solution.py:489
  113.3 10.9 %collective-permute-start.34 = (f32[1,1,144,256]{3,2,1,0:T(8,128)S(1)}, f32[1,1,144,256]{3,2,1,0:T(8,128)S(1)}, u32[]{:S(2)}, u32[]{:S(2)}) collective-permute-start(f32[1,1,144,256]{3,2,1,0:T(8,128)S(1)} %collective-permute-done.32.refs_1_), channel_id=1, source_target_pairs={{0,2},{1,3},{2,0},{3,1},{4,6},{5,7},{6,4},{7,5},{8,10},{9,11},{10,... | collective-permute-start | bytes 442376 | tf_op jit(solution)/shard_map/ppermute | solution.py:489
  121.5 2.7 %collective-permute-start.43 = (f32[1,2,144,256]{3,2,1,0:T(8,128)S(1)}, f32[1,2,144,256]{3,2,1,0:T(8,128)S(1)}, u32[]{:S(2)}, u32[]{:S(2)}) collective-permute-start(f32[1,2,144,256]{3,2,1,0:T(8,128)S(1)} %collective-permute-done.39.refs_1_), channel_id=1, source_target_pairs={{0,1},{1,0},{2,3},{3,2},{4,5},{5,4},{6,7},{7,6},{8,9},{9,8},{10,11... | collective-permute-start | bytes 884744 | tf_op jit(solution)/shard_map/ppermute | solution.py:489
  121.5 3.2 %collective-permute-start.44 = (f32[1,2,144,256]{3,2,1,0:T(8,128)S(1)}, f32[1,2,144,256]{3,2,1,0:T(8,128)S(1)}, u32[]{:S(2)}, u32[]{:S(2)}) collective-permute-start(f32[1,2,144,256]{3,2,1,0:T(8,128)S(1)} %collective-permute-done.40.refs_2_), channel_id=1, source_target_pairs={{0,1},{1,0},{2,3},{3,2},{4,5},{5,4},{6,7},{7,6},{8,9},{9,8},{10,11... | collective-permute-start | bytes 884744 | tf_op jit(solution)/shard_map/ppermute | solution.py:489
  122.0 3.5 %collective-permute-start.45 = (f32[1,2,144,256]{3,2,1,0:T(8,128)S(1)}, f32[1,2,144,256]{3,2,1,0:T(8,128)S(1)}, u32[]{:S(2)}, u32[]{:S(2)}) collective-permute-start(f32[1,2,144,256]{3,2,1,0:T(8,128)S(1)} %collective-permute-done.41.refs_3_), channel_id=1, source_target_pairs={{0,1},{1,0},{2,3},{3,2},{4,5},{5,4},{6,7},{7,6},{8,9},{9,8},{10,11... | collective-permute-start | bytes 884744 | tf_op jit(solution)/shard_map/ppermute | solution.py:489
  123.7 8.0 %collective-permute-start.35 = (f32[1,1,144,256]{3,2,1,0:T(8,128)S(1)}, f32[1,1,144,256]{3,2,1,0:T(8,128)S(1)}, u32[]{:S(2)}, u32[]{:S(2)}) collective-permute-start(f32[1,1,144,256]{3,2,1,0:T(8,128)S(1)} %sums.19.refs_4_.refs_0_), channel_id=1, source_target_pairs={{0,1},{1,0},{2,3},{3,2},{4,5},{5,4},{6,7},{7,6},{8,9},{9,8},{10,11... | collective-permute-start | bytes 442376 | tf_op jit(solution)/shard_map/ppermute | solution.py:489
  124.1 7.5 %collective-permute-start.36 = (f32[1,1,144,256]{3,2,1,0:T(8,128)S(1)}, f32[1,1,144,256]{3,2,1,0:T(8,128)S(1)}, u32[]{:S(2)}, u32[]{:S(2)}) collective-permute-start(f32[1,1,144,256]{3,2,1,0:T(8,128)S(1)} %collective-permute-done.32.refs_1_), channel_id=1, source_target_pairs={{0,1},{1,0},{2,3},{3,2},{4,5},{5,4},{6,7},{7,6},{8,9},{9,8},{10,11... | collective-permute-start | bytes 442376 | tf_op jit(solution)/shard_map/ppermute | solution.py:489
  124.2 7.5 %collective-permute-start.37 = (f32[1,1,144,256]{3,2,1,0:T(8,128)S(1)}, f32[1,1,144,256]{3,2,1,0:T(8,128)S(1)}, u32[]{:S(2)}, u32[]{:S(2)}) collective-permute-start(f32[1,1,144,256]{3,2,1,0:T(8,128)S(1)} %collective-permute-done.33.refs_2_), channel_id=1, source_target_pairs={{0,1},{1,0},{2,3},{3,2},{4,5},{5,4},{6,7},{7,6},{8,9},{9,8},{10,11... | collective-permute-start | bytes 442376 | tf_op jit(solution)/shard_map/ppermute | solution.py:489
  124.7 12.1 %collective-permute-start.31 = (bf16[4,1,216,256]{3,2,1,0:T(8,128)(2,1)S(1)}, bf16[4,1,216,256]{3,2,1,0:T(8,128)(2,1)S(1)}, u32[]{:S(2)}, u32[]{:S(2)}) collective-permute-start(bf16[4,1,216,256]{3,2,1,0:T(8,128)(2,1)S(1)} %collect.3.refs_5_.refs_2_), channel_id=1, source_target_pairs={{0,4},{4,0},{8,12},{12,8},{16,20},{20,16},{24,28},{28,24},{1,5},{5... | collective-permute-start | bytes 1327112 | tf_op jit(solution)/shard_map/ppermute | solution.py:489
  125.5 6.2 %collective-permute-start.38 = (f32[1,1,144,256]{3,2,1,0:T(8,128)S(1)}, f32[1,1,144,256]{3,2,1,0:T(8,128)S(1)}, u32[]{:S(2)}, u32[]{:S(2)}) collective-permute-start(f32[1,1,144,256]{3,2,1,0:T(8,128)S(1)} %collective-permute-done.34.refs_3_), channel_id=1, source_target_pairs={{0,1},{1,0},{2,3},{3,2},{4,5},{5,4},{6,7},{7,6},{8,9},{9,8},{10,11... | collective-permute-start | bytes 442376 | tf_op jit(solution)/shard_map/ppermute | solution.py:489
  (3 other events, 42.4 us)

commit v4 on v3

--- a/solution.py
+++ b/solution.py
@@ -16,11 +16,12 @@
 TOKEN = jax.ShapeDtypeStruct((8, 128), jnp.float32)
 GROUPS = ((0, 1), (2,))
 G_X = (False, False)
-X_FIRST = (False, False)
-Y_SPLIT = (False, False)
-X_HIGH = (False, False)
-Z_SPLIT = (False, False)
+X_FIRST = (False, True)
+X_HIGH = (False, True)
+Z_NEAR = (False, False)
 U_FAR = (False, False)
+JOIN_BACK = (False, False)
+CUT_LIMIT = 32
 COST = {"newton_schulz": 10}
 PLAN = (
     "cut:0",
@@ -29,29 +30,23 @@
     "project:1",
     "core:0",
     "core:1",
+    "pair:1",
     "join:0",
     "y:0",
-    "wait:g03",
     "y:1",
     "x:0",
+    "x:1",
     "collect:0",
-    "x:1",
     "far:0",
     "join:1",
     "far:1",
     "near:0",
     "near:1",
     "weight:1",
-    "wait:un0",
-    "collect:1",
     "weight:0",
-    "basis:0",
-    "basis:1",
     "weight:2",
+    "basis:9",
 )
-PARAMS = pltpu.CompilerParams(vmem_limit_bytes=32 * 1024 * 1024)
-
-
 def dot(a, b, dims, **kw):
     return lax.dot_general(a, b, (dims, ((), ())), preferred_element_type=jnp.float32, **kw)
 
@@ -85,6 +80,7 @@
     scratch=(),
     name=None,
     us=0.5,
+    limit=32,
 ):
     in_specs = in_specs or [block(x.shape) for x in inputs]
     out_specs = out_specs or [block(x.shape) for x in outs]
@@ -101,7 +97,7 @@
         out_shape=outs,
         scratch_shapes=list(scratch),
         input_output_aliases={count + i: first_out + i for i in range(len(earlier))},
-        compiler_params=PARAMS,
+        compiler_params=pltpu.CompilerParams(vmem_limit_bytes=limit * 1024 * 1024),
         cost_estimate=pl.CostEstimate(
             flops=int(us * COST.get(name, 5) * 1e9), bytes_accessed=int(us * COST.get(name, 5) * 3e6), transcendentals=0
         ),
@@ -180,6 +176,7 @@
         scratch=[pltpu.VMEM((parts, size, LANES), gradients.dtype)],
         name="cut_columns",
         us=len(group),
+        limit=CUT_LIMIT,
     )
 
 
@@ -199,11 +196,11 @@
     return rows + rows // 2 + fold_plan(rows, cols)[2]
 
 
-def project_kernel(offsets, x_high, rows, cols, *refs):
+def project_kernel(offsets, highs, rows, cols, *refs):
     count = len(offsets)
     parts = sum(len(ks) for ks in offsets)
     blocks, (p_ref, first_ref, second_ref), refs = refs[:count], refs[count : count + 3], refs[count + 3 :]
-    update_ref, first_out, second_out, send_ref, keep_ref, grad = refs
+    update_ref, first_out, second_out, *terms, grad = refs
     me = lax.axis_index("shard")
     size = folded_rows(rows, cols)
     for ref, ks in zip(blocks, offsets):
@@ -212,13 +209,13 @@
             grad[pl.ds(pl.multiple_of((me ^ k) * rows, rows), rows), :] = part.astype(grad.dtype)
     projected = tn(grad[...], p_ref[0])
     back = projected.astype(jnp.bfloat16)
-    own = row_owner(x_high)
     half = parts // 2
-    for j in list(range(half, parts)) + list(range(half)):
-        at = pl.multiple_of((own ^ j) * rows, rows)
-        term = nn(grad[pl.ds(at, rows), :], back)
-        out = send_ref if j >= half else keep_ref
-        out[j % half, 0] = term
+    for h, x_high in enumerate(highs):
+        own = row_owner(x_high)
+        columns = back[:, h * LANES : (h + 1) * LANES]
+        for j in range(parts):
+            at = pl.multiple_of((own ^ j) * rows, rows)
+            terms[2 * h + j // half][j % half, 0] = nn(grad[pl.ds(at, rows), :], columns)
     projected = projected[:cols]
     first_new = 0.9 * first_ref[0] + 0.1 * projected
     second_new = 0.999 * second_ref[0] + 0.001 * projected * projected
@@ -229,7 +226,7 @@
     ).astype(jnp.bfloat16)
 
 
-def project(blocks, offsets, x_high, group, rows, projectors, first, second, earlier, after=()):
+def project(blocks, offsets, highs, group, rows, projectors, first, second, earlier, after=()):
     mats, width, rank = projectors.shape
     cols = first.shape[1]
     parts = sum(len(ks) for ks in offsets)
@@ -237,21 +234,21 @@
     wide = -(-cols // LANES) * LANES
     of_group = lambda *shape: pl.BlockSpec((1, *shape), lambda i: (group[0] + i, 0, 0))
     own = lambda *shape: pl.BlockSpec((1, *shape), lambda i: (i, 0, 0))
-    half = pl.BlockSpec((parts // 2, 1, rows, rank), lambda i: (0, i, 0, 0))
-    term = jax.ShapeDtypeStruct((parts // 2, count, rows, rank), jnp.float32)
+    half = pl.BlockSpec((parts // 2, 1, rows, LANES), lambda i: (0, i, 0, 0))
+    term = jax.ShapeDtypeStruct((parts // 2, count, rows, LANES), jnp.float32)
+    number = 2 * len(highs)
     moment = of_group(cols, rank)
     return call(
-        functools.partial(project_kernel, offsets, x_high, rows, cols),
+        functools.partial(project_kernel, offsets, highs, rows, cols),
         [*blocks, projectors, first, second],
         [own(*b.shape[1:]) for b in blocks] + [of_group(width, rank), moment, moment],
         [
             jax.ShapeDtypeStruct((count, cols, rank), jnp.bfloat16),
             jax.ShapeDtypeStruct(first.shape, first.dtype),
             jax.ShapeDtypeStruct(second.shape, second.dtype),
-            term,
-            term,
-        ],
-        out_specs=[own(cols, rank), moment, moment, half, half],
+        ]
+        + [term] * number,
+        out_specs=[own(cols, rank), moment, moment] + [half] * number,
         grid=count,
         earlier=earlier,
         first_out=1,
@@ -285,23 +282,24 @@
     )
 
 
-def halve_kernel(count, *refs):
-    ins, outs = refs[:count], refs[count:]
-    rows = outs[0].shape[2]
-    for i, out in enumerate(outs):
-        total = None
-        for ref in ins:
-            value = ref[:1, :, i * rows : (i + 1) * rows, :]
-            total = value if total is None else total + value
-        out[...] = total
-
-
-def halve(inputs, after=()):
-    _, count, rows, rank = inputs[0].shape
-    shape = jax.ShapeDtypeStruct((1, count, rows // 2, rank), jnp.float32)
+def merge_kernel(count, *refs):
+    ins, (sent_ref, low_ref) = refs[: 2 * count], refs[2 * count :]
+    half = sent_ref.shape[0]
+    at = 0
+    for keep, got in zip(ins[:count], ins[count:]):
+        span = slice(at, at + keep.shape[1])
+        low_ref[:, span] = keep[:half] + got[:half]
+        sent_ref[:, span] = keep[half:] + got[half:]
+        at += keep.shape[1]
+
+
+def merge(keeps, gots, after=()):
+    blocks, _, rows, lanes = keeps[0].shape
+    mats = sum(keep.shape[1] for keep in keeps)
+    shape = jax.ShapeDtypeStruct((blocks // 2, mats, rows, lanes), jnp.float32)
     return call(
-        functools.partial(halve_kernel, len(inputs)),
-        inputs,
+        functools.partial(merge_kernel, len(keeps)),
+        [*keeps, *gots],
         None,
         [shape] * 2,
         after=after,
@@ -310,17 +308,13 @@
     )
 
 
-def whole_kernel(a_ref, b_ref, c_ref, d_ref, out_ref):
-    rows = a_ref.shape[2]
-    out_ref[:, :, :rows, :] = a_ref[...] + b_ref[...]
-    out_ref[:, :, rows:, :] = c_ref[...] + d_ref[...]
-
-
-def whole(halves, got, after=()):
-    _, count, rows, rank = halves[0].shape
-    shape = jax.ShapeDtypeStruct((1, count, 2 * rows, rank), jnp.float32)
-    ins = [halves[0], got[0], halves[1], got[1]]
-    return call(whole_kernel, ins, None, [shape], after=after, name="sums", us=0.6)
+def hold_kernel(in_ref, out_ref):
+    out_ref[...] = in_ref[...]
+
+
+def hold(x, after=()):
+    shape = jax.ShapeDtypeStruct(x.shape, x.dtype)
+    return call(hold_kernel, [x], None, [shape], after=after, name="join", us=0.3)
 
 
 def join_kernel(a_ref, b_ref, out_ref):
@@ -363,25 +357,32 @@
     return nn(jnp.concatenate([a[0], a[0], a[1]], axis=1), jnp.concatenate([b[0], b[1], b[0]], axis=0))
 
 
-def basis_kernel(factor, x_high, *refs):
-    pieces, (out_ref, token_ref, held_high, held_low) = refs[:-4], refs[-4:]
+def basis_kernel(factor, highs, *refs):
+    refs, (out_ref, token_ref, held_high, held_low) = refs[:-4], refs[-4:]
     token_ref[...] = jnp.zeros_like(token_ref)
     count, width, rank = held_high.shape
     rows = width // 8
+    mats = range(count)
+    square, grams = [0.0] * count, []
+    first = 0
+    for h, (x_high, number) in enumerate(highs):
+        half = refs[first : first + number]
+        first += number
+        own = row_owner(x_high)
+        lanes = slice(h * LANES, (h + 1) * LANES)
+        for j, (ref, i) in enumerate([(ref, i) for ref in half for i in range(ref.shape[0])]):
+            at = pl.multiple_of((own ^ j) * rows, rows)
+            for m in mats:
+                value = ref[i, m]
+                square[m] = square[m] + jnp.sum(value * value)
+                high, low = split(value)
+                held_high[m, pl.ds(at, rows), lanes] = high
+                held_low[m, pl.ds(at, rows), lanes] = low
+    square = [total + 1e-06 for total in square]
     eye = (
         lax.broadcasted_iota(jnp.int32, (rank, rank), 0)
         == lax.broadcasted_iota(jnp.int32, (rank, rank), 1)
     ).astype(jnp.float32)
-    mats = range(count)
-    square, grams = [], []
-    for m in mats:
-        total = 0.0
-        for j, piece in enumerate(pieces):
-            value = piece[0, m]
-            total = total + jnp.sum(value * value)
-            span = slice(j * rows, (j + 1) * rows)
-            held_high[m, span, :], held_low[m, span, :] = split(value)
-        square.append(total + 1e-06)
     for m in mats:
         high, low = held_high[m], held_low[m]
         both = tn(high, jnp.concatenate([high, low], axis=1))
@@ -399,31 +400,26 @@
         if sweep < NS_STEPS - 1:
             cubes = [thrice(split(squares[m]), parts[m]) for m in mats]
             grams = [2.25 * grams[m] - 1.5 * squares[m] + 0.25 * cubes[m] for m in mats]
-    own = row_owner(x_high)
     for m in mats:
         total = split(totals[m] * (factor / jnp.sqrt(square[m])))
         for j in range(8):
             span = slice(j * rows, (j + 1) * rows)
             value = thrice((held_high[m, span, :], held_low[m, span, :]), total)
-            at = pl.multiple_of((own ^ j) * rows, rows)
-            out_ref[m, pl.ds(at, rows), :] = value.astype(jnp.bfloat16)
-
-
-def basis(pieces, x_high, group, mats, factor, earlier, after=()):
-    _, count, rows, rank = pieces[0].shape
+            out_ref[m, span, :] = value.astype(jnp.bfloat16)
+
+
+def basis(pieces, highs, rank, factor, after=()):
+    _, count, rows, _ = pieces[0].shape
     width = 8 * rows
-    span = pl.BlockSpec((count, width, rank), lambda i: (group[0] // count, 0, 0))
     return call(
-        functools.partial(basis_kernel, factor, x_high),
+        functools.partial(basis_kernel, factor, highs),
         pieces,
         None,
-        [jax.ShapeDtypeStruct((mats, width, rank), jnp.bfloat16), TOKEN],
-        out_specs=[span, block(TOKEN.shape)],
-        earlier=earlier,
+        [jax.ShapeDtypeStruct((count, width, rank), jnp.bfloat16), TOKEN],
         after=after,
         scratch=[pltpu.VMEM((count, width, rank), jnp.bfloat16)] * 2,
         name="newton_schulz",
-        us=4 * count,
+        us=8,
     )
 
 
@@ -546,7 +542,7 @@
 
     groups, count = GROUPS, len(GROUPS)
     moments, bases, new_weight = (), (), ()
-    update, state, send, spread = {}, {}, {}, {}
+    update, state, send, spread, kept, sent = {}, {}, {}, {}, {}, {}
     blocks, offsets = {}, {}
 
     def by_offset(k):
@@ -570,71 +566,59 @@
 
     def step_project(g):
         nonlocal moments
-        update[g], *moments, sent, state[g] = mark(
-            project(blocks[g], offsets[g], X_HIGH[g], groups[g], rows, across, first, second, moments, after())
+        update[g], first_new, second_new, *terms = mark(
+            project(
+                blocks[g], offsets[g], X_HIGH, groups[g], rows, across, first, second, moments, after()
+            )
         )
-        send[g] = move(f"c{g}", core, sent)
+        moments = first_new, second_new
+        kept[g] = terms[0::2]
+        sent[g] = [move(f"c{g}{h}", core, term) for h, term in enumerate(terms[1::2])]
         update[g] = update[g][None]
         if X_FIRST[g]:
             spread[g] = move(f"ux{g}", along_x, update[g])
-        else:
+        elif f"un:{g}" not in PLAN:
             spread[g] = move(f"un{g}", z_near, update[g])
 
-    def step_core(g):
-        low, got = state[g], send[g]
-        if not Y_SPLIT[g]:
-            sent, state[g] = mark(
-                sums([low, got], [([(0, 2), (1, 2)], 2), ([(0, 0), (1, 0)], 2)], after())
-            )
-            send[g] = (move(f"y{g}", axes(g)[0], sent),)
+    def step_un(g):
+        (update[g],) = mark(hold(update[g], after()))
+        spread[g] = move(f"un{g}", z_near, update[g])
+
+
+    def step_core(h):
+        upper, state[h] = mark(
+            merge([kept[g][h] for g in range(count)], [sent[g][h] for g in range(count)], after())
+        )
+        send[h] = move(f"y{h}", axes(h)[0], upper)
+
+    def step_y(h):
+        one, state[h] = mark(
+            sums([state[h], send[h]], [([(0, 1), (1, 1)], 1), ([(0, 0), (1, 0)], 1)], after())
+        )
+        send[h] = move(f"x{h}", axes(h)[1], one)
+
+    def step_x(h):
+        (state[h],) = mark(sums([state[h], send[h]], [([(0, 0), (1, 0)], 1)], after()))
+        send[h] = move(f"f{h}", z_near if Z_NEAR[h] else z_far, state[h])
+
+    def step_far(h):
+        (state[h],) = mark(sums([state[h], send[h]], [([(0, 0), (1, 0)], 1)], after()))
+        send[h] = move(f"n{h}", z_far if Z_NEAR[h] else z_near, state[h])
+
+    def step_near(h):
+        (a,) = mark(sums([state[h], send[h]], [([(0, 0), (1, 0)], 1)], after()))
+        first_way, second_way = axes(h)
+        b = move(f"X{h}", second_way, a)
+        if JOIN_BACK[h]:
+            state[h] = a, b
             return
-        third, other, state[g] = mark(
-            sums(
-                [low, got],
-                [([(0, 3), (1, 3)], 1), ([(0, 2), (1, 2)], 1), ([(0, 0), (1, 0)], 2)],
-                after(),
-            )
-        )
-        send[g] = move(f"y{g}", axes(g)[0], third), move(f"w{g}", axes(g)[0], other)
-
-    def step_y(g):
-        if not Y_SPLIT[g]:
-            one, state[g] = mark(
-                sums([state[g], *send[g]], [([(0, 1), (1, 1)], 1), ([(0, 0), (1, 0)], 1)], after())
-            )
-            send[g] = (move(f"x{g}", axes(g)[1], one),)
-            return
-        third, other = send[g]
-        (one,) = mark(sums([state[g], third], [([(0, 1), (1, 0)], 1)], after()))
-        send[g] = other, move(f"x{g}", axes(g)[1], one)
-
-    def step_x(g):
-        adds = [state[g], *send[g]]
-        if Z_SPLIT[g]:
-            state[g] = mark(halve(adds, after()))
-            send[g] = move(f"f{g}", z_far, state[g][0]), move(f"p{g}", z_near, state[g][1])
-            return
-        (state[g],) = mark(sums(adds, [([(i, 0) for i in range(len(adds))], 1)], after()))
-        send[g] = move(f"f{g}", z_far, state[g])
-
-    def step_far(g):
-        if Z_SPLIT[g]:
-            inputs = [state[g][0], send[g][0], state[g][1], send[g][1]]
-            state[g] = mark(sums(inputs, [([(0, 0), (1, 0)], 1), ([(2, 0), (3, 0)], 1)], after()))
-            send[g] = move(f"n{g}", z_near, state[g][0]), move(f"q{g}", z_far, state[g][1])
-            return
-        (state[g],) = mark(sums([state[g], send[g]], [([(0, 0), (1, 0)], 1)], after()))
-        send[g] = move(f"n{g}", z_near, state[g])
-
-    def step_near(g):
-        if Z_SPLIT[g]:
-            (a,) = mark(whole(state[g], send[g], after()))
-        else:
-            (a,) = mark(sums([state[g], send[g]], [([(0, 0), (1, 0)], 1)], after()))
-        first_way, second_way = axes(g)
-        b = move(f"X{g}", second_way, a)
-        low = [a, b, move(f"Y{g}", first_way, a), move(f"W{g}", first_way, b)]
-        state[g] = low + [move(f"C{g}{i}", core, piece) for i, piece in enumerate(low)]
+        low = [a, b, move(f"Y{h}", first_way, a), move(f"W{h}", first_way, b)]
+        state[h] = low + [move(f"C{h}{i}", core, piece) for i, piece in enumerate(low)]
+
+    def step_low(h):
+        (low,) = mark(join(*state[h], after()))
+        low = [low, move(f"Y{h}", axes(h)[0], low)]
+        state[h] = low + [move(f"C{h}{i}", core, piece) for i, piece in enumerate(low)]
 
     def step_pair(g):
         update[g] = mark(join(update[g], spread[g], after()))[0]
@@ -662,9 +646,15 @@
         )
         mark([token])
 
-    def step_basis(g):
+    def step_basis(_):
         nonlocal bases
-        *bases, token = basis(state[g], X_HIGH[g], groups[g], mats, factor, bases, after())
+        *bases, token = basis(
+            [piece for h in sorted(state) for piece in state[h]],
+            [(X_HIGH[h], len(state[h])) for h in sorted(state)],
+            across.shape[2],
+            factor,
+            after(),
+        )
         mark([token])
 
     steps = {
@@ -676,6 +666,8 @@
         "x": step_x,
         "far": step_far,
         "near": step_near,
+        "low": step_low,
+        "un": step_un,
         "pair": step_pair,
         "join": step_join,
         "collect": step_collect,

time: 139 us -> 134 us (0.964)
  Pallas kernels: 24.6 us -> 22.8 us
  waiting for transfers between devices: 52 us -> 50.2 us
    ppermute x42 -> x44, waiting for transfers between devices: 46.2 us -> 40.4 us  [swap(): return lax.ppermute(x, axis, [(i, i ^ bit) for i in range(size)])]
    ppermute x2, waiting for transfers between devices: 5.84 us -> 9.83 us  [z_outer(): return lax.ppermute(x, 'shard', [(2, 0), (3, 1), (4, 6), (5, 7)])]
    pallas_call x23 -> x22, Pallas kernels: 24.6 us -> 22.8 us  [call(): pl.pallas_call(body, grid=(grid,), in_specs=in_specs + [pl.BlockSpec(memo...]
    ppermute x42 -> x44, starting transfers between devices: 55.6 us -> 54.9 us  [swap(): return lax.ppermute(x, axis, [(i, i ^ bit) for i in range(size)])]
  transfers between devices with their start and end apart: 46 -> 48, of which waited for: 16 -> 17; matrix products, arithmetic and copies ran while one was open for 0% -> 0% of each run, Pallas kernels for 15% -> 9%
where the time goes in v4:
time: 134 us
  starting transfers between devices  58.9 us (44%)
  waiting for transfers between devices  50.2 us (37%)
  Pallas kernels  22.8 us (17%)
  local copies, waits for them, and re-layouts  1.41 us (1%)
    ppermute x44, starting transfers between devices, swap(): return lax.ppermute(x, axis, [(i, i ^ bit) for i in range(size)])  54.9 us
    ppermute x44, waiting for transfers between devices, swap(): return lax.ppermute(x, axis, [(i, i ^ bit) for i in range(size)])  40.4 us
    pallas_call x22, Pallas kernels, call(): pl.pallas_call(body, grid=(grid,), in_specs=in_specs + [pl.BlockSpec(memo...  22.8 us
    ppermute x2, waiting for transfers between devices, z_outer(): return lax.ppermute(x, 'shard', [(2, 0), (3, 1), (4, 6), (5, 7)])  9.83 us
  transfers between devices with their start and end apart: 48, of which 17 were waited for; matrix products, arithmetic and copies ran while one was open for 0% of the time, Pallas kernels for 9%

profile of v4, /device:TPU:0, one launch (start us, length us, event | category | flops | bytes accessed | tf_op | source)
XLA Modules:
  0.0 134.1 jit_solution(3640646943791099931)
XLA Ops:
  0.6 1.4 %copy-done.2 = bf16[3,144,1728]{2,1,0:T(8,128)(2,1)S(1)} copy-done((bf16[3,144,1728]{2,1,0:T(8,128)(2,1)S(1)}, bf16[3,144,1728]{2,1,0:T(8,128)(2,1)}, u32[]{:S(2)}) %copy-start.2) | copy-done | bytes 1493016
  2.0 2.0 %cut_columns.2 = (bf16[2,256,128]{2,1,0:T(8,128)(2,1)S(1)}, bf16[2,256,128]{2,1,0:T(8,128)(2,1)S(1)}, bf16[2,256,128]{2,1,0:T(8,128)(2,1)S(1)}, bf16[2,256,128]{...) custom-call(bf16[3,144,1728]{2,1,0:T(8,128)(2,1)S(1)} %copy-done.2), custom_call_target="tpu_custom_call" | custom-call | flops 10000000000 | bytes 30000000 | tf_op jit(solution)/shard_map/cut_columns/pallas_call | solution.py:92
  4.1 4.1 %collective-permute-start.10 = (bf16[2,256,128]{2,1,0:T(8,128)(2,1)S(1)}, bf16[2,256,128]{2,1,0:T(8,128)(2,1)S(1)}, u32[]{:S(2)}, u32[]{:S(2)}) collective-permute-start(bf16[2,256,128]{2,1,0:T(8,128)(2,1)S(1)} %get-tuple-element.61), channel_id=1, source_target_pairs={{0,16},{4,20},{8,24},{12,28},{16,0},{20,4},{24,8},{28,12},{1,17},{... | collective-permute-start | bytes 393224 | tf_op jit(solution)/shard_map/ppermute | solution.py:485
  8.2 1.3 collective-permute-start.11
  9.5 1.0 cut_columns.3
  10.8 1.8 %collective-permute-start.1 = (bf16[1,256,128]{2,1,0:T(8,128)(2,1)S(1)}, bf16[1,256,128]{2,1,0:T(8,128)(2,1)S(1)}, u32[]{:S(2)}, u32[]{:S(2)}) collective-permute-start(bf16[1,256,128]{2,1,0:T(8,128)(2,1)S(1)} %get-tuple-element.52), channel_id=1, source_target_pairs={{0,8},{4,12},{8,0},{12,4},{16,24},{20,28},{24,16},{28,20},{1,9},{5... | collective-permute-start | bytes 196616 | tf_op jit(solution)/shard_map/ppermute | solution.py:485
  12.7 2.5 %collective-permute-start.12 = (bf16[2,256,128]{2,1,0:T(8,128)(2,1)S(1)}, bf16[2,256,128]{2,1,0:T(8,128)(2,1)S(1)}, u32[]{:S(2)}, u32[]{:S(2)}) collective-permute-start(bf16[2,256,128]{2,1,0:T(8,128)(2,1)S(1)} %get-tuple-element.63), channel_id=1, source_target_pairs={{0,24},{4,28},{8,16},{12,20},{16,8},{20,12},{24,0},{28,4},{1,25},{... | collective-permute-start | bytes 393224 | tf_op jit(solution)/shard_map/ppermute | solution.py:485
  15.1 3.2 %collective-permute-start.13 = (bf16[2,256,128]{2,1,0:T(8,128)(2,1)S(1)}, bf16[2,256,128]{2,1,0:T(8,128)(2,1)S(1)}, u32[]{:S(2)}, u32[]{:S(2)}) collective-permute-start(bf16[2,256,128]{2,1,0:T(8,128)(2,1)S(1)} %get-tuple-element.64), channel_id=1, source_target_pairs={{0,28},{4,24},{8,20},{12,16},{16,12},{20,8},{24,4},{28,0},{1,29},{... | collective-permute-start | bytes 393224 | tf_op jit(solution)/shard_map/ppermute | solution.py:485
  18.4 1.5 %collective-permute-start.7 = (bf16[2,256,128]{2,1,0:T(8,128)(2,1)S(1)}, bf16[2,256,128]{2,1,0:T(8,128)(2,1)S(1)}, u32[]{:S(2)}, u32[]{:S(2)}) collective-permute-start(bf16[2,256,128]{2,1,0:T(8,128)(2,1)S(1)} %get-tuple-element.58), channel_id=1, source_target_pairs={{0,4},{4,0},{8,12},{12,8},{16,20},{20,16},{24,28},{28,24},{1,5},{5... | collective-permute-start | bytes 393224 | tf_op jit(solution)/shard_map/ppermute | solution.py:485
  19.9 3.9 %collective-permute-done.10.refs_4_ = bf16[2,256,128]{2,1,0:T(8,128)(2,1)S(1)} collective-permute-done((bf16[2,256,128]{2,1,0:T(8,128)(2,1)S(1)}, bf16[2,256,128]{2,1,0:T(8,128)(2,1)S(1)}, u32[]{:S(2)}, u32[]{:S(2)}) %collective-permute-start.10) | collective-permute-done | bytes 131104 | tf_op jit(solution)/shard_map/ppermute | solution.py:485
  23.8 4.1 %collective-permute-done.11.refs_5_ = bf16[2,256,128]{2,1,0:T(8,128)(2,1)S(1)} collective-permute-done((bf16[2,256,128]{2,1,0:T(8,128)(2,1)S(1)}, bf16[2,256,128]{2,1,0:T(8,128)(2,1)S(1)}, u32[]{:S(2)}, u32[]{:S(2)}) %collective-permute-start.11) | collective-permute-done | bytes 131104 | tf_op jit(solution)/shard_map/ppermute | solution.py:485
  27.8 3.4 %collective-permute-start.2 = (bf16[1,256,128]{2,1,0:T(8,128)(2,1)S(1)}, bf16[1,256,128]{2,1,0:T(8,128)(2,1)S(1)}, u32[]{:S(2)}, u32[]{:S(2)}) collective-permute-start(bf16[1,256,128]{2,1,0:T(8,128)(2,1)S(1)} %get-tuple-element.53), channel_id=1, source_target_pairs={{0,12},{4,8},{8,4},{12,0},{16,28},{20,24},{24,20},{28,16},{1,13},{... | collective-permute-start | bytes 196616 | tf_op jit(solution)/shard_map/ppermute | solution.py:485
  31.2 5.3 %collective-permute-start.3 = (bf16[1,256,128]{2,1,0:T(8,128)(2,1)S(1)}, bf16[1,256,128]{2,1,0:T(8,128)(2,1)S(1)}, u32[]{:S(2)}, u32[]{:S(2)}) collective-permute-start(bf16[1,256,128]{2,1,0:T(8,128)(2,1)S(1)} %get-tuple-element.54), channel_id=1, source_target_pairs={{0,16},{4,20},{8,24},{12,28},{16,0},{20,4},{24,8},{28,12},{1,17},{... | collective-permute-start | bytes 196616 | tf_op jit(solution)/shard_map/ppermute | solution.py:485
  37.4 3.9 %collective-permute-start.6 = (bf16[1,256,128]{2,1,0:T(8,128)(2,1)S(1)}, bf16[1,256,128]{2,1,0:T(8,128)(2,1)S(1)}, u32[]{:S(2)}, u32[]{:S(2)}) collective-permute-start(bf16[1,256,128]{2,1,0:T(8,128)(2,1)S(1)} %get-tuple-element.57), channel_id=1, source_target_pairs={{0,28},{4,24},{8,20},{12,16},{16,12},{20,8},{24,4},{28,0},{1,29},{... | collective-permute-start | bytes 196616 | tf_op jit(solution)/shard_map/ppermute | solution.py:485
  41.3 3.5 %project.2 = (bf16[2,216,256]{2,1,0:T(8,128)(2,1)S(1)}, f32[3,216,256]{2,1,0:T(8,128)}, f32[3,216,256]{2,1,0:T(8,128)}, f32[4,2,144,128]{3,2,1,0:T(8,128)S(1)}, ...) custom-call(bf16[2,256,128]{2,1,0:T(8,128)(2,1)S(1)} %get-tuple-element.49.refs_1_.ref, ...), custom_call_target="tpu_custom_call" | custom-call | flops 20000000000 | bytes 60000000 | tf_op jit(solution)/shard_map/project/pallas_call | solution.py:92
  45.9 1.9 %project.3 = (bf16[1,216,256]{2,1,0:T(8,128)(2,1)S(1)}, f32[3,216,256]{2,1,0:T(8,128)}, f32[3,216,256]{2,1,0:T(8,128)}, f32[4,1,144,128]{3,2,1,0:T(8,128)S(1)}, ...) custom-call(bf16[1,256,128]{2,1,0:T(8,128)(2,1)S(1)} %get-tuple-elem, ...), custom_call_target="tpu_custom_call", output_to_operand_aliasing={{1}: (11, {}), {2}: (12, {})} | custom-call | flops 10000000000 | bytes 30000000 | tf_op jit(solution)/shard_map/project/pallas_call | solution.py:92
  48.4 1.2 collective-permute-start.14
  49.5 2.9 %collective-permute-start.21 = (bf16[1,2,216,256]{3,2,1,0:T(8,128)(2,1)S(1)}, bf16[1,2,216,256]{3,2,1,0:T(8,128)(2,1)S(1)}, u32[]{:S(2)}, u32[]{:S(2)}) collective-permute-start(bf16[1,2,216,256]{3,2,1,0:T(8,128)(2,1)S(1)} %bitcast.29), channel_id=1, source_target_pairs={{0,8},{4,12},{8,0},{12,4},{16,24},{20,28},{24,16},{28,20},{1,9},{5... | collective-permute-start | bytes 663560 | tf_op jit(solution)/shard_map/ppermute | solution.py:485
  52.6 1.6 %collective-permute-start.20 = (f32[2,3,144,128]{3,2,1,0:T(8,128)S(1)}, f32[2,3,144,128]{3,2,1,0:T(8,128)S(1)}, u32[]{:S(2)}, u32[]{:S(2)}) collective-permute-start(f32[2,3,144,128]{3,2,1,0:T(8,128)S(1)} %get-tuple-element.77.refs_4_), channel_id=1, source_target_pairs={{0,2},{1,3},{2,0},{3,1},{4,6},{5,7},{6,4},{7,5},{8,10},{9,11},{10,... | collective-permute-start | bytes 1327112 | tf_op jit(solution)/shard_map/ppermute | solution.py:485
  54.2 1.1 collective-permute-start.23
  55.4 1.0 collective-permute-start.19
  56.4 2.3 %collective-permute-done.21.refs_1_ = bf16[1,2,216,256]{3,2,1,0:T(8,128)(2,1)S(1)} collective-permute-done((bf16[1,2,216,256]{3,2,1,0:T(8,128)(2,1)S(1)}, bf16[1,2,216,256]{3,2,1,0:T(8,128)(2,1)S(1)}, u32[]{:S(2)}, u32[]{:S(2)}) %collective-permute-start.21) | collective-permute-done | bytes 221216 | tf_op jit(solution)/shard_map/ppermute | solution.py:485
  59.4 5.1 %collective-permute-done.20.refs_1_ = f32[2,3,144,128]{3,2,1,0:T(8,128)S(1)} collective-permute-done((f32[2,3,144,128]{3,2,1,0:T(8,128)S(1)}, f32[2,3,144,128]{3,2,1,0:T(8,128)S(1)}, u32[]{:S(2)}, u32[]{:S(2)}) %collective-permute-start.20) | collective-permute-done | bytes 442400 | tf_op jit(solution)/shard_map/ppermute | solution.py:485
  64.6 1.2 collective-permute-start.22
  66.0 1.4 %collective-permute-start.27 = (f32[1,3,144,128]{3,2,1,0:T(8,128)S(1)}, f32[1,3,144,128]{3,2,1,0:T(8,128)S(1)}, u32[]{:S(2)}, u32[]{:S(2)}) collective-permute-start(f32[1,3,144,128]{3,2,1,0:T(8,128)S(1)} %get-tuple-element.83.refs_2_), channel_id=1, source_target_pairs={{0,2},{1,3},{2,0},{3,1},{4,6},{5,7},{6,4},{7,5},{8,10},{9,11},{10,... | collective-permute-start | bytes 663560 | tf_op jit(solution)/shard_map/ppermute | solution.py:485
  67.4 1.3 collective-permute-start.26
  68.7 2.2 %collective-permute-done.22.refs_1_ = f32[1,3,144,128]{3,2,1,0:T(8,128)S(1)} collective-permute-done((f32[1,3,144,128]{3,2,1,0:T(8,128)S(1)}, f32[1,3,144,128]{3,2,1,0:T(8,128)S(1)}, u32[]{:S(2)}, u32[]{:S(2)}) %collective-permute-start.22) | collective-permute-done | bytes 221216 | tf_op jit(solution)/shard_map/ppermute | solution.py:485
  70.9 3.6 %collective-permute-start.24 = (f32[1,3,144,128]{3,2,1,0:T(8,128)S(1)}, f32[1,3,144,128]{3,2,1,0:T(8,128)S(1)}, u32[]{:S(2)}, u32[]{:S(2)}) collective-permute-start(f32[1,3,144,128]{3,2,1,0:T(8,128)S(1)} %sums.14.refs_2_.refs_0_), channel_id=1, source_target_pairs={{0,16},{4,20},{8,24},{12,28},{16,0},{20,4},{24,8},{28,12},{1,17},{... | collective-permute-start | bytes 663560 | tf_op jit(solution)/shard_map/ppermute | solution.py:485
  74.7 9.8 %collective-permute-done.26.refs_2_ = bf16[2,2,216,256]{3,2,1,0:T(8,128)(2,1)S(1)} collective-permute-done((bf16[2,2,216,256]{3,2,1,0:T(8,128)(2,1)S(1)}, bf16[2,2,216,256]{3,2,1,0:T(8,128)(2,1)S(1)}, u32[]{:S(2)}, u32[]{:S(2)}) %collective-permute-start.26) | collective-permute-done | bytes 442400 | tf_op jit(solution)/shard_map/ppermute | solution.py:513
  85.4 3.9 %collective-permute-done.24.refs_1_ = f32[1,3,144,128]{3,2,1,0:T(8,128)S(1)} collective-permute-done((f32[1,3,144,128]{3,2,1,0:T(8,128)S(1)}, f32[1,3,144,128]{3,2,1,0:T(8,128)S(1)}, u32[]{:S(2)}, u32[]{:S(2)}) %collective-permute-start.24) | collective-permute-done | bytes 221216 | tf_op jit(solution)/shard_map/ppermute | solution.py:485
  90.2 1.5 %collective-permute-done.31.refs_1_ = f32[1,3,144,128]{3,2,1,0:T(8,128)S(1)} collective-permute-done((f32[1,3,144,128]{3,2,1,0:T(8,128)S(1)}, f32[1,3,144,128]{3,2,1,0:T(8,128)S(1)}, u32[]{:S(2)}, u32[]{:S(2)}) %collective-permute-start.31) | collective-permute-done | bytes 221216 | tf_op jit(solution)/shard_map/ppermute | solution.py:485
  91.7 2.1 %collective-permute-start.32 = (f32[1,3,144,128]{3,2,1,0:T(8,128)S(1)}, f32[1,3,144,128]{3,2,1,0:T(8,128)S(1)}, u32[]{:S(2)}, u32[]{:S(2)}) collective-permute-start(f32[1,3,144,128]{3,2,1,0:T(8,128)S(1)} %sums.17.refs_2_.refs_0_), channel_id=1, source_target_pairs={{0,8},{4,12},{8,0},{12,4},{16,24},{20,28},{24,16},{28,20},{1,9},{5... | collective-permute-start | bytes 663560 | tf_op jit(solution)/shard_map/ppermute | solution.py:485
  93.8 4.0 %collective-permute-done.33.refs_1_ = f32[1,3,144,128]{3,2,1,0:T(8,128)S(1)} collective-permute-done((f32[1,3,144,128]{3,2,1,0:T(8,128)S(1)}, f32[1,3,144,128]{3,2,1,0:T(8,128)S(1)}, u32[]{:S(2)}, u32[]{:S(2)}) %collective-permute-start.33) | collective-permute-done | bytes 221216 | tf_op jit(solution)/shard_map/ppermute | solution.py:485
  97.8 1.5 %collective-permute-start.34 = (f32[1,3,144,128]{3,2,1,0:T(8,128)S(1)}, f32[1,3,144,128]{3,2,1,0:T(8,128)S(1)}, u32[]{:S(2)}, u32[]{:S(2)}) collective-permute-start(f32[1,3,144,128]{3,2,1,0:T(8,128)S(1)} %sums.18.refs_2_.refs_0_), channel_id=1, source_target_pairs={{0,4},{4,0},{8,12},{12,8},{16,20},{20,16},{24,28},{28,24},{1,5},{5... | collective-permute-start | bytes 663560 | tf_op jit(solution)/shard_map/ppermute | solution.py:485
  99.3 1.8 %collective-permute-done.32.refs_1_ = f32[1,3,144,128]{3,2,1,0:T(8,128)S(1)} collective-permute-done((f32[1,3,144,128]{3,2,1,0:T(8,128)S(1)}, f32[1,3,144,128]{3,2,1,0:T(8,128)S(1)}, u32[]{:S(2)}, u32[]{:S(2)}) %collective-permute-start.32) | collective-permute-done | bytes 221216 | tf_op jit(solution)/shard_map/ppermute | solution.py:485
  101.1 1.6 %collective-permute-start.41 = (f32[1,3,144,128]{3,2,1,0:T(8,128)S(1)}, f32[1,3,144,128]{3,2,1,0:T(8,128)S(1)}, u32[]{:S(2)}, u32[]{:S(2)}) collective-permute-start(f32[1,3,144,128]{3,2,1,0:T(8,128)S(1)} %sums.19.refs_4_.refs_8_), channel_id=1, source_target_pairs={{0,2},{1,3},{2,0},{3,1},{4,6},{5,7},{6,4},{7,5},{8,10},{9,11},{10,... | collective-permute-start | bytes 663560 | tf_op jit(solution)/shard_map/ppermute | solution.py:485
  102.7 1.9 %collective-permute-start.42 = (f32[1,3,144,128]{3,2,1,0:T(8,128)S(1)}, f32[1,3,144,128]{3,2,1,0:T(8,128)S(1)}, u32[]{:S(2)}, u32[]{:S(2)}) collective-permute-start(f32[1,3,144,128]{3,2,1,0:T(8,128)S(1)} %sums.19.refs_4_.refs_8_), channel_id=1, source_target_pairs={{0,4},{4,0},{8,12},{12,8},{16,20},{20,16},{24,28},{28,24},{1,5},{5... | collective-permute-start | bytes 663560 | tf_op jit(solution)/shard_map/ppermute | solution.py:485
  105.1 2.1 %collective-permute-done.30.refs_3_ = bf16[4,2,216,256]{3,2,1,0:T(8,128)(2,1)S(1)} collective-permute-done((bf16[4,2,216,256]{3,2,1,0:T(8,128)(2,1)S(1)}, bf16[4,2,216,256]{3,2,1,0:T(8,128)(2,1)S(1)}, u32[]{:S(2)}, u32[]{:S(2)}) %collective-permute-start.30) | collective-permute-done | bytes 884768 | tf_op jit(solution)/shard_map/ppermute | solution.py:485
  107.3 1.6 %weight_step.3 = (f32[3,144,1728]{2,1,0:T(8,128)}, f32[8,128]{1,0:T(8,128)S(1)}) custom-call(f32[3,144,1728]{2,1,0:T(8,128)S(1)} %copy-done, bf16[3,1152,256]{2,1,0:T(8,128)(2,1)S(1)} %bitcast.22, bf16[4,2,216,256]{3,2,1,0:T(8,128)(2,1)S(1)} %collect.1.refs_2_, bf16[4,2,216,256]{3,2,1,0:T(8,128)(2,1)S(1)} %collective-permute-done.30.refs_3_, ...), custom_call_target="tpu_custom_call" | custom-call | flops 8000000000 | bytes 24000000 | tf_op jit(solution)/shard_map/weight_step/pallas_call | solution.py:92
  109.4 2.6 %collective-permute-done.34.refs_1_ = f32[1,3,144,128]{3,2,1,0:T(8,128)S(1)} collective-permute-done((f32[1,3,144,128]{3,2,1,0:T(8,128)S(1)}, f32[1,3,144,128]{3,2,1,0:T(8,128)S(1)}, u32[]{:S(2)}, u32[]{:S(2)}) %collective-permute-start.34) | collective-permute-done | bytes 221216 | tf_op jit(solution)/shard_map/ppermute | solution.py:485
  112.0 1.3 collective-permute-start.29
  113.3 1.6 %collective-permute-done.42.refs_10_ = f32[1,3,144,128]{3,2,1,0:T(8,128)S(1)} collective-permute-done((f32[1,3,144,128]{3,2,1,0:T(8,128)S(1)}, f32[1,3,144,128]{3,2,1,0:T(8,128)S(1)}, u32[]{:S(2)}, u32[]{:S(2)}) %collective-permute-start.42) | collective-permute-done | bytes 221216 | tf_op jit(solution)/shard_map/ppermute | solution.py:485
  115.2 1.6 %collective-permute-start.36 = (f32[1,3,144,128]{3,2,1,0:T(8,128)S(1)}, f32[1,3,144,128]{3,2,1,0:T(8,128)S(1)}, u32[]{:S(2)}, u32[]{:S(2)}) collective-permute-start(f32[1,3,144,128]{3,2,1,0:T(8,128)S(1)} %collective-permute-done.34.refs_1_), channel_id=1, source_target_pairs={{0,2},{1,3},{2,0},{3,1},{4,6},{5,7},{6,4},{7,5},{8,10},{9,11},{10,... | collective-permute-start | bytes 663560 | tf_op jit(solution)/shard_map/ppermute | solution.py:485
  116.8 1.6 %weight_step.4 = (f32[3,144,1728]{2,1,0:T(8,128)}, f32[8,128]{1,0:T(8,128)S(1)}) custom-call(f32[3,144,1728]{2,1,0:T(8,128)S(1)} %copy-done, bf16[3,1152,256]{2,1,0:T(8,128)(2,1)S(1)} %bitcast.23, bf16[4,2,216,256]{3,2,1,0:T(8,128)(2,1)S(1)} %collect.1.refs_2_, ...), custom_call_target="tpu_custom_call", output_to_operand_aliasing={{0}: (4, {})} | custom-call | flops 8000000000 | bytes 24000000 | tf_op jit(solution)/shard_map/weight_step/pallas_call | solution.py:92
  118.6 2.2 %collective-permute-done.43.refs_11_ = f32[1,3,144,128]{3,2,1,0:T(8,128)S(1)} collective-permute-done((f32[1,3,144,128]{3,2,1,0:T(8,128)S(1)}, f32[1,3,144,128]{3,2,1,0:T(8,128)S(1)}, u32[]{:S(2)}, u32[]{:S(2)}) %collective-permute-start.43) | collective-permute-done | bytes 221216 | tf_op jit(solution)/shard_map/ppermute | solution.py:485
  120.8 2.3 %collective-permute-done.36.refs_3_ = f32[1,3,144,128]{3,2,1,0:T(8,128)S(1)} collective-permute-done((f32[1,3,144,128]{3,2,1,0:T(8,128)S(1)}, f32[1,3,144,128]{3,2,1,0:T(8,128)S(1)}, u32[]{:S(2)}, u32[]{:S(2)}) %collective-permute-start.36) | collective-permute-done | bytes 221216 | tf_op jit(solution)/shard_map/ppermute | solution.py:485
  123.6 1.8 %weight_step.5 = (f32[3,144,1728]{2,1,0:T(8,128)}, f32[8,128]{1,0:T(8,128)S(1)}) custom-call(f32[3,144,1728]{2,1,0:T(8,128)S(1)} %copy-done, bf16[3,1152,256]{2,1,0:T(8,128)(2,1)S(1)} %bitcast.24, bf16[4,1,216,256]{3,2,1,0:T(8,128)(2,1)S(1)} %join.5.refs_2_, ...), custom_call_target="tpu_custom_call", output_to_operand_aliasing={{0}: (5, {})} | custom-call | flops 8000000000 | bytes 24000000 | tf_op jit(solution)/shard_map/weight_step/pallas_call | solution.py:92
  125.5 8.6 %newton_schulz.1 = (bf16[3,1152,256]{2,1,0:T(8,128)(2,1)}, f32[8,128]{1,0:T(8,128)}) custom-call(f32[1,3,144,128]{3,2,1,0:T(8,128)S(1)} %sums.18.refs_2_.refs_0_, f32[1,3,144,128]{3,2,1,0:T(8,128)S(1)} %collective-permute-done.34.refs_1_, f32[1,3,144,128]{3,2,1,0:T(8,128)S(1)} %collective-permute-done.35.refs_2_, ...), custom_call_target="tpu_custom_call" | custom-call | flops 80000000000 | bytes 240000000 | tf_op jit(solution)/shard_map/newton_schulz/pallas_call | solution.py:92
  (80 shorter events, 8.1 us)
Async XLA Ops:
  4.1 19.7 %collective-permute-start.10 = (bf16[2,256,128]{2,1,0:T(8,128)(2,1)S(1)}, bf16[2,256,128]{2,1,0:T(8,128)(2,1)S(1)}, u32[]{:S(2)}, u32[]{:S(2)}) collective-permute-start(bf16[2,256,128]{2,1,0:T(8,128)(2,1)S(1)} %get-tuple-element.61), channel_id=1, source_target_pairs={{0,16},{4,20},{8,24},{12,28},{16,0},{20,4},{24,8},{28,12},{1,17},{... | collective-permute-start | bytes 393224 | tf_op jit(solution)/shard_map/ppermute | solution.py:485
  8.2 19.6 %collective-permute-start.11 = (bf16[2,256,128]{2,1,0:T(8,128)(2,1)S(1)}, bf16[2,256,128]{2,1,0:T(8,128)(2,1)S(1)}, u32[]{:S(2)}, u32[]{:S(2)}) collective-permute-start(bf16[2,256,128]{2,1,0:T(8,128)(2,1)S(1)} %get-tuple-element.62), channel_id=1, source_target_pairs={{0,20},{4,16},{8,28},{12,24},{16,4},{20,0},{24,12},{28,8},{1,21},{... | collective-permute-start | bytes 393224 | tf_op jit(solution)/shard_map/ppermute | solution.py:485
  10.5 4.7 %collective-permute-start = (bf16[1,256,128]{2,1,0:T(8,128)(2,1)S(1)}, bf16[1,256,128]{2,1,0:T(8,128)(2,1)S(1)}, u32[]{:S(2)}, u32[]{:S(2)}) collective-permute-start(bf16[1,256,128]{2,1,0:T(8,128)(2,1)S(1)} %get-tuple-element.51), channel_id=1, source_target_pairs={{0,4},{4,0},{8,12},{12,8},{16,20},{20,16},{24,28},{28,24},{1,5},{5... | collective-permute-start | bytes 196616 | tf_op jit(solution)/shard_map/ppermute | solution.py:485
  10.8 7.6 %collective-permute-start.1 = (bf16[1,256,128]{2,1,0:T(8,128)(2,1)S(1)}, bf16[1,256,128]{2,1,0:T(8,128)(2,1)S(1)}, u32[]{:S(2)}, u32[]{:S(2)}) collective-permute-start(bf16[1,256,128]{2,1,0:T(8,128)(2,1)S(1)} %get-tuple-element.52), channel_id=1, source_target_pairs={{0,8},{4,12},{8,0},{12,4},{16,24},{20,28},{24,16},{28,20},{1,9},{5... | collective-permute-start | bytes 196616 | tf_op jit(solution)/shard_map/ppermute | solution.py:485
  12.7 15.2 %collective-permute-start.12 = (bf16[2,256,128]{2,1,0:T(8,128)(2,1)S(1)}, bf16[2,256,128]{2,1,0:T(8,128)(2,1)S(1)}, u32[]{:S(2)}, u32[]{:S(2)}) collective-permute-start(bf16[2,256,128]{2,1,0:T(8,128)(2,1)S(1)} %get-tuple-element.63), channel_id=1, source_target_pairs={{0,24},{4,28},{8,16},{12,20},{16,8},{20,12},{24,0},{28,4},{1,25},{... | collective-permute-start | bytes 393224 | tf_op jit(solution)/shard_map/ppermute | solution.py:485
  15.1 16.1 %collective-permute-start.13 = (bf16[2,256,128]{2,1,0:T(8,128)(2,1)S(1)}, bf16[2,256,128]{2,1,0:T(8,128)(2,1)S(1)}, u32[]{:S(2)}, u32[]{:S(2)}) collective-permute-start(bf16[2,256,128]{2,1,0:T(8,128)(2,1)S(1)} %get-tuple-element.64), channel_id=1, source_target_pairs={{0,28},{4,24},{8,20},{12,16},{16,12},{20,8},{24,4},{28,0},{1,29},{... | collective-permute-start | bytes 393224 | tf_op jit(solution)/shard_map/ppermute | solution.py:485
  18.4 18.2 %collective-permute-start.7 = (bf16[2,256,128]{2,1,0:T(8,128)(2,1)S(1)}, bf16[2,256,128]{2,1,0:T(8,128)(2,1)S(1)}, u32[]{:S(2)}, u32[]{:S(2)}) collective-permute-start(bf16[2,256,128]{2,1,0:T(8,128)(2,1)S(1)} %get-tuple-element.58), channel_id=1, source_target_pairs={{0,4},{4,0},{8,12},{12,8},{16,20},{20,16},{24,28},{28,24},{1,5},{5... | collective-permute-start | bytes 393224 | tf_op jit(solution)/shard_map/ppermute | solution.py:485
  23.8 13.2 %collective-permute-start.8 = (bf16[2,256,128]{2,1,0:T(8,128)(2,1)S(1)}, bf16[2,256,128]{2,1,0:T(8,128)(2,1)S(1)}, u32[]{:S(2)}, u32[]{:S(2)}) collective-permute-start(bf16[2,256,128]{2,1,0:T(8,128)(2,1)S(1)} %get-tuple-element.59), channel_id=1, source_target_pairs={{0,8},{4,12},{8,0},{12,4},{16,24},{20,28},{24,16},{28,20},{1,9},{5... | collective-permute-start | bytes 393224 | tf_op jit(solution)/shard_map/ppermute | solution.py:485
  27.8 9.5 %collective-permute-start.9 = (bf16[2,256,128]{2,1,0:T(8,128)(2,1)S(1)}, bf16[2,256,128]{2,1,0:T(8,128)(2,1)S(1)}, u32[]{:S(2)}, u32[]{:S(2)}) collective-permute-start(bf16[2,256,128]{2,1,0:T(8,128)(2,1)S(1)} %get-tuple-element.60), channel_id=1, source_target_pairs={{0,12},{4,8},{8,4},{12,0},{16,28},{20,24},{24,20},{28,16},{1,13},{... | collective-permute-start | bytes 393224 | tf_op jit(solution)/shard_map/ppermute | solution.py:485
  27.8 17.0 %collective-permute-start.2 = (bf16[1,256,128]{2,1,0:T(8,128)(2,1)S(1)}, bf16[1,256,128]{2,1,0:T(8,128)(2,1)S(1)}, u32[]{:S(2)}, u32[]{:S(2)}) collective-permute-start(bf16[1,256,128]{2,1,0:T(8,128)(2,1)S(1)} %get-tuple-element.53), channel_id=1, source_target_pairs={{0,12},{4,8},{8,4},{12,0},{16,28},{20,24},{24,20},{28,16},{1,13},{... | collective-permute-start | bytes 196616 | tf_op jit(solution)/shard_map/ppermute | solution.py:485
  31.2 13.6 %collective-permute-start.3 = (bf16[1,256,128]{2,1,0:T(8,128)(2,1)S(1)}, bf16[1,256,128]{2,1,0:T(8,128)(2,1)S(1)}, u32[]{:S(2)}, u32[]{:S(2)}) collective-permute-start(bf16[1,256,128]{2,1,0:T(8,128)(2,1)S(1)} %get-tuple-element.54), channel_id=1, source_target_pairs={{0,16},{4,20},{8,24},{12,28},{16,0},{20,4},{24,8},{28,12},{1,17},{... | collective-permute-start | bytes 196616 | tf_op jit(solution)/shard_map/ppermute | solution.py:485
  36.6 9.4 %collective-permute-start.4 = (bf16[1,256,128]{2,1,0:T(8,128)(2,1)S(1)}, bf16[1,256,128]{2,1,0:T(8,128)(2,1)S(1)}, u32[]{:S(2)}, u32[]{:S(2)}) collective-permute-start(bf16[1,256,128]{2,1,0:T(8,128)(2,1)S(1)} %get-tuple-element.55), channel_id=1, source_target_pairs={{0,20},{4,16},{8,28},{12,24},{16,4},{20,0},{24,12},{28,8},{1,21},{... | collective-permute-start | bytes 196616 | tf_op jit(solution)/shard_map/ppermute | solution.py:485
  36.9 9.0 %collective-permute-start.5 = (bf16[1,256,128]{2,1,0:T(8,128)(2,1)S(1)}, bf16[1,256,128]{2,1,0:T(8,128)(2,1)S(1)}, u32[]{:S(2)}, u32[]{:S(2)}) collective-permute-start(bf16[1,256,128]{2,1,0:T(8,128)(2,1)S(1)} %get-tuple-element.56), channel_id=1, source_target_pairs={{0,24},{4,28},{8,16},{12,20},{16,8},{20,12},{24,0},{28,4},{1,25},{... | collective-permute-start | bytes 196616 | tf_op jit(solution)/shard_map/ppermute | solution.py:485
  37.4 8.6 %collective-permute-start.6 = (bf16[1,256,128]{2,1,0:T(8,128)(2,1)S(1)}, bf16[1,256,128]{2,1,0:T(8,128)(2,1)S(1)}, u32[]{:S(2)}, u32[]{:S(2)}) collective-permute-start(bf16[1,256,128]{2,1,0:T(8,128)(2,1)S(1)} %get-tuple-element.57), channel_id=1, source_target_pairs={{0,28},{4,24},{8,20},{12,16},{16,12},{20,8},{24,4},{28,0},{1,29},{... | collective-permute-start | bytes 196616 | tf_op jit(solution)/shard_map/ppermute | solution.py:485
  44.8 7.7 %collective-permute-start.17 = (f32[4,2,144,128]{3,2,1,0:T(8,128)S(1)}, f32[4,2,144,128]{3,2,1,0:T(8,128)S(1)}, u32[]{:S(2)}, u32[]{:S(2)}) collective-permute-start(f32[4,2,144,128]{3,2,1,0:T(8,128)S(1)} %get-tuple-element.75), channel_id=1, source_target_pairs={{0,1},{1,0},{2,3},{3,2},{4,5},{5,4},{6,7},{7,6},{8,9},{9,8},{10,11... | collective-permute-start | bytes 1769480 | tf_op jit(solution)/shard_map/ppermute | solution.py:485
  44.8 9.3 %collective-permute-start.15 = (f32[4,2,144,128]{3,2,1,0:T(8,128)S(1)}, f32[4,2,144,128]{3,2,1,0:T(8,128)S(1)}, u32[]{:S(2)}, u32[]{:S(2)}) collective-permute-start(f32[4,2,144,128]{3,2,1,0:T(8,128)S(1)} %get-tuple-element.71), channel_id=1, source_target_pairs={{0,1},{1,0},{2,3},{3,2},{4,5},{5,4},{6,7},{7,6},{8,9},{9,8},{10,11... | collective-permute-start | bytes 1769480 | tf_op jit(solution)/shard_map/ppermute | solution.py:485
  47.8 1.7 %collective-permute-start.18 = (f32[4,1,144,128]{3,2,1,0:T(8,128)S(1)}, f32[4,1,144,128]{3,2,1,0:T(8,128)S(1)}, u32[]{:S(2)}, u32[]{:S(2)}) collective-permute-start(f32[4,1,144,128]{3,2,1,0:T(8,128)S(1)} %get-tuple-element.76), channel_id=1, source_target_pairs={{0,1},{1,0},{2,3},{3,2},{4,5},{5,4},{6,7},{7,6},{8,9},{9,8},{10,11... | collective-permute-start | bytes 884744 | tf_op jit(solution)/shard_map/ppermute | solution.py:485
  47.8 6.3 %collective-permute-start.16 = (f32[4,1,144,128]{3,2,1,0:T(8,128)S(1)}, f32[4,1,144,128]{3,2,1,0:T(8,128)S(1)}, u32[]{:S(2)}, u32[]{:S(2)}) collective-permute-start(f32[4,1,144,128]{3,2,1,0:T(8,128)S(1)} %get-tuple-element.72), channel_id=1, source_target_pairs={{0,1},{1,0},{2,3},{3,2},{4,5},{5,4},{6,7},{7,6},{8,9},{9,8},{10,11... | collective-permute-start | bytes 884744 | tf_op jit(solution)/shard_map/ppermute | solution.py:485
  48.4 7.0 %collective-permute-start.14 = (bf16[1,1,216,256]{3,2,1,0:T(8,128)(2,1)S(1)}, bf16[1,1,216,256]{3,2,1,0:T(8,128)(2,1)S(1)}, u32[]{:S(2)}, u32[]{:S(2)}) collective-permute-start(bf16[1,1,216,256]{3,2,1,0:T(8,128)(2,1)S(1)} %bitcast.31), channel_id=1, source_target_pairs={{0,4},{4,0},{8,12},{12,8},{16,20},{20,16},{24,28},{28,24},{1,5},{5... | collective-permute-start | bytes 331784 | tf_op jit(solution)/shard_map/ppermute | solution.py:485
  49.5 9.1 %collective-permute-start.21 = (bf16[1,2,216,256]{3,2,1,0:T(8,128)(2,1)S(1)}, bf16[1,2,216,256]{3,2,1,0:T(8,128)(2,1)S(1)}, u32[]{:S(2)}, u32[]{:S(2)}) collective-permute-start(bf16[1,2,216,256]{3,2,1,0:T(8,128)(2,1)S(1)} %bitcast.29), channel_id=1, source_target_pairs={{0,8},{4,12},{8,0},{12,4},{16,24},{20,28},{24,16},{28,20},{1,9},{5... | collective-permute-start | bytes 663560 | tf_op jit(solution)/shard_map/ppermute | solution.py:485
  52.6 12.0 %collective-permute-start.20 = (f32[2,3,144,128]{3,2,1,0:T(8,128)S(1)}, f32[2,3,144,128]{3,2,1,0:T(8,128)S(1)}, u32[]{:S(2)}, u32[]{:S(2)}) collective-permute-start(f32[2,3,144,128]{3,2,1,0:T(8,128)S(1)} %get-tuple-element.77.refs_4_), channel_id=1, source_target_pairs={{0,2},{1,3},{2,0},{3,1},{4,6},{5,7},{6,4},{7,5},{8,10},{9,11},{10,... | collective-permute-start | bytes 1327112 | tf_op jit(solution)/shard_map/ppermute | solution.py:485
  54.2 11.7 %collective-permute-start.23 = (f32[2,3,144,128]{3,2,1,0:T(8,128)S(1)}, f32[2,3,144,128]{3,2,1,0:T(8,128)S(1)}, u32[]{:S(2)}, u32[]{:S(2)}) collective-permute-start(f32[2,3,144,128]{3,2,1,0:T(8,128)S(1)} %get-tuple-element.78.refs_2_), channel_id=1, source_target_pairs={{0,4},{4,0},{8,12},{12,8},{16,20},{20,16},{24,28},{28,24},{1,5},{5... | collective-permute-start | bytes 1327112 | tf_op jit(solution)/shard_map/ppermute | solution.py:485
  55.4 34.0 %collective-permute-start.19 = (bf16[2,1,216,256]{3,2,1,0:T(8,128)(2,1)S(1)}, bf16[2,1,216,256]{3,2,1,0:T(8,128)(2,1)S(1)}, u32[]{:S(2)}, u32[]{:S(2)}) collective-permute-start(bf16[2,1,216,256]{3,2,1,0:T(8,128)(2,1)S(1)} %join.3.refs_2_.refs_0_), channel_id=1, source_target_pairs={{0,8},{4,12},{8,0},{12,4},{16,24},{20,28},{24,16},{28,20},{1,9},{5... | collective-permute-start | bytes 663560 | tf_op jit(solution)/shard_map/ppermute | solution.py:485
  58.7 8.7 %collective-permute-start.25 = (bf16[2,2,216,256]{3,2,1,0:T(8,128)(2,1)S(1)}, bf16[2,2,216,256]{3,2,1,0:T(8,128)(2,1)S(1)}, u32[]{:S(2)}, u32[]{:S(2)}) collective-permute-start(bf16[2,2,216,256]{3,2,1,0:T(8,128)(2,1)S(1)} %join.4.refs_2_.refs_0_), channel_id=1, source_target_pairs={{8,16},{12,20},{16,8},{20,12},{9,17},{13,21},{17,9},{21,13},{10,18... | collective-permute-start | bytes 1327112 | tf_op jit(solution)/shard_map/ppermute | solution.py:509
  64.6 6.3 %collective-permute-start.22 = (f32[1,3,144,128]{3,2,1,0:T(8,128)S(1)}, f32[1,3,144,128]{3,2,1,0:T(8,128)S(1)}, u32[]{:S(2)}, u32[]{:S(2)}) collective-permute-start(f32[1,3,144,128]{3,2,1,0:T(8,128)S(1)} %get-tuple-element.81.refs_2_), channel_id=1, source_target_pairs={{0,4},{4,0},{8,12},{12,8},{16,20},{20,16},{24,28},{28,24},{1,5},{5... | collective-permute-start | bytes 663560 | tf_op jit(solution)/shard_map/ppermute | solution.py:485
  66.0 8.6 %collective-permute-start.27 = (f32[1,3,144,128]{3,2,1,0:T(8,128)S(1)}, f32[1,3,144,128]{3,2,1,0:T(8,128)S(1)}, u32[]{:S(2)}, u32[]{:S(2)}) collective-permute-start(f32[1,3,144,128]{3,2,1,0:T(8,128)S(1)} %get-tuple-element.83.refs_2_), channel_id=1, source_target_pairs={{0,2},{1,3},{2,0},{3,1},{4,6},{5,7},{6,4},{7,5},{8,10},{9,11},{10,... | collective-permute-start | bytes 663560 | tf_op jit(solution)/shard_map/ppermute | solution.py:485
  67.4 17.2 %collective-permute-start.26 = (bf16[2,2,216,256]{3,2,1,0:T(8,128)(2,1)S(1)}, bf16[2,2,216,256]{3,2,1,0:T(8,128)(2,1)S(1)}, u32[]{:S(2)}, u32[]{:S(2)}) collective-permute-start(bf16[2,2,216,256]{3,2,1,0:T(8,128)(2,1)S(1)} %collective-permute-done.25.refs_1_), channel_id=1, source_target_pairs={{8,0},{12,4},{16,24},{20,28},{9,1},{13,5},{17,25},{21,29},{10,2},{... | collective-permute-start | bytes 1327112 | tf_op jit(solution)/shard_map/ppermute | solution.py:513
  70.9 18.4 %collective-permute-start.24 = (f32[1,3,144,128]{3,2,1,0:T(8,128)S(1)}, f32[1,3,144,128]{3,2,1,0:T(8,128)S(1)}, u32[]{:S(2)}, u32[]{:S(2)}) collective-permute-start(f32[1,3,144,128]{3,2,1,0:T(8,128)S(1)} %sums.14.refs_2_.refs_0_), channel_id=1, source_target_pairs={{0,16},{4,20},{8,24},{12,28},{16,0},{20,4},{24,8},{28,12},{1,17},{... | collective-permute-start | bytes 663560 | tf_op jit(solution)/shard_map/ppermute | solution.py:485
  74.6 17.1 %collective-permute-start.31 = (f32[1,3,144,128]{3,2,1,0:T(8,128)S(1)}, f32[1,3,144,128]{3,2,1,0:T(8,128)S(1)}, u32[]{:S(2)}, u32[]{:S(2)}) collective-permute-start(f32[1,3,144,128]{3,2,1,0:T(8,128)S(1)} %sums.15.refs_3_.refs_0_), channel_id=1, source_target_pairs={{0,16},{4,20},{8,24},{12,28},{16,0},{20,4},{24,8},{28,12},{1,17},{... | collective-permute-start | bytes 663560 | tf_op jit(solution)/shard_map/ppermute | solution.py:485
  84.6 22.6 %collective-permute-start.30 = (bf16[4,2,216,256]{3,2,1,0:T(8,128)(2,1)S(1)}, bf16[4,2,216,256]{3,2,1,0:T(8,128)(2,1)S(1)}, u32[]{:S(2)}, u32[]{:S(2)}) collective-permute-start(bf16[4,2,216,256]{3,2,1,0:T(8,128)(2,1)S(1)} %collect.1.refs_2_), channel_id=1, source_target_pairs={{0,4},{4,0},{8,12},{12,8},{16,20},{20,16},{24,28},{28,24},{1,5},{5... | collective-permute-start | bytes 2654216 | tf_op jit(solution)/shard_map/ppermute | solution.py:485
  89.4 8.4 %collective-permute-start.33 = (f32[1,3,144,128]{3,2,1,0:T(8,128)S(1)}, f32[1,3,144,128]{3,2,1,0:T(8,128)S(1)}, u32[]{:S(2)}, u32[]{:S(2)}) collective-permute-start(f32[1,3,144,128]{3,2,1,0:T(8,128)S(1)} %sums.16.refs_2_.refs_0_), channel_id=1, source_target_pairs={{0,8},{4,12},{8,0},{12,4},{16,24},{20,28},{24,16},{28,20},{1,9},{5... | collective-permute-start | bytes 663560 | tf_op jit(solution)/shard_map/ppermute | solution.py:485
  89.5 15.1 %collective-permute-start.28 = (bf16[4,1,216,256]{3,2,1,0:T(8,128)(2,1)S(1)}, bf16[4,1,216,256]{3,2,1,0:T(8,128)(2,1)S(1)}, u32[]{:S(2)}, u32[]{:S(2)}) collective-permute-start(bf16[4,1,216,256]{3,2,1,0:T(8,128)(2,1)S(1)} %join.5.refs_2_), channel_id=1, source_target_pairs={{8,16},{12,20},{16,8},{20,12},{9,17},{13,21},{17,9},{21,13},{10,18... | collective-permute-start | bytes 1327112 | tf_op jit(solution)/shard_map/ppermute | solution.py:509
  91.7 9.3 %collective-permute-start.32 = (f32[1,3,144,128]{3,2,1,0:T(8,128)S(1)}, f32[1,3,144,128]{3,2,1,0:T(8,128)S(1)}, u32[]{:S(2)}, u32[]{:S(2)}) collective-permute-start(f32[1,3,144,128]{3,2,1,0:T(8,128)S(1)} %sums.17.refs_2_.refs_0_), channel_id=1, source_target_pairs={{0,8},{4,12},{8,0},{12,4},{16,24},{20,28},{24,16},{28,20},{1,9},{5... | collective-permute-start | bytes 663560 | tf_op jit(solution)/shard_map/ppermute | solution.py:485
  97.8 14.2 %collective-permute-start.34 = (f32[1,3,144,128]{3,2,1,0:T(8,128)S(1)}, f32[1,3,144,128]{3,2,1,0:T(8,128)S(1)}, u32[]{:S(2)}, u32[]{:S(2)}) collective-permute-start(f32[1,3,144,128]{3,2,1,0:T(8,128)S(1)} %sums.18.refs_2_.refs_0_), channel_id=1, source_target_pairs={{0,4},{4,0},{8,12},{12,8},{16,20},{20,16},{24,28},{28,24},{1,5},{5... | collective-permute-start | bytes 663560 | tf_op jit(solution)/shard_map/ppermute | solution.py:485
  101.1 7.8 %collective-permute-start.41 = (f32[1,3,144,128]{3,2,1,0:T(8,128)S(1)}, f32[1,3,144,128]{3,2,1,0:T(8,128)S(1)}, u32[]{:S(2)}, u32[]{:S(2)}) collective-permute-start(f32[1,3,144,128]{3,2,1,0:T(8,128)S(1)} %sums.19.refs_4_.refs_8_), channel_id=1, source_target_pairs={{0,2},{1,3},{2,0},{3,1},{4,6},{5,7},{6,4},{7,5},{8,10},{9,11},{10,... | collective-permute-start | bytes 663560 | tf_op jit(solution)/shard_map/ppermute | solution.py:485
  102.7 12.1 %collective-permute-start.42 = (f32[1,3,144,128]{3,2,1,0:T(8,128)S(1)}, f32[1,3,144,128]{3,2,1,0:T(8,128)S(1)}, u32[]{:S(2)}, u32[]{:S(2)}) collective-permute-start(f32[1,3,144,128]{3,2,1,0:T(8,128)S(1)} %sums.19.refs_4_.refs_8_), channel_id=1, source_target_pairs={{0,4},{4,0},{8,12},{12,8},{16,20},{20,16},{24,28},{28,24},{1,5},{5... | collective-permute-start | bytes 663560 | tf_op jit(solution)/shard_map/ppermute | solution.py:485
  104.6 10.6 %collective-permute-start.35 = (f32[1,3,144,128]{3,2,1,0:T(8,128)S(1)}, f32[1,3,144,128]{3,2,1,0:T(8,128)S(1)}, u32[]{:S(2)}, u32[]{:S(2)}) collective-permute-start(f32[1,3,144,128]{3,2,1,0:T(8,128)S(1)} %sums.18.refs_2_.refs_0_), channel_id=1, source_target_pairs={{0,2},{1,3},{2,0},{3,1},{4,6},{5,7},{6,4},{7,5},{8,10},{9,11},{10,... | collective-permute-start | bytes 663560 | tf_op jit(solution)/shard_map/ppermute | solution.py:485
  107.3 7.9 %collective-permute-start.44 = (f32[1,3,144,128]{3,2,1,0:T(8,128)S(1)}, f32[1,3,144,128]{3,2,1,0:T(8,128)S(1)}, u32[]{:S(2)}, u32[]{:S(2)}) collective-permute-start(f32[1,3,144,128]{3,2,1,0:T(8,128)S(1)} %sums.19.refs_4_.refs_8_), channel_id=1, source_target_pairs={{0,1},{1,0},{2,3},{3,2},{4,5},{5,4},{6,7},{7,6},{8,9},{9,8},{10,11... | collective-permute-start | bytes 663560 | tf_op jit(solution)/shard_map/ppermute | solution.py:485
  108.9 9.5 %collective-permute-start.37 = (f32[1,3,144,128]{3,2,1,0:T(8,128)S(1)}, f32[1,3,144,128]{3,2,1,0:T(8,128)S(1)}, u32[]{:S(2)}, u32[]{:S(2)}) collective-permute-start(f32[1,3,144,128]{3,2,1,0:T(8,128)S(1)} %sums.18.refs_2_.refs_0_), channel_id=1, source_target_pairs={{0,1},{1,0},{2,3},{3,2},{4,5},{5,4},{6,7},{7,6},{8,9},{9,8},{10,11... | collective-permute-start | bytes 663560 | tf_op jit(solution)/shard_map/ppermute | solution.py:485
  112.0 11.6 %collective-permute-start.29 = (bf16[4,1,216,256]{3,2,1,0:T(8,128)(2,1)S(1)}, bf16[4,1,216,256]{3,2,1,0:T(8,128)(2,1)S(1)}, u32[]{:S(2)}, u32[]{:S(2)}) collective-permute-start(bf16[4,1,216,256]{3,2,1,0:T(8,128)(2,1)S(1)} %collective-permute-done.28.refs_3_), channel_id=1, source_target_pairs={{8,0},{12,4},{16,24},{20,28},{9,1},{13,5},{17,25},{21,29},{10,2},{... | collective-permute-start | bytes 1327112 | tf_op jit(solution)/shard_map/ppermute | solution.py:513
  114.8 5.9 %collective-permute-start.43 = (f32[1,3,144,128]{3,2,1,0:T(8,128)S(1)}, f32[1,3,144,128]{3,2,1,0:T(8,128)S(1)}, u32[]{:S(2)}, u32[]{:S(2)}) collective-permute-start(f32[1,3,144,128]{3,2,1,0:T(8,128)S(1)} %collective-permute-done.41.refs_9_), channel_id=1, source_target_pairs={{0,4},{4,0},{8,12},{12,8},{16,20},{20,16},{24,28},{28,24},{1,5},{5... | collective-permute-start | bytes 663560 | tf_op jit(solution)/shard_map/ppermute | solution.py:485
  115.2 7.9 %collective-permute-start.45 = (f32[1,3,144,128]{3,2,1,0:T(8,128)S(1)}, f32[1,3,144,128]{3,2,1,0:T(8,128)S(1)}, u32[]{:S(2)}, u32[]{:S(2)}) collective-permute-start(f32[1,3,144,128]{3,2,1,0:T(8,128)S(1)} %collective-permute-done.41.refs_9_), channel_id=1, source_target_pairs={{0,1},{1,0},{2,3},{3,2},{4,5},{5,4},{6,7},{7,6},{8,9},{9,8},{10,11... | collective-permute-start | bytes 663560 | tf_op jit(solution)/shard_map/ppermute | solution.py:485
  115.2 7.8 %collective-permute-start.36 = (f32[1,3,144,128]{3,2,1,0:T(8,128)S(1)}, f32[1,3,144,128]{3,2,1,0:T(8,128)S(1)}, u32[]{:S(2)}, u32[]{:S(2)}) collective-permute-start(f32[1,3,144,128]{3,2,1,0:T(8,128)S(1)} %collective-permute-done.34.refs_1_), channel_id=1, source_target_pairs={{0,2},{1,3},{2,0},{3,1},{4,6},{5,7},{6,4},{7,5},{8,10},{9,11},{10,... | collective-permute-start | bytes 663560 | tf_op jit(solution)/shard_map/ppermute | solution.py:485
  118.4 7.0 %collective-permute-start.38 = (f32[1,3,144,128]{3,2,1,0:T(8,128)S(1)}, f32[1,3,144,128]{3,2,1,0:T(8,128)S(1)}, u32[]{:S(2)}, u32[]{:S(2)}) collective-permute-start(f32[1,3,144,128]{3,2,1,0:T(8,128)S(1)} %collective-permute-done.34.refs_1_), channel_id=1, source_target_pairs={{0,1},{1,0},{2,3},{3,2},{4,5},{5,4},{6,7},{7,6},{8,9},{9,8},{10,11... | collective-permute-start | bytes 663560 | tf_op jit(solution)/shard_map/ppermute | solution.py:485
  120.8 4.7 %collective-permute-start.46 = (f32[1,3,144,128]{3,2,1,0:T(8,128)S(1)}, f32[1,3,144,128]{3,2,1,0:T(8,128)S(1)}, u32[]{:S(2)}, u32[]{:S(2)}) collective-permute-start(f32[1,3,144,128]{3,2,1,0:T(8,128)S(1)} %collective-permute-done.42.refs_10_), channel_id=1, source_target_pairs={{0,1},{1,0},{2,3},{3,2},{4,5},{5,4},{6,7},{7,6},{8,9},{9,8},{10,11... | collective-permute-start | bytes 663560 | tf_op jit(solution)/shard_map/ppermute | solution.py:485
  123.0 2.4 %collective-permute-start.39 = (f32[1,3,144,128]{3,2,1,0:T(8,128)S(1)}, f32[1,3,144,128]{3,2,1,0:T(8,128)S(1)}, u32[]{:S(2)}, u32[]{:S(2)}) collective-permute-start(f32[1,3,144,128]{3,2,1,0:T(8,128)S(1)} %collective-permute-done.35.refs_2_), channel_id=1, source_target_pairs={{0,1},{1,0},{2,3},{3,2},{4,5},{5,4},{6,7},{7,6},{8,9},{9,8},{10,11... | collective-permute-start | bytes 663560 | tf_op jit(solution)/shard_map/ppermute | solution.py:485
  123.0 2.4 %collective-permute-start.47 = (f32[1,3,144,128]{3,2,1,0:T(8,128)S(1)}, f32[1,3,144,128]{3,2,1,0:T(8,128)S(1)}, u32[]{:S(2)}, u32[]{:S(2)}) collective-permute-start(f32[1,3,144,128]{3,2,1,0:T(8,128)S(1)} %collective-permute-done.43.refs_11_), channel_id=1, source_target_pairs={{0,1},{1,0},{2,3},{3,2},{4,5},{5,4},{6,7},{7,6},{8,9},{9,8},{10,11... | collective-permute-start | bytes 663560 | tf_op jit(solution)/shard_map/ppermute | solution.py:485
  123.5 1.9 %collective-permute-start.40 = (f32[1,3,144,128]{3,2,1,0:T(8,128)S(1)}, f32[1,3,144,128]{3,2,1,0:T(8,128)S(1)}, u32[]{:S(2)}, u32[]{:S(2)}) collective-permute-start(f32[1,3,144,128]{3,2,1,0:T(8,128)S(1)} %collective-permute-done.36.refs_3_), channel_id=1, source_target_pairs={{0,1},{1,0},{2,3},{3,2},{4,5},{5,4},{6,7},{7,6},{8,9},{9,8},{10,11... | collective-permute-start | bytes 663560 | tf_op jit(solution)/shard_map/ppermute | solution.py:485
  (5 other events, 106.4 us)

commit v5 on v4

--- a/solution.py
+++ b/solution.py
@@ -42,9 +42,10 @@
     "far:1",
     "near:0",
     "near:1",
+    "weight:0",
     "weight:1",
-    "weight:0",
     "weight:2",
+    "wait:g06",
     "basis:9",
 )
 def dot(a, b, dims, **kw):

time: 134 us -> 133 us (level)
  waiting for transfers between devices: 50.2 us -> 46.6 us
  starting transfers between devices: 58.9 us -> 60.3 us
    ppermute x44, waiting for transfers between devices: 40.4 us -> 37 us  [swap(): return lax.ppermute(x, axis, [(i, i ^ bit) for i in range(size)])]
    ppermute x44, starting transfers between devices: 54.9 us -> 56.3 us  [swap(): return lax.ppermute(x, axis, [(i, i ^ bit) for i in range(size)])]
  transfers between devices with their start and end apart: 48 -> 48, of which waited for: 17 -> 16; matrix products, arithmetic and copies ran while one was open for 0% -> 0% of each run, Pallas kernels for 9% -> 9%
where the time goes in v5:
time: 133 us; the launch traced here: 132 us
  starting transfers between devices  60.3 us (45%)
  waiting for transfers between devices  46.6 us (35%)
  Pallas kernels  22.8 us (17%)
  local copies, waits for them, and re-layouts  1.41 us (1%)
    ppermute x44, starting transfers between devices, swap(): return lax.ppermute(x, axis, [(i, i ^ bit) for i in range(size)])  56.3 us
    ppermute x44, waiting for transfers between devices, swap(): return lax.ppermute(x, axis, [(i, i ^ bit) for i in range(size)])  37 us
    pallas_call x22, Pallas kernels, call(): pl.pallas_call(body, grid=(grid,), in_specs=in_specs + [pl.BlockSpec(memo...  22.8 us
    ppermute x2, waiting for transfers between devices, z_outer(): return lax.ppermute(x, 'shard', [(2, 0), (3, 1), (4, 6), (5, 7)])  9.62 us
  transfers between devices with their start and end apart: 48, of which 16 were waited for; matrix products, arithmetic and copies ran while one was open for 0% of the time, Pallas kernels for 9%

profile of v5, /device:TPU:0, one launch (start us, length us, event | category | flops | bytes accessed | tf_op | source)
XLA Modules:
  0.0 131.9 jit_solution(6292173449112247419)
XLA Ops:
  0.6 1.4 %copy-done.2 = bf16[3,144,1728]{2,1,0:T(8,128)(2,1)S(1)} copy-done((bf16[3,144,1728]{2,1,0:T(8,128)(2,1)S(1)}, bf16[3,144,1728]{2,1,0:T(8,128)(2,1)}, u32[]{:S(2)}) %copy-start.2) | copy-done | bytes 1493016
  2.0 2.0 %cut_columns.2 = (bf16[2,256,128]{2,1,0:T(8,128)(2,1)S(1)}, bf16[2,256,128]{2,1,0:T(8,128)(2,1)S(1)}, bf16[2,256,128]{2,1,0:T(8,128)(2,1)S(1)}, bf16[2,256,128]{...) custom-call(bf16[3,144,1728]{2,1,0:T(8,128)(2,1)S(1)} %copy-done.2), custom_call_target="tpu_custom_call" | custom-call | flops 10000000000 | bytes 30000000 | tf_op jit(solution)/shard_map/cut_columns/pallas_call | solution.py:93
  4.1 5.1 %collective-permute-start.12 = (bf16[2,256,128]{2,1,0:T(8,128)(2,1)S(1)}, bf16[2,256,128]{2,1,0:T(8,128)(2,1)S(1)}, u32[]{:S(2)}, u32[]{:S(2)}) collective-permute-start(bf16[2,256,128]{2,1,0:T(8,128)(2,1)S(1)} %get-tuple-element.63), channel_id=1, source_target_pairs={{0,24},{4,28},{8,16},{12,20},{16,8},{20,12},{24,0},{28,4},{1,25},{... | collective-permute-start | bytes 393224 | tf_op jit(solution)/shard_map/ppermute | solution.py:486
  9.2 1.0 cut_columns.3
  10.2 1.6 %collective-permute-start = (bf16[1,256,128]{2,1,0:T(8,128)(2,1)S(1)}, bf16[1,256,128]{2,1,0:T(8,128)(2,1)S(1)}, u32[]{:S(2)}, u32[]{:S(2)}) collective-permute-start(bf16[1,256,128]{2,1,0:T(8,128)(2,1)S(1)} %get-tuple-element.51), channel_id=1, source_target_pairs={{0,4},{4,0},{8,12},{12,8},{16,20},{20,16},{24,28},{28,24},{1,5},{5... | collective-permute-start | bytes 196616 | tf_op jit(solution)/shard_map/ppermute | solution.py:486
  12.6 2.1 %collective-permute-start.11 = (bf16[2,256,128]{2,1,0:T(8,128)(2,1)S(1)}, bf16[2,256,128]{2,1,0:T(8,128)(2,1)S(1)}, u32[]{:S(2)}, u32[]{:S(2)}) collective-permute-start(bf16[2,256,128]{2,1,0:T(8,128)(2,1)S(1)} %get-tuple-element.62), channel_id=1, source_target_pairs={{0,20},{4,16},{8,28},{12,24},{16,4},{20,0},{24,12},{28,8},{1,21},{... | collective-permute-start | bytes 393224 | tf_op jit(solution)/shard_map/ppermute | solution.py:486
  14.7 2.7 %collective-permute-start.13 = (bf16[2,256,128]{2,1,0:T(8,128)(2,1)S(1)}, bf16[2,256,128]{2,1,0:T(8,128)(2,1)S(1)}, u32[]{:S(2)}, u32[]{:S(2)}) collective-permute-start(bf16[2,256,128]{2,1,0:T(8,128)(2,1)S(1)} %get-tuple-element.64), channel_id=1, source_target_pairs={{0,28},{4,24},{8,20},{12,16},{16,12},{20,8},{24,4},{28,0},{1,29},{... | collective-permute-start | bytes 393224 | tf_op jit(solution)/shard_map/ppermute | solution.py:486
  17.4 1.4 %collective-permute-start.7 = (bf16[2,256,128]{2,1,0:T(8,128)(2,1)S(1)}, bf16[2,256,128]{2,1,0:T(8,128)(2,1)S(1)}, u32[]{:S(2)}, u32[]{:S(2)}) collective-permute-start(bf16[2,256,128]{2,1,0:T(8,128)(2,1)S(1)} %get-tuple-element.58), channel_id=1, source_target_pairs={{0,4},{4,0},{8,12},{12,8},{16,20},{20,16},{24,28},{28,24},{1,5},{5... | collective-permute-start | bytes 393224 | tf_op jit(solution)/shard_map/ppermute | solution.py:486
  18.8 5.7 %collective-permute-start.8 = (bf16[2,256,128]{2,1,0:T(8,128)(2,1)S(1)}, bf16[2,256,128]{2,1,0:T(8,128)(2,1)S(1)}, u32[]{:S(2)}, u32[]{:S(2)}) collective-permute-start(bf16[2,256,128]{2,1,0:T(8,128)(2,1)S(1)} %get-tuple-element.59), channel_id=1, source_target_pairs={{0,8},{4,12},{8,0},{12,4},{16,24},{20,28},{24,16},{28,20},{1,9},{5... | collective-permute-start | bytes 393224 | tf_op jit(solution)/shard_map/ppermute | solution.py:486
  24.5 2.4 %collective-permute-done.10.refs_4_ = bf16[2,256,128]{2,1,0:T(8,128)(2,1)S(1)} collective-permute-done((bf16[2,256,128]{2,1,0:T(8,128)(2,1)S(1)}, bf16[2,256,128]{2,1,0:T(8,128)(2,1)S(1)}, u32[]{:S(2)}, u32[]{:S(2)}) %collective-permute-start.10) | collective-permute-done | bytes 131104 | tf_op jit(solution)/shard_map/ppermute | solution.py:486
  27.6 3.0 %collective-permute-done.11.refs_5_ = bf16[2,256,128]{2,1,0:T(8,128)(2,1)S(1)} collective-permute-done((bf16[2,256,128]{2,1,0:T(8,128)(2,1)S(1)}, bf16[2,256,128]{2,1,0:T(8,128)(2,1)S(1)}, u32[]{:S(2)}, u32[]{:S(2)}) %collective-permute-start.11) | collective-permute-done | bytes 131104 | tf_op jit(solution)/shard_map/ppermute | solution.py:486
  30.6 5.0 %collective-permute-start.3 = (bf16[1,256,128]{2,1,0:T(8,128)(2,1)S(1)}, bf16[1,256,128]{2,1,0:T(8,128)(2,1)S(1)}, u32[]{:S(2)}, u32[]{:S(2)}) collective-permute-start(bf16[1,256,128]{2,1,0:T(8,128)(2,1)S(1)} %get-tuple-element.54), channel_id=1, source_target_pairs={{0,16},{4,20},{8,24},{12,28},{16,0},{20,4},{24,8},{28,12},{1,17},{... | collective-permute-start | bytes 196616 | tf_op jit(solution)/shard_map/ppermute | solution.py:486
  35.6 1.3 collective-permute-start.5
  36.9 3.4 %collective-permute-start.6 = (bf16[1,256,128]{2,1,0:T(8,128)(2,1)S(1)}, bf16[1,256,128]{2,1,0:T(8,128)(2,1)S(1)}, u32[]{:S(2)}, u32[]{:S(2)}) collective-permute-start(bf16[1,256,128]{2,1,0:T(8,128)(2,1)S(1)} %get-tuple-element.57), channel_id=1, source_target_pairs={{0,28},{4,24},{8,20},{12,16},{16,12},{20,8},{24,4},{28,0},{1,29},{... | collective-permute-start | bytes 196616 | tf_op jit(solution)/shard_map/ppermute | solution.py:486
  40.3 3.5 %project.2 = (bf16[2,216,256]{2,1,0:T(8,128)(2,1)S(1)}, f32[3,216,256]{2,1,0:T(8,128)}, f32[3,216,256]{2,1,0:T(8,128)}, f32[4,2,144,128]{3,2,1,0:T(8,128)S(1)}, ...) custom-call(bf16[2,256,128]{2,1,0:T(8,128)(2,1)S(1)} %get-tuple-element.49.refs_1_.ref, ...), custom_call_target="tpu_custom_call" | custom-call | flops 20000000000 | bytes 60000000 | tf_op jit(solution)/shard_map/project/pallas_call | solution.py:93
  44.4 1.9 %project.3 = (bf16[1,216,256]{2,1,0:T(8,128)(2,1)S(1)}, f32[3,216,256]{2,1,0:T(8,128)}, f32[3,216,256]{2,1,0:T(8,128)}, f32[4,1,144,128]{3,2,1,0:T(8,128)S(1)}, ...) custom-call(bf16[1,256,128]{2,1,0:T(8,128)(2,1)S(1)} %get-tuple-elem, ...), custom_call_target="tpu_custom_call", output_to_operand_aliasing={{1}: (11, {}), {2}: (12, {})} | custom-call | flops 10000000000 | bytes 30000000 | tf_op jit(solution)/shard_map/project/pallas_call | solution.py:93
  46.8 1.2 collective-permute-start.14
  48.1 2.5 %collective-permute-start.21 = (bf16[1,2,216,256]{3,2,1,0:T(8,128)(2,1)S(1)}, bf16[1,2,216,256]{3,2,1,0:T(8,128)(2,1)S(1)}, u32[]{:S(2)}, u32[]{:S(2)}) collective-permute-start(bf16[1,2,216,256]{3,2,1,0:T(8,128)(2,1)S(1)} %bitcast.29), channel_id=1, source_target_pairs={{0,8},{4,12},{8,0},{12,4},{16,24},{20,28},{24,16},{28,20},{1,9},{5... | collective-permute-start | bytes 663560 | tf_op jit(solution)/shard_map/ppermute | solution.py:486
  50.6 1.6 %collective-permute-start.20 = (f32[2,3,144,128]{3,2,1,0:T(8,128)S(1)}, f32[2,3,144,128]{3,2,1,0:T(8,128)S(1)}, u32[]{:S(2)}, u32[]{:S(2)}) collective-permute-start(f32[2,3,144,128]{3,2,1,0:T(8,128)S(1)} %get-tuple-element.77.refs_4_), channel_id=1, source_target_pairs={{0,2},{1,3},{2,0},{3,1},{4,6},{5,7},{6,4},{7,5},{8,10},{9,11},{10,... | collective-permute-start | bytes 1327112 | tf_op jit(solution)/shard_map/ppermute | solution.py:486
  52.3 1.1 collective-permute-start.23
  53.5 0.9 collective-permute-start.19
  54.4 2.3 %collective-permute-done.21.refs_1_ = bf16[1,2,216,256]{3,2,1,0:T(8,128)(2,1)S(1)} collective-permute-done((bf16[1,2,216,256]{3,2,1,0:T(8,128)(2,1)S(1)}, bf16[1,2,216,256]{3,2,1,0:T(8,128)(2,1)S(1)}, u32[]{:S(2)}, u32[]{:S(2)}) %collective-permute-start.21) | collective-permute-done | bytes 221216 | tf_op jit(solution)/shard_map/ppermute | solution.py:486
  57.5 5.1 %collective-permute-done.20.refs_1_ = f32[2,3,144,128]{3,2,1,0:T(8,128)S(1)} collective-permute-done((f32[2,3,144,128]{3,2,1,0:T(8,128)S(1)}, f32[2,3,144,128]{3,2,1,0:T(8,128)S(1)}, u32[]{:S(2)}, u32[]{:S(2)}) %collective-permute-start.20) | collective-permute-done | bytes 442400 | tf_op jit(solution)/shard_map/ppermute | solution.py:486
  62.6 1.2 collective-permute-start.22
  64.0 1.4 %collective-permute-start.27 = (f32[1,3,144,128]{3,2,1,0:T(8,128)S(1)}, f32[1,3,144,128]{3,2,1,0:T(8,128)S(1)}, u32[]{:S(2)}, u32[]{:S(2)}) collective-permute-start(f32[1,3,144,128]{3,2,1,0:T(8,128)S(1)} %get-tuple-element.83.refs_2_), channel_id=1, source_target_pairs={{0,2},{1,3},{2,0},{3,1},{4,6},{5,7},{6,4},{7,5},{8,10},{9,11},{10,... | collective-permute-start | bytes 663560 | tf_op jit(solution)/shard_map/ppermute | solution.py:486
  65.4 1.3 collective-permute-start.26
  66.7 2.2 %collective-permute-done.22.refs_1_ = f32[1,3,144,128]{3,2,1,0:T(8,128)S(1)} collective-permute-done((f32[1,3,144,128]{3,2,1,0:T(8,128)S(1)}, f32[1,3,144,128]{3,2,1,0:T(8,128)S(1)}, u32[]{:S(2)}, u32[]{:S(2)}) %collective-permute-start.22) | collective-permute-done | bytes 221216 | tf_op jit(solution)/shard_map/ppermute | solution.py:486
  68.9 3.8 %collective-permute-start.24 = (f32[1,3,144,128]{3,2,1,0:T(8,128)S(1)}, f32[1,3,144,128]{3,2,1,0:T(8,128)S(1)}, u32[]{:S(2)}, u32[]{:S(2)}) collective-permute-start(f32[1,3,144,128]{3,2,1,0:T(8,128)S(1)} %sums.14.refs_2_.refs_0_), channel_id=1, source_target_pairs={{0,16},{4,20},{8,24},{12,28},{16,0},{20,4},{24,8},{28,12},{1,17},{... | collective-permute-start | bytes 663560 | tf_op jit(solution)/shard_map/ppermute | solution.py:486
  72.9 9.6 %collective-permute-done.26.refs_2_ = bf16[2,2,216,256]{3,2,1,0:T(8,128)(2,1)S(1)} collective-permute-done((bf16[2,2,216,256]{3,2,1,0:T(8,128)(2,1)S(1)}, bf16[2,2,216,256]{3,2,1,0:T(8,128)(2,1)S(1)}, u32[]{:S(2)}, u32[]{:S(2)}) %collective-permute-start.26) | collective-permute-done | bytes 442400 | tf_op jit(solution)/shard_map/ppermute | solution.py:514
  83.3 4.1 %collective-permute-done.24.refs_1_ = f32[1,3,144,128]{3,2,1,0:T(8,128)S(1)} collective-permute-done((f32[1,3,144,128]{3,2,1,0:T(8,128)S(1)}, f32[1,3,144,128]{3,2,1,0:T(8,128)S(1)}, u32[]{:S(2)}, u32[]{:S(2)}) %collective-permute-start.24) | collective-permute-done | bytes 221216 | tf_op jit(solution)/shard_map/ppermute | solution.py:486
  88.2 1.5 %collective-permute-done.31.refs_1_ = f32[1,3,144,128]{3,2,1,0:T(8,128)S(1)} collective-permute-done((f32[1,3,144,128]{3,2,1,0:T(8,128)S(1)}, f32[1,3,144,128]{3,2,1,0:T(8,128)S(1)}, u32[]{:S(2)}, u32[]{:S(2)}) %collective-permute-start.31) | collective-permute-done | bytes 221216 | tf_op jit(solution)/shard_map/ppermute | solution.py:486
  89.8 2.1 %collective-permute-start.32 = (f32[1,3,144,128]{3,2,1,0:T(8,128)S(1)}, f32[1,3,144,128]{3,2,1,0:T(8,128)S(1)}, u32[]{:S(2)}, u32[]{:S(2)}) collective-permute-start(f32[1,3,144,128]{3,2,1,0:T(8,128)S(1)} %sums.17.refs_2_.refs_0_), channel_id=1, source_target_pairs={{0,8},{4,12},{8,0},{12,4},{16,24},{20,28},{24,16},{28,20},{1,9},{5... | collective-permute-start | bytes 663560 | tf_op jit(solution)/shard_map/ppermute | solution.py:486
  91.8 4.0 %collective-permute-done.33.refs_1_ = f32[1,3,144,128]{3,2,1,0:T(8,128)S(1)} collective-permute-done((f32[1,3,144,128]{3,2,1,0:T(8,128)S(1)}, f32[1,3,144,128]{3,2,1,0:T(8,128)S(1)}, u32[]{:S(2)}, u32[]{:S(2)}) %collective-permute-start.33) | collective-permute-done | bytes 221216 | tf_op jit(solution)/shard_map/ppermute | solution.py:486
  95.9 1.4 %collective-permute-start.34 = (f32[1,3,144,128]{3,2,1,0:T(8,128)S(1)}, f32[1,3,144,128]{3,2,1,0:T(8,128)S(1)}, u32[]{:S(2)}, u32[]{:S(2)}) collective-permute-start(f32[1,3,144,128]{3,2,1,0:T(8,128)S(1)} %sums.18.refs_2_.refs_0_), channel_id=1, source_target_pairs={{0,4},{4,0},{8,12},{12,8},{16,20},{20,16},{24,28},{28,24},{1,5},{5... | collective-permute-start | bytes 663560 | tf_op jit(solution)/shard_map/ppermute | solution.py:486
  97.3 1.8 %collective-permute-done.32.refs_1_ = f32[1,3,144,128]{3,2,1,0:T(8,128)S(1)} collective-permute-done((f32[1,3,144,128]{3,2,1,0:T(8,128)S(1)}, f32[1,3,144,128]{3,2,1,0:T(8,128)S(1)}, u32[]{:S(2)}, u32[]{:S(2)}) %collective-permute-start.32) | collective-permute-done | bytes 221216 | tf_op jit(solution)/shard_map/ppermute | solution.py:486
  99.2 1.6 %collective-permute-start.41 = (f32[1,3,144,128]{3,2,1,0:T(8,128)S(1)}, f32[1,3,144,128]{3,2,1,0:T(8,128)S(1)}, u32[]{:S(2)}, u32[]{:S(2)}) collective-permute-start(f32[1,3,144,128]{3,2,1,0:T(8,128)S(1)} %sums.19.refs_4_.refs_8_), channel_id=1, source_target_pairs={{0,2},{1,3},{2,0},{3,1},{4,6},{5,7},{6,4},{7,5},{8,10},{9,11},{10,... | collective-permute-start | bytes 663560 | tf_op jit(solution)/shard_map/ppermute | solution.py:486
  100.7 2.1 %collective-permute-start.42 = (f32[1,3,144,128]{3,2,1,0:T(8,128)S(1)}, f32[1,3,144,128]{3,2,1,0:T(8,128)S(1)}, u32[]{:S(2)}, u32[]{:S(2)}) collective-permute-start(f32[1,3,144,128]{3,2,1,0:T(8,128)S(1)} %sums.19.refs_4_.refs_8_), channel_id=1, source_target_pairs={{0,4},{4,0},{8,12},{12,8},{16,20},{20,16},{24,28},{28,24},{1,5},{5... | collective-permute-start | bytes 663560 | tf_op jit(solution)/shard_map/ppermute | solution.py:486
  103.4 1.8 %collective-permute-done.30.refs_3_ = bf16[4,2,216,256]{3,2,1,0:T(8,128)(2,1)S(1)} collective-permute-done((bf16[4,2,216,256]{3,2,1,0:T(8,128)(2,1)S(1)}, bf16[4,2,216,256]{3,2,1,0:T(8,128)(2,1)S(1)}, u32[]{:S(2)}, u32[]{:S(2)}) %collective-permute-start.30) | collective-permute-done | bytes 884768 | tf_op jit(solution)/shard_map/ppermute | solution.py:486
  105.2 1.6 %weight_step.3 = (f32[3,144,1728]{2,1,0:T(8,128)}, f32[8,128]{1,0:T(8,128)S(1)}) custom-call(f32[3,144,1728]{2,1,0:T(8,128)S(1)} %copy-done, bf16[3,1152,256]{2,1,0:T(8,128)(2,1)S(1)} %bitcast.22, bf16[4,2,216,256]{3,2,1,0:T(8,128)(2,1)S(1)} %collect.1.refs_2_, bf16[4,2,216,256]{3,2,1,0:T(8,128)(2,1)S(1)} %collective-permute-done.30.refs_3_, ...), custom_call_target="tpu_custom_call" | custom-call | flops 8000000000 | bytes 24000000 | tf_op jit(solution)/shard_map/weight_step/pallas_call | solution.py:93
  107.3 2.6 %collective-permute-done.34.refs_1_ = f32[1,3,144,128]{3,2,1,0:T(8,128)S(1)} collective-permute-done((f32[1,3,144,128]{3,2,1,0:T(8,128)S(1)}, f32[1,3,144,128]{3,2,1,0:T(8,128)S(1)}, u32[]{:S(2)}, u32[]{:S(2)}) %collective-permute-start.34) | collective-permute-done | bytes 221216 | tf_op jit(solution)/shard_map/ppermute | solution.py:486
  109.9 1.3 collective-permute-start.29
  111.2 1.5 %collective-permute-done.42.refs_10_ = f32[1,3,144,128]{3,2,1,0:T(8,128)S(1)} collective-permute-done((f32[1,3,144,128]{3,2,1,0:T(8,128)S(1)}, f32[1,3,144,128]{3,2,1,0:T(8,128)S(1)}, u32[]{:S(2)}, u32[]{:S(2)}) %collective-permute-start.42) | collective-permute-done | bytes 221216 | tf_op jit(solution)/shard_map/ppermute | solution.py:486
  113.0 1.6 %collective-permute-start.36 = (f32[1,3,144,128]{3,2,1,0:T(8,128)S(1)}, f32[1,3,144,128]{3,2,1,0:T(8,128)S(1)}, u32[]{:S(2)}, u32[]{:S(2)}) collective-permute-start(f32[1,3,144,128]{3,2,1,0:T(8,128)S(1)} %collective-permute-done.34.refs_1_), channel_id=1, source_target_pairs={{0,2},{1,3},{2,0},{3,1},{4,6},{5,7},{6,4},{7,5},{8,10},{9,11},{10,... | collective-permute-start | bytes 663560 | tf_op jit(solution)/shard_map/ppermute | solution.py:486
  114.6 1.6 %weight_step.4 = (f32[3,144,1728]{2,1,0:T(8,128)}, f32[8,128]{1,0:T(8,128)S(1)}) custom-call(f32[3,144,1728]{2,1,0:T(8,128)S(1)} %copy-done, bf16[3,1152,256]{2,1,0:T(8,128)(2,1)S(1)} %bitcast.23, bf16[4,2,216,256]{3,2,1,0:T(8,128)(2,1)S(1)} %collect.1.refs_2_, ...), custom_call_target="tpu_custom_call", output_to_operand_aliasing={{0}: (4, {})} | custom-call | flops 8000000000 | bytes 24000000 | tf_op jit(solution)/shard_map/weight_step/pallas_call | solution.py:93
  116.4 2.2 %collective-permute-done.43.refs_11_ = f32[1,3,144,128]{3,2,1,0:T(8,128)S(1)} collective-permute-done((f32[1,3,144,128]{3,2,1,0:T(8,128)S(1)}, f32[1,3,144,128]{3,2,1,0:T(8,128)S(1)}, u32[]{:S(2)}, u32[]{:S(2)}) %collective-permute-start.43) | collective-permute-done | bytes 221216 | tf_op jit(solution)/shard_map/ppermute | solution.py:486
  118.7 2.2 %collective-permute-done.36.refs_3_ = f32[1,3,144,128]{3,2,1,0:T(8,128)S(1)} collective-permute-done((f32[1,3,144,128]{3,2,1,0:T(8,128)S(1)}, f32[1,3,144,128]{3,2,1,0:T(8,128)S(1)}, u32[]{:S(2)}, u32[]{:S(2)}) %collective-permute-start.36) | collective-permute-done | bytes 221216 | tf_op jit(solution)/shard_map/ppermute | solution.py:486
  121.4 1.8 %weight_step.5 = (f32[3,144,1728]{2,1,0:T(8,128)}, f32[8,128]{1,0:T(8,128)S(1)}) custom-call(f32[3,144,1728]{2,1,0:T(8,128)S(1)} %copy-done, bf16[3,1152,256]{2,1,0:T(8,128)(2,1)S(1)} %bitcast.24, bf16[4,1,216,256]{3,2,1,0:T(8,128)(2,1)S(1)} %join.5.refs_2_, ...), custom_call_target="tpu_custom_call", output_to_operand_aliasing={{0}: (5, {})} | custom-call | flops 8000000000 | bytes 24000000 | tf_op jit(solution)/shard_map/weight_step/pallas_call | solution.py:93
  123.3 8.6 %newton_schulz.1 = (bf16[3,1152,256]{2,1,0:T(8,128)(2,1)}, f32[8,128]{1,0:T(8,128)}) custom-call(f32[1,3,144,128]{3,2,1,0:T(8,128)S(1)} %sums.18.refs_2_.refs_0_, f32[1,3,144,128]{3,2,1,0:T(8,128)S(1)} %collective-permute-done.34.refs_1_, f32[1,3,144,128]{3,2,1,0:T(8,128)S(1)} %collective-permute-done.35.refs_2_, ...), custom_call_target="tpu_custom_call" | custom-call | flops 80000000000 | bytes 240000000 | tf_op jit(solution)/shard_map/newton_schulz/pallas_call | solution.py:93
  (80 shorter events, 7.7 us)
Async XLA Ops:
  4.1 14.7 %collective-permute-start.12 = (bf16[2,256,128]{2,1,0:T(8,128)(2,1)S(1)}, bf16[2,256,128]{2,1,0:T(8,128)(2,1)S(1)}, u32[]{:S(2)}, u32[]{:S(2)}) collective-permute-start(bf16[2,256,128]{2,1,0:T(8,128)(2,1)S(1)} %get-tuple-element.63), channel_id=1, source_target_pairs={{0,24},{4,28},{8,16},{12,20},{16,8},{20,12},{24,0},{28,4},{1,25},{... | collective-permute-start | bytes 393224 | tf_op jit(solution)/shard_map/ppermute | solution.py:486
  9.2 17.7 %collective-permute-start.10 = (bf16[2,256,128]{2,1,0:T(8,128)(2,1)S(1)}, bf16[2,256,128]{2,1,0:T(8,128)(2,1)S(1)}, u32[]{:S(2)}, u32[]{:S(2)}) collective-permute-start(bf16[2,256,128]{2,1,0:T(8,128)(2,1)S(1)} %get-tuple-element.61), channel_id=1, source_target_pairs={{0,16},{4,20},{8,24},{12,28},{16,0},{20,4},{24,8},{28,12},{1,17},{... | collective-permute-start | bytes 393224 | tf_op jit(solution)/shard_map/ppermute | solution.py:486
  10.2 4.4 %collective-permute-start = (bf16[1,256,128]{2,1,0:T(8,128)(2,1)S(1)}, bf16[1,256,128]{2,1,0:T(8,128)(2,1)S(1)}, u32[]{:S(2)}, u32[]{:S(2)}) collective-permute-start(bf16[1,256,128]{2,1,0:T(8,128)(2,1)S(1)} %get-tuple-element.51), channel_id=1, source_target_pairs={{0,4},{4,0},{8,12},{12,8},{16,20},{20,16},{24,28},{28,24},{1,5},{5... | collective-permute-start | bytes 196616 | tf_op jit(solution)/shard_map/ppermute | solution.py:486
  11.8 5.6 %collective-permute-start.1 = (bf16[1,256,128]{2,1,0:T(8,128)(2,1)S(1)}, bf16[1,256,128]{2,1,0:T(8,128)(2,1)S(1)}, u32[]{:S(2)}, u32[]{:S(2)}) collective-permute-start(bf16[1,256,128]{2,1,0:T(8,128)(2,1)S(1)} %get-tuple-element.52), channel_id=1, source_target_pairs={{0,8},{4,12},{8,0},{12,4},{16,24},{20,28},{24,16},{28,20},{1,9},{5... | collective-permute-start | bytes 196616 | tf_op jit(solution)/shard_map/ppermute | solution.py:486
  12.6 18.0 %collective-permute-start.11 = (bf16[2,256,128]{2,1,0:T(8,128)(2,1)S(1)}, bf16[2,256,128]{2,1,0:T(8,128)(2,1)S(1)}, u32[]{:S(2)}, u32[]{:S(2)}) collective-permute-start(bf16[2,256,128]{2,1,0:T(8,128)(2,1)S(1)} %get-tuple-element.62), channel_id=1, source_target_pairs={{0,20},{4,16},{8,28},{12,24},{16,4},{20,0},{24,12},{28,8},{1,21},{... | collective-permute-start | bytes 393224 | tf_op jit(solution)/shard_map/ppermute | solution.py:486
  14.7 15.9 %collective-permute-start.13 = (bf16[2,256,128]{2,1,0:T(8,128)(2,1)S(1)}, bf16[2,256,128]{2,1,0:T(8,128)(2,1)S(1)}, u32[]{:S(2)}, u32[]{:S(2)}) collective-permute-start(bf16[2,256,128]{2,1,0:T(8,128)(2,1)S(1)} %get-tuple-element.64), channel_id=1, source_target_pairs={{0,28},{4,24},{8,20},{12,16},{16,12},{20,8},{24,4},{28,0},{1,29},{... | collective-permute-start | bytes 393224 | tf_op jit(solution)/shard_map/ppermute | solution.py:486
  17.4 18.2 %collective-permute-start.7 = (bf16[2,256,128]{2,1,0:T(8,128)(2,1)S(1)}, bf16[2,256,128]{2,1,0:T(8,128)(2,1)S(1)}, u32[]{:S(2)}, u32[]{:S(2)}) collective-permute-start(bf16[2,256,128]{2,1,0:T(8,128)(2,1)S(1)} %get-tuple-element.58), channel_id=1, source_target_pairs={{0,4},{4,0},{8,12},{12,8},{16,20},{20,16},{24,28},{28,24},{1,5},{5... | collective-permute-start | bytes 393224 | tf_op jit(solution)/shard_map/ppermute | solution.py:486
  18.8 16.8 %collective-permute-start.8 = (bf16[2,256,128]{2,1,0:T(8,128)(2,1)S(1)}, bf16[2,256,128]{2,1,0:T(8,128)(2,1)S(1)}, u32[]{:S(2)}, u32[]{:S(2)}) collective-permute-start(bf16[2,256,128]{2,1,0:T(8,128)(2,1)S(1)} %get-tuple-element.59), channel_id=1, source_target_pairs={{0,8},{4,12},{8,0},{12,4},{16,24},{20,28},{24,16},{28,20},{1,9},{5... | collective-permute-start | bytes 393224 | tf_op jit(solution)/shard_map/ppermute | solution.py:486
  26.9 10.0 %collective-permute-start.9 = (bf16[2,256,128]{2,1,0:T(8,128)(2,1)S(1)}, bf16[2,256,128]{2,1,0:T(8,128)(2,1)S(1)}, u32[]{:S(2)}, u32[]{:S(2)}) collective-permute-start(bf16[2,256,128]{2,1,0:T(8,128)(2,1)S(1)} %get-tuple-element.60), channel_id=1, source_target_pairs={{0,12},{4,8},{8,4},{12,0},{16,28},{20,24},{24,20},{28,16},{1,13},{... | collective-permute-start | bytes 393224 | tf_op jit(solution)/shard_map/ppermute | solution.py:486
  30.6 13.3 %collective-permute-start.2 = (bf16[1,256,128]{2,1,0:T(8,128)(2,1)S(1)}, bf16[1,256,128]{2,1,0:T(8,128)(2,1)S(1)}, u32[]{:S(2)}, u32[]{:S(2)}) collective-permute-start(bf16[1,256,128]{2,1,0:T(8,128)(2,1)S(1)} %get-tuple-element.53), channel_id=1, source_target_pairs={{0,12},{4,8},{8,4},{12,0},{16,28},{20,24},{24,20},{28,16},{1,13},{... | collective-permute-start | bytes 196616 | tf_op jit(solution)/shard_map/ppermute | solution.py:486
  30.6 13.3 %collective-permute-start.3 = (bf16[1,256,128]{2,1,0:T(8,128)(2,1)S(1)}, bf16[1,256,128]{2,1,0:T(8,128)(2,1)S(1)}, u32[]{:S(2)}, u32[]{:S(2)}) collective-permute-start(bf16[1,256,128]{2,1,0:T(8,128)(2,1)S(1)} %get-tuple-element.54), channel_id=1, source_target_pairs={{0,16},{4,20},{8,24},{12,28},{16,0},{20,4},{24,8},{28,12},{1,17},{... | collective-permute-start | bytes 196616 | tf_op jit(solution)/shard_map/ppermute | solution.py:486
  35.6 8.8 %collective-permute-start.4 = (bf16[1,256,128]{2,1,0:T(8,128)(2,1)S(1)}, bf16[1,256,128]{2,1,0:T(8,128)(2,1)S(1)}, u32[]{:S(2)}, u32[]{:S(2)}) collective-permute-start(bf16[1,256,128]{2,1,0:T(8,128)(2,1)S(1)} %get-tuple-element.55), channel_id=1, source_target_pairs={{0,20},{4,16},{8,28},{12,24},{16,4},{20,0},{24,12},{28,8},{1,21},{... | collective-permute-start | bytes 196616 | tf_op jit(solution)/shard_map/ppermute | solution.py:486
  35.6 8.8 %collective-permute-start.5 = (bf16[1,256,128]{2,1,0:T(8,128)(2,1)S(1)}, bf16[1,256,128]{2,1,0:T(8,128)(2,1)S(1)}, u32[]{:S(2)}, u32[]{:S(2)}) collective-permute-start(bf16[1,256,128]{2,1,0:T(8,128)(2,1)S(1)} %get-tuple-element.56), channel_id=1, source_target_pairs={{0,24},{4,28},{8,16},{12,20},{16,8},{20,12},{24,0},{28,4},{1,25},{... | collective-permute-start | bytes 196616 | tf_op jit(solution)/shard_map/ppermute | solution.py:486
  36.9 7.5 %collective-permute-start.6 = (bf16[1,256,128]{2,1,0:T(8,128)(2,1)S(1)}, bf16[1,256,128]{2,1,0:T(8,128)(2,1)S(1)}, u32[]{:S(2)}, u32[]{:S(2)}) collective-permute-start(bf16[1,256,128]{2,1,0:T(8,128)(2,1)S(1)} %get-tuple-element.57), channel_id=1, source_target_pairs={{0,28},{4,24},{8,20},{12,16},{16,12},{20,8},{24,4},{28,0},{1,29},{... | collective-permute-start | bytes 196616 | tf_op jit(solution)/shard_map/ppermute | solution.py:486
  43.8 6.7 %collective-permute-start.17 = (f32[4,2,144,128]{3,2,1,0:T(8,128)S(1)}, f32[4,2,144,128]{3,2,1,0:T(8,128)S(1)}, u32[]{:S(2)}, u32[]{:S(2)}) collective-permute-start(f32[4,2,144,128]{3,2,1,0:T(8,128)S(1)} %get-tuple-element.75), channel_id=1, source_target_pairs={{0,1},{1,0},{2,3},{3,2},{4,5},{5,4},{6,7},{7,6},{8,9},{9,8},{10,11... | collective-permute-start | bytes 1769480 | tf_op jit(solution)/shard_map/ppermute | solution.py:486
  43.8 8.4 %collective-permute-start.15 = (f32[4,2,144,128]{3,2,1,0:T(8,128)S(1)}, f32[4,2,144,128]{3,2,1,0:T(8,128)S(1)}, u32[]{:S(2)}, u32[]{:S(2)}) collective-permute-start(f32[4,2,144,128]{3,2,1,0:T(8,128)S(1)} %get-tuple-element.71), channel_id=1, source_target_pairs={{0,1},{1,0},{2,3},{3,2},{4,5},{5,4},{6,7},{7,6},{8,9},{9,8},{10,11... | collective-permute-start | bytes 1769480 | tf_op jit(solution)/shard_map/ppermute | solution.py:486
  46.3 1.8 %collective-permute-start.18 = (f32[4,1,144,128]{3,2,1,0:T(8,128)S(1)}, f32[4,1,144,128]{3,2,1,0:T(8,128)S(1)}, u32[]{:S(2)}, u32[]{:S(2)}) collective-permute-start(f32[4,1,144,128]{3,2,1,0:T(8,128)S(1)} %get-tuple-element.76), channel_id=1, source_target_pairs={{0,1},{1,0},{2,3},{3,2},{4,5},{5,4},{6,7},{7,6},{8,9},{9,8},{10,11... | collective-permute-start | bytes 884744 | tf_op jit(solution)/shard_map/ppermute | solution.py:486
  46.4 5.8 %collective-permute-start.16 = (f32[4,1,144,128]{3,2,1,0:T(8,128)S(1)}, f32[4,1,144,128]{3,2,1,0:T(8,128)S(1)}, u32[]{:S(2)}, u32[]{:S(2)}) collective-permute-start(f32[4,1,144,128]{3,2,1,0:T(8,128)S(1)} %get-tuple-element.72), channel_id=1, source_target_pairs={{0,1},{1,0},{2,3},{3,2},{4,5},{5,4},{6,7},{7,6},{8,9},{9,8},{10,11... | collective-permute-start | bytes 884744 | tf_op jit(solution)/shard_map/ppermute | solution.py:486
  46.8 6.6 %collective-permute-start.14 = (bf16[1,1,216,256]{3,2,1,0:T(8,128)(2,1)S(1)}, bf16[1,1,216,256]{3,2,1,0:T(8,128)(2,1)S(1)}, u32[]{:S(2)}, u32[]{:S(2)}) collective-permute-start(bf16[1,1,216,256]{3,2,1,0:T(8,128)(2,1)S(1)} %bitcast.31), channel_id=1, source_target_pairs={{0,4},{4,0},{8,12},{12,8},{16,20},{20,16},{24,28},{28,24},{1,5},{5... | collective-permute-start | bytes 331784 | tf_op jit(solution)/shard_map/ppermute | solution.py:486
  48.1 8.7 %collective-permute-start.21 = (bf16[1,2,216,256]{3,2,1,0:T(8,128)(2,1)S(1)}, bf16[1,2,216,256]{3,2,1,0:T(8,128)(2,1)S(1)}, u32[]{:S(2)}, u32[]{:S(2)}) collective-permute-start(bf16[1,2,216,256]{3,2,1,0:T(8,128)(2,1)S(1)} %bitcast.29), channel_id=1, source_target_pairs={{0,8},{4,12},{8,0},{12,4},{16,24},{20,28},{24,16},{28,20},{1,9},{5... | collective-permute-start | bytes 663560 | tf_op jit(solution)/shard_map/ppermute | solution.py:486
  50.6 11.9 %collective-permute-start.20 = (f32[2,3,144,128]{3,2,1,0:T(8,128)S(1)}, f32[2,3,144,128]{3,2,1,0:T(8,128)S(1)}, u32[]{:S(2)}, u32[]{:S(2)}) collective-permute-start(f32[2,3,144,128]{3,2,1,0:T(8,128)S(1)} %get-tuple-element.77.refs_4_), channel_id=1, source_target_pairs={{0,2},{1,3},{2,0},{3,1},{4,6},{5,7},{6,4},{7,5},{8,10},{9,11},{10,... | collective-permute-start | bytes 1327112 | tf_op jit(solution)/shard_map/ppermute | solution.py:486
  52.3 11.6 %collective-permute-start.23 = (f32[2,3,144,128]{3,2,1,0:T(8,128)S(1)}, f32[2,3,144,128]{3,2,1,0:T(8,128)S(1)}, u32[]{:S(2)}, u32[]{:S(2)}) collective-permute-start(f32[2,3,144,128]{3,2,1,0:T(8,128)S(1)} %get-tuple-element.78.refs_2_), channel_id=1, source_target_pairs={{0,4},{4,0},{8,12},{12,8},{16,20},{20,16},{24,28},{28,24},{1,5},{5... | collective-permute-start | bytes 1327112 | tf_op jit(solution)/shard_map/ppermute | solution.py:486
  53.5 34.0 %collective-permute-start.19 = (bf16[2,1,216,256]{3,2,1,0:T(8,128)(2,1)S(1)}, bf16[2,1,216,256]{3,2,1,0:T(8,128)(2,1)S(1)}, u32[]{:S(2)}, u32[]{:S(2)}) collective-permute-start(bf16[2,1,216,256]{3,2,1,0:T(8,128)(2,1)S(1)} %join.3.refs_2_.refs_0_), channel_id=1, source_target_pairs={{0,8},{4,12},{8,0},{12,4},{16,24},{20,28},{24,16},{28,20},{1,9},{5... | collective-permute-start | bytes 663560 | tf_op jit(solution)/shard_map/ppermute | solution.py:486
  56.8 8.7 %collective-permute-start.25 = (bf16[2,2,216,256]{3,2,1,0:T(8,128)(2,1)S(1)}, bf16[2,2,216,256]{3,2,1,0:T(8,128)(2,1)S(1)}, u32[]{:S(2)}, u32[]{:S(2)}) collective-permute-start(bf16[2,2,216,256]{3,2,1,0:T(8,128)(2,1)S(1)} %join.4.refs_2_.refs_0_), channel_id=1, source_target_pairs={{8,16},{12,20},{16,8},{20,12},{9,17},{13,21},{17,9},{21,13},{10,18... | collective-permute-start | bytes 1327112 | tf_op jit(solution)/shard_map/ppermute | solution.py:510
  62.6 6.3 %collective-permute-start.22 = (f32[1,3,144,128]{3,2,1,0:T(8,128)S(1)}, f32[1,3,144,128]{3,2,1,0:T(8,128)S(1)}, u32[]{:S(2)}, u32[]{:S(2)}) collective-permute-start(f32[1,3,144,128]{3,2,1,0:T(8,128)S(1)} %get-tuple-element.81.refs_2_), channel_id=1, source_target_pairs={{0,4},{4,0},{8,12},{12,8},{16,20},{20,16},{24,28},{28,24},{1,5},{5... | collective-permute-start | bytes 663560 | tf_op jit(solution)/shard_map/ppermute | solution.py:486
  64.0 8.7 %collective-permute-start.27 = (f32[1,3,144,128]{3,2,1,0:T(8,128)S(1)}, f32[1,3,144,128]{3,2,1,0:T(8,128)S(1)}, u32[]{:S(2)}, u32[]{:S(2)}) collective-permute-start(f32[1,3,144,128]{3,2,1,0:T(8,128)S(1)} %get-tuple-element.83.refs_2_), channel_id=1, source_target_pairs={{0,2},{1,3},{2,0},{3,1},{4,6},{5,7},{6,4},{7,5},{8,10},{9,11},{10,... | collective-permute-start | bytes 663560 | tf_op jit(solution)/shard_map/ppermute | solution.py:486
  65.4 17.0 %collective-permute-start.26 = (bf16[2,2,216,256]{3,2,1,0:T(8,128)(2,1)S(1)}, bf16[2,2,216,256]{3,2,1,0:T(8,128)(2,1)S(1)}, u32[]{:S(2)}, u32[]{:S(2)}) collective-permute-start(bf16[2,2,216,256]{3,2,1,0:T(8,128)(2,1)S(1)} %collective-permute-done.25.refs_1_), channel_id=1, source_target_pairs={{8,0},{12,4},{16,24},{20,28},{9,1},{13,5},{17,25},{21,29},{10,2},{... | collective-permute-start | bytes 1327112 | tf_op jit(solution)/shard_map/ppermute | solution.py:514
  68.9 18.4 %collective-permute-start.24 = (f32[1,3,144,128]{3,2,1,0:T(8,128)S(1)}, f32[1,3,144,128]{3,2,1,0:T(8,128)S(1)}, u32[]{:S(2)}, u32[]{:S(2)}) collective-permute-start(f32[1,3,144,128]{3,2,1,0:T(8,128)S(1)} %sums.14.refs_2_.refs_0_), channel_id=1, source_target_pairs={{0,16},{4,20},{8,24},{12,28},{16,0},{20,4},{24,8},{28,12},{1,17},{... | collective-permute-start | bytes 663560 | tf_op jit(solution)/shard_map/ppermute | solution.py:486
  72.8 17.0 %collective-permute-start.31 = (f32[1,3,144,128]{3,2,1,0:T(8,128)S(1)}, f32[1,3,144,128]{3,2,1,0:T(8,128)S(1)}, u32[]{:S(2)}, u32[]{:S(2)}) collective-permute-start(f32[1,3,144,128]{3,2,1,0:T(8,128)S(1)} %sums.15.refs_3_.refs_0_), channel_id=1, source_target_pairs={{0,16},{4,20},{8,24},{12,28},{16,0},{20,4},{24,8},{28,12},{1,17},{... | collective-permute-start | bytes 663560 | tf_op jit(solution)/shard_map/ppermute | solution.py:486
  82.5 22.6 %collective-permute-start.30 = (bf16[4,2,216,256]{3,2,1,0:T(8,128)(2,1)S(1)}, bf16[4,2,216,256]{3,2,1,0:T(8,128)(2,1)S(1)}, u32[]{:S(2)}, u32[]{:S(2)}) collective-permute-start(bf16[4,2,216,256]{3,2,1,0:T(8,128)(2,1)S(1)} %collect.1.refs_2_), channel_id=1, source_target_pairs={{0,4},{4,0},{8,12},{12,8},{16,20},{20,16},{24,28},{28,24},{1,5},{5... | collective-permute-start | bytes 2654216 | tf_op jit(solution)/shard_map/ppermute | solution.py:486
  87.4 8.4 %collective-permute-start.33 = (f32[1,3,144,128]{3,2,1,0:T(8,128)S(1)}, f32[1,3,144,128]{3,2,1,0:T(8,128)S(1)}, u32[]{:S(2)}, u32[]{:S(2)}) collective-permute-start(f32[1,3,144,128]{3,2,1,0:T(8,128)S(1)} %sums.16.refs_2_.refs_0_), channel_id=1, source_target_pairs={{0,8},{4,12},{8,0},{12,4},{16,24},{20,28},{24,16},{28,20},{1,9},{5... | collective-permute-start | bytes 663560 | tf_op jit(solution)/shard_map/ppermute | solution.py:486
  87.5 15.3 %collective-permute-start.28 = (bf16[4,1,216,256]{3,2,1,0:T(8,128)(2,1)S(1)}, bf16[4,1,216,256]{3,2,1,0:T(8,128)(2,1)S(1)}, u32[]{:S(2)}, u32[]{:S(2)}) collective-permute-start(bf16[4,1,216,256]{3,2,1,0:T(8,128)(2,1)S(1)} %join.5.refs_2_), channel_id=1, source_target_pairs={{8,16},{12,20},{16,8},{20,12},{9,17},{13,21},{17,9},{21,13},{10,18... | collective-permute-start | bytes 1327112 | tf_op jit(solution)/shard_map/ppermute | solution.py:510
  89.8 9.3 %collective-permute-start.32 = (f32[1,3,144,128]{3,2,1,0:T(8,128)S(1)}, f32[1,3,144,128]{3,2,1,0:T(8,128)S(1)}, u32[]{:S(2)}, u32[]{:S(2)}) collective-permute-start(f32[1,3,144,128]{3,2,1,0:T(8,128)S(1)} %sums.17.refs_2_.refs_0_), channel_id=1, source_target_pairs={{0,8},{4,12},{8,0},{12,4},{16,24},{20,28},{24,16},{28,20},{1,9},{5... | collective-permute-start | bytes 663560 | tf_op jit(solution)/shard_map/ppermute | solution.py:486
  95.9 14.1 %collective-permute-start.34 = (f32[1,3,144,128]{3,2,1,0:T(8,128)S(1)}, f32[1,3,144,128]{3,2,1,0:T(8,128)S(1)}, u32[]{:S(2)}, u32[]{:S(2)}) collective-permute-start(f32[1,3,144,128]{3,2,1,0:T(8,128)S(1)} %sums.18.refs_2_.refs_0_), channel_id=1, source_target_pairs={{0,4},{4,0},{8,12},{12,8},{16,20},{20,16},{24,28},{28,24},{1,5},{5... | collective-permute-start | bytes 663560 | tf_op jit(solution)/shard_map/ppermute | solution.py:486
  99.2 7.7 %collective-permute-start.41 = (f32[1,3,144,128]{3,2,1,0:T(8,128)S(1)}, f32[1,3,144,128]{3,2,1,0:T(8,128)S(1)}, u32[]{:S(2)}, u32[]{:S(2)}) collective-permute-start(f32[1,3,144,128]{3,2,1,0:T(8,128)S(1)} %sums.19.refs_4_.refs_8_), channel_id=1, source_target_pairs={{0,2},{1,3},{2,0},{3,1},{4,6},{5,7},{6,4},{7,5},{8,10},{9,11},{10,... | collective-permute-start | bytes 663560 | tf_op jit(solution)/shard_map/ppermute | solution.py:486
  100.7 12.0 %collective-permute-start.42 = (f32[1,3,144,128]{3,2,1,0:T(8,128)S(1)}, f32[1,3,144,128]{3,2,1,0:T(8,128)S(1)}, u32[]{:S(2)}, u32[]{:S(2)}) collective-permute-start(f32[1,3,144,128]{3,2,1,0:T(8,128)S(1)} %sums.19.refs_4_.refs_8_), channel_id=1, source_target_pairs={{0,4},{4,0},{8,12},{12,8},{16,20},{20,16},{24,28},{28,24},{1,5},{5... | collective-permute-start | bytes 663560 | tf_op jit(solution)/shard_map/ppermute | solution.py:486
  102.9 10.2 %collective-permute-start.35 = (f32[1,3,144,128]{3,2,1,0:T(8,128)S(1)}, f32[1,3,144,128]{3,2,1,0:T(8,128)S(1)}, u32[]{:S(2)}, u32[]{:S(2)}) collective-permute-start(f32[1,3,144,128]{3,2,1,0:T(8,128)S(1)} %sums.18.refs_2_.refs_0_), channel_id=1, source_target_pairs={{0,2},{1,3},{2,0},{3,1},{4,6},{5,7},{6,4},{7,5},{8,10},{9,11},{10,... | collective-permute-start | bytes 663560 | tf_op jit(solution)/shard_map/ppermute | solution.py:486
  105.2 7.8 %collective-permute-start.44 = (f32[1,3,144,128]{3,2,1,0:T(8,128)S(1)}, f32[1,3,144,128]{3,2,1,0:T(8,128)S(1)}, u32[]{:S(2)}, u32[]{:S(2)}) collective-permute-start(f32[1,3,144,128]{3,2,1,0:T(8,128)S(1)} %sums.19.refs_4_.refs_8_), channel_id=1, source_target_pairs={{0,1},{1,0},{2,3},{3,2},{4,5},{5,4},{6,7},{7,6},{8,9},{9,8},{10,11... | collective-permute-start | bytes 663560 | tf_op jit(solution)/shard_map/ppermute | solution.py:486
  106.8 9.4 %collective-permute-start.37 = (f32[1,3,144,128]{3,2,1,0:T(8,128)S(1)}, f32[1,3,144,128]{3,2,1,0:T(8,128)S(1)}, u32[]{:S(2)}, u32[]{:S(2)}) collective-permute-start(f32[1,3,144,128]{3,2,1,0:T(8,128)S(1)} %sums.18.refs_2_.refs_0_), channel_id=1, source_target_pairs={{0,1},{1,0},{2,3},{3,2},{4,5},{5,4},{6,7},{7,6},{8,9},{9,8},{10,11... | collective-permute-start | bytes 663560 | tf_op jit(solution)/shard_map/ppermute | solution.py:486
  109.9 11.4 %collective-permute-start.29 = (bf16[4,1,216,256]{3,2,1,0:T(8,128)(2,1)S(1)}, bf16[4,1,216,256]{3,2,1,0:T(8,128)(2,1)S(1)}, u32[]{:S(2)}, u32[]{:S(2)}) collective-permute-start(bf16[4,1,216,256]{3,2,1,0:T(8,128)(2,1)S(1)} %collective-permute-done.28.refs_3_), channel_id=1, source_target_pairs={{8,0},{12,4},{16,24},{20,28},{9,1},{13,5},{17,25},{21,29},{10,2},{... | collective-permute-start | bytes 1327112 | tf_op jit(solution)/shard_map/ppermute | solution.py:514
  112.7 5.9 %collective-permute-start.43 = (f32[1,3,144,128]{3,2,1,0:T(8,128)S(1)}, f32[1,3,144,128]{3,2,1,0:T(8,128)S(1)}, u32[]{:S(2)}, u32[]{:S(2)}) collective-permute-start(f32[1,3,144,128]{3,2,1,0:T(8,128)S(1)} %collective-permute-done.41.refs_9_), channel_id=1, source_target_pairs={{0,4},{4,0},{8,12},{12,8},{16,20},{20,16},{24,28},{28,24},{1,5},{5... | collective-permute-start | bytes 663560 | tf_op jit(solution)/shard_map/ppermute | solution.py:486
  113.0 7.9 %collective-permute-start.45 = (f32[1,3,144,128]{3,2,1,0:T(8,128)S(1)}, f32[1,3,144,128]{3,2,1,0:T(8,128)S(1)}, u32[]{:S(2)}, u32[]{:S(2)}) collective-permute-start(f32[1,3,144,128]{3,2,1,0:T(8,128)S(1)} %collective-permute-done.41.refs_9_), channel_id=1, source_target_pairs={{0,1},{1,0},{2,3},{3,2},{4,5},{5,4},{6,7},{7,6},{8,9},{9,8},{10,11... | collective-permute-start | bytes 663560 | tf_op jit(solution)/shard_map/ppermute | solution.py:486
  113.0 7.8 %collective-permute-start.36 = (f32[1,3,144,128]{3,2,1,0:T(8,128)S(1)}, f32[1,3,144,128]{3,2,1,0:T(8,128)S(1)}, u32[]{:S(2)}, u32[]{:S(2)}) collective-permute-start(f32[1,3,144,128]{3,2,1,0:T(8,128)S(1)} %collective-permute-done.34.refs_1_), channel_id=1, source_target_pairs={{0,2},{1,3},{2,0},{3,1},{4,6},{5,7},{6,4},{7,5},{8,10},{9,11},{10,... | collective-permute-start | bytes 663560 | tf_op jit(solution)/shard_map/ppermute | solution.py:486
  116.2 7.0 %collective-permute-start.38 = (f32[1,3,144,128]{3,2,1,0:T(8,128)S(1)}, f32[1,3,144,128]{3,2,1,0:T(8,128)S(1)}, u32[]{:S(2)}, u32[]{:S(2)}) collective-permute-start(f32[1,3,144,128]{3,2,1,0:T(8,128)S(1)} %collective-permute-done.34.refs_1_), channel_id=1, source_target_pairs={{0,1},{1,0},{2,3},{3,2},{4,5},{5,4},{6,7},{7,6},{8,9},{9,8},{10,11... | collective-permute-start | bytes 663560 | tf_op jit(solution)/shard_map/ppermute | solution.py:486
  118.7 4.6 %collective-permute-start.46 = (f32[1,3,144,128]{3,2,1,0:T(8,128)S(1)}, f32[1,3,144,128]{3,2,1,0:T(8,128)S(1)}, u32[]{:S(2)}, u32[]{:S(2)}) collective-permute-start(f32[1,3,144,128]{3,2,1,0:T(8,128)S(1)} %collective-permute-done.42.refs_10_), channel_id=1, source_target_pairs={{0,1},{1,0},{2,3},{3,2},{4,5},{5,4},{6,7},{7,6},{8,9},{9,8},{10,11... | collective-permute-start | bytes 663560 | tf_op jit(solution)/shard_map/ppermute | solution.py:486
  120.9 2.4 %collective-permute-start.39 = (f32[1,3,144,128]{3,2,1,0:T(8,128)S(1)}, f32[1,3,144,128]{3,2,1,0:T(8,128)S(1)}, u32[]{:S(2)}, u32[]{:S(2)}) collective-permute-start(f32[1,3,144,128]{3,2,1,0:T(8,128)S(1)} %collective-permute-done.35.refs_2_), channel_id=1, source_target_pairs={{0,1},{1,0},{2,3},{3,2},{4,5},{5,4},{6,7},{7,6},{8,9},{9,8},{10,11... | collective-permute-start | bytes 663560 | tf_op jit(solution)/shard_map/ppermute | solution.py:486
  120.9 2.4 %collective-permute-start.47 = (f32[1,3,144,128]{3,2,1,0:T(8,128)S(1)}, f32[1,3,144,128]{3,2,1,0:T(8,128)S(1)}, u32[]{:S(2)}, u32[]{:S(2)}) collective-permute-start(f32[1,3,144,128]{3,2,1,0:T(8,128)S(1)} %collective-permute-done.43.refs_11_), channel_id=1, source_target_pairs={{0,1},{1,0},{2,3},{3,2},{4,5},{5,4},{6,7},{7,6},{8,9},{9,8},{10,11... | collective-permute-start | bytes 663560 | tf_op jit(solution)/shard_map/ppermute | solution.py:486
  121.4 1.9 %collective-permute-start.40 = (f32[1,3,144,128]{3,2,1,0:T(8,128)S(1)}, f32[1,3,144,128]{3,2,1,0:T(8,128)S(1)}, u32[]{:S(2)}, u32[]{:S(2)}) collective-permute-start(f32[1,3,144,128]{3,2,1,0:T(8,128)S(1)} %collective-permute-done.36.refs_3_), channel_id=1, source_target_pairs={{0,1},{1,0},{2,3},{3,2},{4,5},{5,4},{6,7},{7,6},{8,9},{9,8},{10,11... | collective-permute-start | bytes 663560 | tf_op jit(solution)/shard_map/ppermute | solution.py:486
  (5 other events, 104.1 us)

commit v6 on v5

--- a/solution.py
+++ b/solution.py
@@ -20,7 +20,7 @@
 X_HIGH = (False, True)
 Z_NEAR = (False, False)
 U_FAR = (False, False)
-JOIN_BACK = (False, False)
+JOIN_BACK = (True, True)
 CUT_LIMIT = 32
 COST = {"newton_schulz": 10}
 PLAN = (
@@ -43,6 +43,8 @@
     "near:0",
     "near:1",
     "weight:0",
+    "low:0",
+    "low:1",
     "weight:1",
     "weight:2",
     "wait:g06",

time: 133 us -> 131 us (0.985)
  starting transfers between devices: 60.3 us -> 57.4 us
  waiting for transfers between devices: 46.6 us -> 48.2 us
    ppermute x44 -> x38, starting transfers between devices: 56.3 us -> 53.5 us  [swap(): return lax.ppermute(x, axis, [(i, i ^ bit) for i in range(size)])]
    ppermute x44 -> x38, waiting for transfers between devices: 37 us -> 38.5 us  [swap(): return lax.ppermute(x, axis, [(i, i ^ bit) for i in range(size)])]
    pallas_call x22 -> x24, Pallas kernels: 22.8 us -> 22.9 us  [call(): pl.pallas_call(body, grid=(grid,), in_specs=in_specs + [pl.BlockSpec(memo...]
  transfers between devices with their start and end apart: 48 -> 42, of which waited for: 16 -> 15; matrix products, arithmetic and copies ran while one was open for 0% -> 0% of each run, Pallas kernels for 9% -> 9%
where the time goes in v6:
time: 131 us
  starting transfers between devices  57.4 us (44%)
  waiting for transfers between devices  48.2 us (37%)
  Pallas kernels  22.9 us (17%)
  local copies, waits for them, and re-layouts  1.41 us (1%)
    ppermute x38, starting transfers between devices, swap(): return lax.ppermute(x, axis, [(i, i ^ bit) for i in range(size)])  53.5 us
    ppermute x38, waiting for transfers between devices, swap(): return lax.ppermute(x, axis, [(i, i ^ bit) for i in range(size)])  38.5 us
    pallas_call x24, Pallas kernels, call(): pl.pallas_call(body, grid=(grid,), in_specs=in_specs + [pl.BlockSpec(memo...  22.9 us
    ppermute x2, waiting for transfers between devices, z_outer(): return lax.ppermute(x, 'shard', [(2, 0), (3, 1), (4, 6), (5, 7)])  9.62 us
  transfers between devices with their start and end apart: 42, of which 15 were waited for; matrix products, arithmetic and copies ran while one was open for 0% of the time, Pallas kernels for 9%

profile of v6, /device:TPU:0, one launch (start us, length us, event | category | flops | bytes accessed | tf_op | source)
XLA Modules:
  0.0 130.7 jit_solution(10000020575387995644)
XLA Ops:
  0.6 1.4 %copy-done.2 = bf16[3,144,1728]{2,1,0:T(8,128)(2,1)S(1)} copy-done((bf16[3,144,1728]{2,1,0:T(8,128)(2,1)S(1)}, bf16[3,144,1728]{2,1,0:T(8,128)(2,1)}, u32[]{:S(2)}) %copy-start.2) | copy-done | bytes 1493016
  2.0 2.0 %cut_columns.2 = (bf16[2,256,128]{2,1,0:T(8,128)(2,1)S(1)}, bf16[2,256,128]{2,1,0:T(8,128)(2,1)S(1)}, bf16[2,256,128]{2,1,0:T(8,128)(2,1)S(1)}, bf16[2,256,128]{...) custom-call(bf16[3,144,1728]{2,1,0:T(8,128)(2,1)S(1)} %copy-done.2), custom_call_target="tpu_custom_call" | custom-call | flops 10000000000 | bytes 30000000 | tf_op jit(solution)/shard_map/cut_columns/pallas_call | solution.py:95
  4.1 5.1 %collective-permute-start.12 = (bf16[2,256,128]{2,1,0:T(8,128)(2,1)S(1)}, bf16[2,256,128]{2,1,0:T(8,128)(2,1)S(1)}, u32[]{:S(2)}, u32[]{:S(2)}) collective-permute-start(bf16[2,256,128]{2,1,0:T(8,128)(2,1)S(1)} %get-tuple-element.63), channel_id=1, source_target_pairs={{0,24},{4,28},{8,16},{12,20},{16,8},{20,12},{24,0},{28,4},{1,25},{... | collective-permute-start | bytes 393224 | tf_op jit(solution)/shard_map/ppermute | solution.py:488
  9.2 1.0 cut_columns.3
  10.2 1.6 %collective-permute-start = (bf16[1,256,128]{2,1,0:T(8,128)(2,1)S(1)}, bf16[1,256,128]{2,1,0:T(8,128)(2,1)S(1)}, u32[]{:S(2)}, u32[]{:S(2)}) collective-permute-start(bf16[1,256,128]{2,1,0:T(8,128)(2,1)S(1)} %get-tuple-element.51), channel_id=1, source_target_pairs={{0,4},{4,0},{8,12},{12,8},{16,20},{20,16},{24,28},{28,24},{1,5},{5... | collective-permute-start | bytes 196616 | tf_op jit(solution)/shard_map/ppermute | solution.py:488
  11.8 0.8 collective-permute-start.1
  12.6 2.1 %collective-permute-start.11 = (bf16[2,256,128]{2,1,0:T(8,128)(2,1)S(1)}, bf16[2,256,128]{2,1,0:T(8,128)(2,1)S(1)}, u32[]{:S(2)}, u32[]{:S(2)}) collective-permute-start(bf16[2,256,128]{2,1,0:T(8,128)(2,1)S(1)} %get-tuple-element.62), channel_id=1, source_target_pairs={{0,20},{4,16},{8,28},{12,24},{16,4},{20,0},{24,12},{28,8},{1,21},{... | collective-permute-start | bytes 393224 | tf_op jit(solution)/shard_map/ppermute | solution.py:488
  14.7 2.7 %collective-permute-start.13 = (bf16[2,256,128]{2,1,0:T(8,128)(2,1)S(1)}, bf16[2,256,128]{2,1,0:T(8,128)(2,1)S(1)}, u32[]{:S(2)}, u32[]{:S(2)}) collective-permute-start(bf16[2,256,128]{2,1,0:T(8,128)(2,1)S(1)} %get-tuple-element.64), channel_id=1, source_target_pairs={{0,28},{4,24},{8,20},{12,16},{16,12},{20,8},{24,4},{28,0},{1,29},{... | collective-permute-start | bytes 393224 | tf_op jit(solution)/shard_map/ppermute | solution.py:488
  17.4 1.4 %collective-permute-start.7 = (bf16[2,256,128]{2,1,0:T(8,128)(2,1)S(1)}, bf16[2,256,128]{2,1,0:T(8,128)(2,1)S(1)}, u32[]{:S(2)}, u32[]{:S(2)}) collective-permute-start(bf16[2,256,128]{2,1,0:T(8,128)(2,1)S(1)} %get-tuple-element.58), channel_id=1, source_target_pairs={{0,4},{4,0},{8,12},{12,8},{16,20},{20,16},{24,28},{28,24},{1,5},{5... | collective-permute-start | bytes 393224 | tf_op jit(solution)/shard_map/ppermute | solution.py:488
  18.8 5.7 %collective-permute-start.8 = (bf16[2,256,128]{2,1,0:T(8,128)(2,1)S(1)}, bf16[2,256,128]{2,1,0:T(8,128)(2,1)S(1)}, u32[]{:S(2)}, u32[]{:S(2)}) collective-permute-start(bf16[2,256,128]{2,1,0:T(8,128)(2,1)S(1)} %get-tuple-element.59), channel_id=1, source_target_pairs={{0,8},{4,12},{8,0},{12,4},{16,24},{20,28},{24,16},{28,20},{1,9},{5... | collective-permute-start | bytes 393224 | tf_op jit(solution)/shard_map/ppermute | solution.py:488
  24.5 2.4 %collective-permute-done.10.refs_4_ = bf16[2,256,128]{2,1,0:T(8,128)(2,1)S(1)} collective-permute-done((bf16[2,256,128]{2,1,0:T(8,128)(2,1)S(1)}, bf16[2,256,128]{2,1,0:T(8,128)(2,1)S(1)}, u32[]{:S(2)}, u32[]{:S(2)}) %collective-permute-start.10) | collective-permute-done | bytes 131104 | tf_op jit(solution)/shard_map/ppermute | solution.py:488
  26.9 0.7 collective-permute-start.9
  27.6 3.0 %collective-permute-done.11.refs_5_ = bf16[2,256,128]{2,1,0:T(8,128)(2,1)S(1)} collective-permute-done((bf16[2,256,128]{2,1,0:T(8,128)(2,1)S(1)}, bf16[2,256,128]{2,1,0:T(8,128)(2,1)S(1)}, u32[]{:S(2)}, u32[]{:S(2)}) %collective-permute-start.11) | collective-permute-done | bytes 131104 | tf_op jit(solution)/shard_map/ppermute | solution.py:488
  30.6 5.0 %collective-permute-start.3 = (bf16[1,256,128]{2,1,0:T(8,128)(2,1)S(1)}, bf16[1,256,128]{2,1,0:T(8,128)(2,1)S(1)}, u32[]{:S(2)}, u32[]{:S(2)}) collective-permute-start(bf16[1,256,128]{2,1,0:T(8,128)(2,1)S(1)} %get-tuple-element.54), channel_id=1, source_target_pairs={{0,16},{4,20},{8,24},{12,28},{16,0},{20,4},{24,8},{28,12},{1,17},{... | collective-permute-start | bytes 196616 | tf_op jit(solution)/shard_map/ppermute | solution.py:488
  35.6 1.3 collective-permute-start.5
  36.9 3.4 %collective-permute-start.6 = (bf16[1,256,128]{2,1,0:T(8,128)(2,1)S(1)}, bf16[1,256,128]{2,1,0:T(8,128)(2,1)S(1)}, u32[]{:S(2)}, u32[]{:S(2)}) collective-permute-start(bf16[1,256,128]{2,1,0:T(8,128)(2,1)S(1)} %get-tuple-element.57), channel_id=1, source_target_pairs={{0,28},{4,24},{8,20},{12,16},{16,12},{20,8},{24,4},{28,0},{1,29},{... | collective-permute-start | bytes 196616 | tf_op jit(solution)/shard_map/ppermute | solution.py:488
  40.3 3.5 %project.2 = (bf16[2,216,256]{2,1,0:T(8,128)(2,1)S(1)}, f32[3,216,256]{2,1,0:T(8,128)}, f32[3,216,256]{2,1,0:T(8,128)}, f32[4,2,144,128]{3,2,1,0:T(8,128)S(1)}, ...) custom-call(bf16[2,256,128]{2,1,0:T(8,128)(2,1)S(1)} %get-tuple-element.49.refs_1_.ref, ...), custom_call_target="tpu_custom_call" | custom-call | flops 20000000000 | bytes 60000000 | tf_op jit(solution)/shard_map/project/pallas_call | solution.py:95
  44.4 1.9 %project.3 = (bf16[1,216,256]{2,1,0:T(8,128)(2,1)S(1)}, f32[3,216,256]{2,1,0:T(8,128)}, f32[3,216,256]{2,1,0:T(8,128)}, f32[4,1,144,128]{3,2,1,0:T(8,128)S(1)}, ...) custom-call(bf16[1,256,128]{2,1,0:T(8,128)(2,1)S(1)} %get-tuple-elem, ...), custom_call_target="tpu_custom_call", output_to_operand_aliasing={{1}: (11, {}), {2}: (12, {})} | custom-call | flops 10000000000 | bytes 30000000 | tf_op jit(solution)/shard_map/project/pallas_call | solution.py:95
  46.8 1.2 collective-permute-start.14
  48.1 2.5 %collective-permute-start.21 = (bf16[1,2,216,256]{3,2,1,0:T(8,128)(2,1)S(1)}, bf16[1,2,216,256]{3,2,1,0:T(8,128)(2,1)S(1)}, u32[]{:S(2)}, u32[]{:S(2)}) collective-permute-start(bf16[1,2,216,256]{3,2,1,0:T(8,128)(2,1)S(1)} %bitcast.29), channel_id=1, source_target_pairs={{0,8},{4,12},{8,0},{12,4},{16,24},{20,28},{24,16},{28,20},{1,9},{5... | collective-permute-start | bytes 663560 | tf_op jit(solution)/shard_map/ppermute | solution.py:488
  50.6 1.6 %collective-permute-start.20 = (f32[2,3,144,128]{3,2,1,0:T(8,128)S(1)}, f32[2,3,144,128]{3,2,1,0:T(8,128)S(1)}, u32[]{:S(2)}, u32[]{:S(2)}) collective-permute-start(f32[2,3,144,128]{3,2,1,0:T(8,128)S(1)} %get-tuple-element.77.refs_4_), channel_id=1, source_target_pairs={{0,2},{1,3},{2,0},{3,1},{4,6},{5,7},{6,4},{7,5},{8,10},{9,11},{10,... | collective-permute-start | bytes 1327112 | tf_op jit(solution)/shard_map/ppermute | solution.py:488
  52.3 1.1 collective-permute-start.23
  53.5 0.9 collective-permute-start.19
  54.4 2.3 %collective-permute-done.21.refs_1_ = bf16[1,2,216,256]{3,2,1,0:T(8,128)(2,1)S(1)} collective-permute-done((bf16[1,2,216,256]{3,2,1,0:T(8,128)(2,1)S(1)}, bf16[1,2,216,256]{3,2,1,0:T(8,128)(2,1)S(1)}, u32[]{:S(2)}, u32[]{:S(2)}) %collective-permute-start.21) | collective-permute-done | bytes 221216 | tf_op jit(solution)/shard_map/ppermute | solution.py:488
  57.5 5.1 %collective-permute-done.20.refs_1_ = f32[2,3,144,128]{3,2,1,0:T(8,128)S(1)} collective-permute-done((f32[2,3,144,128]{3,2,1,0:T(8,128)S(1)}, f32[2,3,144,128]{3,2,1,0:T(8,128)S(1)}, u32[]{:S(2)}, u32[]{:S(2)}) %collective-permute-start.20) | collective-permute-done | bytes 442400 | tf_op jit(solution)/shard_map/ppermute | solution.py:488
  62.6 1.2 collective-permute-start.22
  64.0 1.4 %collective-permute-start.27 = (f32[1,3,144,128]{3,2,1,0:T(8,128)S(1)}, f32[1,3,144,128]{3,2,1,0:T(8,128)S(1)}, u32[]{:S(2)}, u32[]{:S(2)}) collective-permute-start(f32[1,3,144,128]{3,2,1,0:T(8,128)S(1)} %get-tuple-element.83.refs_2_), channel_id=1, source_target_pairs={{0,2},{1,3},{2,0},{3,1},{4,6},{5,7},{6,4},{7,5},{8,10},{9,11},{10,... | collective-permute-start | bytes 663560 | tf_op jit(solution)/shard_map/ppermute | solution.py:488
  65.5 1.3 collective-permute-start.26
  66.7 2.2 %collective-permute-done.22.refs_1_ = f32[1,3,144,128]{3,2,1,0:T(8,128)S(1)} collective-permute-done((f32[1,3,144,128]{3,2,1,0:T(8,128)S(1)}, f32[1,3,144,128]{3,2,1,0:T(8,128)S(1)}, u32[]{:S(2)}, u32[]{:S(2)}) %collective-permute-start.22) | collective-permute-done | bytes 221216 | tf_op jit(solution)/shard_map/ppermute | solution.py:488
  69.0 3.8 %collective-permute-start.24 = (f32[1,3,144,128]{3,2,1,0:T(8,128)S(1)}, f32[1,3,144,128]{3,2,1,0:T(8,128)S(1)}, u32[]{:S(2)}, u32[]{:S(2)}) collective-permute-start(f32[1,3,144,128]{3,2,1,0:T(8,128)S(1)} %sums.14.refs_2_.refs_0_), channel_id=1, source_target_pairs={{0,16},{4,20},{8,24},{12,28},{16,0},{20,4},{24,8},{28,12},{1,17},{... | collective-permute-start | bytes 663560 | tf_op jit(solution)/shard_map/ppermute | solution.py:488
  72.9 9.6 %collective-permute-done.26.refs_2_ = bf16[2,2,216,256]{3,2,1,0:T(8,128)(2,1)S(1)} collective-permute-done((bf16[2,2,216,256]{3,2,1,0:T(8,128)(2,1)S(1)}, bf16[2,2,216,256]{3,2,1,0:T(8,128)(2,1)S(1)}, u32[]{:S(2)}, u32[]{:S(2)}) %collective-permute-start.26) | collective-permute-done | bytes 442400 | tf_op jit(solution)/shard_map/ppermute | solution.py:516
  82.5 0.7 collective-permute-start.30
  83.3 4.1 %collective-permute-done.24.refs_1_ = f32[1,3,144,128]{3,2,1,0:T(8,128)S(1)} collective-permute-done((f32[1,3,144,128]{3,2,1,0:T(8,128)S(1)}, f32[1,3,144,128]{3,2,1,0:T(8,128)S(1)}, u32[]{:S(2)}, u32[]{:S(2)}) %collective-permute-start.24) | collective-permute-done | bytes 221216 | tf_op jit(solution)/shard_map/ppermute | solution.py:488
  88.2 1.5 %collective-permute-done.31.refs_1_ = f32[1,3,144,128]{3,2,1,0:T(8,128)S(1)} collective-permute-done((f32[1,3,144,128]{3,2,1,0:T(8,128)S(1)}, f32[1,3,144,128]{3,2,1,0:T(8,128)S(1)}, u32[]{:S(2)}, u32[]{:S(2)}) %collective-permute-start.31) | collective-permute-done | bytes 221216 | tf_op jit(solution)/shard_map/ppermute | solution.py:488
  89.8 2.1 %collective-permute-start.32 = (f32[1,3,144,128]{3,2,1,0:T(8,128)S(1)}, f32[1,3,144,128]{3,2,1,0:T(8,128)S(1)}, u32[]{:S(2)}, u32[]{:S(2)}) collective-permute-start(f32[1,3,144,128]{3,2,1,0:T(8,128)S(1)} %sums.17.refs_2_.refs_0_), channel_id=1, source_target_pairs={{0,8},{4,12},{8,0},{12,4},{16,24},{20,28},{24,16},{28,20},{1,9},{5... | collective-permute-start | bytes 663560 | tf_op jit(solution)/shard_map/ppermute | solution.py:488
  91.8 4.0 %collective-permute-done.33.refs_1_ = f32[1,3,144,128]{3,2,1,0:T(8,128)S(1)} collective-permute-done((f32[1,3,144,128]{3,2,1,0:T(8,128)S(1)}, f32[1,3,144,128]{3,2,1,0:T(8,128)S(1)}, u32[]{:S(2)}, u32[]{:S(2)}) %collective-permute-start.33) | collective-permute-done | bytes 221216 | tf_op jit(solution)/shard_map/ppermute | solution.py:488
  95.9 1.4 %collective-permute-start.35 = (f32[1,3,144,128]{3,2,1,0:T(8,128)S(1)}, f32[1,3,144,128]{3,2,1,0:T(8,128)S(1)}, u32[]{:S(2)}, u32[]{:S(2)}) collective-permute-start(f32[1,3,144,128]{3,2,1,0:T(8,128)S(1)} %sums.18.refs_2_.refs_0_), channel_id=1, source_target_pairs={{0,4},{4,0},{8,12},{12,8},{16,20},{20,16},{24,28},{28,24},{1,5},{5... | collective-permute-start | bytes 663560 | tf_op jit(solution)/shard_map/ppermute | solution.py:488
  97.3 1.8 %collective-permute-done.32.refs_1_ = f32[1,3,144,128]{3,2,1,0:T(8,128)S(1)} collective-permute-done((f32[1,3,144,128]{3,2,1,0:T(8,128)S(1)}, f32[1,3,144,128]{3,2,1,0:T(8,128)S(1)}, u32[]{:S(2)}, u32[]{:S(2)}) %collective-permute-start.32) | collective-permute-done | bytes 221216 | tf_op jit(solution)/shard_map/ppermute | solution.py:488
  99.1 1.6 %collective-permute-start.34 = (f32[1,3,144,128]{3,2,1,0:T(8,128)S(1)}, f32[1,3,144,128]{3,2,1,0:T(8,128)S(1)}, u32[]{:S(2)}, u32[]{:S(2)}) collective-permute-start(f32[1,3,144,128]{3,2,1,0:T(8,128)S(1)} %sums.19.refs_4_.refs_0_), channel_id=1, source_target_pairs={{0,2},{1,3},{2,0},{3,1},{4,6},{5,7},{6,4},{7,5},{8,10},{9,11},{10,... | collective-permute-start | bytes 663560 | tf_op jit(solution)/shard_map/ppermute | solution.py:488
  100.7 1.3 collective-permute-start.29
  102.0 3.2 %collective-permute-done.30.refs_3_ = bf16[4,2,216,256]{3,2,1,0:T(8,128)(2,1)S(1)} collective-permute-done((bf16[4,2,216,256]{3,2,1,0:T(8,128)(2,1)S(1)}, bf16[4,2,216,256]{3,2,1,0:T(8,128)(2,1)S(1)}, u32[]{:S(2)}, u32[]{:S(2)}) %collective-permute-start.30) | collective-permute-done | bytes 884768 | tf_op jit(solution)/shard_map/ppermute | solution.py:488
  105.2 1.6 %weight_step.3 = (f32[3,144,1728]{2,1,0:T(8,128)}, f32[8,128]{1,0:T(8,128)S(1)}) custom-call(f32[3,144,1728]{2,1,0:T(8,128)S(1)} %copy-done, bf16[3,1152,256]{2,1,0:T(8,128)(2,1)S(1)} %bitcast.22, bf16[4,2,216,256]{3,2,1,0:T(8,128)(2,1)S(1)} %collect.1.refs_2_, bf16[4,2,216,256]{3,2,1,0:T(8,128)(2,1)S(1)} %collective-permute-done.30.refs_3_, ...), custom_call_target="tpu_custom_call" | custom-call | flops 8000000000 | bytes 24000000 | tf_op jit(solution)/shard_map/weight_step/pallas_call | solution.py:95
  106.8 1.2 collective-permute-done.35.refs_1_
  108.0 1.6 %collective-permute-start.36 = (f32[2,3,144,128]{3,2,1,0:T(8,128)S(1)}, f32[2,3,144,128]{3,2,1,0:T(8,128)S(1)}, u32[]{:S(2)}, u32[]{:S(2)}) collective-permute-start(f32[2,3,144,128]{3,2,1,0:T(8,128)S(1)} %join.8.refs_2_.refs_0_), channel_id=1, source_target_pairs={{0,2},{1,3},{2,0},{3,1},{4,6},{5,7},{6,4},{7,5},{8,10},{9,11},{10,... | collective-permute-start | bytes 1327112 | tf_op jit(solution)/shard_map/ppermute | solution.py:488
  110.5 1.6 %weight_step.4 = (f32[3,144,1728]{2,1,0:T(8,128)}, f32[8,128]{1,0:T(8,128)S(1)}) custom-call(f32[3,144,1728]{2,1,0:T(8,128)S(1)} %copy-done, bf16[3,1152,256]{2,1,0:T(8,128)(2,1)S(1)} %bitcast.23, bf16[4,2,216,256]{3,2,1,0:T(8,128)(2,1)S(1)} %collect.1.refs_2_, ...), custom_call_target="tpu_custom_call", output_to_operand_aliasing={{0}: (4, {})} | custom-call | flops 8000000000 | bytes 24000000 | tf_op jit(solution)/shard_map/weight_step/pallas_call | solution.py:95
  112.1 7.5 %collective-permute-done.39.refs_5_ = f32[2,3,144,128]{3,2,1,0:T(8,128)S(1)} collective-permute-done((f32[2,3,144,128]{3,2,1,0:T(8,128)S(1)}, f32[2,3,144,128]{3,2,1,0:T(8,128)S(1)}, u32[]{:S(2)}, u32[]{:S(2)}) %collective-permute-start.39) | collective-permute-done | bytes 442400 | tf_op jit(solution)/shard_map/ppermute | solution.py:488
  120.2 1.8 %weight_step.5 = (f32[3,144,1728]{2,1,0:T(8,128)}, f32[8,128]{1,0:T(8,128)S(1)}) custom-call(f32[3,144,1728]{2,1,0:T(8,128)S(1)} %copy-done, bf16[3,1152,256]{2,1,0:T(8,128)(2,1)S(1)} %bitcast.24, bf16[4,1,216,256]{3,2,1,0:T(8,128)(2,1)S(1)} %join.7.refs_2_, ...), custom_call_target="tpu_custom_call", output_to_operand_aliasing={{0}: (5, {})} | custom-call | flops 8000000000 | bytes 24000000 | tf_op jit(solution)/shard_map/weight_step/pallas_call | solution.py:95
  122.1 8.6 %newton_schulz.1 = (bf16[3,1152,256]{2,1,0:T(8,128)(2,1)}, f32[8,128]{1,0:T(8,128)}) custom-call(f32[2,3,144,128]{3,2,1,0:T(8,128)S(1)} %join.8.refs_2_.refs_0_, f32[2,3,144,128]{3,2,1,0:T(8,128)S(1)} %collective-permute-done.36.refs_1_, f32[2,3,144,128]{3,2,1,0:T(8,128)S(1)} %collective-permute-done.37.refs_2_, ...), custom_call_target="tpu_custom_call" | custom-call | flops 80000000000 | bytes 240000000 | tf_op jit(solution)/shard_map/newton_schulz/pallas_call | solution.py:95
  (70 shorter events, 4.9 us)
Async XLA Ops:
  0.6 1.4 %copy-start.2 = (bf16[3,144,1728]{2,1,0:T(8,128)(2,1)S(1)}, bf16[3,144,1728]{2,1,0:T(8,128)(2,1)}, u32[]{:S(2)}) copy-start(bf16[3,144,1728]{2,1,0:T(8,128)(2,1)} %refs_0_.6) | copy-start | bytes 4478980
  4.1 14.7 %collective-permute-start.12 = (bf16[2,256,128]{2,1,0:T(8,128)(2,1)S(1)}, bf16[2,256,128]{2,1,0:T(8,128)(2,1)S(1)}, u32[]{:S(2)}, u32[]{:S(2)}) collective-permute-start(bf16[2,256,128]{2,1,0:T(8,128)(2,1)S(1)} %get-tuple-element.63), channel_id=1, source_target_pairs={{0,24},{4,28},{8,16},{12,20},{16,8},{20,12},{24,0},{28,4},{1,25},{... | collective-permute-start | bytes 393224 | tf_op jit(solution)/shard_map/ppermute | solution.py:488
  9.2 17.7 %collective-permute-start.10 = (bf16[2,256,128]{2,1,0:T(8,128)(2,1)S(1)}, bf16[2,256,128]{2,1,0:T(8,128)(2,1)S(1)}, u32[]{:S(2)}, u32[]{:S(2)}) collective-permute-start(bf16[2,256,128]{2,1,0:T(8,128)(2,1)S(1)} %get-tuple-element.61), channel_id=1, source_target_pairs={{0,16},{4,20},{8,24},{12,28},{16,0},{20,4},{24,8},{28,12},{1,17},{... | collective-permute-start | bytes 393224 | tf_op jit(solution)/shard_map/ppermute | solution.py:488
  9.2 31.1 %copy-start.1 = (bf16[1152,3,256]{2,0,1:T(8,128)(2,1)S(1)}, bf16[1152,3,256]{2,0,1:T(8,128)(2,1)}, u32[]{:S(2)}) copy-start(bf16[1152,3,256]{2,0,1:T(8,128)(2,1)} %param.7) | copy-start | bytes 5308420
  9.2 31.1 %copy-start.3 = (f32[3,256,1,216]{1,3,2,0:T(8,128)S(1)}, f32[3,256,1,216]{1,3,2,0:T(8,128)}, u32[]{:S(2)}) copy-start(f32[3,256,1,216]{1,3,2,0:T(8,128)} %param.8) | copy-start | bytes 1990660
  9.2 31.1 %copy-start.4 = (f32[3,256,1,216]{1,3,2,0:T(8,128)S(1)}, f32[3,256,1,216]{1,3,2,0:T(8,128)}, u32[]{:S(2)}) copy-start(f32[3,256,1,216]{1,3,2,0:T(8,128)} %param.9) | copy-start | bytes 1990660
  10.2 4.4 %collective-permute-start = (bf16[1,256,128]{2,1,0:T(8,128)(2,1)S(1)}, bf16[1,256,128]{2,1,0:T(8,128)(2,1)S(1)}, u32[]{:S(2)}, u32[]{:S(2)}) collective-permute-start(bf16[1,256,128]{2,1,0:T(8,128)(2,1)S(1)} %get-tuple-element.51), channel_id=1, source_target_pairs={{0,4},{4,0},{8,12},{12,8},{16,20},{20,16},{24,28},{28,24},{1,5},{5... | collective-permute-start | bytes 196616 | tf_op jit(solution)/shard_map/ppermute | solution.py:488
  11.8 5.6 %collective-permute-start.1 = (bf16[1,256,128]{2,1,0:T(8,128)(2,1)S(1)}, bf16[1,256,128]{2,1,0:T(8,128)(2,1)S(1)}, u32[]{:S(2)}, u32[]{:S(2)}) collective-permute-start(bf16[1,256,128]{2,1,0:T(8,128)(2,1)S(1)} %get-tuple-element.52), channel_id=1, source_target_pairs={{0,8},{4,12},{8,0},{12,4},{16,24},{20,28},{24,16},{28,20},{1,9},{5... | collective-permute-start | bytes 196616 | tf_op jit(solution)/shard_map/ppermute | solution.py:488
  12.6 18.0 %collective-permute-start.11 = (bf16[2,256,128]{2,1,0:T(8,128)(2,1)S(1)}, bf16[2,256,128]{2,1,0:T(8,128)(2,1)S(1)}, u32[]{:S(2)}, u32[]{:S(2)}) collective-permute-start(bf16[2,256,128]{2,1,0:T(8,128)(2,1)S(1)} %get-tuple-element.62), channel_id=1, source_target_pairs={{0,20},{4,16},{8,28},{12,24},{16,4},{20,0},{24,12},{28,8},{1,21},{... | collective-permute-start | bytes 393224 | tf_op jit(solution)/shard_map/ppermute | solution.py:488
  14.7 15.9 %collective-permute-start.13 = (bf16[2,256,128]{2,1,0:T(8,128)(2,1)S(1)}, bf16[2,256,128]{2,1,0:T(8,128)(2,1)S(1)}, u32[]{:S(2)}, u32[]{:S(2)}) collective-permute-start(bf16[2,256,128]{2,1,0:T(8,128)(2,1)S(1)} %get-tuple-element.64), channel_id=1, source_target_pairs={{0,28},{4,24},{8,20},{12,16},{16,12},{20,8},{24,4},{28,0},{1,29},{... | collective-permute-start | bytes 393224 | tf_op jit(solution)/shard_map/ppermute | solution.py:488
  17.4 18.2 %collective-permute-start.7 = (bf16[2,256,128]{2,1,0:T(8,128)(2,1)S(1)}, bf16[2,256,128]{2,1,0:T(8,128)(2,1)S(1)}, u32[]{:S(2)}, u32[]{:S(2)}) collective-permute-start(bf16[2,256,128]{2,1,0:T(8,128)(2,1)S(1)} %get-tuple-element.58), channel_id=1, source_target_pairs={{0,4},{4,0},{8,12},{12,8},{16,20},{20,16},{24,28},{28,24},{1,5},{5... | collective-permute-start | bytes 393224 | tf_op jit(solution)/shard_map/ppermute | solution.py:488
  18.8 16.8 %collective-permute-start.8 = (bf16[2,256,128]{2,1,0:T(8,128)(2,1)S(1)}, bf16[2,256,128]{2,1,0:T(8,128)(2,1)S(1)}, u32[]{:S(2)}, u32[]{:S(2)}) collective-permute-start(bf16[2,256,128]{2,1,0:T(8,128)(2,1)S(1)} %get-tuple-element.59), channel_id=1, source_target_pairs={{0,8},{4,12},{8,0},{12,4},{16,24},{20,28},{24,16},{28,20},{1,9},{5... | collective-permute-start | bytes 393224 | tf_op jit(solution)/shard_map/ppermute | solution.py:488
  26.9 10.0 %collective-permute-start.9 = (bf16[2,256,128]{2,1,0:T(8,128)(2,1)S(1)}, bf16[2,256,128]{2,1,0:T(8,128)(2,1)S(1)}, u32[]{:S(2)}, u32[]{:S(2)}) collective-permute-start(bf16[2,256,128]{2,1,0:T(8,128)(2,1)S(1)} %get-tuple-element.60), channel_id=1, source_target_pairs={{0,12},{4,8},{8,4},{12,0},{16,28},{20,24},{24,20},{28,16},{1,13},{... | collective-permute-start | bytes 393224 | tf_op jit(solution)/shard_map/ppermute | solution.py:488
  30.6 13.3 %collective-permute-start.2 = (bf16[1,256,128]{2,1,0:T(8,128)(2,1)S(1)}, bf16[1,256,128]{2,1,0:T(8,128)(2,1)S(1)}, u32[]{:S(2)}, u32[]{:S(2)}) collective-permute-start(bf16[1,256,128]{2,1,0:T(8,128)(2,1)S(1)} %get-tuple-element.53), channel_id=1, source_target_pairs={{0,12},{4,8},{8,4},{12,0},{16,28},{20,24},{24,20},{28,16},{1,13},{... | collective-permute-start | bytes 196616 | tf_op jit(solution)/shard_map/ppermute | solution.py:488
  30.6 13.3 %collective-permute-start.3 = (bf16[1,256,128]{2,1,0:T(8,128)(2,1)S(1)}, bf16[1,256,128]{2,1,0:T(8,128)(2,1)S(1)}, u32[]{:S(2)}, u32[]{:S(2)}) collective-permute-start(bf16[1,256,128]{2,1,0:T(8,128)(2,1)S(1)} %get-tuple-element.54), channel_id=1, source_target_pairs={{0,16},{4,20},{8,24},{12,28},{16,0},{20,4},{24,8},{28,12},{1,17},{... | collective-permute-start | bytes 196616 | tf_op jit(solution)/shard_map/ppermute | solution.py:488
  35.6 8.8 %collective-permute-start.4 = (bf16[1,256,128]{2,1,0:T(8,128)(2,1)S(1)}, bf16[1,256,128]{2,1,0:T(8,128)(2,1)S(1)}, u32[]{:S(2)}, u32[]{:S(2)}) collective-permute-start(bf16[1,256,128]{2,1,0:T(8,128)(2,1)S(1)} %get-tuple-element.55), channel_id=1, source_target_pairs={{0,20},{4,16},{8,28},{12,24},{16,4},{20,0},{24,12},{28,8},{1,21},{... | collective-permute-start | bytes 196616 | tf_op jit(solution)/shard_map/ppermute | solution.py:488
  35.6 8.8 %collective-permute-start.5 = (bf16[1,256,128]{2,1,0:T(8,128)(2,1)S(1)}, bf16[1,256,128]{2,1,0:T(8,128)(2,1)S(1)}, u32[]{:S(2)}, u32[]{:S(2)}) collective-permute-start(bf16[1,256,128]{2,1,0:T(8,128)(2,1)S(1)} %get-tuple-element.56), channel_id=1, source_target_pairs={{0,24},{4,28},{8,16},{12,20},{16,8},{20,12},{24,0},{28,4},{1,25},{... | collective-permute-start | bytes 196616 | tf_op jit(solution)/shard_map/ppermute | solution.py:488
  36.9 7.5 %collective-permute-start.6 = (bf16[1,256,128]{2,1,0:T(8,128)(2,1)S(1)}, bf16[1,256,128]{2,1,0:T(8,128)(2,1)S(1)}, u32[]{:S(2)}, u32[]{:S(2)}) collective-permute-start(bf16[1,256,128]{2,1,0:T(8,128)(2,1)S(1)} %get-tuple-element.57), channel_id=1, source_target_pairs={{0,28},{4,24},{8,20},{12,16},{16,12},{20,8},{24,4},{28,0},{1,29},{... | collective-permute-start | bytes 196616 | tf_op jit(solution)/shard_map/ppermute | solution.py:488
  43.8 6.7 %collective-permute-start.17 = (f32[4,2,144,128]{3,2,1,0:T(8,128)S(1)}, f32[4,2,144,128]{3,2,1,0:T(8,128)S(1)}, u32[]{:S(2)}, u32[]{:S(2)}) collective-permute-start(f32[4,2,144,128]{3,2,1,0:T(8,128)S(1)} %get-tuple-element.75), channel_id=1, source_target_pairs={{0,1},{1,0},{2,3},{3,2},{4,5},{5,4},{6,7},{7,6},{8,9},{9,8},{10,11... | collective-permute-start | bytes 1769480 | tf_op jit(solution)/shard_map/ppermute | solution.py:488
  43.9 8.4 %collective-permute-start.15 = (f32[4,2,144,128]{3,2,1,0:T(8,128)S(1)}, f32[4,2,144,128]{3,2,1,0:T(8,128)S(1)}, u32[]{:S(2)}, u32[]{:S(2)}) collective-permute-start(f32[4,2,144,128]{3,2,1,0:T(8,128)S(1)} %get-tuple-element.71), channel_id=1, source_target_pairs={{0,1},{1,0},{2,3},{3,2},{4,5},{5,4},{6,7},{7,6},{8,9},{9,8},{10,11... | collective-permute-start | bytes 1769480 | tf_op jit(solution)/shard_map/ppermute | solution.py:488
  46.3 1.7 %collective-permute-start.18 = (f32[4,1,144,128]{3,2,1,0:T(8,128)S(1)}, f32[4,1,144,128]{3,2,1,0:T(8,128)S(1)}, u32[]{:S(2)}, u32[]{:S(2)}) collective-permute-start(f32[4,1,144,128]{3,2,1,0:T(8,128)S(1)} %get-tuple-element.76), channel_id=1, source_target_pairs={{0,1},{1,0},{2,3},{3,2},{4,5},{5,4},{6,7},{7,6},{8,9},{9,8},{10,11... | collective-permute-start | bytes 884744 | tf_op jit(solution)/shard_map/ppermute | solution.py:488
  46.4 5.8 %collective-permute-start.16 = (f32[4,1,144,128]{3,2,1,0:T(8,128)S(1)}, f32[4,1,144,128]{3,2,1,0:T(8,128)S(1)}, u32[]{:S(2)}, u32[]{:S(2)}) collective-permute-start(f32[4,1,144,128]{3,2,1,0:T(8,128)S(1)} %get-tuple-element.72), channel_id=1, source_target_pairs={{0,1},{1,0},{2,3},{3,2},{4,5},{5,4},{6,7},{7,6},{8,9},{9,8},{10,11... | collective-permute-start | bytes 884744 | tf_op jit(solution)/shard_map/ppermute | solution.py:488
  46.8 6.7 %collective-permute-start.14 = (bf16[1,1,216,256]{3,2,1,0:T(8,128)(2,1)S(1)}, bf16[1,1,216,256]{3,2,1,0:T(8,128)(2,1)S(1)}, u32[]{:S(2)}, u32[]{:S(2)}) collective-permute-start(bf16[1,1,216,256]{3,2,1,0:T(8,128)(2,1)S(1)} %bitcast.31), channel_id=1, source_target_pairs={{0,4},{4,0},{8,12},{12,8},{16,20},{20,16},{24,28},{28,24},{1,5},{5... | collective-permute-start | bytes 331784 | tf_op jit(solution)/shard_map/ppermute | solution.py:488
  48.1 8.7 %collective-permute-start.21 = (bf16[1,2,216,256]{3,2,1,0:T(8,128)(2,1)S(1)}, bf16[1,2,216,256]{3,2,1,0:T(8,128)(2,1)S(1)}, u32[]{:S(2)}, u32[]{:S(2)}) collective-permute-start(bf16[1,2,216,256]{3,2,1,0:T(8,128)(2,1)S(1)} %bitcast.29), channel_id=1, source_target_pairs={{0,8},{4,12},{8,0},{12,4},{16,24},{20,28},{24,16},{28,20},{1,9},{5... | collective-permute-start | bytes 663560 | tf_op jit(solution)/shard_map/ppermute | solution.py:488
  50.6 11.9 %collective-permute-start.20 = (f32[2,3,144,128]{3,2,1,0:T(8,128)S(1)}, f32[2,3,144,128]{3,2,1,0:T(8,128)S(1)}, u32[]{:S(2)}, u32[]{:S(2)}) collective-permute-start(f32[2,3,144,128]{3,2,1,0:T(8,128)S(1)} %get-tuple-element.77.refs_4_), channel_id=1, source_target_pairs={{0,2},{1,3},{2,0},{3,1},{4,6},{5,7},{6,4},{7,5},{8,10},{9,11},{10,... | collective-permute-start | bytes 1327112 | tf_op jit(solution)/shard_map/ppermute | solution.py:488
  52.3 11.7 %collective-permute-start.23 = (f32[2,3,144,128]{3,2,1,0:T(8,128)S(1)}, f32[2,3,144,128]{3,2,1,0:T(8,128)S(1)}, u32[]{:S(2)}, u32[]{:S(2)}) collective-permute-start(f32[2,3,144,128]{3,2,1,0:T(8,128)S(1)} %get-tuple-element.78.refs_2_), channel_id=1, source_target_pairs={{0,4},{4,0},{8,12},{12,8},{16,20},{20,16},{24,28},{28,24},{1,5},{5... | collective-permute-start | bytes 1327112 | tf_op jit(solution)/shard_map/ppermute | solution.py:488
  53.5 34.0 %collective-permute-start.19 = (bf16[2,1,216,256]{3,2,1,0:T(8,128)(2,1)S(1)}, bf16[2,1,216,256]{3,2,1,0:T(8,128)(2,1)S(1)}, u32[]{:S(2)}, u32[]{:S(2)}) collective-permute-start(bf16[2,1,216,256]{3,2,1,0:T(8,128)(2,1)S(1)} %join.5.refs_2_.refs_0_), channel_id=1, source_target_pairs={{0,8},{4,12},{8,0},{12,4},{16,24},{20,28},{24,16},{28,20},{1,9},{5... | collective-permute-start | bytes 663560 | tf_op jit(solution)/shard_map/ppermute | solution.py:488
  56.8 8.7 %collective-permute-start.25 = (bf16[2,2,216,256]{3,2,1,0:T(8,128)(2,1)S(1)}, bf16[2,2,216,256]{3,2,1,0:T(8,128)(2,1)S(1)}, u32[]{:S(2)}, u32[]{:S(2)}) collective-permute-start(bf16[2,2,216,256]{3,2,1,0:T(8,128)(2,1)S(1)} %join.6.refs_2_.refs_0_), channel_id=1, source_target_pairs={{8,16},{12,20},{16,8},{20,12},{9,17},{13,21},{17,9},{21,13},{10,18... | collective-permute-start | bytes 1327112 | tf_op jit(solution)/shard_map/ppermute | solution.py:512
  62.6 6.3 %collective-permute-start.22 = (f32[1,3,144,128]{3,2,1,0:T(8,128)S(1)}, f32[1,3,144,128]{3,2,1,0:T(8,128)S(1)}, u32[]{:S(2)}, u32[]{:S(2)}) collective-permute-start(f32[1,3,144,128]{3,2,1,0:T(8,128)S(1)} %get-tuple-element.81.refs_2_), channel_id=1, source_target_pairs={{0,4},{4,0},{8,12},{12,8},{16,20},{20,16},{24,28},{28,24},{1,5},{5... | collective-permute-start | bytes 663560 | tf_op jit(solution)/shard_map/ppermute | solution.py:488
  64.0 8.7 %collective-permute-start.27 = (f32[1,3,144,128]{3,2,1,0:T(8,128)S(1)}, f32[1,3,144,128]{3,2,1,0:T(8,128)S(1)}, u32[]{:S(2)}, u32[]{:S(2)}) collective-permute-start(f32[1,3,144,128]{3,2,1,0:T(8,128)S(1)} %get-tuple-element.83.refs_2_), channel_id=1, source_target_pairs={{0,2},{1,3},{2,0},{3,1},{4,6},{5,7},{6,4},{7,5},{8,10},{9,11},{10,... | collective-permute-start | bytes 663560 | tf_op jit(solution)/shard_map/ppermute | solution.py:488
  65.5 17.0 %collective-permute-start.26 = (bf16[2,2,216,256]{3,2,1,0:T(8,128)(2,1)S(1)}, bf16[2,2,216,256]{3,2,1,0:T(8,128)(2,1)S(1)}, u32[]{:S(2)}, u32[]{:S(2)}) collective-permute-start(bf16[2,2,216,256]{3,2,1,0:T(8,128)(2,1)S(1)} %collective-permute-done.25.refs_1_), channel_id=1, source_target_pairs={{8,0},{12,4},{16,24},{20,28},{9,1},{13,5},{17,25},{21,29},{10,2},{... | collective-permute-start | bytes 1327112 | tf_op jit(solution)/shard_map/ppermute | solution.py:516
  69.0 18.4 %collective-permute-start.24 = (f32[1,3,144,128]{3,2,1,0:T(8,128)S(1)}, f32[1,3,144,128]{3,2,1,0:T(8,128)S(1)}, u32[]{:S(2)}, u32[]{:S(2)}) collective-permute-start(f32[1,3,144,128]{3,2,1,0:T(8,128)S(1)} %sums.14.refs_2_.refs_0_), channel_id=1, source_target_pairs={{0,16},{4,20},{8,24},{12,28},{16,0},{20,4},{24,8},{28,12},{1,17},{... | collective-permute-start | bytes 663560 | tf_op jit(solution)/shard_map/ppermute | solution.py:488
  72.8 17.0 %collective-permute-start.31 = (f32[1,3,144,128]{3,2,1,0:T(8,128)S(1)}, f32[1,3,144,128]{3,2,1,0:T(8,128)S(1)}, u32[]{:S(2)}, u32[]{:S(2)}) collective-permute-start(f32[1,3,144,128]{3,2,1,0:T(8,128)S(1)} %sums.15.refs_3_.refs_0_), channel_id=1, source_target_pairs={{0,16},{4,20},{8,24},{12,28},{16,0},{20,4},{24,8},{28,12},{1,17},{... | collective-permute-start | bytes 663560 | tf_op jit(solution)/shard_map/ppermute | solution.py:488
  82.5 22.6 %collective-permute-start.30 = (bf16[4,2,216,256]{3,2,1,0:T(8,128)(2,1)S(1)}, bf16[4,2,216,256]{3,2,1,0:T(8,128)(2,1)S(1)}, u32[]{:S(2)}, u32[]{:S(2)}) collective-permute-start(bf16[4,2,216,256]{3,2,1,0:T(8,128)(2,1)S(1)} %collect.1.refs_2_), channel_id=1, source_target_pairs={{0,4},{4,0},{8,12},{12,8},{16,20},{20,16},{24,28},{28,24},{1,5},{5... | collective-permute-start | bytes 2654216 | tf_op jit(solution)/shard_map/ppermute | solution.py:488
  87.4 8.4 %collective-permute-start.33 = (f32[1,3,144,128]{3,2,1,0:T(8,128)S(1)}, f32[1,3,144,128]{3,2,1,0:T(8,128)S(1)}, u32[]{:S(2)}, u32[]{:S(2)}) collective-permute-start(f32[1,3,144,128]{3,2,1,0:T(8,128)S(1)} %sums.16.refs_2_.refs_0_), channel_id=1, source_target_pairs={{0,8},{4,12},{8,0},{12,4},{16,24},{20,28},{24,16},{28,20},{1,9},{5... | collective-permute-start | bytes 663560 | tf_op jit(solution)/shard_map/ppermute | solution.py:488
  87.5 13.2 %collective-permute-start.28 = (bf16[4,1,216,256]{3,2,1,0:T(8,128)(2,1)S(1)}, bf16[4,1,216,256]{3,2,1,0:T(8,128)(2,1)S(1)}, u32[]{:S(2)}, u32[]{:S(2)}) collective-permute-start(bf16[4,1,216,256]{3,2,1,0:T(8,128)(2,1)S(1)} %join.7.refs_2_), channel_id=1, source_target_pairs={{8,16},{12,20},{16,8},{20,12},{9,17},{13,21},{17,9},{21,13},{10,18... | collective-permute-start | bytes 1327112 | tf_op jit(solution)/shard_map/ppermute | solution.py:512
  89.8 9.3 %collective-permute-start.32 = (f32[1,3,144,128]{3,2,1,0:T(8,128)S(1)}, f32[1,3,144,128]{3,2,1,0:T(8,128)S(1)}, u32[]{:S(2)}, u32[]{:S(2)}) collective-permute-start(f32[1,3,144,128]{3,2,1,0:T(8,128)S(1)} %sums.17.refs_2_.refs_0_), channel_id=1, source_target_pairs={{0,8},{4,12},{8,0},{12,4},{16,24},{20,28},{24,16},{28,20},{1,9},{5... | collective-permute-start | bytes 663560 | tf_op jit(solution)/shard_map/ppermute | solution.py:488
  95.9 9.3 %copy-start = (f32[3,144,1728]{2,1,0:T(8,128)S(1)}, f32[3,144,1728]{2,1,0:T(8,128)}, u32[]{:S(2)}) copy-start(f32[3,144,1728]{2,1,0:T(8,128)} %refs_0_.9) | copy-start | bytes 8957956
  95.9 12.1 %collective-permute-start.35 = (f32[1,3,144,128]{3,2,1,0:T(8,128)S(1)}, f32[1,3,144,128]{3,2,1,0:T(8,128)S(1)}, u32[]{:S(2)}, u32[]{:S(2)}) collective-permute-start(f32[1,3,144,128]{3,2,1,0:T(8,128)S(1)} %sums.18.refs_2_.refs_0_), channel_id=1, source_target_pairs={{0,4},{4,0},{8,12},{12,8},{16,20},{20,16},{24,28},{28,24},{1,5},{5... | collective-permute-start | bytes 663560 | tf_op jit(solution)/shard_map/ppermute | solution.py:488
  99.1 10.5 %collective-permute-start.34 = (f32[1,3,144,128]{3,2,1,0:T(8,128)S(1)}, f32[1,3,144,128]{3,2,1,0:T(8,128)S(1)}, u32[]{:S(2)}, u32[]{:S(2)}) collective-permute-start(f32[1,3,144,128]{3,2,1,0:T(8,128)S(1)} %sums.19.refs_4_.refs_0_), channel_id=1, source_target_pairs={{0,2},{1,3},{2,0},{3,1},{4,6},{5,7},{6,4},{7,5},{8,10},{9,11},{10,... | collective-permute-start | bytes 663560 | tf_op jit(solution)/shard_map/ppermute | solution.py:488
  100.7 19.5 %collective-permute-start.29 = (bf16[4,1,216,256]{3,2,1,0:T(8,128)(2,1)S(1)}, bf16[4,1,216,256]{3,2,1,0:T(8,128)(2,1)S(1)}, u32[]{:S(2)}, u32[]{:S(2)}) collective-permute-start(bf16[4,1,216,256]{3,2,1,0:T(8,128)(2,1)S(1)} %collective-permute-done.28.refs_3_), channel_id=1, source_target_pairs={{8,0},{12,4},{16,24},{20,28},{9,1},{13,5},{17,25},{21,29},{10,2},{... | collective-permute-start | bytes 1327112 | tf_op jit(solution)/shard_map/ppermute | solution.py:516
  108.0 11.6 %collective-permute-start.36 = (f32[2,3,144,128]{3,2,1,0:T(8,128)S(1)}, f32[2,3,144,128]{3,2,1,0:T(8,128)S(1)}, u32[]{:S(2)}, u32[]{:S(2)}) collective-permute-start(f32[2,3,144,128]{3,2,1,0:T(8,128)S(1)} %join.8.refs_2_.refs_0_), channel_id=1, source_target_pairs={{0,2},{1,3},{2,0},{3,1},{4,6},{5,7},{6,4},{7,5},{8,10},{9,11},{10,... | collective-permute-start | bytes 1327112 | tf_op jit(solution)/shard_map/ppermute | solution.py:488
  109.6 10.0 %collective-permute-start.39 = (f32[2,3,144,128]{3,2,1,0:T(8,128)S(1)}, f32[2,3,144,128]{3,2,1,0:T(8,128)S(1)}, u32[]{:S(2)}, u32[]{:S(2)}) collective-permute-start(f32[2,3,144,128]{3,2,1,0:T(8,128)S(1)} %join.9.refs_5_.refs_4_), channel_id=1, source_target_pairs={{0,4},{4,0},{8,12},{12,8},{16,20},{20,16},{24,28},{28,24},{1,5},{5... | collective-permute-start | bytes 1327112 | tf_op jit(solution)/shard_map/ppermute | solution.py:488
  110.0 12.0 %collective-permute-start.40 = (f32[2,3,144,128]{3,2,1,0:T(8,128)S(1)}, f32[2,3,144,128]{3,2,1,0:T(8,128)S(1)}, u32[]{:S(2)}, u32[]{:S(2)}) collective-permute-start(f32[2,3,144,128]{3,2,1,0:T(8,128)S(1)} %join.9.refs_5_.refs_4_), channel_id=1, source_target_pairs={{0,1},{1,0},{2,3},{3,2},{4,5},{5,4},{6,7},{7,6},{8,9},{9,8},{10,11... | collective-permute-start | bytes 1327112 | tf_op jit(solution)/shard_map/ppermute | solution.py:488
  110.0 12.0 %collective-permute-start.37 = (f32[2,3,144,128]{3,2,1,0:T(8,128)S(1)}, f32[2,3,144,128]{3,2,1,0:T(8,128)S(1)}, u32[]{:S(2)}, u32[]{:S(2)}) collective-permute-start(f32[2,3,144,128]{3,2,1,0:T(8,128)S(1)} %join.8.refs_2_.refs_0_), channel_id=1, source_target_pairs={{0,1},{1,0},{2,3},{3,2},{4,5},{5,4},{6,7},{7,6},{8,9},{9,8},{10,11... | collective-permute-start | bytes 1327112 | tf_op jit(solution)/shard_map/ppermute | solution.py:488
  119.7 2.4 %collective-permute-start.41 = (f32[2,3,144,128]{3,2,1,0:T(8,128)S(1)}, f32[2,3,144,128]{3,2,1,0:T(8,128)S(1)}, u32[]{:S(2)}, u32[]{:S(2)}) collective-permute-start(f32[2,3,144,128]{3,2,1,0:T(8,128)S(1)} %collective-permute-done.39.refs_5_), channel_id=1, source_target_pairs={{0,1},{1,0},{2,3},{3,2},{4,5},{5,4},{6,7},{7,6},{8,9},{9,8},{10,11... | collective-permute-start | bytes 1327112 | tf_op jit(solution)/shard_map/ppermute | solution.py:488
  119.7 2.4 %collective-permute-start.38 = (f32[2,3,144,128]{3,2,1,0:T(8,128)S(1)}, f32[2,3,144,128]{3,2,1,0:T(8,128)S(1)}, u32[]{:S(2)}, u32[]{:S(2)}) collective-permute-start(f32[2,3,144,128]{3,2,1,0:T(8,128)S(1)} %collective-permute-done.36.refs_1_), channel_id=1, source_target_pairs={{0,1},{1,0},{2,3},{3,2},{4,5},{5,4},{6,7},{7,6},{8,9},{9,8},{10,11... | collective-permute-start | bytes 1327112 | tf_op jit(solution)/shard_map/ppermute | solution.py:488
